TPU v7x, 32 devices: a whole 2x2x4 slice. The times are simulated.
32 devices in a mesh: row: 8 (over z, y), col: 4 (over x, core).
Axes of the slice: x: 2, y: 2, z: 4, core: 2. Of those that a mesh axis runs over, the one named last changes fastest.
Arguments:
- pair_slab: bfloat16 [16, 256, 128], P('col', 'row'), may hold values from -6 to 6
- pair_full: bfloat16 [256, 256, 128], P('col', 'row'), may hold values from -6 to 6
- grad_out: bfloat16 [16, 256, 128], P('row', 'col'), may hold values from -0.59765625 to 0.59765625
- w_a_lin: bfloat16 [128, 128], replicated, may hold values from -0.5 to 0.5
- w_a_gate: bfloat16 [128, 128], replicated, may hold values from -0.5 to 0.5
- w_b_lin: bfloat16 [128, 128], replicated, may hold values from -0.5 to 0.5
- w_b_gate: bfloat16 [128, 128], replicated, may hold values from -0.5 to 0.5
- mask_slab: int32 [16], replicated, may hold values 0 or 1
- mask_residue: int32 [256], replicated, may hold values 0 or 1
Outputs:
- grad_slab: bfloat16 [16, 256, 128], P('col', 'row')
- grad_pair: bfloat16 [256, 256, 128], P('col', 'row')
- grad_weights: float32 [4, 128, 128], replicated
All inputs are finite; a program needn't handle non-finite values.
Results may differ from a plain program's by a relative error of at most 0.0057.
Values may be sent and summed in bfloat16 or wider, within the bound.
No kernel may reach another device: no remote copies, remote signals or barrier semaphores. Data moves between devices by JAX's collectives and lax.ppermute only.
A program may use at most 64 MiB of HBM per device.

v0:
```python
import jax
import jax.numpy as jnp
from jax import lax
from jax.sharding import PartitionSpec as P


def forward_gate(pair, w_linear, w_gate, mask):
    linear = jnp.einsum("rkd,dc->rkc", pair, w_linear, preferred_element_type=jnp.float32)
    gate = jnp.einsum("rkd,dc->rkc", pair, w_gate, preferred_element_type=jnp.float32)
    sigmoid = jax.nn.sigmoid(gate)
    value = (mask * sigmoid * linear).astype(jnp.bfloat16)
    return (linear, sigmoid, value)


def gate_back(grad, mask, linear, sigmoid):
    d_linear = (grad * mask * sigmoid).astype(jnp.bfloat16)
    d_gate = (grad * mask * linear * sigmoid * (1.0 - sigmoid)).astype(jnp.bfloat16)
    return (d_linear, d_gate)


def input_grads(pair, d_linear, d_gate, w_linear, w_gate):
    input_grad = jnp.einsum("rkc,dc->rkd", d_linear, w_linear, preferred_element_type=jnp.float32)
    input_grad = input_grad + jnp.einsum(
        "rkc,dc->rkd", d_gate, w_gate, preferred_element_type=jnp.float32
    )
    weight_linear = jnp.einsum("rkd,rkc->dc", pair, d_linear, preferred_element_type=jnp.float32)
    weight_gate = jnp.einsum("rkd,rkc->dc", pair, d_gate, preferred_element_type=jnp.float32)
    return (input_grad.astype(jnp.bfloat16), weight_linear, weight_gate)


def on_device(
    pair_slab, pair_full, grad_out, w_a_lin, w_a_gate, w_b_lin, w_b_gate, mask_slab, mask_residue
):
    own_rows = pair_slab.shape[0]
    own_keys = pair_slab.shape[1]
    own_cols = pair_full.shape[0]
    row_index = lax.axis_index("row")
    col_index = lax.axis_index("col")
    slab_flags = lax.dynamic_slice_in_dim(mask_slab, col_index * own_rows, own_rows).astype(
        jnp.float32
    )
    key_flags = lax.dynamic_slice_in_dim(mask_residue, row_index * own_keys, own_keys).astype(
        jnp.float32
    )
    col_flags = lax.dynamic_slice_in_dim(mask_residue, col_index * own_cols, own_cols).astype(
        jnp.float32
    )
    slab_mask = (slab_flags[:, None] * key_flags[None, :])[:, :, None]
    pair_mask = (col_flags[:, None] * key_flags[None, :])[:, :, None]
    slab_linear, slab_sigmoid, slab_value = forward_gate(pair_slab, w_a_lin, w_a_gate, slab_mask)
    slab_all = lax.all_gather(slab_value, "col", axis=0, tiled=True)
    grad_all = lax.all_gather(grad_out, "row", axis=0, tiled=True)
    pair_linear, pair_sigmoid, pair_value = forward_gate(pair_full, w_b_lin, w_b_gate, pair_mask)
    pair_grad = jnp.einsum("ijc,ikc->jkc", grad_all, slab_all, preferred_element_type=jnp.float32)
    pair_dlin, pair_dgate = gate_back(pair_grad, pair_mask, pair_linear, pair_sigmoid)
    grad_pair, pair_lin_w, pair_gate_w = input_grads(
        pair_full, pair_dlin, pair_dgate, w_b_lin, w_b_gate
    )
    partial_value = jnp.einsum(
        "ijc,jkc->ikc", grad_all, pair_value, preferred_element_type=jnp.float32
    )
    summed = lax.psum(partial_value, "col")
    slab_grad = lax.dynamic_slice_in_dim(summed, col_index * own_rows, own_rows, 0)
    slab_dlin, slab_dgate = gate_back(slab_grad, slab_mask, slab_linear, slab_sigmoid)
    grad_slab, slab_lin_w, slab_gate_w = input_grads(
        pair_slab, slab_dlin, slab_dgate, w_a_lin, w_a_gate
    )
    local_weights = jnp.stack([slab_lin_w, slab_gate_w, pair_lin_w, pair_gate_w])
    shares = lax.psum_scatter(local_weights, "col", scatter_dimension=1, tiled=True)
    shares = lax.psum(shares, "row")
    total_weights = lax.all_gather(shares, "col", axis=1, tiled=True)
    residues = own_keys * lax.axis_size("row")
    grad_weights = total_weights / residues
    return (grad_slab, grad_pair, grad_weights)


def solution(mesh):
    return jax.shard_map(
        on_device,
        mesh=mesh,
        in_specs=(
            P("col", "row", None),
            P("col", "row", None),
            P("row", "col", None),
            P(),
            P(),
            P(),
            P(),
            P(),
            P(),
        ),
        out_specs=(P("col", "row", None), P("col", "row", None), P()),
        check_vma=False,
    )
```

profile of v0, /device:TPU:0, one launch (start us, length us, event | category | flops | bytes accessed | tf_op | source)
XLA Modules:
  0.0 215.3 jit_solution(2308602988863661064)
XLA Ops:
  7.2 0.8 dynamic-slice_convert_fusion
  8.0 0.8 dynamic-slice_convert_fusion.1
  8.8 0.9 fusion.6
  9.8 0.9 multiply_convert_fusion.3
  10.7 6.5 %all_gather.10 = bf16[16,32,128]{2,1,0:T(8,128)(2,1)S(1)} all-gather(bf16[4,32,128]{2,1,0:T(8,128)(2,1)S(1)} %get-tuple-element.17), channel_id=1, replica_groups=mesh['row'=8,'col'=4] {'col'}, dimensions={0}, use_global_device_ids=true | all-gather | bytes 163840 | tf_op jit(solution)/shard_map/all_gather | solution.py:51
  17.2 1.2 copy.49
  18.4 31.8 %all_gather.9 = bf16[16,64,128]{2,1,0:T(8,128)(2,1)S(1)} all-gather(bf16[2,64,128]{2,1,0:T(8,128)(2,1)} %param.11), channel_id=1, replica_groups=mesh['row'=8,'col'=4] {'row'}, dimensions={0}, use_global_device_ids=true | all-gather | bytes 294912 | tf_op jit(solution)/shard_map/all_gather | solution.py:52
  50.6 1.6 fusion.21
  52.2 2.5 %copy.51 = f32[128,32,64]{0,1,2:T(8,128)} copy(f32[128,32,64]{2,1,0:T(8,128)S(1)} %fusion.21) | data formatting | bytes 2097152 | tf_op jit(solution)/shard_map/ijc,ikc->jkc/dot_general | solution.py:54
  55.2 2.9 %multiply_convert_fusion = (bf16[64,32,128]{2,1,0:T(8,128)(2,1)}, bf16[64,32,128]{2,1,0:T(8,128)(2,1)}, bf16[64,32,128]{2,1,0:T(8,128)(2,1)S(1)}) fusion(f32[64,32,128]{2,1,0:T(8,128)S(1)} %fusion.16, f32[128,32,64]{0,1,2:T(8,128)} %copy.51, f32[64,32]{1,0:T(8,128)S(1)} %broadcast_multiply_fusion.1, bf16[64,32,128]{2,1,0:T(8,128)(2,1)S(1)} %copy-done, ...), kind=kOutput, calls=%fused_computation.17 | convolution fusion | flops 70778880 | bytes 4235264 | tf_op jit(solution)/shard_map/rkd,dc->rkc/dot_general | solution.py:9
  58.1 1.7 copy.46
  59.8 0.7 fusion.20
  60.5 1.1 copy.48
  61.7 1.4 convolution_bitcast_fusion
  64.7 1.1 fusion.3
  66.1 28.4 %all-reduce.5.cloned.1.call-done = f32[16,32,128]{2,1,0:T(8,128)} async-done(((f32[16,32,128]{2,1,0:T(8,128)}), f32[16,32,128]{2,1,0:T(8,128)}) %all-reduce.5.cloned.1.call-update) | async-done | bytes 262160 | tf_op jit(solution)/shard_map/psum | solution.py:62
  94.5 0.9 multiply_convert_fusion.4
  95.9 0.8 copy.52
  96.9 32.6 %all-reduce.9.cloned.1.call-done = f32[4,128,128]{2,0,1:T(4,128)} async-done(((f32[4,128,128]{2,0,1:T(4,128)}), f32[4,128,128]{2,0,1:T(4,128)}) %all-reduce.9.cloned.1.call-update) | async-done | bytes 262160
  129.5 1.5 constant_dynamic-slice_fusion
  131.0 0.8 fusion.7
  131.8 70.2 %all-reduce.7.cloned.1.call-done = f32[4,32,128]{2,0,1:T(4,128)} async-done(((f32[4,32,128]{2,0,1:T(4,128)}), f32[4,32,128]{2,0,1:T(4,128)}) %all-reduce.7.cloned.1.call-update) | async-done | bytes 65552 | tf_op jit(solution)/shard_map/psum | solution.py:70
  202.0 6.0 %all_gather.11 = f32[4,128,128]{2,0,1:T(4,128)S(1)} all-gather(f32[4,32,128]{2,0,1:T(4,128)} %all-reduce.7.cloned.1.call-done), channel_id=1, replica_groups=mesh['row'=8,'col'=4] {'col'}, dimensions={1}, use_global_device_ids=true | all-gather | bytes 327680 | tf_op jit(solution)/shard_map/all_gather | solution.py:71
  208.1 0.7 copy.53
  (39 shorter events, 2.9 us)
Async XLA Ops:
  7.2 47.7 %copy-start = (bf16[64,32,128]{2,1,0:T(8,128)(2,1)S(1)}, bf16[64,32,128]{2,1,0:T(8,128)(2,1)}, u32[]{:S(2)}) copy-start(bf16[64,32,128]{2,1,0:T(8,128)(2,1)} %param.10) | copy-start | bytes 1572868
  7.2 87.3 %all-reduce.5.cloned.1.call-start = ((), (), s32[]{:S(2)}) async-start(), calls=%async_computation | async-start | bytes 524288 | tf_op jit(solution)/shard_map/psum | solution.py:62
  52.2 2.6 %copy-start.8 = (s32[256]{0:T(256)S(1)}, s32[256]{0:T(256)}, u32[]{:S(2)}) copy-start(s32[256]{0:T(256)} %param.17) | copy-start | bytes 3076
  52.2 2.7 %copy-start.4 = (bf16[128,128]{1,0:T(8,128)(2,1)S(1)}, bf16[128,128]{1,0:T(8,128)(2,1)}, u32[]{:S(2)}) copy-start(bf16[128,128]{1,0:T(8,128)(2,1)} %param.14) | copy-start | bytes 98308
  52.2 3.0 %copy-start.6 = (bf16[128,128]{1,0:T(8,128)(2,1)S(1)}, bf16[128,128]{1,0:T(8,128)(2,1)}, u32[]{:S(2)}) copy-start(bf16[128,128]{1,0:T(8,128)(2,1)} %param.15) | copy-start | bytes 98308
  60.5 2.7 %copy-start.9 = (u32[32]{0:T(128)S(1)}, u32[32]{0:T(128)}, u32[]{:S(2)}) copy-start(u32[32]{0:T(128)} %constant.30) | copy-start | bytes 388
  60.5 3.9 %copy-start.1 = (bf16[64,32,128]{2,1,0:T(8,128)(2,1)S(1)}, bf16[64,32,128]{2,1,0:T(8,128)(2,1)}, u32[]{:S(2)}) copy-start(bf16[64,32,128]{2,1,0:T(8,128)(2,1)} %get-tuple-element.13) | copy-start | bytes 1572868
  61.6 3.1 %copy-start.2 = (bf16[64,32,128]{2,1,0:T(8,128)(2,1)S(1)}, bf16[64,32,128]{2,1,0:T(8,128)(2,1)}, u32[]{:S(2)}) copy-start(bf16[64,32,128]{2,1,0:T(8,128)(2,1)} %get-tuple-element.12) | copy-start | bytes 1572868
  61.6 67.9 %all-reduce.9.cloned.1.call-start = ((), (), s32[]{:S(2)}) async-start(), calls=%async_computation.2 | async-start | bytes 524288
  64.7 30.8 %copy-start.3 = (bf16[4,32,128]{2,1,0:T(8,128)(2,1)S(1)}, bf16[4,32,128]{2,1,0:T(8,128)(2,1)}, u32[]{:S(2)}) copy-start(bf16[4,32,128]{2,1,0:T(8,128)(2,1)} %param.9) | copy-start | bytes 98308
  65.8 31.0 %copy-start.5 = (bf16[128,128]{1,0:T(8,128)(2,1)S(1)}, bf16[128,128]{1,0:T(8,128)(2,1)}, u32[]{:S(2)}) copy-start(bf16[128,128]{1,0:T(8,128)(2,1)} %param.12) | copy-start | bytes 98308
  65.8 65.3 %copy-start.7 = (bf16[128,128]{1,0:T(8,128)(2,1)S(1)}, bf16[128,128]{1,0:T(8,128)(2,1)}, u32[]{:S(2)}) copy-start(bf16[128,128]{1,0:T(8,128)(2,1)} %param.13) | copy-start | bytes 98308
  96.7 105.3 %all-reduce.7.cloned.1.call-start = ((), (), s32[]{:S(2)}) async-start(), calls=%async_computation.1 | async-start | bytes 131072 | tf_op jit(solution)/shard_map/psum | solution.py:70
Sparse Core Ops, SparseCore 0:
  61.7 32.7 all-reduce.4
  97.5 31.9 all-reduce.8
  133.5 68.4 all-reduce.6
where the time goes:
time: 216 us; the launch traced here: 215 us
  waiting for transfers between devices  131 us (61%)
  blocking collectives  44.3 us (21%)
  between operations  14.6 us (7%)
  matrix products  11.7 us (5%)
  local copies, waits for them, and re-layouts  10.6 us (5%)
  other arithmetic  2.76 us (1%)
    psum x1, waiting for transfers between devices, on_device(): shares = lax.psum(shares, 'row')  70.2 us
    unnamed x4, waiting for transfers between devices  32.7 us
    all_gather x1, blocking collectives, on_device(): grad_all = lax.all_gather(grad_out, 'row', axis=0, tiled=True)  31.8 us
    psum x1, waiting for transfers between devices, on_device(): summed = lax.psum(partial_value, 'col')  28.4 us
    all_gather x1, blocking collectives, on_device(): slab_all = lax.all_gather(slab_value, 'col', axis=0, tiled=True)  6.48 us
    all_gather x1, blocking collectives, on_device(): total_weights = lax.all_gather(shares, 'col', axis=1, tiled=True)  5.98 us
  transfers between devices with their start and end apart: 3, of which 3 were waited for; matrix products, arithmetic and copies ran while one was open for 2% of the time, Pallas kernels for 0%

commit v1 on v0

v1 whole, which is shorter than its diff:
```python
import functools

import jax
import jax.numpy as jnp
from jax import lax
from jax.experimental import pallas as pl
from jax.experimental.pallas import tpu as pltpu
from jax.sharding import PartitionSpec as P

F32 = jnp.float32
BF16 = jnp.bfloat16
VMEM = pl.BlockSpec(memory_space=pltpu.VMEM)
SMEM = pl.BlockSpec(memory_space=pltpu.SMEM)
J_STEP = 4
I_STEP = 16


def bits_of(size):
    return [1 << b for b in range(size.bit_length() - 1)]


def swap(value, axis, bit):
    size = lax.axis_size(axis)
    return lax.ppermute(value, axis, [(d, d ^ bit) for d in range(size)])


def params(mib=32):
    return pltpu.CompilerParams(vmem_limit_bytes=mib * 1024 * 1024)


def cost(flops, bytes_accessed, transcendentals=0):
    return pl.CostEstimate(
        flops=flops, bytes_accessed=bytes_accessed, transcendentals=transcendentals
    )


def key_mask(flags_row, start, keys):
    residues = flags_row.shape[1]
    lane = lax.broadcasted_iota(jnp.int32, (keys, residues), 1)
    want = lax.broadcasted_iota(jnp.int32, (keys, residues), 0) + start
    picked = jnp.where(lane == want, flags_row.astype(F32), 0.0)
    return jnp.sum(picked, axis=1, keepdims=True)


def project(rows, w_lin, w_gate):
    both = jnp.dot(
        rows, jnp.concatenate([w_lin, w_gate], axis=1), preferred_element_type=F32
    )
    ch = w_lin.shape[1]
    linear = both[:, :ch]
    sigmoid = 1.0 / (1.0 + jnp.exp(-both[:, ch:]))
    return linear, sigmoid


def pair_forward_kernel(
    pair_ref, w_lin_ref, w_gate_ref, flags_ref, flags_row_ref, value_ref, lin_ref, gate_ref
):
    cols, keys, cz = pair_ref.shape
    ch = w_lin_ref.shape[1]
    row, col = lax.axis_index("row"), lax.axis_index("col")
    km = jnp.broadcast_to(key_mask(flags_row_ref[...], row * keys, keys), (keys, ch))
    step = 8

    def body(s, carry):
        j0 = pl.multiple_of(s * step, step)
        rows = pair_ref[pl.ds(j0, step)].reshape(step * keys, cz)
        linear, sigmoid = project(rows, w_lin_ref[...], w_gate_ref[...])
        linear = linear.reshape(step, keys, ch)
        sigmoid = sigmoid.reshape(step, keys, ch)
        for j in range(step):
            m = km * flags_ref[col * cols + j0 + j].astype(F32)
            masked = m * sigmoid[j]
            lin = linear[j]
            value_ref[j0 + j] = (masked * lin).astype(BF16).astype(F32)
            lin_ref[j0 + j] = masked
            gate_ref[j0 + j] = masked * lin * (1.0 - sigmoid[j])
        return carry

    lax.fori_loop(0, cols // step, body, 0)


def pair_forward(pair, w_lin, w_gate, flags):
    cols, keys, cz = pair.shape
    ch = w_lin.shape[1]
    out = jax.ShapeDtypeStruct((cols, keys, ch), F32)
    return pl.pallas_call(
        pair_forward_kernel,
        out_shape=(out, out, out),
        in_specs=[VMEM, VMEM, VMEM, SMEM, VMEM],
        out_specs=(VMEM, VMEM, VMEM),
        compiler_params=params(),
        cost_estimate=cost(4 * cols * keys * cz * ch, 14 * cols * keys * ch, cols * keys * ch),
        name="pair_forward",
    )(pair, w_lin, w_gate, flags, flags[None, :])


def slab_forward_kernel(n_blocks, *refs):
    blocks = refs[:n_blocks]
    (w_lin_ref, w_gate_ref, slab_flags_ref, flags_row_ref) = refs[n_blocks : n_blocks + 4]
    slab_ref, value_ref, lin_ref, gate_ref = refs[n_blocks + 4 :]
    rows, keys, cz = blocks[0].shape
    ch = w_lin_ref.shape[1]
    row, col = lax.axis_index("row"), lax.axis_index("col")
    km = jnp.broadcast_to(key_mask(flags_row_ref[...], row * keys, keys), (keys, ch))
    for b in range(n_blocks):
        first = (col ^ b) * rows
        block = blocks[b][...]
        linear, sigmoid = project(
            block.reshape(rows * keys, cz), w_lin_ref[...], w_gate_ref[...]
        )
        linear = linear.reshape(rows, keys, ch)
        sigmoid = sigmoid.reshape(rows, keys, ch)
        for r in range(rows):
            i = first + r
            m = km * slab_flags_ref[i].astype(F32)
            masked = m * sigmoid[r]
            slab_ref[i] = block[r]
            value_ref[i] = (masked * linear[r]).astype(BF16).astype(F32)
            lin_ref[i] = masked
            gate_ref[i] = masked * linear[r] * (1.0 - sigmoid[r])


def slab_forward(blocks, w_lin, w_gate, slab_flags, flags):
    rows, keys, cz = blocks[0].shape
    n = len(blocks)
    ch = w_lin.shape[1]
    out = jax.ShapeDtypeStruct((n * rows, keys, ch), F32)
    raw = jax.ShapeDtypeStruct((n * rows, keys, cz), BF16)
    return pl.pallas_call(
        functools.partial(slab_forward_kernel, n),
        out_shape=(raw, out, out, out),
        in_specs=[VMEM] * n + [VMEM, VMEM, SMEM, VMEM],
        out_specs=(VMEM,) * 4,
        compiler_params=params(),
        cost_estimate=cost(4 * n * rows * keys * cz * ch, 16 * n * rows * keys * ch),
        name="slab_forward",
    )(*blocks, w_lin, w_gate, slab_flags, flags[None, :])


def main_kernel(
    order,
    grad_ref,
    pair_ref,
    value_ref,
    lin_ref,
    gate_ref,
    slab_ref,
    slab_value_ref,
    slab_lin_ref,
    slab_gate_ref,
    d_lin_ref,
    d_gate_ref,
    sum_keep_ref,
    sum_send_ref,
    w_keep_ref,
    w_send_ref,
    grad_wide,
    slab_sum,
):
    cols, keys, cz = pair_ref.shape
    ch = value_ref.shape[2]
    slab_rows = slab_ref.shape[0]
    per = slab_rows // len(order)
    row, col = lax.axis_index("row"), lax.axis_index("col")
    for p in range(slab_rows):
        i = (row ^ order[p // per]) * per + p % per
        grad_wide[i] = grad_ref[p].astype(F32)
    slab_sum[...] = jnp.zeros_like(slab_sum)

    def step(s, carry):
        j0 = pl.multiple_of(s * J_STEP, J_STEP)
        values = [value_ref[j0 + j] for j in range(J_STEP)]

        def rows_of(t, totals):
            totals = list(totals)
            for u in range(I_STEP):
                i = t * I_STEP + u
                mine = slab_value_ref[i]
                total = slab_sum[i]
                for j in range(J_STEP):
                    g = jnp.broadcast_to(grad_wide[i, pl.ds(j0 + j, 1), :], (keys, ch))
                    totals[j] = totals[j] + g * mine
                    total = total + g * values[j]
                slab_sum[i] = total
            return tuple(totals)

        totals = tuple(jnp.zeros((keys, ch), F32) for _ in range(J_STEP))
        if slab_rows == I_STEP:
            totals = rows_of(0, totals)
        else:
            totals = lax.fori_loop(0, slab_rows // I_STEP, rows_of, totals)
        for j in range(J_STEP):
            d_lin_ref[j0 + j] = (totals[j] * lin_ref[j0 + j]).astype(BF16)
            d_gate_ref[j0 + j] = (totals[j] * gate_ref[j0 + j]).astype(BF16)
        return carry

    lax.fori_loop(0, cols // J_STEP, step, 0)

    def weights(rows, d_lin, d_gate):
        both = jnp.concatenate([d_lin, d_gate], axis=1)
        return lax.dot_general(
            rows, both, (((0,), (0,)), ((), ())), preferred_element_type=F32
        )

    sums = slab_sum[...]
    s_lin = (sums * slab_lin_ref[...]).astype(BF16).reshape(slab_rows * keys, ch)
    s_gate = (sums * slab_gate_ref[...]).astype(BF16).reshape(slab_rows * keys, ch)
    slab_w = weights(slab_ref[...].reshape(slab_rows * keys, cz), s_lin, s_gate)
    pair_w = weights(
        pair_ref[...].reshape(cols * keys, cz),
        d_lin_ref[...].reshape(cols * keys, ch),
        d_gate_ref[...].reshape(cols * keys, ch),
    )
    first = col % 2 == 0
    keep = jnp.where(first, slab_w, pair_w)
    send = jnp.where(first, pair_w, slab_w)
    for h in range(2):
        w_keep_ref[h] = keep[:, h * ch : (h + 1) * ch]
        w_send_ref[h] = send[:, h * ch : (h + 1) * ch]
    halves, own = sum_keep_ref.shape[:2]
    for b in range(halves):
        sum_keep_ref[b] = slab_sum[pl.ds((col ^ (2 * b)) * own, own)]
        sum_send_ref[b] = slab_sum[pl.ds((col ^ (2 * b + 1)) * own, own)]


def main_part(order, n_col, grads, pair, value, lin, gate, slab, s_value, s_lin, s_gate):
    cols, keys, cz = pair.shape
    ch = value.shape[2]
    slab_rows = slab.shape[0]
    own = slab_rows // n_col
    d_type = jax.ShapeDtypeStruct((cols, keys, ch), BF16)
    s_type = jax.ShapeDtypeStruct((n_col // 2, own, keys, ch), F32)
    w_type = jax.ShapeDtypeStruct((2, cz, ch), F32)
    return pl.pallas_call(
        functools.partial(main_kernel, order),
        out_shape=(d_type, d_type, s_type, s_type, w_type, w_type),
        in_specs=[VMEM] * 9,
        out_specs=(VMEM,) * 6,
        scratch_shapes=[
            pltpu.VMEM((slab_rows, cols, ch), F32),
            pltpu.VMEM((slab_rows, keys, ch), F32),
        ],
        compiler_params=params(),
        cost_estimate=cost(8 * cols * keys * cz * ch, 16 * cols * keys * ch),
        name="pair_and_slab_sums",
    )(grads, pair, value, lin, gate, slab, s_value, s_lin, s_gate)


def pair_out_kernel(d_lin_ref, d_gate_ref, w_lin_ref, w_gate_ref, out_ref):
    rows, ch = d_lin_ref.shape
    weights = jnp.concatenate([w_lin_ref[...], w_gate_ref[...]], axis=1)
    step = 256

    def body(s, carry):
        at = pl.ds(pl.multiple_of(s * step, step), step)
        both = jnp.concatenate([d_lin_ref[at, :], d_gate_ref[at, :]], axis=1)
        out = lax.dot_general(
            both, weights, (((1,), (1,)), ((), ())), preferred_element_type=F32
        )
        out_ref[at, :] = out.astype(BF16)
        return carry

    lax.fori_loop(0, rows // step, body, 0)


def pair_out(d_lin, d_gate, w_lin, w_gate):
    cols, keys, ch = d_lin.shape
    cz = w_lin.shape[0]
    out = pl.pallas_call(
        pair_out_kernel,
        out_shape=jax.ShapeDtypeStruct((cols * keys, cz), BF16),
        in_specs=[VMEM] * 4,
        out_specs=VMEM,
        compiler_params=params(),
        cost_estimate=cost(4 * cols * keys * cz * ch, 6 * cols * keys * ch),
        name="pair_input_grad",
    )(d_lin.reshape(cols * keys, ch), d_gate.reshape(cols * keys, ch), w_lin, w_gate)
    return out.reshape(cols, keys, cz)


def slab_out_kernel(sum_ref, got_ref, lin_ref, gate_ref, w_lin_ref, w_gate_ref, out_ref):
    own, keys, ch = sum_ref.shape
    col = lax.axis_index("col")
    at = pl.ds(col * own, own)
    total = sum_ref[...] + got_ref[...].astype(F32)
    d_lin = (total * lin_ref[at]).astype(BF16).reshape(own * keys, ch)
    d_gate = (total * gate_ref[at]).astype(BF16).reshape(own * keys, ch)
    both = jnp.concatenate([d_lin, d_gate], axis=1)
    weights = jnp.concatenate([w_lin_ref[...], w_gate_ref[...]], axis=1)
    out = lax.dot_general(both, weights, (((1,), (1,)), ((), ())), preferred_element_type=F32)
    out_ref[...] = out.astype(BF16).reshape(own, keys, w_lin_ref.shape[0])


def slab_out(total, got, lin, gate, w_lin, w_gate):
    own, keys, ch = total.shape
    cz = w_lin.shape[0]
    return pl.pallas_call(
        slab_out_kernel,
        out_shape=jax.ShapeDtypeStruct((own, keys, cz), BF16),
        in_specs=[VMEM] * 6,
        out_specs=VMEM,
        compiler_params=params(),
        cost_estimate=cost(4 * own * keys * cz * ch, 16 * own * keys * ch),
        name="slab_input_grad",
    )(total, got, lin, gate, w_lin, w_gate)


def on_device(
    pair_slab, pair_full, grad_out, w_a_lin, w_a_gate, w_b_lin, w_b_gate, mask_slab, mask_residue
):
    n_row, n_col = lax.axis_size("row"), lax.axis_size("col")
    row_bits, col_bits = bits_of(n_row), bits_of(n_col)
    residues = mask_residue.shape[0]

    blocks = {0: pair_slab}
    for bit in reversed(col_bits):
        for b in list(blocks):
            blocks[b ^ bit] = swap(blocks[b], "col", bit)
    blocks = [blocks[b] for b in range(n_col)]
    grads, order = grad_out, [0]
    for bit in row_bits[1:] + row_bits[:1]:
        grads = jnp.concatenate([grads, swap(grads, "row", bit)], axis=0)
        order = order + [n ^ bit for n in order]

    value, lin, gate = pair_forward(pair_full, w_b_lin, w_b_gate, mask_residue)
    slab, s_value, s_lin, s_gate = slab_forward(
        blocks, w_a_lin, w_a_gate, mask_slab, mask_residue
    )
    d_lin, d_gate, sum_keep, sum_send, w_keep, w_send = main_part(
        order, n_col, grads, pair_full, value, lin, gate, slab, s_value, s_lin, s_gate
    )
    weights = w_keep + swap(w_send, "col", 1)
    sums = sum_keep + swap(sum_send, "col", 1)
    for bit in col_bits[1:]:
        narrow = weights.astype(BF16)
        weights = narrow.astype(F32) + swap(narrow, "col", bit).astype(F32)
    for bit in row_bits:
        narrow = weights.astype(BF16)
        weights = narrow.astype(F32) + swap(narrow, "row", bit).astype(F32)
    for bit in reversed(col_bits[2:]):
        half = sums.shape[0] // 2
        sums = sums[:half] + swap(sums[half:].astype(BF16), "col", bit).astype(F32)
    got = swap(sums[1].astype(BF16), "col", 2)
    grad_slab = slab_out(sums[0], got, s_lin, s_gate, w_a_lin, w_a_gate)
    grad_pair = pair_out(d_lin, d_gate, w_b_lin, w_b_gate)
    weights = weights / residues
    other = swap(weights, "col", 1)
    first = lax.axis_index("col") % 2 == 0
    grad_weights = jnp.where(
        first,
        jnp.concatenate([weights, other], axis=0),
        jnp.concatenate([other, weights], axis=0),
    )
    return (grad_slab, grad_pair, grad_weights)


def solution(mesh):
    return jax.shard_map(
        on_device,
        mesh=mesh,
        in_specs=(
            P("col", "row", None),
            P("col", "row", None),
            P("row", "col", None),
            P(),
            P(),
            P(),
            P(),
            P(),
            P(),
        ),
        out_specs=(P("col", "row", None), P("col", "row", None), P()),
        check_vma=False,
    )
```

time: 216 us -> 48.6 us (0.23)
  waiting for transfers between devices: 131 us -> 17.3 us
  blocking collectives: 44.3 us -> 0 us
  starting transfers between devices: 0.12 us -> 18.2 us
  between operations: 14.6 us -> 0.83 us
  matrix products: 11.7 us -> 0 us
  local copies, waits for them, and re-layouts: 10.6 us -> 1.09 us
  Pallas kernels: 0 us -> 9.3 us
    psum x2 -> x0, waiting for transfers between devices: 98.6 us -> none  [the longest x1 70.2 us: on_device(): shares = lax.psum(shares, 'row')]
    all_gather x3 -> x0, blocking collectives: 44.3 us -> none  [the longest x1 31.8 us: on_device(): grad_all = lax.all_gather(grad_out, 'row', axis=0, tiled=True)]
    unnamed x4 -> x0, waiting for transfers between devices: 32.7 us -> none
    ppermute x0 -> x14, starting transfers between devices: none -> 18.2 us  [swap(): return lax.ppermute(value, axis, [(d, d ^ bit) for d in range(size)])]
    ppermute x0 -> x14, waiting for transfers between devices: none -> 17.3 us  [swap(): return lax.ppermute(value, axis, [(d, d ^ bit) for d in range(size)])]
    dot_general x14 -> x0, matrix products: 11.7 us -> none  [the longest x2 3.85 us: forward_gate(): jnp.einsum('rkd,dc->rkc', pair, w_gate, preferred_element_type=jnp.float32)]
    pallas_call x0 -> x5, Pallas kernels: none -> 9.3 us  [the longest x1 3.15 us: main_part(): pl.pallas_call(functools.partial(main_kernel, order), out_shape=(d_type,...]
    dot_general x2 -> x0, local copies, waits for them, and re-layouts: 3.64 us -> none  [the longest x1 2.51 us: on_device(): jnp.einsum('ijc,ikc->jkc', grad_all, slab_all, preferred_element_type=jnp...]
  transfers between devices with their start and end apart: 3 -> 14, of which waited for: 3 -> 9; matrix products, arithmetic and copies ran while one was open for 2% -> 0% of each run, Pallas kernels for 0% -> 13%
where the time goes in v1:
time: 48.6 us; the launch traced here: 48.4 us
  starting transfers between devices  18.2 us (37%)
  waiting for transfers between devices  17.3 us (36%)
  Pallas kernels  9.3 us (19%)
  other arithmetic  1.65 us (3%)
  local copies, waits for them, and re-layouts  1.09 us (2%)
  between operations  0.83 us (2%)
    ppermute x14, starting transfers between devices, swap(): return lax.ppermute(value, axis, [(d, d ^ bit) for d in range(size)])  18.2 us
    ppermute x14, waiting for transfers between devices, swap(): return lax.ppermute(value, axis, [(d, d ^ bit) for d in range(size)])  17.3 us
    pallas_call x1, Pallas kernels, main_part(): pl.pallas_call(functools.partial(main_kernel, order), out_shape=(d_type,...  3.15 us
    pallas_call x1, Pallas kernels, pair_out(): pl.pallas_call(pair_out_kernel, out_shape=jax.ShapeDtypeStruct((cols * ke...  2.3 us
    pallas_call x1, Pallas kernels, pair_forward(): pl.pallas_call(pair_forward_kernel, out_shape=(out, out, out), in_specs=[...  2.26 us
    unnamed x20, local copies, waits for them, and re-layouts  1.08 us
  transfers between devices with their start and end apart: 14, of which 9 were waited for; matrix products, arithmetic and copies ran while one was open for 0% of the time, Pallas kernels for 13%

profile of v1, /device:TPU:0, one launch (start us, length us, event | category | flops | bytes accessed | tf_op | source)
XLA Modules:
  0.0 48.4 jit_solution(6244288582727373806)
XLA Ops:
  0.6 3.1 %collective-permute-start = (bf16[2,64,128]{2,1,0:T(8,128)(2,1)}, bf16[2,64,128]{2,1,0:T(8,128)(2,1)S(1)}, u32[]{:S(2)}, u32[]{:S(2)}) collective-permute-start(bf16[2,64,128]{2,1,0:T(8,128)(2,1)} %param.11), channel_id=1, source_target_pairs={{0,8},{4,12},{8,0},{12,4},{16,24},{20,28},{24,16},{28,20},{1,9},{5... | collective-permute-start | bytes 98312 | tf_op jit(solution)/shard_map/ppermute | solution.py:24
  3.7 2.1 %collective-permute-done = bf16[2,64,128]{2,1,0:T(8,128)(2,1)S(1)} collective-permute-done((bf16[2,64,128]{2,1,0:T(8,128)(2,1)}, bf16[2,64,128]{2,1,0:T(8,128)(2,1)S(1)}, u32[]{:S(2)}, u32[]{:S(2)}) %collective-permute-start) | collective-permute-done | bytes 32800 | tf_op jit(solution)/shard_map/ppermute | solution.py:24
  5.8 0.8 %pad_maximum_fusion.2 = bf16[4,64,128]{2,1,0:T(8,128)(2,1)S(1)} fusion(bf16[2,64,128]{2,1,0:T(8,128)(2,1)S(1)} %collective-permute-done, bf16[2,64,128]{2,1,0:T(8,128)(2,1)} %param.11), kind=kLoop, calls=%fused_computation.10 | loop fusion | flops 32768 | bytes 131072 | tf_op jit(solution)/shard_map/concatenate | solution.py:322
  6.6 3.1 %collective-permute-start.1 = (bf16[4,64,128]{2,1,0:T(8,128)(2,1)S(1)}, bf16[4,64,128]{2,1,0:T(8,128)(2,1)S(1)}, u32[]{:S(2)}, u32[]{:S(2)}) collective-permute-start(bf16[4,64,128]{2,1,0:T(8,128)(2,1)S(1)} %pad_maximum_fusion.2), channel_id=1, source_target_pairs={{0,16},{4,20},{8,24},{12,28},{16,0},{20,4},{24,8},{28,12},{1,17},{... | collective-permute-start | bytes 196616 | tf_op jit(solution)/shard_map/ppermute | solution.py:24
  9.7 2.2 %collective-permute-done.1 = bf16[4,64,128]{2,1,0:T(8,128)(2,1)S(1)} collective-permute-done((bf16[4,64,128]{2,1,0:T(8,128)(2,1)S(1)}, bf16[4,64,128]{2,1,0:T(8,128)(2,1)S(1)}, u32[]{:S(2)}, u32[]{:S(2)}) %collective-permute-start.1) | collective-permute-done | bytes 65568 | tf_op jit(solution)/shard_map/ppermute | solution.py:24
  12.0 1.9 %collective-permute-start.2 = (bf16[8,64,128]{2,1,0:T(8,128)(2,1)S(1)}, bf16[8,64,128]{2,1,0:T(8,128)(2,1)S(1)}, u32[]{:S(2)}, u32[]{:S(2)}) collective-permute-start(bf16[8,64,128]{2,1,0:T(8,128)(2,1)S(1)} %pad_maximum_fusion.1), channel_id=1, source_target_pairs={{0,4},{4,0},{8,12},{12,8},{16,20},{20,16},{24,28},{28,24},{1,5},{5... | collective-permute-start | bytes 393224 | tf_op jit(solution)/shard_map/ppermute | solution.py:24
  13.9 1.5 %collective-permute-start.4 = (bf16[4,32,128]{2,1,0:T(8,128)(2,1)S(1)}, bf16[4,32,128]{2,1,0:T(8,128)(2,1)S(1)}, u32[]{:S(2)}, u32[]{:S(2)}) collective-permute-start(bf16[4,32,128]{2,1,0:T(8,128)(2,1)S(1)} %copy-done.6), channel_id=1, source_target_pairs={{0,2},{1,3},{2,0},{3,1},{4,6},{5,7},{6,4},{7,5},{8,10},{9,11},{10,... | collective-permute-start | bytes 98312 | tf_op jit(solution)/shard_map/ppermute | solution.py:24
  15.4 2.4 %collective-permute-done.4.refs_2_ = bf16[4,32,128]{2,1,0:T(8,128)(2,1)S(1)} collective-permute-done((bf16[4,32,128]{2,1,0:T(8,128)(2,1)S(1)}, bf16[4,32,128]{2,1,0:T(8,128)(2,1)S(1)}, u32[]{:S(2)}, u32[]{:S(2)}) %collective-permute-start.4) | collective-permute-done | bytes 32800 | tf_op jit(solution)/shard_map/ppermute | solution.py:24
  17.9 1.0 %copy-done = bf16[64,32,128]{2,1,0:T(8,128)(2,1)S(1)} copy-done((bf16[64,32,128]{2,1,0:T(8,128)(2,1)S(1)}, bf16[64,32,128]{2,1,0:T(8,128)(2,1)}, u32[]{:S(2)}) %copy-start) | copy-done | bytes 524312
  18.9 2.3 %pair_forward.1 = (f32[64,32,128]{2,1,0:T(8,128)S(1)}, f32[64,32,128]{2,1,0:T(8,128)S(1)}, f32[64,32,128]{2,1,0:T(8,128)S(1)}) custom-call(bf16[64,32,128]{2,1,0:T(8,128)(2,1)S(1)} %copy-done, bf16[128,128]{1,0:T(8,128)(2,1)S(1)} %copy-done.2, bf16[128,128]{1,0:T(8,128)(2,1)S(1)} %copy-done.3, s32[256]{0:T(256)S(1)} %copy-done.7, s32[1,256]{1,0:T(1,128)S(1)} %bitcast.10), custom_call_target="tpu_custom_call" | custom-call | flops 134217728 | bytes 3670016 | tf_op jit(solution)/shard_map/pair_forward/pallas_call | solution.py:86
  21.2 0.8 %slab_forward.1 = (bf16[16,32,128]{2,1,0:T(8,128)(2,1)S(1)}, f32[16,32,128]{2,1,0:T(8,128)S(1)}, f32[16,32,128]{2,1,0:T(8,128)S(1)}, f32[16,32,128]{2,1,0:T(8,128)S(1)}) custom-call(bf16[4,32,128]{2,1,0:T(8,128)(2,1)S(1)} %copy-done.6, bf16[4,32,128]{2,1,0:T(8,128)(2,1)S(1)} %collective-permute-done.3.refs_1_, ...), custom_call_target="tpu_custom_call" | custom-call | flops 33554432 | bytes 1048576 | tf_op jit(solution)/shard_map/slab_forward/pallas_call | solution.py:129
  22.1 3.1 %pair_and_slab_sums.1 = (bf16[64,32,128]{2,1,0:T(8,128)(2,1)S(1)}, bf16[64,32,128]{2,1,0:T(8,128)(2,1)S(1)}, f32[2,4,32,128]{3,2,1,0:T(8,128)S(1)}, f32[2,4,32,1...) custom-call(bf16[16,64,128]{2,1,0:T(8,128)(2,1)S(1)} %pad_maximum_fusion.grad_ref, ...), custom_call_target="tpu_custom_call" | custom-call | flops 268435456 | bytes 4194304 | tf_op jit(solution)/shard_map/pair_and_slab_sums/pallas_call | solution.py:234
  25.8 1.0 %collective-permute-done.8 = f32[2,128,128]{2,1,0:T(8,128)S(1)} collective-permute-done((f32[2,128,128]{2,1,0:T(8,128)S(1)}, f32[2,128,128]{2,1,0:T(8,128)S(1)}, u32[]{:S(2)}, u32[]{:S(2)}) %collective-permute-start.8) | collective-permute-done | bytes 131104 | tf_op jit(solution)/shard_map/ppermute | solution.py:24
  26.8 1.6 %collective-permute-start.9 = (bf16[2,128,128]{2,1,0:T(8,128)(2,1)S(1)}, bf16[2,128,128]{2,1,0:T(8,128)(2,1)S(1)}, u32[]{:S(2)}, u32[]{:S(2)}) collective-permute-start(bf16[2,128,128]{2,1,0:T(8,128)(2,1)S(1)} %add_convert_fusion.3), channel_id=1, source_target_pairs={{0,2},{1,3},{2,0},{3,1},{4,6},{5,7},{6,4},{7,5},{8,10},{9,11},{10,... | collective-permute-start | bytes 196616 | tf_op jit(solution)/shard_map/ppermute | solution.py:24
  28.4 2.9 %collective-permute-done.9 = bf16[2,128,128]{2,1,0:T(8,128)(2,1)S(1)} collective-permute-done((bf16[2,128,128]{2,1,0:T(8,128)(2,1)S(1)}, bf16[2,128,128]{2,1,0:T(8,128)(2,1)S(1)}, u32[]{:S(2)}, u32[]{:S(2)}) %collective-permute-start.9) | collective-permute-done | bytes 65568 | tf_op jit(solution)/shard_map/ppermute | solution.py:24
  31.6 4.0 %collective-permute-done.10 = bf16[2,128,128]{2,1,0:T(8,128)(2,1)S(1)} collective-permute-done((bf16[2,128,128]{2,1,0:T(8,128)(2,1)S(1)}, bf16[2,128,128]{2,1,0:T(8,128)(2,1)S(1)}, u32[]{:S(2)}, u32[]{:S(2)}) %collective-permute-start.10) | collective-permute-done | bytes 65568 | tf_op jit(solution)/shard_map/ppermute | solution.py:24
  35.6 1.6 %collective-permute-start.11 = (bf16[2,128,128]{2,1,0:T(8,128)(2,1)S(1)}, bf16[2,128,128]{2,1,0:T(8,128)(2,1)S(1)}, u32[]{:S(2)}, u32[]{:S(2)}) collective-permute-start(bf16[2,128,128]{2,1,0:T(8,128)(2,1)S(1)} %add_convert_fusion.1), channel_id=1, source_target_pairs={{0,8},{4,12},{8,0},{12,4},{16,24},{20,28},{24,16},{28,20},{1,9},{5... | collective-permute-start | bytes 196616 | tf_op jit(solution)/shard_map/ppermute | solution.py:24
  37.3 2.3 %pair_input_grad.1 = bf16[2048,128]{1,0:T(8,128)(2,1)} custom-call(bf16[2048,128]{1,0:T(8,128)(2,1)S(1)} %bitcast.8, bf16[2048,128]{1,0:T(8,128)(2,1)S(1)} %bitcast.9, bf16[128,128]{1,0:T(8,128)(2,1)S(1)} %copy-done.2, bf16[128,128]{1,0:T(8,128)(2,1)S(1)} %copy-done.3), custom_call_target="tpu_custom_call" | custom-call | flops 134217728 | bytes 1572864 | tf_op jit(solution)/shard_map/pair_input_grad/pallas_call | solution.py:269
  40.0 2.9 %collective-permute-start.12 = (bf16[2,128,128]{2,1,0:T(8,128)(2,1)S(1)}, bf16[2,128,128]{2,1,0:T(8,128)(2,1)S(1)}, u32[]{:S(2)}, u32[]{:S(2)}) collective-permute-start(bf16[2,128,128]{2,1,0:T(8,128)(2,1)S(1)} %add_convert_fusion), channel_id=1, source_target_pairs={{0,16},{4,20},{8,24},{12,28},{16,0},{20,4},{24,8},{28,12},{1,17},{... | collective-permute-start | bytes 196616 | tf_op jit(solution)/shard_map/ppermute | solution.py:24
  42.9 1.5 %collective-permute-start.7 = (bf16[4,32,128]{2,1,0:T(8,128)(2,1)S(1)}, bf16[4,32,128]{2,1,0:T(8,128)(2,1)S(1)}, u32[]{:S(2)}, u32[]{:S(2)}) collective-permute-start(bf16[4,32,128]{2,1,0:T(8,128)(2,1)S(1)} %fusion), channel_id=1, source_target_pairs={{0,2},{1,3},{2,0},{3,1},{4,6},{5,7},{6,4},{7,5},{8,10},{9,11},{10,... | collective-permute-start | bytes 98312 | tf_op jit(solution)/shard_map/ppermute | solution.py:24
  44.5 0.8 %collective-permute-done.12 = bf16[2,128,128]{2,1,0:T(8,128)(2,1)S(1)} collective-permute-done((bf16[2,128,128]{2,1,0:T(8,128)(2,1)S(1)}, bf16[2,128,128]{2,1,0:T(8,128)(2,1)S(1)}, u32[]{:S(2)}, u32[]{:S(2)}) %collective-permute-start.12) | collective-permute-done | bytes 65568 | tf_op jit(solution)/shard_map/ppermute | solution.py:24
  45.4 1.5 %collective-permute-done.7.got_ref = bf16[4,32,128]{2,1,0:T(8,128)(2,1)S(1)} collective-permute-done((bf16[4,32,128]{2,1,0:T(8,128)(2,1)S(1)}, bf16[4,32,128]{2,1,0:T(8,128)(2,1)S(1)}, u32[]{:S(2)}, u32[]{:S(2)}) %collective-permute-start.7) | collective-permute-done | bytes 32800 | tf_op jit(solution)/shard_map/ppermute | solution.py:24
  46.9 0.8 %slab_input_grad.1 = bf16[4,32,128]{2,1,0:T(8,128)(2,1)} custom-call(f32[4,32,128]{2,1,0:T(8,128)S(1)} %slice_bitcast_fusion.sum_ref, bf16[4,32,128]{2,1,0:T(8,128)(2,1)S(1)} %collective-permute-done.7.got_ref, f32[16,32,128]{2,1,0:T(8,128)S(1)} %get-tuple-element.21.slab_lin_ref.lin_ref, f32[16,32,128]{2,1,0:T(8,128)S(1)} %get-tuple-element.22.slab_gate_ref.gate_ref, ...), custom_call_target="tpu_custom_call" | custom-call | flops 8388608 | bytes 262144 | tf_op jit(solution)/shard_map/slab_input_grad/pallas_call | solution.py:297
  47.7 0.7 %maximum_select_fusion = f32[4,128,128]{2,1,0:T(8,128)} fusion(f32[2,128,128]{2,1,0:T(8,128)S(1)} %collective-permute-done.13, f32[2,128,128]{2,1,0:T(8,128)S(1)} %add_multiply_fusion, pred[]{:T(512)S(6)} %eq.5), kind=kLoop, calls=%fused_computation.1 | loop fusion | flops 196608 | bytes 524289 | tf_op jit(solution)/shard_map/jit(_where)/select_n | solution.py:349
  (41 shorter events, 1.6 us)
Async XLA Ops:
  0.6 11.3 %copy-start.9 = (bf16[2,64,128]{2,1,0:T(8,128)(2,1)S(1)}, bf16[2,64,128]{2,1,0:T(8,128)(2,1)}, u32[]{:S(2)}) copy-start(bf16[2,64,128]{2,1,0:T(8,128)(2,1)} %param.11) | copy-start | bytes 98308
  0.6 5.2 %collective-permute-start = (bf16[2,64,128]{2,1,0:T(8,128)(2,1)}, bf16[2,64,128]{2,1,0:T(8,128)(2,1)S(1)}, u32[]{:S(2)}, u32[]{:S(2)}) collective-permute-start(bf16[2,64,128]{2,1,0:T(8,128)(2,1)} %param.11), channel_id=1, source_target_pairs={{0,8},{4,12},{8,0},{12,4},{16,24},{20,28},{24,16},{28,20},{1,9},{5... | collective-permute-start | bytes 98312 | tf_op jit(solution)/shard_map/ppermute | solution.py:24
  6.6 7.3 %copy-start.6 = (bf16[4,32,128]{2,1,0:T(8,128)(2,1)S(1)}, bf16[4,32,128]{2,1,0:T(8,128)(2,1)}, u32[]{:S(2)}) copy-start(bf16[4,32,128]{2,1,0:T(8,128)(2,1)} %refs_0_.1) | copy-start | bytes 98308
  6.6 11.2 %copy-start.2 = (bf16[128,128]{1,0:T(8,128)(2,1)S(1)}, bf16[128,128]{1,0:T(8,128)(2,1)}, u32[]{:S(2)}) copy-start(bf16[128,128]{1,0:T(8,128)(2,1)} %w_lin_ref.5) | copy-start | bytes 98308
  6.6 11.2 %copy-start.3 = (bf16[128,128]{1,0:T(8,128)(2,1)S(1)}, bf16[128,128]{1,0:T(8,128)(2,1)}, u32[]{:S(2)}) copy-start(bf16[128,128]{1,0:T(8,128)(2,1)} %w_gate_ref.5) | copy-start | bytes 98308
  6.6 5.3 %collective-permute-start.1 = (bf16[4,64,128]{2,1,0:T(8,128)(2,1)S(1)}, bf16[4,64,128]{2,1,0:T(8,128)(2,1)S(1)}, u32[]{:S(2)}, u32[]{:S(2)}) collective-permute-start(bf16[4,64,128]{2,1,0:T(8,128)(2,1)S(1)} %pad_maximum_fusion.2), channel_id=1, source_target_pairs={{0,16},{4,20},{8,24},{12,28},{16,0},{20,4},{24,8},{28,12},{1,17},{... | collective-permute-start | bytes 196616 | tf_op jit(solution)/shard_map/ppermute | solution.py:24
  12.0 5.9 %copy-start.7 = (s32[256]{0:T(256)S(1)}, s32[256]{0:T(256)}, u32[]{:S(2)}) copy-start(s32[256]{0:T(256)} %flags_ref.1) | copy-start | bytes 3076
  12.0 10.1 %collective-permute-start.2 = (bf16[8,64,128]{2,1,0:T(8,128)(2,1)S(1)}, bf16[8,64,128]{2,1,0:T(8,128)(2,1)S(1)}, u32[]{:S(2)}, u32[]{:S(2)}) collective-permute-start(bf16[8,64,128]{2,1,0:T(8,128)(2,1)S(1)} %pad_maximum_fusion.1), channel_id=1, source_target_pairs={{0,4},{4,0},{8,12},{12,8},{16,20},{20,16},{24,28},{28,24},{1,5},{5... | collective-permute-start | bytes 393224 | tf_op jit(solution)/shard_map/ppermute | solution.py:24
  13.9 3.9 %collective-permute-start.4 = (bf16[4,32,128]{2,1,0:T(8,128)(2,1)S(1)}, bf16[4,32,128]{2,1,0:T(8,128)(2,1)S(1)}, u32[]{:S(2)}, u32[]{:S(2)}) collective-permute-start(bf16[4,32,128]{2,1,0:T(8,128)(2,1)S(1)} %copy-done.6), channel_id=1, source_target_pairs={{0,2},{1,3},{2,0},{3,1},{4,6},{5,7},{6,4},{7,5},{8,10},{9,11},{10,... | collective-permute-start | bytes 98312 | tf_op jit(solution)/shard_map/ppermute | solution.py:24
  15.4 5.8 %collective-permute-start.3 = (bf16[4,32,128]{2,1,0:T(8,128)(2,1)S(1)}, bf16[4,32,128]{2,1,0:T(8,128)(2,1)S(1)}, u32[]{:S(2)}, u32[]{:S(2)}) collective-permute-start(bf16[4,32,128]{2,1,0:T(8,128)(2,1)S(1)} %copy-done.6), channel_id=1, source_target_pairs={{0,1},{1,0},{2,3},{3,2},{4,5},{5,4},{6,7},{7,6},{8,9},{9,8},{10,11... | collective-permute-start | bytes 98312 | tf_op jit(solution)/shard_map/ppermute | solution.py:24
  17.8 3.4 %collective-permute-start.5 = (bf16[4,32,128]{2,1,0:T(8,128)(2,1)S(1)}, bf16[4,32,128]{2,1,0:T(8,128)(2,1)S(1)}, u32[]{:S(2)}, u32[]{:S(2)}) collective-permute-start(bf16[4,32,128]{2,1,0:T(8,128)(2,1)S(1)} %collective-permute-done.4.refs_2_), channel_id=1, source_target_pairs={{0,1},{1,0},{2,3},{3,2},{4,5},{5,4},{6,7},{7,6},{8,9},{9,8},{10,11... | collective-permute-start | bytes 98312 | tf_op jit(solution)/shard_map/ppermute | solution.py:24
  17.9 1.0 %copy-start = (bf16[64,32,128]{2,1,0:T(8,128)(2,1)S(1)}, bf16[64,32,128]{2,1,0:T(8,128)(2,1)}, u32[]{:S(2)}) copy-start(bf16[64,32,128]{2,1,0:T(8,128)(2,1)} %pair_ref.3) | copy-start | bytes 1572868
  18.9 2.3 %copy-start.4 = (bf16[128,128]{1,0:T(8,128)(2,1)S(1)}, bf16[128,128]{1,0:T(8,128)(2,1)}, u32[]{:S(2)}) copy-start(bf16[128,128]{1,0:T(8,128)(2,1)} %w_lin_ref.4) | copy-start | bytes 98308
  18.9 2.3 %copy-start.5 = (bf16[128,128]{1,0:T(8,128)(2,1)S(1)}, bf16[128,128]{1,0:T(8,128)(2,1)}, u32[]{:S(2)}) copy-start(bf16[128,128]{1,0:T(8,128)(2,1)} %w_gate_ref.4) | copy-start | bytes 98308
  18.9 2.3 %copy-start.8 = (s32[16]{0:T(128)S(1)}, s32[16]{0:T(128)}, u32[]{:S(2)}) copy-start(s32[16]{0:T(128)} %refs_6_.1) | copy-start | bytes 196
  18.9 3.2 %copy-start.1 = (bf16[64,32,128]{2,1,0:T(8,128)(2,1)S(1)}, bf16[64,32,128]{2,1,0:T(8,128)(2,1)}, u32[]{:S(2)}) copy-start(bf16[64,32,128]{2,1,0:T(8,128)(2,1)} %pair_ref.3) | copy-start | bytes 1572868
  25.3 1.5 %collective-permute-start.8 = (f32[2,128,128]{2,1,0:T(8,128)S(1)}, f32[2,128,128]{2,1,0:T(8,128)S(1)}, u32[]{:S(2)}, u32[]{:S(2)}) collective-permute-start(f32[2,128,128]{2,1,0:T(8,128)S(1)} %get-tuple-element.28), channel_id=1, source_target_pairs={{0,1},{1,0},{2,3},{3,2},{4,5},{5,4},{6,7},{7,6},{8,9},{9,8},{10,11... | collective-permute-start | bytes 393224 | tf_op jit(solution)/shard_map/ppermute | solution.py:24
  26.8 4.4 %collective-permute-start.9 = (bf16[2,128,128]{2,1,0:T(8,128)(2,1)S(1)}, bf16[2,128,128]{2,1,0:T(8,128)(2,1)S(1)}, u32[]{:S(2)}, u32[]{:S(2)}) collective-permute-start(bf16[2,128,128]{2,1,0:T(8,128)(2,1)S(1)} %add_convert_fusion.3), channel_id=1, source_target_pairs={{0,2},{1,3},{2,0},{3,1},{4,6},{5,7},{6,4},{7,5},{8,10},{9,11},{10,... | collective-permute-start | bytes 196616 | tf_op jit(solution)/shard_map/ppermute | solution.py:24
  31.3 4.3 %collective-permute-start.10 = (bf16[2,128,128]{2,1,0:T(8,128)(2,1)S(1)}, bf16[2,128,128]{2,1,0:T(8,128)(2,1)S(1)}, u32[]{:S(2)}, u32[]{:S(2)}) collective-permute-start(bf16[2,128,128]{2,1,0:T(8,128)(2,1)S(1)} %add_convert_fusion.2), channel_id=1, source_target_pairs={{0,4},{4,0},{8,12},{12,8},{16,20},{20,16},{24,28},{28,24},{1,5},{5... | collective-permute-start | bytes 196616 | tf_op jit(solution)/shard_map/ppermute | solution.py:24
  31.6 8.0 %collective-permute-start.6 = (f32[2,4,32,128]{3,2,1,0:T(8,128)S(1)}, f32[2,4,32,128]{3,2,1,0:T(8,128)S(1)}, u32[]{:S(2)}, u32[]{:S(2)}) collective-permute-start(f32[2,4,32,128]{3,2,1,0:T(8,128)S(1)} %get-tuple-element.24), channel_id=1, source_target_pairs={{0,1},{1,0},{2,3},{3,2},{4,5},{5,4},{6,7},{7,6},{8,9},{9,8},{10,11... | collective-permute-start | bytes 393224 | tf_op jit(solution)/shard_map/ppermute | solution.py:24
  35.6 4.3 %collective-permute-start.11 = (bf16[2,128,128]{2,1,0:T(8,128)(2,1)S(1)}, bf16[2,128,128]{2,1,0:T(8,128)(2,1)S(1)}, u32[]{:S(2)}, u32[]{:S(2)}) collective-permute-start(bf16[2,128,128]{2,1,0:T(8,128)(2,1)S(1)} %add_convert_fusion.1), channel_id=1, source_target_pairs={{0,8},{4,12},{8,0},{12,4},{16,24},{20,28},{24,16},{28,20},{1,9},{5... | collective-permute-start | bytes 196616 | tf_op jit(solution)/shard_map/ppermute | solution.py:24
  40.0 5.2 %collective-permute-start.12 = (bf16[2,128,128]{2,1,0:T(8,128)(2,1)S(1)}, bf16[2,128,128]{2,1,0:T(8,128)(2,1)S(1)}, u32[]{:S(2)}, u32[]{:S(2)}) collective-permute-start(bf16[2,128,128]{2,1,0:T(8,128)(2,1)S(1)} %add_convert_fusion), channel_id=1, source_target_pairs={{0,16},{4,20},{8,24},{12,28},{16,0},{20,4},{24,8},{28,12},{1,17},{... | collective-permute-start | bytes 196616 | tf_op jit(solution)/shard_map/ppermute | solution.py:24
  42.9 4.0 %collective-permute-start.7 = (bf16[4,32,128]{2,1,0:T(8,128)(2,1)S(1)}, bf16[4,32,128]{2,1,0:T(8,128)(2,1)S(1)}, u32[]{:S(2)}, u32[]{:S(2)}) collective-permute-start(bf16[4,32,128]{2,1,0:T(8,128)(2,1)S(1)} %fusion), channel_id=1, source_target_pairs={{0,2},{1,3},{2,0},{3,1},{4,6},{5,7},{6,4},{7,5},{8,10},{9,11},{10,... | collective-permute-start | bytes 98312 | tf_op jit(solution)/shard_map/ppermute | solution.py:24
  45.3 2.4 %collective-permute-start.13 = (f32[2,128,128]{2,1,0:T(8,128)S(1)}, f32[2,128,128]{2,1,0:T(8,128)S(1)}, u32[]{:S(2)}, u32[]{:S(2)}) collective-permute-start(f32[2,128,128]{2,1,0:T(8,128)S(1)} %add_multiply_fusion), channel_id=1, source_target_pairs={{0,1},{1,0},{2,3},{3,2},{4,5},{5,4},{6,7},{7,6},{8,9},{9,8},{10,11... | collective-permute-start | bytes 393224 | tf_op jit(solution)/shard_map/ppermute | solution.py:24

commit v2 on v1

--- a/solution.py
+++ b/solution.py
@@ -10,9 +10,10 @@
 F32 = jnp.float32
 BF16 = jnp.bfloat16
 VMEM = pl.BlockSpec(memory_space=pltpu.VMEM)
+WHOLE = pl.BlockSpec()
 SMEM = pl.BlockSpec(memory_space=pltpu.SMEM)
 J_STEP = 4
-I_STEP = 16
+STAGE_COST = 400000
 
 
 def bits_of(size):
@@ -32,14 +33,6 @@
     return pl.CostEstimate(
         flops=flops, bytes_accessed=bytes_accessed, transcendentals=transcendentals
     )
-
-
-def key_mask(flags_row, start, keys):
-    residues = flags_row.shape[1]
-    lane = lax.broadcasted_iota(jnp.int32, (keys, residues), 1)
-    want = lax.broadcasted_iota(jnp.int32, (keys, residues), 0) + start
-    picked = jnp.where(lane == want, flags_row.astype(F32), 0.0)
-    return jnp.sum(picked, axis=1, keepdims=True)
 
 
 def project(rows, w_lin, w_gate):
@@ -52,23 +45,39 @@
     return linear, sigmoid
 
 
-def pair_forward_kernel(
-    pair_ref, w_lin_ref, w_gate_ref, flags_ref, flags_row_ref, value_ref, lin_ref, gate_ref
-):
+def stage_kernel(n, *refs):
+    for source_ref, copy_ref in zip(refs[:n], refs[n:]):
+        copy_ref[...] = source_ref[...]
+
+
+def stage(*sources):
+    n = len(sources)
+    return pl.pallas_call(
+        functools.partial(stage_kernel, n),
+        out_shape=tuple(jax.ShapeDtypeStruct(s.shape, s.dtype) for s in sources),
+        in_specs=[VMEM] * n,
+        out_specs=(VMEM,) * n,
+        compiler_params=params(),
+        cost_estimate=cost(STAGE_COST * sources[0].size, 4 * sources[0].size),
+        name="stage",
+    )(*sources)
+
+
+def pair_forward_kernel(pair_ref, w_lin_ref, w_gate_ref, flags_ref, value_ref, lin_ref, gate_ref):
     cols, keys, cz = pair_ref.shape
-    ch = w_lin_ref.shape[1]
     row, col = lax.axis_index("row"), lax.axis_index("col")
-    km = jnp.broadcast_to(key_mask(flags_row_ref[...], row * keys, keys), (keys, ch))
+    km = flags_ref[pl.ds(pl.multiple_of(row * keys, 16), keys)].astype(F32)
     step = 8
 
     def body(s, carry):
         j0 = pl.multiple_of(s * step, step)
         rows = pair_ref[pl.ds(j0, step)].reshape(step * keys, cz)
         linear, sigmoid = project(rows, w_lin_ref[...], w_gate_ref[...])
-        linear = linear.reshape(step, keys, ch)
-        sigmoid = sigmoid.reshape(step, keys, ch)
+        linear = linear.reshape(step, keys, -1)
+        sigmoid = sigmoid.reshape(step, keys, -1)
+        flags = flags_ref[pl.ds(pl.multiple_of(col * cols + j0, step), step)].astype(F32)
         for j in range(step):
-            m = km * flags_ref[col * cols + j0 + j].astype(F32)
+            m = km * flags[j : j + 1]
             masked = m * sigmoid[j]
             lin = linear[j]
             value_ref[j0 + j] = (masked * lin).astype(BF16).astype(F32)
@@ -86,115 +95,182 @@
     return pl.pallas_call(
         pair_forward_kernel,
         out_shape=(out, out, out),
-        in_specs=[VMEM, VMEM, VMEM, SMEM, VMEM],
+        in_specs=[VMEM] * 4,
         out_specs=(VMEM, VMEM, VMEM),
         compiler_params=params(),
         cost_estimate=cost(4 * cols * keys * cz * ch, 14 * cols * keys * ch, cols * keys * ch),
         name="pair_forward",
-    )(pair, w_lin, w_gate, flags, flags[None, :])
-
-
-def slab_forward_kernel(n_blocks, *refs):
-    blocks = refs[:n_blocks]
-    (w_lin_ref, w_gate_ref, slab_flags_ref, flags_row_ref) = refs[n_blocks : n_blocks + 4]
-    slab_ref, value_ref, lin_ref, gate_ref = refs[n_blocks + 4 :]
-    rows, keys, cz = blocks[0].shape
-    ch = w_lin_ref.shape[1]
+    )(pair, w_lin, w_gate, flags)
+
+
+def slab_forward_kernel(
+    n_blocks,
+    even_ref,
+    odd_ref,
+    w_lin_ref,
+    w_gate_ref,
+    slab_flags_ref,
+    flags_ref,
+    slab_ref,
+    value_ref,
+    lin_ref,
+    gate_ref,
+):
+    _, keys, cz = even_ref.shape
+    rows = 2 * even_ref.shape[0] // n_blocks
     row, col = lax.axis_index("row"), lax.axis_index("col")
-    km = jnp.broadcast_to(key_mask(flags_row_ref[...], row * keys, keys), (keys, ch))
+    km = flags_ref[pl.ds(pl.multiple_of(row * keys, 16), keys)].astype(F32)
+    flags = slab_flags_ref[...].astype(F32)
+    for i in range(n_blocks * rows):
+        value_ref[i] = km * flags[i : i + 1]
     for b in range(n_blocks):
         first = (col ^ b) * rows
-        block = blocks[b][...]
+        block = (odd_ref if b % 2 else even_ref)[(b // 2) * rows : (b // 2 + 1) * rows]
         linear, sigmoid = project(
-            block.reshape(rows * keys, cz), w_lin_ref[...], w_gate_ref[...]
+            block.reshape(rows * keys, cz),
+            w_lin_ref[...],
+            w_gate_ref[...],
         )
-        linear = linear.reshape(rows, keys, ch)
-        sigmoid = sigmoid.reshape(rows, keys, ch)
+        linear = linear.reshape(rows, keys, -1)
+        sigmoid = sigmoid.reshape(rows, keys, -1)
         for r in range(rows):
             i = first + r
-            m = km * slab_flags_ref[i].astype(F32)
-            masked = m * sigmoid[r]
+            masked = value_ref[i] * sigmoid[r]
             slab_ref[i] = block[r]
             value_ref[i] = (masked * linear[r]).astype(BF16).astype(F32)
             lin_ref[i] = masked
             gate_ref[i] = masked * linear[r] * (1.0 - sigmoid[r])
 
 
-def slab_forward(blocks, w_lin, w_gate, slab_flags, flags):
-    rows, keys, cz = blocks[0].shape
-    n = len(blocks)
+def slab_forward(blocks, n, w_lin, w_gate, slab_flags, flags):
+    half, keys, cz = blocks[0].shape
+    rows = 2 * half // n
     ch = w_lin.shape[1]
     out = jax.ShapeDtypeStruct((n * rows, keys, ch), F32)
     raw = jax.ShapeDtypeStruct((n * rows, keys, cz), BF16)
     return pl.pallas_call(
         functools.partial(slab_forward_kernel, n),
         out_shape=(raw, out, out, out),
-        in_specs=[VMEM] * n + [VMEM, VMEM, SMEM, VMEM],
+        in_specs=[VMEM] * 6,
         out_specs=(VMEM,) * 4,
         compiler_params=params(),
         cost_estimate=cost(4 * n * rows * keys * cz * ch, 16 * n * rows * keys * ch),
         name="slab_forward",
-    )(*blocks, w_lin, w_gate, slab_flags, flags[None, :])
-
-
-def main_kernel(
-    order,
-    grad_ref,
-    pair_ref,
-    value_ref,
-    lin_ref,
-    gate_ref,
-    slab_ref,
-    slab_value_ref,
-    slab_lin_ref,
-    slab_gate_ref,
-    d_lin_ref,
-    d_gate_ref,
-    sum_keep_ref,
-    sum_send_ref,
-    w_keep_ref,
-    w_send_ref,
-    grad_wide,
-    slab_sum,
-):
+    )(*blocks, w_lin, w_gate, slab_flags, flags)
+
+
+def row_of(order, per, p):
+    return (lax.axis_index("row") ^ order[p // per]) * per + p % per
+
+
+def add_rows(cols, keys, grad_ref, rows, value_ref, slab_value_ref, sums_ref, start, finish):
+    ch = value_ref.shape[2]
+
+    def step(s, carry):
+        j0 = pl.multiple_of(s * J_STEP, J_STEP)
+        values = [value_ref[j0 + j] for j in range(J_STEP)]
+        totals = [start(j0 + j) for j in range(J_STEP)]
+        for p, i in enumerate(rows):
+            mine = slab_value_ref[i]
+            total = sums_ref[p]
+            for j in range(J_STEP):
+                g = jnp.broadcast_to(grad_ref[p, pl.ds(j0 + j, 1), :], (keys, ch))
+                totals[j] = totals[j] + g * mine
+                total = total + g * values[j]
+            sums_ref[p] = total
+        for j in range(J_STEP):
+            finish(j0 + j, totals[j])
+        return carry
+
+    lax.fori_loop(0, cols // J_STEP, step, 0)
+
+
+def first_kernel(order, n_grads, *refs):
+    grads, (value_ref, slab_value_ref, total_ref, sums_ref, wide) = refs[:n_grads], refs[n_grads:]
+    cols, keys, ch = value_ref.shape
+    per = grads[0].shape[0] * n_grads // len(order)
+    at = 0
+    for grad_ref in grads:
+        wide[at : at + grad_ref.shape[0]] = grad_ref[...].astype(F32)
+        at += grad_ref.shape[0]
+    sums_ref[...] = jnp.zeros_like(sums_ref)
+    rows = [row_of(order, per, p) for p in range(at)]
+
+    def start(j):
+        return jnp.zeros((keys, ch), F32)
+
+    def finish(j, total):
+        total_ref[j] = total
+
+    add_rows(cols, keys, wide, rows, value_ref, slab_value_ref, sums_ref, start, finish)
+
+
+def first_part(order, grads, value, slab_value):
+    cols, keys, ch = value.shape
+    rows = sum(g.shape[0] for g in grads)
+    return pl.pallas_call(
+        functools.partial(first_kernel, order, len(grads)),
+        out_shape=(
+            jax.ShapeDtypeStruct((cols, keys, ch), F32),
+            jax.ShapeDtypeStruct((rows, keys, ch), F32),
+        ),
+        in_specs=[VMEM] * (len(grads) + 2),
+        out_specs=(VMEM, VMEM),
+        scratch_shapes=[pltpu.VMEM((rows, cols, ch), F32)],
+        compiler_params=params(),
+        cost_estimate=cost(4 * rows * cols * keys * ch, 8 * cols * keys * ch),
+        name="first_rows",
+    )(*grads, value, slab_value)
+
+
+def main_kernel(order, n_grads, *refs):
+    grads = refs[:n_grads]
+    (
+        total_ref,
+        first_sums_ref,
+        pair_ref,
+        value_ref,
+        lin_ref,
+        gate_ref,
+        slab_ref,
+        slab_value_ref,
+        slab_lin_ref,
+        slab_gate_ref,
+        d_lin_ref,
+        d_gate_ref,
+        sum_keep_ref,
+        sum_send_ref,
+        w_keep_ref,
+        w_send_ref,
+        wide,
+        sums_ref,
+        slab_sum,
+    ) = refs[n_grads:]
     cols, keys, cz = pair_ref.shape
     ch = value_ref.shape[2]
     slab_rows = slab_ref.shape[0]
+    done = first_sums_ref.shape[0]
     per = slab_rows // len(order)
-    row, col = lax.axis_index("row"), lax.axis_index("col")
-    for p in range(slab_rows):
-        i = (row ^ order[p // per]) * per + p % per
-        grad_wide[i] = grad_ref[p].astype(F32)
-    slab_sum[...] = jnp.zeros_like(slab_sum)
-
-    def step(s, carry):
-        j0 = pl.multiple_of(s * J_STEP, J_STEP)
-        values = [value_ref[j0 + j] for j in range(J_STEP)]
-
-        def rows_of(t, totals):
-            totals = list(totals)
-            for u in range(I_STEP):
-                i = t * I_STEP + u
-                mine = slab_value_ref[i]
-                total = slab_sum[i]
-                for j in range(J_STEP):
-                    g = jnp.broadcast_to(grad_wide[i, pl.ds(j0 + j, 1), :], (keys, ch))
-                    totals[j] = totals[j] + g * mine
-                    total = total + g * values[j]
-                slab_sum[i] = total
-            return tuple(totals)
-
-        totals = tuple(jnp.zeros((keys, ch), F32) for _ in range(J_STEP))
-        if slab_rows == I_STEP:
-            totals = rows_of(0, totals)
-        else:
-            totals = lax.fori_loop(0, slab_rows // I_STEP, rows_of, totals)
-        for j in range(J_STEP):
-            d_lin_ref[j0 + j] = (totals[j] * lin_ref[j0 + j]).astype(BF16)
-            d_gate_ref[j0 + j] = (totals[j] * gate_ref[j0 + j]).astype(BF16)
-        return carry
-
-    lax.fori_loop(0, cols // J_STEP, step, 0)
+    col = lax.axis_index("col")
+    at = 0
+    for grad_ref in grads:
+        wide[at : at + grad_ref.shape[0]] = grad_ref[...].astype(F32)
+        at += grad_ref.shape[0]
+    sums_ref[...] = jnp.zeros_like(sums_ref)
+    rows = [row_of(order, per, done + p) for p in range(at)]
+
+    def start(j):
+        return total_ref[j]
+
+    def finish(j, total):
+        d_lin_ref[j] = (total * lin_ref[j]).astype(BF16)
+        d_gate_ref[j] = (total * gate_ref[j]).astype(BF16)
+
+    add_rows(cols, keys, wide, rows, value_ref, slab_value_ref, sums_ref, start, finish)
+    for p in range(done):
+        slab_sum[row_of(order, per, p)] = first_sums_ref[p]
+    for p in range(at):
+        slab_sum[rows[p]] = sums_ref[p]
 
     def weights(rows, d_lin, d_gate):
         both = jnp.concatenate([d_lin, d_gate], axis=1)
@@ -223,27 +299,29 @@
         sum_send_ref[b] = slab_sum[pl.ds((col ^ (2 * b + 1)) * own, own)]
 
 
-def main_part(order, n_col, grads, pair, value, lin, gate, slab, s_value, s_lin, s_gate):
+def main_part(order, n_col, grads, first, pair, value, lin, gate, slab, s_value, s_lin, s_gate):
     cols, keys, cz = pair.shape
     ch = value.shape[2]
     slab_rows = slab.shape[0]
+    rows = sum(g.shape[0] for g in grads)
     own = slab_rows // n_col
     d_type = jax.ShapeDtypeStruct((cols, keys, ch), BF16)
     s_type = jax.ShapeDtypeStruct((n_col // 2, own, keys, ch), F32)
     w_type = jax.ShapeDtypeStruct((2, cz, ch), F32)
     return pl.pallas_call(
-        functools.partial(main_kernel, order),
+        functools.partial(main_kernel, order, len(grads)),
         out_shape=(d_type, d_type, s_type, s_type, w_type, w_type),
-        in_specs=[VMEM] * 9,
+        in_specs=[VMEM] * (len(grads) + 10),
         out_specs=(VMEM,) * 6,
         scratch_shapes=[
-            pltpu.VMEM((slab_rows, cols, ch), F32),
+            pltpu.VMEM((rows, cols, ch), F32),
+            pltpu.VMEM((rows, keys, ch), F32),
             pltpu.VMEM((slab_rows, keys, ch), F32),
         ],
         compiler_params=params(),
         cost_estimate=cost(8 * cols * keys * cz * ch, 16 * cols * keys * ch),
-        name="pair_and_slab_sums",
-    )(grads, pair, value, lin, gate, slab, s_value, s_lin, s_gate)
+        name="last_rows",
+    )(*grads, *first, pair, value, lin, gate, slab, s_value, s_lin, s_gate)
 
 
 def pair_out_kernel(d_lin_ref, d_gate_ref, w_lin_ref, w_gate_ref, out_ref):
@@ -312,22 +390,35 @@
     row_bits, col_bits = bits_of(n_row), bits_of(n_col)
     residues = mask_residue.shape[0]
 
-    blocks = {0: pair_slab}
-    for bit in reversed(col_bits):
+    steps = [row_bits[-1]] + row_bits[1:-1] + row_bits[:1]
+    held, own_slab = stage(grad_out, pair_slab)
+    slab_flags, flags = (
+        jnp.broadcast_to(m.astype(BF16)[:, None], m.shape + (w_a_lin.shape[1],))
+        for m in (mask_slab, mask_residue)
+    )
+    order = [0]
+    blocks = {0: own_slab}
+    for bit in reversed(col_bits[1:]):
         for b in list(blocks):
             blocks[b ^ bit] = swap(blocks[b], "col", bit)
-    blocks = [blocks[b] for b in range(n_col)]
-    grads, order = grad_out, [0]
-    for bit in row_bits[1:] + row_bits[:1]:
-        grads = jnp.concatenate([grads, swap(grads, "row", bit)], axis=0)
-        order = order + [n ^ bit for n in order]
-
-    value, lin, gate = pair_forward(pair_full, w_b_lin, w_b_gate, mask_residue)
+    got = swap(grad_out, "row", steps[0])
+    tied = lax.optimization_barrier((flags, got))[0]
+    value, lin, gate = pair_forward(pair_full, w_b_lin, w_b_gate, tied)
+    for bit, last in zip(steps, steps[1:]):
+        if last == steps[-1]:
+            got, value, blocks = lax.optimization_barrier((got, value, blocks))
+        held = jnp.concatenate([held, got], axis=0)
+        order = order + [r ^ bit for r in order]
+        got = swap(held, "row", last)
+    slabs = jnp.concatenate([blocks[b] for b in sorted(blocks)], axis=0)
+    slabs = [slabs, swap(slabs, "col", 1)]
     slab, s_value, s_lin, s_gate = slab_forward(
-        blocks, w_a_lin, w_a_gate, mask_slab, mask_residue
-    )
+        slabs, n_col, w_a_lin, w_a_gate, slab_flags, flags
+    )
+    order = order + [r ^ last for r in order]
+    first = first_part(order[: len(order) // 2], [held], value, s_value)
     d_lin, d_gate, sum_keep, sum_send, w_keep, w_send = main_part(
-        order, n_col, grads, pair_full, value, lin, gate, slab, s_value, s_lin, s_gate
+        order, n_col, [got], first, pair_full, value, lin, gate, slab, s_value, s_lin, s_gate
     )
     weights = w_keep + swap(w_send, "col", 1)
     sums = sum_keep + swap(sum_send, "col", 1)

time: 48.6 us -> 41.9 us (0.86)
  waiting for transfers between devices: 17.3 us -> 12.6 us
  starting transfers between devices: 18.2 us -> 16.2 us
  local copies, waits for them, and re-layouts: 1.09 us -> 3.08 us
  Pallas kernels: 9.3 us -> 8.03 us
  other arithmetic: 1.65 us -> 0.86 us
    ppermute x14 -> x13, waiting for transfers between devices: 17.3 us -> 12.6 us  [swap(): return lax.ppermute(value, axis, [(d, d ^ bit) for d in range(size)])]
    ppermute x14 -> x13, starting transfers between devices: 18.2 us -> 16.2 us  [swap(): return lax.ppermute(value, axis, [(d, d ^ bit) for d in range(size)])]
    unnamed x20 -> x21, local copies, waits for them, and re-layouts: 1.08 us -> 2.88 us
    concatenate x3 -> x1, other arithmetic: 0.81 us -> 0.01 us  [on_device(): held = jnp.concatenate([held, got], axis=0)]
    pallas_call x1, Pallas kernels: 2.26 us -> 1.62 us  [pair_forward(): pl.pallas_call(pair_forward_kernel, out_shape=(out, out, out), in_specs=[...]
    pallas_call x1, Pallas kernels: 0.82 us -> 0.27 us  [slab_forward(): pl.pallas_call(functools.partial(slab_forward_kernel, n), out_shape=(raw,...]
    pallas_call x1 -> x3, Pallas kernels: 3.15 us -> 3.06 us  [the longest x1 1.82 us: main_part(): pl.pallas_call(functools.partial(main_kernel, order, len(grads)), out_sha...]
  transfers between devices with their start and end apart: 14 -> 13, of which waited for: 9 -> 9; matrix products, arithmetic and copies ran while one was open for 0% -> 1% of each run, Pallas kernels for 13% -> 15%
where the time goes in v2:
time: 41.9 us; the launch traced here: 41.6 us
  starting transfers between devices  16.2 us (39%)
  waiting for transfers between devices  12.6 us (30%)
  Pallas kernels  8.03 us (19%)
  local copies, waits for them, and re-layouts  3.08 us (7%)
  other arithmetic  0.86 us (2%)
  between operations  0.8 us (2%)
    ppermute x13, starting transfers between devices, swap(): return lax.ppermute(value, axis, [(d, d ^ bit) for d in range(size)])  16.2 us
    ppermute x13, waiting for transfers between devices, swap(): return lax.ppermute(value, axis, [(d, d ^ bit) for d in range(size)])  12.6 us
    unnamed x21, local copies, waits for them, and re-layouts  2.88 us
    pallas_call x1, Pallas kernels, pair_out(): pl.pallas_call(pair_out_kernel, out_shape=jax.ShapeDtypeStruct((cols * ke...  2.3 us
    pallas_call x1, Pallas kernels, main_part(): pl.pallas_call(functools.partial(main_kernel, order, len(grads)), out_sha...  1.82 us
    pallas_call x1, Pallas kernels, pair_forward(): pl.pallas_call(pair_forward_kernel, out_shape=(out, out, out), in_specs=[...  1.62 us
    pallas_call x1, Pallas kernels, first_part(): pl.pallas_call(functools.partial(first_kernel, order, len(grads)), out_sh...  1.24 us
  transfers between devices with their start and end apart: 13, of which 9 were waited for; matrix products, arithmetic and copies ran while one was open for 1% of the time, Pallas kernels for 15%

profile of v2, /device:TPU:0, one launch (start us, length us, event | category | flops | bytes accessed | tf_op | source)
XLA Modules:
  0.0 41.6 jit_solution(6133825791279297024)
XLA Ops:
  0.6 4.1 %collective-permute-start = (bf16[2,64,128]{2,1,0:T(8,128)(2,1)}, bf16[2,64,128]{2,1,0:T(8,128)(2,1)S(1)}, u32[]{:S(2)}, u32[]{:S(2)}) collective-permute-start(bf16[2,64,128]{2,1,0:T(8,128)(2,1)} %refs_0_.1), channel_id=1, source_target_pairs={{0,16},{4,20},{8,24},{12,28},{16,0},{20,4},{24,8},{28,12},{1,17},{... | collective-permute-start | bytes 98312 | tf_op jit(solution)/shard_map/ppermute | solution.py:25
  4.7 0.8 %copy-done.5 = bf16[4,32,128]{2,1,0:T(8,128)(2,1)S(1)} copy-done((bf16[4,32,128]{2,1,0:T(8,128)(2,1)S(1)}, bf16[4,32,128]{2,1,0:T(8,128)(2,1)}, u32[]{:S(2)}) %copy-start.5) | copy-done | bytes 32792
  5.5 0.8 %copy-done.6 = bf16[2,64,128]{2,1,0:T(8,128)(2,1)S(1)} copy-done((bf16[2,64,128]{2,1,0:T(8,128)(2,1)S(1)}, bf16[2,64,128]{2,1,0:T(8,128)(2,1)}, u32[]{:S(2)}) %copy-start.6) | copy-done | bytes 32792
  6.3 1.5 %collective-permute-start.2 = (bf16[4,32,128]{2,1,0:T(8,128)(2,1)S(1)}, bf16[4,32,128]{2,1,0:T(8,128)(2,1)S(1)}, u32[]{:S(2)}, u32[]{:S(2)}) collective-permute-start(bf16[4,32,128]{2,1,0:T(8,128)(2,1)S(1)} %get-tuple-element.31), channel_id=1, source_target_pairs={{0,2},{1,3},{2,0},{3,1},{4,6},{5,7},{6,4},{7,5},{8,10},{9,11},{10,... | collective-permute-start | bytes 98312 | tf_op jit(solution)/shard_map/ppermute | solution.py:25
  7.8 0.7 %copy-done.7 = s32[256]{0:T(256)S(1)} copy-done((s32[256]{0:T(256)S(1)}, s32[256]{0:T(256)}, u32[]{:S(2)}) %copy-start.7) | copy-done | bytes 1048
  8.5 1.6 %collective-permute-start.1 = (bf16[4,64,128]{2,1,0:T(8,128)(2,1)S(1)}, bf16[4,64,128]{2,1,0:T(8,128)(2,1)S(1)}, u32[]{:S(2)}, u32[]{:S(2)}) collective-permute-start(bf16[4,64,128]{2,1,0:T(8,128)(2,1)S(1)} %pad_maximum_fusion), channel_id=1, source_target_pairs={{0,8},{4,12},{8,0},{12,4},{16,24},{20,28},{24,16},{28,20},{1,9},{5... | collective-permute-start | bytes 196616 | tf_op jit(solution)/shard_map/ppermute | solution.py:25
  10.2 0.6 %copy-done.1 = bf16[128,128]{1,0:T(8,128)(2,1)S(1)} copy-done((bf16[128,128]{1,0:T(8,128)(2,1)S(1)}, bf16[128,128]{1,0:T(8,128)(2,1)}, u32[]{:S(2)}) %copy-start.1) | copy-done | bytes 32792
  10.9 1.6 %pair_forward.1 = (f32[64,32,128]{2,1,0:T(8,128)S(1)}, f32[64,32,128]{2,1,0:T(8,128)S(1)}, f32[64,32,128]{2,1,0:T(8,128)S(1)}) custom-call(bf16[64,32,128]{2,1,0:T(8,128)(2,1)S(1)} %copy-done, bf16[128,128]{1,0:T(8,128)(2,1)S(1)} %copy-done.1, bf16[128,128]{1,0:T(8,128)(2,1)S(1)} %copy-done.2, bf16[256,128]{1,0:T(8,128)(2,1)S(1)} %broadcast_in_dim.4.flags_ref), custom_call_target="tpu_custom_call" | custom-call | flops 134217728 | bytes 3670016 | tf_op jit(solution)/shard_map/pair_forward/pallas_call | solution.py:95
  12.8 1.6 %collective-permute-start.3 = (bf16[8,64,128]{2,1,0:T(8,128)(2,1)S(1)}, bf16[8,64,128]{2,1,0:T(8,128)(2,1)S(1)}, u32[]{:S(2)}, u32[]{:S(2)}) collective-permute-start(bf16[8,64,128]{2,1,0:T(8,128)(2,1)S(1)} %constant_dynamic-update-slice_fusion.refs_0_), channel_id=1, source_target_pairs={{0,4},{4,0},{8,12},{12,8},{16,20},{20,16},{24,28},{28,24},{1,5},{5... | collective-permute-start | bytes 393224 | tf_op jit(solution)/shard_map/ppermute | solution.py:25
  14.5 1.2 %collective-permute-done.4.odd_ref = bf16[8,32,128]{2,1,0:T(8,128)(2,1)S(1)} collective-permute-done((bf16[8,32,128]{2,1,0:T(8,128)(2,1)S(1)}, bf16[8,32,128]{2,1,0:T(8,128)(2,1)S(1)}, u32[]{:S(2)}, u32[]{:S(2)}) %collective-permute-start.4) | collective-permute-done | bytes 65568 | tf_op jit(solution)/shard_map/ppermute | solution.py:25
  16.0 1.2 %first_rows.1 = (f32[64,32,128]{2,1,0:T(8,128)S(1)}, f32[8,32,128]{2,1,0:T(8,128)S(1)}) custom-call(bf16[8,64,128]{2,1,0:T(8,128)(2,1)S(1)} %constant_dynamic-update-slice_fusion.refs_0_, f32[64,32,128]{2,1,0:T(8,128)S(1)} %get-tuple-element.30.refs_1_.refs_4_, f32[16,32,128]{2,1,0:T(8,128)S(1)} %get-tuple-element.33.refs_2_.refs_8_), custom_call_target="tpu_custom_call" | custom-call | flops 8388608 | bytes 2097152 | tf_op jit(solution)/shard_map/first_rows/pallas_call | solution.py:211
  17.9 1.8 %last_rows.1 = (bf16[64,32,128]{2,1,0:T(8,128)(2,1)S(1)}, bf16[64,32,128]{2,1,0:T(8,128)(2,1)S(1)}, f32[2,4,32,128]{3,2,1,0:T(8,128)S(1)}, f32[2,4,32,128]{3,2,1...) custom-call(bf16[8,64,128]{2,1,0:T(8,128)(2,1)S(1)} %collective-permute-done.3.refs_0_, ...), custom_call_target="tpu_custom_call" | custom-call | flops 268435456 | bytes 4194304 | tf_op jit(solution)/shard_map/last_rows/pallas_call | solution.py:311
  19.8 1.3 %collective-permute-done.7 = f32[2,128,128]{2,1,0:T(8,128)S(1)} collective-permute-done((f32[2,128,128]{2,1,0:T(8,128)S(1)}, f32[2,128,128]{2,1,0:T(8,128)S(1)}, u32[]{:S(2)}, u32[]{:S(2)}) %collective-permute-start.7) | collective-permute-done | bytes 131104 | tf_op jit(solution)/shard_map/ppermute | solution.py:25
  21.1 0.6 %collective-permute-start.8 = (bf16[2,128,128]{2,1,0:T(8,128)(2,1)S(1)}, bf16[2,128,128]{2,1,0:T(8,128)(2,1)S(1)}, u32[]{:S(2)}, u32[]{:S(2)}) collective-permute-start(bf16[2,128,128]{2,1,0:T(8,128)(2,1)S(1)} %add_convert_fusion.3), channel_id=1, source_target_pairs={{0,2},{1,3},{2,0},{3,1},{4,6},{5,7},{6,4},{7,5},{8,10},{9,11},{10,... | collective-permute-start | bytes 196616 | tf_op jit(solution)/shard_map/ppermute | solution.py:25
  21.7 3.7 %collective-permute-done.8 = bf16[2,128,128]{2,1,0:T(8,128)(2,1)S(1)} collective-permute-done((bf16[2,128,128]{2,1,0:T(8,128)(2,1)S(1)}, bf16[2,128,128]{2,1,0:T(8,128)(2,1)S(1)}, u32[]{:S(2)}, u32[]{:S(2)}) %collective-permute-start.8) | collective-permute-done | bytes 65568 | tf_op jit(solution)/shard_map/ppermute | solution.py:25
  25.5 1.6 %collective-permute-start.9 = (bf16[2,128,128]{2,1,0:T(8,128)(2,1)S(1)}, bf16[2,128,128]{2,1,0:T(8,128)(2,1)S(1)}, u32[]{:S(2)}, u32[]{:S(2)}) collective-permute-start(bf16[2,128,128]{2,1,0:T(8,128)(2,1)S(1)} %add_convert_fusion.2), channel_id=1, source_target_pairs={{0,4},{4,0},{8,12},{12,8},{16,20},{20,16},{24,28},{28,24},{1,5},{5... | collective-permute-start | bytes 196616 | tf_op jit(solution)/shard_map/ppermute | solution.py:25
  27.1 2.7 %collective-permute-done.9 = bf16[2,128,128]{2,1,0:T(8,128)(2,1)S(1)} collective-permute-done((bf16[2,128,128]{2,1,0:T(8,128)(2,1)S(1)}, bf16[2,128,128]{2,1,0:T(8,128)(2,1)S(1)}, u32[]{:S(2)}, u32[]{:S(2)}) %collective-permute-start.9) | collective-permute-done | bytes 65568 | tf_op jit(solution)/shard_map/ppermute | solution.py:25
  29.8 1.6 %collective-permute-start.10 = (bf16[2,128,128]{2,1,0:T(8,128)(2,1)S(1)}, bf16[2,128,128]{2,1,0:T(8,128)(2,1)S(1)}, u32[]{:S(2)}, u32[]{:S(2)}) collective-permute-start(bf16[2,128,128]{2,1,0:T(8,128)(2,1)S(1)} %add_convert_fusion.1), channel_id=1, source_target_pairs={{0,8},{4,12},{8,0},{12,4},{16,24},{20,28},{24,16},{28,20},{1,9},{5... | collective-permute-start | bytes 196616 | tf_op jit(solution)/shard_map/ppermute | solution.py:25
  31.5 2.3 %pair_input_grad.1 = bf16[2048,128]{1,0:T(8,128)(2,1)} custom-call(bf16[2048,128]{1,0:T(8,128)(2,1)S(1)} %bitcast.7, bf16[2048,128]{1,0:T(8,128)(2,1)S(1)} %bitcast.8, bf16[128,128]{1,0:T(8,128)(2,1)S(1)} %copy-done.1, bf16[128,128]{1,0:T(8,128)(2,1)S(1)} %copy-done.2), custom_call_target="tpu_custom_call" | custom-call | flops 134217728 | bytes 1572864 | tf_op jit(solution)/shard_map/pair_input_grad/pallas_call | solution.py:347
  34.2 1.4 %collective-permute-start.11 = (bf16[2,128,128]{2,1,0:T(8,128)(2,1)S(1)}, bf16[2,128,128]{2,1,0:T(8,128)(2,1)S(1)}, u32[]{:S(2)}, u32[]{:S(2)}) collective-permute-start(bf16[2,128,128]{2,1,0:T(8,128)(2,1)S(1)} %add_convert_fusion), channel_id=1, source_target_pairs={{0,16},{4,20},{8,24},{12,28},{16,0},{20,4},{24,8},{28,12},{1,17},{... | collective-permute-start | bytes 196616 | tf_op jit(solution)/shard_map/ppermute | solution.py:25
  35.6 2.0 %collective-permute-start.6 = (bf16[4,32,128]{2,1,0:T(8,128)(2,1)S(1)}, bf16[4,32,128]{2,1,0:T(8,128)(2,1)S(1)}, u32[]{:S(2)}, u32[]{:S(2)}) collective-permute-start(bf16[4,32,128]{2,1,0:T(8,128)(2,1)S(1)} %fusion), channel_id=1, source_target_pairs={{0,2},{1,3},{2,0},{3,1},{4,6},{5,7},{6,4},{7,5},{8,10},{9,11},{10,... | collective-permute-start | bytes 98312 | tf_op jit(solution)/shard_map/ppermute | solution.py:25
  37.6 1.8 %collective-permute-done.11 = bf16[2,128,128]{2,1,0:T(8,128)(2,1)S(1)} collective-permute-done((bf16[2,128,128]{2,1,0:T(8,128)(2,1)S(1)}, bf16[2,128,128]{2,1,0:T(8,128)(2,1)S(1)}, u32[]{:S(2)}, u32[]{:S(2)}) %collective-permute-start.11) | collective-permute-done | bytes 65568 | tf_op jit(solution)/shard_map/ppermute | solution.py:25
  39.6 0.8 %slab_input_grad.1 = bf16[4,32,128]{2,1,0:T(8,128)(2,1)} custom-call(f32[4,32,128]{2,1,0:T(8,128)S(1)} %slice_bitcast_fusion.sum_ref, bf16[4,32,128]{2,1,0:T(8,128)(2,1)S(1)} %collective-permute-done.6.got_ref, f32[16,32,128]{2,1,0:T(8,128)S(1)} %get-tuple-element.39.refs_9_.lin_ref, f32[16,32,128]{2,1,0:T(8,128)S(1)} %get-tuple-element.40.refs_10_.gate_ref, ...), custom_call_target="tpu_custom_call" | custom-call | flops 8388608 | bytes 262144 | tf_op jit(solution)/shard_map/slab_input_grad/pallas_call | solution.py:375
  40.9 0.7 %maximum_select_fusion = f32[4,128,128]{2,1,0:T(8,128)} fusion(f32[2,128,128]{2,1,0:T(8,128)S(1)} %collective-permute-done.12, f32[2,128,128]{2,1,0:T(8,128)S(1)} %add_multiply_fusion, pred[]{:T(512)S(6)} %eq.5), kind=kLoop, calls=%fused_computation | loop fusion | flops 196608 | bytes 524289 | tf_op jit(solution)/shard_map/jit(_where)/select_n | solution.py:440
  (46 shorter events, 2.6 us)
Async XLA Ops:
  0.6 9.6 %copy-start = (bf16[64,32,128]{2,1,0:T(8,128)(2,1)S(1)}, bf16[64,32,128]{2,1,0:T(8,128)(2,1)}, u32[]{:S(2)}) copy-start(bf16[64,32,128]{2,1,0:T(8,128)(2,1)} %refs_3_.1) | copy-start | bytes 1572868
  0.6 7.8 %collective-permute-start = (bf16[2,64,128]{2,1,0:T(8,128)(2,1)}, bf16[2,64,128]{2,1,0:T(8,128)(2,1)S(1)}, u32[]{:S(2)}, u32[]{:S(2)}) collective-permute-start(bf16[2,64,128]{2,1,0:T(8,128)(2,1)} %refs_0_.1), channel_id=1, source_target_pairs={{0,16},{4,20},{8,24},{12,28},{16,0},{20,4},{24,8},{28,12},{1,17},{... | collective-permute-start | bytes 98312 | tf_op jit(solution)/shard_map/ppermute | solution.py:25
  4.7 0.8 %copy-start.5 = (bf16[4,32,128]{2,1,0:T(8,128)(2,1)S(1)}, bf16[4,32,128]{2,1,0:T(8,128)(2,1)}, u32[]{:S(2)}) copy-start(bf16[4,32,128]{2,1,0:T(8,128)(2,1)} %refs_1_.1) | copy-start | bytes 98308
  5.5 0.8 %copy-start.6 = (bf16[2,64,128]{2,1,0:T(8,128)(2,1)S(1)}, bf16[2,64,128]{2,1,0:T(8,128)(2,1)}, u32[]{:S(2)}) copy-start(bf16[2,64,128]{2,1,0:T(8,128)(2,1)} %refs_0_.1) | copy-start | bytes 98308
  6.3 6.2 %collective-permute-start.2 = (bf16[4,32,128]{2,1,0:T(8,128)(2,1)S(1)}, bf16[4,32,128]{2,1,0:T(8,128)(2,1)S(1)}, u32[]{:S(2)}, u32[]{:S(2)}) collective-permute-start(bf16[4,32,128]{2,1,0:T(8,128)(2,1)S(1)} %get-tuple-element.31), channel_id=1, source_target_pairs={{0,2},{1,3},{2,0},{3,1},{4,6},{5,7},{6,4},{7,5},{8,10},{9,11},{10,... | collective-permute-start | bytes 98312 | tf_op jit(solution)/shard_map/ppermute | solution.py:25
  7.8 0.7 %copy-start.7 = (s32[256]{0:T(256)S(1)}, s32[256]{0:T(256)}, u32[]{:S(2)}) copy-start(s32[256]{0:T(256)} %param.17) | copy-start | bytes 3076
  8.5 4.3 %collective-permute-start.1 = (bf16[4,64,128]{2,1,0:T(8,128)(2,1)S(1)}, bf16[4,64,128]{2,1,0:T(8,128)(2,1)S(1)}, u32[]{:S(2)}, u32[]{:S(2)}) collective-permute-start(bf16[4,64,128]{2,1,0:T(8,128)(2,1)S(1)} %pad_maximum_fusion), channel_id=1, source_target_pairs={{0,8},{4,12},{8,0},{12,4},{16,24},{20,28},{24,16},{28,20},{1,9},{5... | collective-permute-start | bytes 196616 | tf_op jit(solution)/shard_map/ppermute | solution.py:25
  10.1 0.8 %copy-start.1 = (bf16[128,128]{1,0:T(8,128)(2,1)S(1)}, bf16[128,128]{1,0:T(8,128)(2,1)}, u32[]{:S(2)}) copy-start(bf16[128,128]{1,0:T(8,128)(2,1)} %w_lin_ref.7) | copy-start | bytes 98308
  10.1 0.8 %copy-start.2 = (bf16[128,128]{1,0:T(8,128)(2,1)S(1)}, bf16[128,128]{1,0:T(8,128)(2,1)}, u32[]{:S(2)}) copy-start(bf16[128,128]{1,0:T(8,128)(2,1)} %w_gate_ref.7) | copy-start | bytes 98308
  12.8 1.6 %copy-start.8 = (s32[16]{0:T(128)S(1)}, s32[16]{0:T(128)}, u32[]{:S(2)}) copy-start(s32[16]{0:T(128)} %param.16) | copy-start | bytes 196
  12.8 2.9 %copy-start.3 = (bf16[128,128]{1,0:T(8,128)(2,1)S(1)}, bf16[128,128]{1,0:T(8,128)(2,1)}, u32[]{:S(2)}) copy-start(bf16[128,128]{1,0:T(8,128)(2,1)} %w_lin_ref.6) | copy-start | bytes 98308
  12.8 2.9 %copy-start.4 = (bf16[128,128]{1,0:T(8,128)(2,1)S(1)}, bf16[128,128]{1,0:T(8,128)(2,1)}, u32[]{:S(2)}) copy-start(bf16[128,128]{1,0:T(8,128)(2,1)} %w_gate_ref.6) | copy-start | bytes 98308
  12.8 5.0 %collective-permute-start.3 = (bf16[8,64,128]{2,1,0:T(8,128)(2,1)S(1)}, bf16[8,64,128]{2,1,0:T(8,128)(2,1)S(1)}, u32[]{:S(2)}, u32[]{:S(2)}) collective-permute-start(bf16[8,64,128]{2,1,0:T(8,128)(2,1)S(1)} %constant_dynamic-update-slice_fusion.refs_0_), channel_id=1, source_target_pairs={{0,4},{4,0},{8,12},{12,8},{16,20},{20,16},{24,28},{28,24},{1,5},{5... | collective-permute-start | bytes 393224 | tf_op jit(solution)/shard_map/ppermute | solution.py:25
  14.4 1.3 %collective-permute-start.4 = (bf16[8,32,128]{2,1,0:T(8,128)(2,1)S(1)}, bf16[8,32,128]{2,1,0:T(8,128)(2,1)S(1)}, u32[]{:S(2)}, u32[]{:S(2)}) collective-permute-start(bf16[8,32,128]{2,1,0:T(8,128)(2,1)S(1)} %constant_dynamic-update-slice_fusion.3.even_ref), channel_id=1, source_target_pairs={{0,1},{1,0},{2,3},{3,2},{4,5},{5,4},{6,7},{7,6},{8,9},{9,8},{10,11... | collective-permute-start | bytes 196616 | tf_op jit(solution)/shard_map/ppermute | solution.py:25
  19.7 1.4 %collective-permute-start.7 = (f32[2,128,128]{2,1,0:T(8,128)S(1)}, f32[2,128,128]{2,1,0:T(8,128)S(1)}, u32[]{:S(2)}, u32[]{:S(2)}) collective-permute-start(f32[2,128,128]{2,1,0:T(8,128)S(1)} %get-tuple-element.46), channel_id=1, source_target_pairs={{0,1},{1,0},{2,3},{3,2},{4,5},{5,4},{6,7},{7,6},{8,9},{9,8},{10,11... | collective-permute-start | bytes 393224 | tf_op jit(solution)/shard_map/ppermute | solution.py:25
  21.1 4.3 %collective-permute-start.8 = (bf16[2,128,128]{2,1,0:T(8,128)(2,1)S(1)}, bf16[2,128,128]{2,1,0:T(8,128)(2,1)S(1)}, u32[]{:S(2)}, u32[]{:S(2)}) collective-permute-start(bf16[2,128,128]{2,1,0:T(8,128)(2,1)S(1)} %add_convert_fusion.3), channel_id=1, source_target_pairs={{0,2},{1,3},{2,0},{3,1},{4,6},{5,7},{6,4},{7,5},{8,10},{9,11},{10,... | collective-permute-start | bytes 196616 | tf_op jit(solution)/shard_map/ppermute | solution.py:25
  25.5 4.3 %collective-permute-start.9 = (bf16[2,128,128]{2,1,0:T(8,128)(2,1)S(1)}, bf16[2,128,128]{2,1,0:T(8,128)(2,1)S(1)}, u32[]{:S(2)}, u32[]{:S(2)}) collective-permute-start(bf16[2,128,128]{2,1,0:T(8,128)(2,1)S(1)} %add_convert_fusion.2), channel_id=1, source_target_pairs={{0,4},{4,0},{8,12},{12,8},{16,20},{20,16},{24,28},{28,24},{1,5},{5... | collective-permute-start | bytes 196616 | tf_op jit(solution)/shard_map/ppermute | solution.py:25
  27.1 6.7 %collective-permute-start.5 = (f32[2,4,32,128]{3,2,1,0:T(8,128)S(1)}, f32[2,4,32,128]{3,2,1,0:T(8,128)S(1)}, u32[]{:S(2)}, u32[]{:S(2)}) collective-permute-start(f32[2,4,32,128]{3,2,1,0:T(8,128)S(1)} %get-tuple-element.42), channel_id=1, source_target_pairs={{0,1},{1,0},{2,3},{3,2},{4,5},{5,4},{6,7},{7,6},{8,9},{9,8},{10,11... | collective-permute-start | bytes 393224 | tf_op jit(solution)/shard_map/ppermute | solution.py:25
  29.8 4.3 %collective-permute-start.10 = (bf16[2,128,128]{2,1,0:T(8,128)(2,1)S(1)}, bf16[2,128,128]{2,1,0:T(8,128)(2,1)S(1)}, u32[]{:S(2)}, u32[]{:S(2)}) collective-permute-start(bf16[2,128,128]{2,1,0:T(8,128)(2,1)S(1)} %add_convert_fusion.1), channel_id=1, source_target_pairs={{0,8},{4,12},{8,0},{12,4},{16,24},{20,28},{24,16},{28,20},{1,9},{5... | collective-permute-start | bytes 196616 | tf_op jit(solution)/shard_map/ppermute | solution.py:25
  34.2 5.2 %collective-permute-start.11 = (bf16[2,128,128]{2,1,0:T(8,128)(2,1)S(1)}, bf16[2,128,128]{2,1,0:T(8,128)(2,1)S(1)}, u32[]{:S(2)}, u32[]{:S(2)}) collective-permute-start(bf16[2,128,128]{2,1,0:T(8,128)(2,1)S(1)} %add_convert_fusion), channel_id=1, source_target_pairs={{0,16},{4,20},{8,24},{12,28},{16,0},{20,4},{24,8},{28,12},{1,17},{... | collective-permute-start | bytes 196616 | tf_op jit(solution)/shard_map/ppermute | solution.py:25
  35.6 4.0 %collective-permute-start.6 = (bf16[4,32,128]{2,1,0:T(8,128)(2,1)S(1)}, bf16[4,32,128]{2,1,0:T(8,128)(2,1)S(1)}, u32[]{:S(2)}, u32[]{:S(2)}) collective-permute-start(bf16[4,32,128]{2,1,0:T(8,128)(2,1)S(1)} %fusion), channel_id=1, source_target_pairs={{0,2},{1,3},{2,0},{3,1},{4,6},{5,7},{6,4},{7,5},{8,10},{9,11},{10,... | collective-permute-start | bytes 98312 | tf_op jit(solution)/shard_map/ppermute | solution.py:25
  39.4 1.4 %collective-permute-start.12 = (f32[2,128,128]{2,1,0:T(8,128)S(1)}, f32[2,128,128]{2,1,0:T(8,128)S(1)}, u32[]{:S(2)}, u32[]{:S(2)}) collective-permute-start(f32[2,128,128]{2,1,0:T(8,128)S(1)} %add_multiply_fusion), channel_id=1, source_target_pairs={{0,1},{1,0},{2,3},{3,2},{4,5},{5,4},{6,7},{7,6},{8,9},{9,8},{10,11... | collective-permute-start | bytes 393224 | tf_op jit(solution)/shard_map/ppermute | solution.py:25

commit v3 on v2

--- a/solution.py
+++ b/solution.py
@@ -13,6 +13,7 @@
 WHOLE = pl.BlockSpec()
 SMEM = pl.BlockSpec(memory_space=pltpu.SMEM)
 J_STEP = 4
+FORWARD_STEP = 32
 STAGE_COST = 400000
 
 
@@ -23,6 +24,19 @@
 def swap(value, axis, bit):
     size = lax.axis_size(axis)
     return lax.ppermute(value, axis, [(d, d ^ bit) for d in range(size)])
+
+
+def swap_chips(value, bit):
+    n_row, n_col = lax.axis_size("row"), lax.axis_size("col")
+    pairs = [(d, d ^ bit ^ 1) for d in range(n_row * n_col)]
+    return lax.ppermute(value, ("row", "col"), pairs)
+
+
+def parity():
+    number = lax.axis_index("row") ^ lax.axis_index("col")
+    for shift in (16, 8, 4, 2, 1):
+        number = number ^ (number >> shift)
+    return number & 1
 
 
 def params(mib=32):
@@ -67,7 +81,7 @@
     cols, keys, cz = pair_ref.shape
     row, col = lax.axis_index("row"), lax.axis_index("col")
     km = flags_ref[pl.ds(pl.multiple_of(row * keys, 16), keys)].astype(F32)
-    step = 8
+    step = min(cols, FORWARD_STEP)
 
     def body(s, carry):
         j0 = pl.multiple_of(s * step, step)
@@ -80,7 +94,7 @@
             m = km * flags[j : j + 1]
             masked = m * sigmoid[j]
             lin = linear[j]
-            value_ref[j0 + j] = (masked * lin).astype(BF16).astype(F32)
+            value_ref[j0 + j] = (masked * lin).astype(BF16)
             lin_ref[j0 + j] = masked
             gate_ref[j0 + j] = masked * lin * (1.0 - sigmoid[j])
         return carry
@@ -94,7 +108,7 @@
     out = jax.ShapeDtypeStruct((cols, keys, ch), F32)
     return pl.pallas_call(
         pair_forward_kernel,
-        out_shape=(out, out, out),
+        out_shape=(jax.ShapeDtypeStruct((cols, keys, ch), BF16), out, out),
         in_specs=[VMEM] * 4,
         out_specs=(VMEM, VMEM, VMEM),
         compiler_params=params(),
@@ -163,113 +177,147 @@
     return (lax.axis_index("row") ^ order[p // per]) * per + p % per
 
 
-def add_rows(cols, keys, grad_ref, rows, value_ref, slab_value_ref, sums_ref, start, finish):
-    ch = value_ref.shape[2]
-
-    def step(s, carry):
-        j0 = pl.multiple_of(s * J_STEP, J_STEP)
-        values = [value_ref[j0 + j] for j in range(J_STEP)]
-        totals = [start(j0 + j) for j in range(J_STEP)]
-        for p, i in enumerate(rows):
-            mine = slab_value_ref[i]
-            total = sums_ref[p]
-            for j in range(J_STEP):
-                g = jnp.broadcast_to(grad_ref[p, pl.ds(j0 + j, 1), :], (keys, ch))
-                totals[j] = totals[j] + g * mine
-                total = total + g * values[j]
-            sums_ref[p] = total
-        for j in range(J_STEP):
-            finish(j0 + j, totals[j])
-        return carry
-
-    lax.fori_loop(0, cols // J_STEP, step, 0)
-
-
-def first_kernel(order, n_grads, *refs):
-    grads, (value_ref, slab_value_ref, total_ref, sums_ref, wide) = refs[:n_grads], refs[n_grads:]
-    cols, keys, ch = value_ref.shape
-    per = grads[0].shape[0] * n_grads // len(order)
+def widen(grads, wide):
     at = 0
     for grad_ref in grads:
         wide[at : at + grad_ref.shape[0]] = grad_ref[...].astype(F32)
         at += grad_ref.shape[0]
+    return at
+
+
+def add_sums(wide, count, j0, keys, values, sums_ref):
+    ch = wide.shape[2]
+    for p in range(count):
+        total = sums_ref[p]
+        for j, value in enumerate(values):
+            total = total + jnp.broadcast_to(wide[p, pl.ds(j0 + j, 1), :], (keys, ch)) * value
+        sums_ref[p] = total
+
+
+def add_totals(wide, rows, j0, slab_value_ref, totals):
+    _, keys, ch = slab_value_ref.shape
+    totals = list(totals)
+    for p, i in enumerate(rows):
+        mine = slab_value_ref[i]
+        for j in range(len(totals)):
+            g = jnp.broadcast_to(wide[p, pl.ds(j0 + j, 1), :], (keys, ch))
+            totals[j] = totals[j] + g * mine
+    return totals
+
+
+def sums_kernel(n_grads, *refs):
+    grads, (value_ref, sums_ref, wide) = refs[:n_grads], refs[n_grads:]
+    cols, keys, ch = value_ref.shape
+    count = widen(grads, wide)
     sums_ref[...] = jnp.zeros_like(sums_ref)
-    rows = [row_of(order, per, p) for p in range(at)]
-
-    def start(j):
-        return jnp.zeros((keys, ch), F32)
-
-    def finish(j, total):
-        total_ref[j] = total
-
-    add_rows(cols, keys, wide, rows, value_ref, slab_value_ref, sums_ref, start, finish)
-
-
-def first_part(order, grads, value, slab_value):
+
+    def step(s, carry):
+        j0 = pl.multiple_of(s * J_STEP, J_STEP)
+        values = [value_ref[j0 + j].astype(F32) for j in range(J_STEP)]
+        add_sums(wide, count, j0, keys, values, sums_ref)
+        return carry
+
+    lax.fori_loop(0, cols // J_STEP, step, 0, unroll=2)
+
+
+def first_sums(grads, value):
     cols, keys, ch = value.shape
     rows = sum(g.shape[0] for g in grads)
     return pl.pallas_call(
-        functools.partial(first_kernel, order, len(grads)),
-        out_shape=(
-            jax.ShapeDtypeStruct((cols, keys, ch), F32),
-            jax.ShapeDtypeStruct((rows, keys, ch), F32),
-        ),
-        in_specs=[VMEM] * (len(grads) + 2),
-        out_specs=(VMEM, VMEM),
+        functools.partial(sums_kernel, len(grads)),
+        out_shape=jax.ShapeDtypeStruct((rows, keys, ch), F32),
+        in_specs=[VMEM] * (len(grads) + 1),
+        out_specs=VMEM,
         scratch_shapes=[pltpu.VMEM((rows, cols, ch), F32)],
         compiler_params=params(),
-        cost_estimate=cost(4 * rows * cols * keys * ch, 8 * cols * keys * ch),
-        name="first_rows",
-    )(*grads, value, slab_value)
-
-
-def main_kernel(order, n_grads, *refs):
-    grads = refs[:n_grads]
-    (
-        total_ref,
-        first_sums_ref,
-        pair_ref,
-        value_ref,
-        lin_ref,
-        gate_ref,
-        slab_ref,
-        slab_value_ref,
-        slab_lin_ref,
-        slab_gate_ref,
-        d_lin_ref,
-        d_gate_ref,
-        sum_keep_ref,
-        sum_send_ref,
-        w_keep_ref,
-        w_send_ref,
-        wide,
-        sums_ref,
-        slab_sum,
-    ) = refs[n_grads:]
+        cost_estimate=cost(2 * rows * cols * keys * ch, 8 * cols * keys * ch),
+        name="first_sums_over_j",
+    )(*grads, value)
+
+
+def totals_kernel(order, n_grads, *refs):
+    grads, (slab_value_ref, total_ref, wide) = refs[:n_grads], refs[n_grads:]
+    cols, keys, ch = total_ref.shape
+    count = widen(grads, wide)
+    per = slab_value_ref.shape[0] // len(order)
+    rows = [row_of(order, per, p) for p in range(count)]
+
+    def step(s, carry):
+        j0 = pl.multiple_of(s * J_STEP, J_STEP)
+        totals = [jnp.zeros((keys, ch), F32)] * J_STEP
+        totals = add_totals(wide, rows, j0, slab_value_ref, totals)
+        for j in range(J_STEP):
+            total_ref[j0 + j] = totals[j]
+        return carry
+
+    lax.fori_loop(0, cols // J_STEP, step, 0, unroll=2)
+
+
+def first_totals(order, grads, slab_value):
+    _, keys, ch = slab_value.shape
+    cols = grads[0].shape[1]
+    rows = sum(g.shape[0] for g in grads)
+    return pl.pallas_call(
+        functools.partial(totals_kernel, order, len(grads)),
+        out_shape=jax.ShapeDtypeStruct((cols, keys, ch), F32),
+        in_specs=[VMEM] * (len(grads) + 1),
+        out_specs=VMEM,
+        scratch_shapes=[pltpu.VMEM((rows, cols, ch), F32)],
+        compiler_params=params(),
+        cost_estimate=cost(2 * rows * cols * keys * ch, 8 * cols * keys * ch),
+        name="first_totals_over_i",
+    )(*grads, slab_value)
+
+
+def main_kernel(
+    order,
+    blocks,
+    grad_ref,
+    total_ref,
+    first_sums_ref,
+    pair_ref,
+    value_ref,
+    lin_ref,
+    gate_ref,
+    slab_ref,
+    slab_value_ref,
+    slab_lin_ref,
+    slab_gate_ref,
+    d_lin_ref,
+    d_gate_ref,
+    sum_keep_ref,
+    sum_send_ref,
+    w_keep_ref,
+    w_send_ref,
+    wide,
+    sums_ref,
+    slab_sum,
+):
     cols, keys, cz = pair_ref.shape
     ch = value_ref.shape[2]
     slab_rows = slab_ref.shape[0]
     done = first_sums_ref.shape[0]
     per = slab_rows // len(order)
     col = lax.axis_index("col")
-    at = 0
-    for grad_ref in grads:
-        wide[at : at + grad_ref.shape[0]] = grad_ref[...].astype(F32)
-        at += grad_ref.shape[0]
+    count = widen([grad_ref], wide)
     sums_ref[...] = jnp.zeros_like(sums_ref)
-    rows = [row_of(order, per, done + p) for p in range(at)]
-
-    def start(j):
-        return total_ref[j]
-
-    def finish(j, total):
-        d_lin_ref[j] = (total * lin_ref[j]).astype(BF16)
-        d_gate_ref[j] = (total * gate_ref[j]).astype(BF16)
-
-    add_rows(cols, keys, wide, rows, value_ref, slab_value_ref, sums_ref, start, finish)
+    rows = [row_of(order, per, done + p) for p in range(count)]
+
+    def step(s, carry):
+        j0 = pl.multiple_of(s * J_STEP, J_STEP)
+        values = [value_ref[j0 + j].astype(F32) for j in range(J_STEP)]
+        add_sums(wide, count, j0, keys, values, sums_ref)
+        totals = [total_ref[j0 + j] for j in range(J_STEP)]
+        totals = add_totals(wide, rows, j0, slab_value_ref, totals)
+        for j in range(J_STEP):
+            d_lin_ref[j0 + j] = (totals[j] * lin_ref[j0 + j]).astype(BF16)
+            d_gate_ref[j0 + j] = (totals[j] * gate_ref[j0 + j]).astype(BF16)
+        return carry
+
+    lax.fori_loop(0, cols // J_STEP, step, 0, unroll=2)
     for p in range(done):
         slab_sum[row_of(order, per, p)] = first_sums_ref[p]
-    for p in range(at):
+    for p in range(count):
         slab_sum[rows[p]] = sums_ref[p]
 
     def weights(rows, d_lin, d_gate):
@@ -287,47 +335,46 @@
         d_lin_ref[...].reshape(cols * keys, ch),
         d_gate_ref[...].reshape(cols * keys, ch),
     )
-    first = col % 2 == 0
+    first = parity() == 0
     keep = jnp.where(first, slab_w, pair_w)
     send = jnp.where(first, pair_w, slab_w)
     for h in range(2):
         w_keep_ref[h] = keep[:, h * ch : (h + 1) * ch]
         w_send_ref[h] = send[:, h * ch : (h + 1) * ch]
-    halves, own = sum_keep_ref.shape[:2]
-    for b in range(halves):
-        sum_keep_ref[b] = slab_sum[pl.ds((col ^ (2 * b)) * own, own)]
-        sum_send_ref[b] = slab_sum[pl.ds((col ^ (2 * b + 1)) * own, own)]
-
-
-def main_part(order, n_col, grads, first, pair, value, lin, gate, slab, s_value, s_lin, s_gate):
+    own = sum_keep_ref.shape[1]
+    for n, b in enumerate(blocks):
+        sum_keep_ref[n] = slab_sum[pl.ds((col ^ b) * own, own)]
+        sum_send_ref[n] = slab_sum[pl.ds((col ^ b ^ 1) * own, own)]
+
+
+def main_part(order, blocks, grads, first, pair, forward, slab):
     cols, keys, cz = pair.shape
-    ch = value.shape[2]
-    slab_rows = slab.shape[0]
-    rows = sum(g.shape[0] for g in grads)
-    own = slab_rows // n_col
+    ch = forward[0].shape[2]
+    slab_rows = slab[0].shape[0]
+    own = slab_rows // (2 * len(blocks))
     d_type = jax.ShapeDtypeStruct((cols, keys, ch), BF16)
-    s_type = jax.ShapeDtypeStruct((n_col // 2, own, keys, ch), F32)
+    s_type = jax.ShapeDtypeStruct((len(blocks), own, keys, ch), F32)
     w_type = jax.ShapeDtypeStruct((2, cz, ch), F32)
     return pl.pallas_call(
-        functools.partial(main_kernel, order, len(grads)),
+        functools.partial(main_kernel, order, blocks),
         out_shape=(d_type, d_type, s_type, s_type, w_type, w_type),
-        in_specs=[VMEM] * (len(grads) + 10),
+        in_specs=[VMEM] * 11,
         out_specs=(VMEM,) * 6,
         scratch_shapes=[
-            pltpu.VMEM((rows, cols, ch), F32),
-            pltpu.VMEM((rows, keys, ch), F32),
+            pltpu.VMEM((grads.shape[0], cols, ch), F32),
+            pltpu.VMEM((grads.shape[0], keys, ch), F32),
             pltpu.VMEM((slab_rows, keys, ch), F32),
         ],
         compiler_params=params(),
         cost_estimate=cost(8 * cols * keys * cz * ch, 16 * cols * keys * ch),
         name="last_rows",
-    )(*grads, *first, pair, value, lin, gate, slab, s_value, s_lin, s_gate)
+    )(grads, *first, pair, *forward, *slab)
 
 
 def pair_out_kernel(d_lin_ref, d_gate_ref, w_lin_ref, w_gate_ref, out_ref):
     rows, ch = d_lin_ref.shape
     weights = jnp.concatenate([w_lin_ref[...], w_gate_ref[...]], axis=1)
-    step = 256
+    step = rows
 
     def body(s, carry):
         at = pl.ds(pl.multiple_of(s * step, step), step)
@@ -354,6 +401,25 @@
         name="pair_input_grad",
     )(d_lin.reshape(cols * keys, ch), d_gate.reshape(cols * keys, ch), w_lin, w_gate)
     return out.reshape(cols, keys, cz)
+
+
+def fold_kernel(kept_ref, got_ref, sum_ref, moved_ref):
+    half = sum_ref.shape[0]
+    sum_ref[...] = kept_ref[:half] + got_ref[:half].astype(F32)
+    moved_ref[...] = (kept_ref[half:] + got_ref[half:].astype(F32)).astype(BF16)
+
+
+def fold(kept, got):
+    half = (kept.shape[0] // 2,) + kept.shape[1:]
+    return pl.pallas_call(
+        fold_kernel,
+        out_shape=(jax.ShapeDtypeStruct(half, F32), jax.ShapeDtypeStruct(half, BF16)),
+        in_specs=[VMEM, VMEM],
+        out_specs=(VMEM, VMEM),
+        compiler_params=params(),
+        cost_estimate=cost(STAGE_COST * kept.size, 8 * kept.size),
+        name="fold",
+    )(kept, got)
 
 
 def slab_out_kernel(sum_ref, got_ref, lin_ref, gate_ref, w_lin_ref, w_gate_ref, out_ref):
@@ -391,57 +457,71 @@
     residues = mask_residue.shape[0]
 
     steps = [row_bits[-1]] + row_bits[1:-1] + row_bits[:1]
+    ch = w_a_lin.shape[1]
     held, own_slab = stage(grad_out, pair_slab)
-    slab_flags, flags = (
-        jnp.broadcast_to(m.astype(BF16)[:, None], m.shape + (w_a_lin.shape[1],))
-        for m in (mask_slab, mask_residue)
-    )
     order = [0]
     blocks = {0: own_slab}
     for bit in reversed(col_bits[1:]):
         for b in list(blocks):
             blocks[b ^ bit] = swap(blocks[b], "col", bit)
     got = swap(grad_out, "row", steps[0])
-    tied = lax.optimization_barrier((flags, got))[0]
-    value, lin, gate = pair_forward(pair_full, w_b_lin, w_b_gate, tied)
-    for bit, last in zip(steps, steps[1:]):
-        if last == steps[-1]:
-            got, value, blocks = lax.optimization_barrier((got, value, blocks))
+    for bit, later in zip(steps, steps[1:-1]):
         held = jnp.concatenate([held, got], axis=0)
         order = order + [r ^ bit for r in order]
-        got = swap(held, "row", last)
+        got = swap(held, "row", later)
+    masks = lax.optimization_barrier(((mask_slab, mask_residue), held, blocks))[0]
+    slab_flags, flags = (
+        jnp.broadcast_to(m.astype(BF16)[:, None], m.shape + (ch,)) for m in masks
+    )
+    value, lin, gate = pair_forward(pair_full, w_b_lin, w_b_gate, flags)
+    got_last = swap(held, "row", steps[-1])
+    got, value = lax.optimization_barrier((got, value))
+    got_both = swap(got, "row", steps[-1])
+    for bit in steps[-2:]:
+        order = order + [r ^ bit for r in order]
     slabs = jnp.concatenate([blocks[b] for b in sorted(blocks)], axis=0)
     slabs = [slabs, swap(slabs, "col", 1)]
-    slab, s_value, s_lin, s_gate = slab_forward(
-        slabs, n_col, w_a_lin, w_a_gate, slab_flags, flags
-    )
-    order = order + [r ^ last for r in order]
-    first = first_part(order[: len(order) // 2], [held], value, s_value)
+    slab = slab_forward(slabs, n_col, w_a_lin, w_a_gate, slab_flags, flags)
+    pieces = [held, got, got_last]
+    first = (first_totals(order, pieces, slab[1]), first_sums(pieces, value))
+    kept = [0]
+    for bit in reversed(col_bits[1:]):
+        kept = kept + [b ^ bit for b in kept]
     d_lin, d_gate, sum_keep, sum_send, w_keep, w_send = main_part(
-        order, n_col, [got], first, pair_full, value, lin, gate, slab, s_value, s_lin, s_gate
-    )
-    weights = w_keep + swap(w_send, "col", 1)
-    sums = sum_keep + swap(sum_send, "col", 1)
-    for bit in col_bits[1:]:
-        narrow = weights.astype(BF16)
-        weights = narrow.astype(F32) + swap(narrow, "col", bit).astype(F32)
-    for bit in row_bits:
-        narrow = weights.astype(BF16)
-        weights = narrow.astype(F32) + swap(narrow, "row", bit).astype(F32)
-    for bit in reversed(col_bits[2:]):
-        half = sums.shape[0] // 2
-        sums = sums[:half] + swap(sums[half:].astype(BF16), "col", bit).astype(F32)
-    got = swap(sums[1].astype(BF16), "col", 2)
-    grad_slab = slab_out(sums[0], got, s_lin, s_gate, w_a_lin, w_a_gate)
-    grad_pair = pair_out(d_lin, d_gate, w_b_lin, w_b_gate)
-    weights = weights / residues
-    other = swap(weights, "col", 1)
-    first = lax.axis_index("col") % 2 == 0
+        order, kept, got_both, first, pair_full, (value, lin, gate), slab
+    )
+    pair_bit, col = col_bits[1], lax.axis_index("col")
+    got_w = swap(w_send, "col", 1)
+    sum_send, _ = lax.optimization_barrier((sum_send, got_w))
+    side = w_keep + got_w
+    upper = (col & pair_bit) != 0
+    moved = jnp.where(upper, side[0], side[1]).astype(BF16)
+    part = jnp.where(upper, side[1], side[0])
+    part = part + swap_chips(moved, pair_bit).astype(F32)
+    bits = col_bits[2:] + [bit * n_col for bit in row_bits]
+    sums, got = sum_keep, swap(sum_send, "col", 1)
+    for bit in bits:
+        narrow = part.astype(BF16)
+        if bit == bits[1]:
+            narrow, got = lax.optimization_barrier((narrow, got))
+            for far in col_bits[1:]:
+                sums, moved = fold(sums, got)
+                got = swap(moved, "col", far)
+        if bit == bits[0]:
+            narrow, d_lin, d_gate = lax.optimization_barrier((narrow, d_lin, d_gate))
+            grad_pair = pair_out(d_lin, d_gate, w_b_lin, w_b_gate)
+        if bit == bits[-1]:
+            narrow, grad_pair = lax.optimization_barrier((narrow, grad_pair))
+        part = narrow.astype(F32) + swap_chips(narrow, bit).astype(F32)
+    narrow = part.astype(BF16)
+    mine = jnp.stack([narrow, swap_chips(narrow, pair_bit)])
+    both = [mine, swap(mine, "col", 1)]
+    both = [jnp.where(upper, m[::-1], m).astype(F32) / residues for m in both]
+    first = parity() == 0
     grad_weights = jnp.where(
-        first,
-        jnp.concatenate([weights, other], axis=0),
-        jnp.concatenate([other, weights], axis=0),
-    )
+        first, jnp.concatenate(both, axis=0), jnp.concatenate(both[::-1], axis=0)
+    )
+    grad_slab = slab_out(sums[0], got[0], slab[2], slab[3], w_a_lin, w_a_gate)
     return (grad_slab, grad_pair, grad_weights)
 
 

time: 41.9 us -> 40.4 us (0.964)
  starting transfers between devices: 16.2 us -> 18.4 us
  Pallas kernels: 8.03 us -> 6.1 us
  waiting for transfers between devices: 12.6 us -> 11.5 us
  local copies, waits for them, and re-layouts: 3.08 us -> 2.3 us
    ppermute x13 -> x10, waiting for transfers between devices: 12.6 us -> 3.89 us  [swap(): return lax.ppermute(value, axis, [(d, d ^ bit) for d in range(size)])]
    ppermute x0 -> x5, waiting for transfers between devices: none -> 7.65 us  [swap_chips(): return lax.ppermute(value, ('row', 'col'), pairs)]
    ppermute x0 -> x5, starting transfers between devices: none -> 5.53 us  [swap_chips(): return lax.ppermute(value, ('row', 'col'), pairs)]
    ppermute x13 -> x10, starting transfers between devices: 16.2 us -> 12.9 us  [swap(): return lax.ppermute(value, axis, [(d, d ^ bit) for d in range(size)])]
    pallas_call x1, Pallas kernels: 2.3 us -> 1.22 us  [pair_out(): pl.pallas_call(pair_out_kernel, out_shape=jax.ShapeDtypeStruct((cols * ke...]
    pallas_call x3 -> x5, Pallas kernels: 4.67 us -> 3.82 us  [the longest x1 1.16 us: main_part(): pl.pallas_call(functools.partial(main_kernel, order, blocks), out_shape=(...]
    unnamed x21 -> x20, local copies, waits for them, and re-layouts: 2.88 us -> 2.12 us
  transfers between devices with their start and end apart: 13 -> 15, of which waited for: 9 -> 9; matrix products, arithmetic and copies ran while one was open for 1% -> 1% of each run, Pallas kernels for 15% -> 12%
where the time goes in v3:
time: 40.4 us; the launch traced here: 40.1 us
  starting transfers between devices  18.4 us (46%)
  waiting for transfers between devices  11.5 us (28%)
  Pallas kernels  6.1 us (15%)
  local copies, waits for them, and re-layouts  2.3 us (6%)
  other arithmetic  0.85 us (2%)
  between operations  0.85 us (2%)
    ppermute x10, starting transfers between devices, swap(): return lax.ppermute(value, axis, [(d, d ^ bit) for d in range(size)])  12.9 us
    ppermute x5, waiting for transfers between devices, swap_chips(): return lax.ppermute(value, ('row', 'col'), pairs)  7.65 us
    ppermute x5, starting transfers between devices, swap_chips(): return lax.ppermute(value, ('row', 'col'), pairs)  5.53 us
    ppermute x10, waiting for transfers between devices, swap(): return lax.ppermute(value, axis, [(d, d ^ bit) for d in range(size)])  3.89 us
    unnamed x20, local copies, waits for them, and re-layouts  2.12 us
    pallas_call x1, Pallas kernels, pair_out(): pl.pallas_call(pair_out_kernel, out_shape=jax.ShapeDtypeStruct((cols * ke...  1.22 us
    pallas_call x1, Pallas kernels, main_part(): pl.pallas_call(functools.partial(main_kernel, order, blocks), out_shape=(...  1.16 us
    pallas_call x1, Pallas kernels, first_sums(): pl.pallas_call(functools.partial(sums_kernel, len(grads)), out_shape=jax....  0.98 us
  transfers between devices with their start and end apart: 15, of which 9 were waited for; matrix products, arithmetic and copies ran while one was open for 1% of the time, Pallas kernels for 12%

profile of v3, /device:TPU:0, one launch (start us, length us, event | category | flops | bytes accessed | tf_op | source)
XLA Modules:
  0.0 40.1 jit_solution(15469802793281362776)
XLA Ops:
  0.6 4.1 %collective-permute-start = (bf16[2,64,128]{2,1,0:T(8,128)(2,1)}, bf16[2,64,128]{2,1,0:T(8,128)(2,1)S(1)}, u32[]{:S(2)}, u32[]{:S(2)}) collective-permute-start(bf16[2,64,128]{2,1,0:T(8,128)(2,1)} %refs_0_.1), channel_id=1, source_target_pairs={{0,16},{4,20},{8,24},{12,28},{16,0},{20,4},{24,8},{28,12},{1,17},{... | collective-permute-start | bytes 98312 | tf_op jit(solution)/shard_map/ppermute | solution.py:26
  6.3 1.5 %collective-permute-start.2 = (bf16[4,32,128]{2,1,0:T(8,128)(2,1)S(1)}, bf16[4,32,128]{2,1,0:T(8,128)(2,1)S(1)}, u32[]{:S(2)}, u32[]{:S(2)}) collective-permute-start(bf16[4,32,128]{2,1,0:T(8,128)(2,1)S(1)} %get-tuple-element.33), channel_id=1, source_target_pairs={{0,2},{1,3},{2,0},{3,1},{4,6},{5,7},{6,4},{7,5},{8,10},{9,11},{10,... | collective-permute-start | bytes 98312 | tf_op jit(solution)/shard_map/ppermute | solution.py:26
  7.8 1.6 %collective-permute-start.1 = (bf16[4,64,128]{2,1,0:T(8,128)(2,1)S(1)}, bf16[4,64,128]{2,1,0:T(8,128)(2,1)S(1)}, u32[]{:S(2)}, u32[]{:S(2)}) collective-permute-start(bf16[4,64,128]{2,1,0:T(8,128)(2,1)S(1)} %constant_dynamic-update-slice_fusion.refs_0_), channel_id=1, source_target_pairs={{0,8},{4,12},{8,0},{12,4},{16,24},{20,28},{24,16},{28,20},{1,9},{5... | collective-permute-start | bytes 196616 | tf_op jit(solution)/shard_map/ppermute | solution.py:26
  9.4 1.5 %collective-permute-start.4 = (bf16[4,64,128]{2,1,0:T(8,128)(2,1)S(1)}, bf16[4,64,128]{2,1,0:T(8,128)(2,1)S(1)}, u32[]{:S(2)}, u32[]{:S(2)}) collective-permute-start(bf16[4,64,128]{2,1,0:T(8,128)(2,1)S(1)} %constant_dynamic-update-slice_fusion.refs_0_), channel_id=1, source_target_pairs={{0,4},{4,0},{8,12},{12,8},{16,20},{20,16},{24,28},{28,24},{1,5},{5... | collective-permute-start | bytes 196616 | tf_op jit(solution)/shard_map/ppermute | solution.py:26
  12.5 1.2 %collective-permute-start.3 = (bf16[4,64,128]{2,1,0:T(8,128)(2,1)S(1)}, bf16[4,64,128]{2,1,0:T(8,128)(2,1)S(1)}, u32[]{:S(2)}, u32[]{:S(2)}) collective-permute-start(bf16[4,64,128]{2,1,0:T(8,128)(2,1)S(1)} %collective-permute-done.1.refs_1_), channel_id=1, source_target_pairs={{0,4},{4,0},{8,12},{12,8},{16,20},{20,16},{24,28},{28,24},{1,5},{5... | collective-permute-start | bytes 196616 | tf_op jit(solution)/shard_map/ppermute | solution.py:26
  14.0 1.0 %first_totals_over_i.1.total_ref = f32[64,32,128]{2,1,0:T(8,128)S(1)} custom-call(bf16[4,64,128]{2,1,0:T(8,128)(2,1)S(1)} %constant_dynamic-update-slice_fusion.refs_0_, bf16[4,64,128]{2,1,0:T(8,128)(2,1)S(1)} %collective-permute-done.1.refs_1_, bf16[4,64,128]{2,1,0:T(8,128)(2,1)S(1)} %collective-permute-done.4.refs_2_, ...), custom_call_target="tpu_custom_call" | custom-call | flops 6291456 | bytes 2097152 | tf_op jit(solution)/shard_map/first_totals_over_i/pallas_call | solution.py:260
  15.0 1.0 %first_sums_over_j.1.first_sums_ref = f32[12,32,128]{2,1,0:T(8,128)S(1)} custom-call(bf16[4,64,128]{2,1,0:T(8,128)(2,1)S(1)} %constant_dynamic-update-slice_fusion.refs_0_, bf16[4,64,128]{2,1,0:T(8,128)(2,1)S(1)} %collective-permute-done.1.refs_1_, bf16[4,64,128]{2,1,0:T(8,128)(2,1)S(1)} %collective-permute-done.4.refs_2_, ...), custom_call_target="tpu_custom_call" | custom-call | flops 6291456 | bytes 2097152 | tf_op jit(solution)/shard_map/first_sums_over_j/pallas_call | solution.py:226
  16.0 0.8 %collective-permute-done.3.grad_ref = bf16[4,64,128]{2,1,0:T(8,128)(2,1)S(1)} collective-permute-done((bf16[4,64,128]{2,1,0:T(8,128)(2,1)S(1)}, bf16[4,64,128]{2,1,0:T(8,128)(2,1)S(1)}, u32[]{:S(2)}, u32[]{:S(2)}) %collective-permute-start.3) | collective-permute-done | bytes 65568 | tf_op jit(solution)/shard_map/ppermute | solution.py:26
  16.8 1.2 %last_rows.1 = (bf16[64,32,128]{2,1,0:T(8,128)(2,1)S(1)}, bf16[64,32,128]{2,1,0:T(8,128)(2,1)S(1)}, f32[2,4,32,128]{3,2,1,0:T(8,128)S(1)}, f32[2,4,32,128]{3,2,1...) custom-call(bf16[4,64,128]{2,1,0:T(8,128)(2,1)S(1)} %collective-permute-done.3.grad_ref, ...), custom_call_target="tpu_custom_call" | custom-call | flops 268435456 | bytes 4194304 | tf_op jit(solution)/shard_map/last_rows/pallas_call | solution.py:358
  18.1 1.3 %collective-permute-done.6 = f32[2,128,128]{2,1,0:T(8,128)S(1)} collective-permute-done((f32[2,128,128]{2,1,0:T(8,128)S(1)}, f32[2,128,128]{2,1,0:T(8,128)S(1)}, u32[]{:S(2)}, u32[]{:S(2)}) %collective-permute-start.6) | collective-permute-done | bytes 131104 | tf_op jit(solution)/shard_map/ppermute | solution.py:26
  20.1 2.7 %collective-permute-done.7 = bf16[128,128]{1,0:T(8,128)(2,1)S(1)} collective-permute-done((bf16[128,128]{1,0:T(8,128)(2,1)S(1)}, bf16[128,128]{1,0:T(8,128)(2,1)S(1)}, u32[]{:S(2)}, u32[]{:S(2)}) %collective-permute-start.7) | collective-permute-done | bytes 32800 | tf_op jit(solution)/shard_map/ppermute | solution.py:32
  22.9 0.9 %collective-permute-start.8 = (bf16[128,128]{1,0:T(8,128)(2,1)S(1)}, bf16[128,128]{1,0:T(8,128)(2,1)S(1)}, u32[]{:S(2)}, u32[]{:S(2)}) collective-permute-start(bf16[128,128]{1,0:T(8,128)(2,1)S(1)} %fusion), channel_id=1, source_target_pairs={{0,5},{1,4},{2,7},{3,6},{4,1},{5,0},{6,3},{7,2},{8,13},{9,12},{10,... | collective-permute-start | bytes 98312 | tf_op jit(solution)/shard_map/ppermute | solution.py:32
  24.2 2.1 %collective-permute-done.8 = bf16[128,128]{1,0:T(8,128)(2,1)S(1)} collective-permute-done((bf16[128,128]{1,0:T(8,128)(2,1)S(1)}, bf16[128,128]{1,0:T(8,128)(2,1)S(1)}, u32[]{:S(2)}, u32[]{:S(2)}) %collective-permute-start.8) | collective-permute-done | bytes 32800 | tf_op jit(solution)/shard_map/ppermute | solution.py:32
  26.3 1.0 %collective-permute-start.11 = (bf16[128,128]{1,0:T(8,128)(2,1)S(1)}, bf16[128,128]{1,0:T(8,128)(2,1)S(1)}, u32[]{:S(2)}, u32[]{:S(2)}) collective-permute-start(bf16[128,128]{1,0:T(8,128)(2,1)S(1)} %add_convert_fusion.2), channel_id=1, source_target_pairs={{0,9},{1,8},{2,11},{3,10},{4,13},{5,12},{6,15},{7,14},{8,1},{9,0},... | collective-permute-start | bytes 98312 | tf_op jit(solution)/shard_map/ppermute | solution.py:32
  27.3 1.2 %pair_input_grad.1 = bf16[2048,128]{1,0:T(8,128)(2,1)} custom-call(bf16[2048,128]{1,0:T(8,128)(2,1)S(1)} %bitcast.13, bf16[2048,128]{1,0:T(8,128)(2,1)S(1)} %bitcast.14, bf16[128,128]{1,0:T(8,128)(2,1)S(1)} %copy-done.1, bf16[128,128]{1,0:T(8,128)(2,1)S(1)} %copy-done.2), custom_call_target="tpu_custom_call" | custom-call | flops 134217728 | bytes 1572864 | tf_op jit(solution)/shard_map/pair_input_grad/pallas_call | solution.py:394
  28.5 1.2 %collective-permute-done.11 = bf16[128,128]{1,0:T(8,128)(2,1)S(1)} collective-permute-done((bf16[128,128]{1,0:T(8,128)(2,1)S(1)}, bf16[128,128]{1,0:T(8,128)(2,1)S(1)}, u32[]{:S(2)}, u32[]{:S(2)}) %collective-permute-start.11) | collective-permute-done | bytes 32800 | tf_op jit(solution)/shard_map/ppermute | solution.py:32
  29.8 2.1 %collective-permute-start.12 = (bf16[128,128]{1,0:T(8,128)(2,1)S(1)}, bf16[128,128]{1,0:T(8,128)(2,1)S(1)}, u32[]{:S(2)}, u32[]{:S(2)}) collective-permute-start(bf16[128,128]{1,0:T(8,128)(2,1)S(1)} %add_convert_fusion.1), channel_id=1, source_target_pairs={{0,17},{1,16},{2,19},{3,18},{4,21},{5,20},{6,23},{7,22},{8,25},{9,... | collective-permute-start | bytes 98312 | tf_op jit(solution)/shard_map/ppermute | solution.py:32
  31.8 1.6 %collective-permute-start.10 = (bf16[1,4,32,128]{3,2,1,0:T(8,128)(2,1)S(1)}, bf16[1,4,32,128]{3,2,1,0:T(8,128)(2,1)S(1)}, u32[]{:S(2)}, u32[]{:S(2)}) collective-permute-start(bf16[1,4,32,128]{3,2,1,0:T(8,128)(2,1)S(1)} %get-tuple-element.55), channel_id=1, source_target_pairs={{0,2},{1,3},{2,0},{3,1},{4,6},{5,7},{6,4},{7,5},{8,10},{9,11},{10,... | collective-permute-start | bytes 98312 | tf_op jit(solution)/shard_map/ppermute | solution.py:26
  34.1 0.9 %collective-permute-start.13 = (bf16[128,128]{1,0:T(8,128)(2,1)S(1)}, bf16[128,128]{1,0:T(8,128)(2,1)S(1)}, u32[]{:S(2)}, u32[]{:S(2)}) collective-permute-start(bf16[128,128]{1,0:T(8,128)(2,1)S(1)} %add_convert_fusion), channel_id=1, source_target_pairs={{0,3},{1,2},{2,1},{3,0},{4,7},{5,6},{6,5},{7,4},{8,11},{9,10},{10,... | collective-permute-start | bytes 98312 | tf_op jit(solution)/shard_map/ppermute | solution.py:32
  35.0 0.9 %collective-permute-done.10 = bf16[1,4,32,128]{3,2,1,0:T(8,128)(2,1)S(1)} collective-permute-done((bf16[1,4,32,128]{3,2,1,0:T(8,128)(2,1)S(1)}, bf16[1,4,32,128]{3,2,1,0:T(8,128)(2,1)S(1)}, u32[]{:S(2)}, u32[]{:S(2)}) %collective-permute-start.10) | collective-permute-done | bytes 32800 | tf_op jit(solution)/shard_map/ppermute | solution.py:26
  35.8 0.8 %slab_input_grad.1 = bf16[4,32,128]{2,1,0:T(8,128)(2,1)} custom-call(f32[4,32,128]{2,1,0:T(8,128)S(1)} %bitcast.15, bf16[4,32,128]{2,1,0:T(8,128)(2,1)S(1)} %bitcast.16, f32[16,32,128]{2,1,0:T(8,128)S(1)} %get-tuple-element.43.slab_lin_ref.lin_ref, f32[16,32,128]{2,1,0:T(8,128)S(1)} %get-tuple-element.44.slab_gate_ref.gate_ref, ...), custom_call_target="tpu_custom_call" | custom-call | flops 8388608 | bytes 262144 | tf_op jit(solution)/shard_map/slab_input_grad/pallas_call | solution.py:441
  36.6 0.9 %collective-permute-done.13 = bf16[128,128]{1,0:T(8,128)(2,1)S(1)} collective-permute-done((bf16[128,128]{1,0:T(8,128)(2,1)S(1)}, bf16[128,128]{1,0:T(8,128)(2,1)S(1)}, u32[]{:S(2)}, u32[]{:S(2)}) %collective-permute-start.13) | collective-permute-done | bytes 32800 | tf_op jit(solution)/shard_map/ppermute | solution.py:32
  37.5 0.9 %collective-permute-start.14 = (bf16[2,128,128]{2,1,0:T(8,128)(2,1)S(1)}, bf16[2,128,128]{2,1,0:T(8,128)(2,1)S(1)}, u32[]{:S(2)}, u32[]{:S(2)}) collective-permute-start(bf16[2,128,128]{2,1,0:T(8,128)(2,1)S(1)} %pad_maximum_fusion), channel_id=1, source_target_pairs={{0,1},{1,0},{2,3},{3,2},{4,5},{5,4},{6,7},{7,6},{8,9},{9,8},{10,11... | collective-permute-start | bytes 196616 | tf_op jit(solution)/shard_map/ppermute | solution.py:26
  38.5 0.9 %collective-permute-done.14 = bf16[2,128,128]{2,1,0:T(8,128)(2,1)S(1)} collective-permute-done((bf16[2,128,128]{2,1,0:T(8,128)(2,1)S(1)}, bf16[2,128,128]{2,1,0:T(8,128)(2,1)S(1)}, u32[]{:S(2)}, u32[]{:S(2)}) %collective-permute-start.14) | collective-permute-done | bytes 65568 | tf_op jit(solution)/shard_map/ppermute | solution.py:26
  (51 shorter events, 6.0 us)
Async XLA Ops:
  0.6 10.6 %copy-start = (bf16[64,32,128]{2,1,0:T(8,128)(2,1)S(1)}, bf16[64,32,128]{2,1,0:T(8,128)(2,1)}, u32[]{:S(2)}) copy-start(bf16[64,32,128]{2,1,0:T(8,128)(2,1)} %pair_ref.3) | copy-start | bytes 1572868
  0.6 7.1 %collective-permute-start = (bf16[2,64,128]{2,1,0:T(8,128)(2,1)}, bf16[2,64,128]{2,1,0:T(8,128)(2,1)S(1)}, u32[]{:S(2)}, u32[]{:S(2)}) collective-permute-start(bf16[2,64,128]{2,1,0:T(8,128)(2,1)} %refs_0_.1), channel_id=1, source_target_pairs={{0,16},{4,20},{8,24},{12,28},{16,0},{20,4},{24,8},{28,12},{1,17},{... | collective-permute-start | bytes 98312 | tf_op jit(solution)/shard_map/ppermute | solution.py:26
  4.7 0.8 %copy-start.5 = (bf16[4,32,128]{2,1,0:T(8,128)(2,1)S(1)}, bf16[4,32,128]{2,1,0:T(8,128)(2,1)}, u32[]{:S(2)}) copy-start(bf16[4,32,128]{2,1,0:T(8,128)(2,1)} %refs_1_.1) | copy-start | bytes 98308
  5.5 0.8 %copy-start.6 = (bf16[2,64,128]{2,1,0:T(8,128)(2,1)S(1)}, bf16[2,64,128]{2,1,0:T(8,128)(2,1)}, u32[]{:S(2)}) copy-start(bf16[2,64,128]{2,1,0:T(8,128)(2,1)} %refs_0_.1) | copy-start | bytes 98308
  6.3 4.7 %collective-permute-start.2 = (bf16[4,32,128]{2,1,0:T(8,128)(2,1)S(1)}, bf16[4,32,128]{2,1,0:T(8,128)(2,1)S(1)}, u32[]{:S(2)}, u32[]{:S(2)}) collective-permute-start(bf16[4,32,128]{2,1,0:T(8,128)(2,1)S(1)} %get-tuple-element.33), channel_id=1, source_target_pairs={{0,2},{1,3},{2,0},{3,1},{4,6},{5,7},{6,4},{7,5},{8,10},{9,11},{10,... | collective-permute-start | bytes 98312 | tf_op jit(solution)/shard_map/ppermute | solution.py:26
  7.8 3.2 %copy-start.7 = (s32[256]{0:T(256)S(1)}, s32[256]{0:T(256)}, u32[]{:S(2)}) copy-start(s32[256]{0:T(256)} %param.17) | copy-start | bytes 3076
  7.8 4.7 %collective-permute-start.1 = (bf16[4,64,128]{2,1,0:T(8,128)(2,1)S(1)}, bf16[4,64,128]{2,1,0:T(8,128)(2,1)S(1)}, u32[]{:S(2)}, u32[]{:S(2)}) collective-permute-start(bf16[4,64,128]{2,1,0:T(8,128)(2,1)S(1)} %constant_dynamic-update-slice_fusion.refs_0_), channel_id=1, source_target_pairs={{0,8},{4,12},{8,0},{12,4},{16,24},{20,28},{24,16},{28,20},{1,9},{5... | collective-permute-start | bytes 196616 | tf_op jit(solution)/shard_map/ppermute | solution.py:26
  9.4 4.6 %collective-permute-start.4 = (bf16[4,64,128]{2,1,0:T(8,128)(2,1)S(1)}, bf16[4,64,128]{2,1,0:T(8,128)(2,1)S(1)}, u32[]{:S(2)}, u32[]{:S(2)}) collective-permute-start(bf16[4,64,128]{2,1,0:T(8,128)(2,1)S(1)} %constant_dynamic-update-slice_fusion.refs_0_), channel_id=1, source_target_pairs={{0,4},{4,0},{8,12},{12,8},{16,20},{20,16},{24,28},{28,24},{1,5},{5... | collective-permute-start | bytes 196616 | tf_op jit(solution)/shard_map/ppermute | solution.py:26
  11.0 0.8 %copy-start.1 = (bf16[128,128]{1,0:T(8,128)(2,1)S(1)}, bf16[128,128]{1,0:T(8,128)(2,1)}, u32[]{:S(2)}) copy-start(bf16[128,128]{1,0:T(8,128)(2,1)} %w_lin_ref.7) | copy-start | bytes 98308
  11.0 0.8 %copy-start.2 = (bf16[128,128]{1,0:T(8,128)(2,1)S(1)}, bf16[128,128]{1,0:T(8,128)(2,1)}, u32[]{:S(2)}) copy-start(bf16[128,128]{1,0:T(8,128)(2,1)} %w_gate_ref.7) | copy-start | bytes 98308
  11.0 2.6 %collective-permute-start.5 = (bf16[8,32,128]{2,1,0:T(8,128)(2,1)S(1)}, bf16[8,32,128]{2,1,0:T(8,128)(2,1)S(1)}, u32[]{:S(2)}, u32[]{:S(2)}) collective-permute-start(bf16[8,32,128]{2,1,0:T(8,128)(2,1)S(1)} %constant_dynamic-update-slice_fusion.2.even_ref), channel_id=1, source_target_pairs={{0,1},{1,0},{2,3},{3,2},{4,5},{5,4},{6,7},{7,6},{8,9},{9,8},{10,11... | collective-permute-start | bytes 196616 | tf_op jit(solution)/shard_map/ppermute | solution.py:26
  11.8 2.0 %copy-start.3 = (bf16[128,128]{1,0:T(8,128)(2,1)S(1)}, bf16[128,128]{1,0:T(8,128)(2,1)}, u32[]{:S(2)}) copy-start(bf16[128,128]{1,0:T(8,128)(2,1)} %w_lin_ref.6) | copy-start | bytes 98308
  11.8 2.0 %copy-start.4 = (bf16[128,128]{1,0:T(8,128)(2,1)S(1)}, bf16[128,128]{1,0:T(8,128)(2,1)}, u32[]{:S(2)}) copy-start(bf16[128,128]{1,0:T(8,128)(2,1)} %w_gate_ref.6) | copy-start | bytes 98308
  12.5 1.2 %copy-start.8 = (s32[16]{0:T(128)S(1)}, s32[16]{0:T(128)}, u32[]{:S(2)}) copy-start(s32[16]{0:T(128)} %param.16) | copy-start | bytes 196
  12.5 4.3 %collective-permute-start.3 = (bf16[4,64,128]{2,1,0:T(8,128)(2,1)S(1)}, bf16[4,64,128]{2,1,0:T(8,128)(2,1)S(1)}, u32[]{:S(2)}, u32[]{:S(2)}) collective-permute-start(bf16[4,64,128]{2,1,0:T(8,128)(2,1)S(1)} %collective-permute-done.1.refs_1_), channel_id=1, source_target_pairs={{0,4},{4,0},{8,12},{12,8},{16,20},{20,16},{24,28},{28,24},{1,5},{5... | collective-permute-start | bytes 196616 | tf_op jit(solution)/shard_map/ppermute | solution.py:26
  18.0 1.4 %collective-permute-start.6 = (f32[2,128,128]{2,1,0:T(8,128)S(1)}, f32[2,128,128]{2,1,0:T(8,128)S(1)}, u32[]{:S(2)}, u32[]{:S(2)}) collective-permute-start(f32[2,128,128]{2,1,0:T(8,128)S(1)} %get-tuple-element.47), channel_id=1, source_target_pairs={{0,1},{1,0},{2,3},{3,2},{4,5},{5,4},{6,7},{7,6},{8,9},{9,8},{10,11... | collective-permute-start | bytes 393224 | tf_op jit(solution)/shard_map/ppermute | solution.py:26
  19.4 3.4 %collective-permute-start.7 = (bf16[128,128]{1,0:T(8,128)(2,1)S(1)}, bf16[128,128]{1,0:T(8,128)(2,1)S(1)}, u32[]{:S(2)}, u32[]{:S(2)}) collective-permute-start(bf16[128,128]{1,0:T(8,128)(2,1)S(1)} %fusion.1), channel_id=1, source_target_pairs={{0,3},{1,2},{2,1},{3,0},{4,7},{5,6},{6,5},{7,4},{8,11},{9,10},{10,... | collective-permute-start | bytes 98312 | tf_op jit(solution)/shard_map/ppermute | solution.py:32
  22.9 3.4 %collective-permute-start.8 = (bf16[128,128]{1,0:T(8,128)(2,1)S(1)}, bf16[128,128]{1,0:T(8,128)(2,1)S(1)}, u32[]{:S(2)}, u32[]{:S(2)}) collective-permute-start(bf16[128,128]{1,0:T(8,128)(2,1)S(1)} %fusion), channel_id=1, source_target_pairs={{0,5},{1,4},{2,7},{3,6},{4,1},{5,0},{6,3},{7,2},{8,13},{9,12},{10,... | collective-permute-start | bytes 98312 | tf_op jit(solution)/shard_map/ppermute | solution.py:32
  23.8 2.5 %collective-permute-start.9 = (f32[2,4,32,128]{3,2,1,0:T(8,128)S(1)}, f32[2,4,32,128]{3,2,1,0:T(8,128)S(1)}, u32[]{:S(2)}, u32[]{:S(2)}) collective-permute-start(f32[2,4,32,128]{3,2,1,0:T(8,128)S(1)} %get-tuple-element.52), channel_id=1, source_target_pairs={{0,1},{1,0},{2,3},{3,2},{4,5},{5,4},{6,7},{7,6},{8,9},{9,8},{10,11... | collective-permute-start | bytes 393224 | tf_op jit(solution)/shard_map/ppermute | solution.py:26
  26.3 3.4 %collective-permute-start.11 = (bf16[128,128]{1,0:T(8,128)(2,1)S(1)}, bf16[128,128]{1,0:T(8,128)(2,1)S(1)}, u32[]{:S(2)}, u32[]{:S(2)}) collective-permute-start(bf16[128,128]{1,0:T(8,128)(2,1)S(1)} %add_convert_fusion.2), channel_id=1, source_target_pairs={{0,9},{1,8},{2,11},{3,10},{4,13},{5,12},{6,15},{7,14},{8,1},{9,0},... | collective-permute-start | bytes 98312 | tf_op jit(solution)/shard_map/ppermute | solution.py:32
  29.8 4.3 %collective-permute-start.12 = (bf16[128,128]{1,0:T(8,128)(2,1)S(1)}, bf16[128,128]{1,0:T(8,128)(2,1)S(1)}, u32[]{:S(2)}, u32[]{:S(2)}) collective-permute-start(bf16[128,128]{1,0:T(8,128)(2,1)S(1)} %add_convert_fusion.1), channel_id=1, source_target_pairs={{0,17},{1,16},{2,19},{3,18},{4,21},{5,20},{6,23},{7,22},{8,25},{9,... | collective-permute-start | bytes 98312 | tf_op jit(solution)/shard_map/ppermute | solution.py:32
  31.8 4.0 %collective-permute-start.10 = (bf16[1,4,32,128]{3,2,1,0:T(8,128)(2,1)S(1)}, bf16[1,4,32,128]{3,2,1,0:T(8,128)(2,1)S(1)}, u32[]{:S(2)}, u32[]{:S(2)}) collective-permute-start(bf16[1,4,32,128]{3,2,1,0:T(8,128)(2,1)S(1)} %get-tuple-element.55), channel_id=1, source_target_pairs={{0,2},{1,3},{2,0},{3,1},{4,6},{5,7},{6,4},{7,5},{8,10},{9,11},{10,... | collective-permute-start | bytes 98312 | tf_op jit(solution)/shard_map/ppermute | solution.py:26
  34.1 3.4 %collective-permute-start.13 = (bf16[128,128]{1,0:T(8,128)(2,1)S(1)}, bf16[128,128]{1,0:T(8,128)(2,1)S(1)}, u32[]{:S(2)}, u32[]{:S(2)}) collective-permute-start(bf16[128,128]{1,0:T(8,128)(2,1)S(1)} %add_convert_fusion), channel_id=1, source_target_pairs={{0,3},{1,2},{2,1},{3,0},{4,7},{5,6},{6,5},{7,4},{8,11},{9,10},{10,... | collective-permute-start | bytes 98312 | tf_op jit(solution)/shard_map/ppermute | solution.py:32
  37.5 1.8 %collective-permute-start.14 = (bf16[2,128,128]{2,1,0:T(8,128)(2,1)S(1)}, bf16[2,128,128]{2,1,0:T(8,128)(2,1)S(1)}, u32[]{:S(2)}, u32[]{:S(2)}) collective-permute-start(bf16[2,128,128]{2,1,0:T(8,128)(2,1)S(1)} %pad_maximum_fusion), channel_id=1, source_target_pairs={{0,1},{1,0},{2,3},{3,2},{4,5},{5,4},{6,7},{7,6},{8,9},{9,8},{10,11... | collective-permute-start | bytes 196616 | tf_op jit(solution)/shard_map/ppermute | solution.py:26

commit v4 on v3

--- a/solution.py
+++ b/solution.py
@@ -14,6 +14,7 @@
 SMEM = pl.BlockSpec(memory_space=pltpu.SMEM)
 J_STEP = 4
 FORWARD_STEP = 32
+W_STEP = 16
 STAGE_COST = 400000
 
 
@@ -59,22 +60,37 @@
     return linear, sigmoid
 
 
-def stage_kernel(n, *refs):
+def lead_kernel(out_ref):
+    out_ref[...] = jnp.zeros_like(out_ref)
+
+
+def lead():
+    return pl.pallas_call(
+        lead_kernel,
+        out_shape=jax.ShapeDtypeStruct((8, 128), F32),
+        out_specs=VMEM,
+        compiler_params=params(),
+        cost_estimate=cost(STAGE_COST * 8192, 4096),
+        name="lead",
+    )()
+
+
+def stage_kernel(n, _, *refs):
     for source_ref, copy_ref in zip(refs[:n], refs[n:]):
         copy_ref[...] = source_ref[...]
 
 
-def stage(*sources):
+def stage(after, *sources):
     n = len(sources)
     return pl.pallas_call(
         functools.partial(stage_kernel, n),
         out_shape=tuple(jax.ShapeDtypeStruct(s.shape, s.dtype) for s in sources),
-        in_specs=[VMEM] * n,
+        in_specs=[VMEM] * (n + 1),
         out_specs=(VMEM,) * n,
         compiler_params=params(),
         cost_estimate=cost(STAGE_COST * sources[0].size, 4 * sources[0].size),
         name="stage",
-    )(*sources)
+    )(after, *sources)
 
 
 def pair_forward_kernel(pair_ref, w_lin_ref, w_gate_ref, flags_ref, value_ref, lin_ref, gate_ref):
@@ -303,38 +319,37 @@
     sums_ref[...] = jnp.zeros_like(sums_ref)
     rows = [row_of(order, per, done + p) for p in range(count)]
 
-    def step(s, carry):
-        j0 = pl.multiple_of(s * J_STEP, J_STEP)
-        values = [value_ref[j0 + j].astype(F32) for j in range(J_STEP)]
-        add_sums(wide, count, j0, keys, values, sums_ref)
-        totals = [total_ref[j0 + j] for j in range(J_STEP)]
-        totals = add_totals(wide, rows, j0, slab_value_ref, totals)
-        for j in range(J_STEP):
-            d_lin_ref[j0 + j] = (totals[j] * lin_ref[j0 + j]).astype(BF16)
-            d_gate_ref[j0 + j] = (totals[j] * gate_ref[j0 + j]).astype(BF16)
-        return carry
-
-    lax.fori_loop(0, cols // J_STEP, step, 0, unroll=2)
-    for p in range(done):
-        slab_sum[row_of(order, per, p)] = first_sums_ref[p]
-    for p in range(count):
-        slab_sum[rows[p]] = sums_ref[p]
-
     def weights(rows, d_lin, d_gate):
         both = jnp.concatenate([d_lin, d_gate], axis=1)
         return lax.dot_general(
             rows, both, (((0,), (0,)), ((), ())), preferred_element_type=F32
         )
 
+    pair_w = jnp.zeros((cz, 2 * ch), F32)
+    for first in range(0, cols, W_STEP):
+        for j0 in range(first, first + W_STEP, J_STEP):
+            values = [value_ref[j0 + j].astype(F32) for j in range(J_STEP)]
+            add_sums(wide, count, j0, keys, values, sums_ref)
+            totals = [total_ref[j0 + j] for j in range(J_STEP)]
+            totals = add_totals(wide, rows, j0, slab_value_ref, totals)
+            for j in range(J_STEP):
+                d_lin_ref[j0 + j] = (totals[j] * lin_ref[j0 + j]).astype(BF16)
+                d_gate_ref[j0 + j] = (totals[j] * gate_ref[j0 + j]).astype(BF16)
+        some = slice(first, first + W_STEP)
+        pair_w = pair_w + weights(
+            pair_ref[some].reshape(W_STEP * keys, cz),
+            d_lin_ref[some].reshape(W_STEP * keys, ch),
+            d_gate_ref[some].reshape(W_STEP * keys, ch),
+        )
+    for p in range(done):
+        slab_sum[row_of(order, per, p)] = first_sums_ref[p]
+    for p in range(count):
+        slab_sum[rows[p]] = sums_ref[p]
+
     sums = slab_sum[...]
     s_lin = (sums * slab_lin_ref[...]).astype(BF16).reshape(slab_rows * keys, ch)
     s_gate = (sums * slab_gate_ref[...]).astype(BF16).reshape(slab_rows * keys, ch)
     slab_w = weights(slab_ref[...].reshape(slab_rows * keys, cz), s_lin, s_gate)
-    pair_w = weights(
-        pair_ref[...].reshape(cols * keys, cz),
-        d_lin_ref[...].reshape(cols * keys, ch),
-        d_gate_ref[...].reshape(cols * keys, ch),
-    )
     first = parity() == 0
     keep = jnp.where(first, slab_w, pair_w)
     send = jnp.where(first, pair_w, slab_w)
@@ -458,7 +473,7 @@
 
     steps = [row_bits[-1]] + row_bits[1:-1] + row_bits[:1]
     ch = w_a_lin.shape[1]
-    held, own_slab = stage(grad_out, pair_slab)
+    held, own_slab = stage(lead(), grad_out, pair_slab)
     order = [0]
     blocks = {0: own_slab}
     for bit in reversed(col_bits[1:]):

time: 40.4 us -> 39.7 us (0.983)
  starting transfers between devices: 18.4 us -> 21.2 us
  waiting for transfers between devices: 11.5 us -> 9.78 us
  local copies, waits for them, and re-layouts: 2.3 us -> 0.79 us
    ppermute x5, starting transfers between devices: 5.53 us -> 8.27 us  [swap_chips(): return lax.ppermute(value, ('row', 'col'), pairs)]
    ppermute x5, waiting for transfers between devices: 7.65 us -> 5.94 us  [swap_chips(): return lax.ppermute(value, ('row', 'col'), pairs)]
    unnamed x20, local copies, waits for them, and re-layouts: 2.12 us -> 0.61 us
  transfers between devices with their start and end apart: 15 -> 15, of which waited for: 9 -> 10; matrix products, arithmetic and copies ran while one was open for 1% -> 1% of each run, Pallas kernels for 12% -> 13%
where the time goes in v4:
time: 39.7 us; the launch traced here: 39.5 us
  starting transfers between devices  21.2 us (53%)
  waiting for transfers between devices  9.78 us (25%)
  Pallas kernels  6 us (15%)
  other arithmetic  0.85 us (2%)
  between operations  0.85 us (2%)
  local copies, waits for them, and re-layouts  0.79 us (2%)
    ppermute x10, starting transfers between devices, swap(): return lax.ppermute(value, axis, [(d, d ^ bit) for d in range(size)])  13 us
    ppermute x5, starting transfers between devices, swap_chips(): return lax.ppermute(value, ('row', 'col'), pairs)  8.27 us
    ppermute x5, waiting for transfers between devices, swap_chips(): return lax.ppermute(value, ('row', 'col'), pairs)  5.94 us
    ppermute x10, waiting for transfers between devices, swap(): return lax.ppermute(value, axis, [(d, d ^ bit) for d in range(size)])  3.84 us
    pallas_call x1, Pallas kernels, pair_out(): pl.pallas_call(pair_out_kernel, out_shape=jax.ShapeDtypeStruct((cols * ke...  1.23 us
    pallas_call x1, Pallas kernels, main_part(): pl.pallas_call(functools.partial(main_kernel, order, blocks), out_shape=(...  1.05 us
    pallas_call x1, Pallas kernels, first_sums(): pl.pallas_call(functools.partial(sums_kernel, len(grads)), out_shape=jax....  0.98 us
    pallas_call x1, Pallas kernels, first_totals(): pl.pallas_call(functools.partial(totals_kernel, order, len(grads)), out_s...  0.98 us
  transfers between devices with their start and end apart: 15, of which 10 were waited for; matrix products, arithmetic and copies ran while one was open for 1% of the time, Pallas kernels for 13%

profile of v4, /device:TPU:0, one launch (start us, length us, event | category | flops | bytes accessed | tf_op | source)
XLA Modules:
  0.0 39.5 jit_solution(10309789411901657191)
XLA Ops:
  0.6 4.1 %collective-permute-start = (bf16[2,64,128]{2,1,0:T(8,128)(2,1)}, bf16[2,64,128]{2,1,0:T(8,128)(2,1)S(1)}, u32[]{:S(2)}, u32[]{:S(2)}) collective-permute-start(bf16[2,64,128]{2,1,0:T(8,128)(2,1)} %refs_0_.1), channel_id=1, source_target_pairs={{0,16},{4,20},{8,24},{12,28},{16,0},{20,4},{24,8},{28,12},{1,17},{... | collective-permute-start | bytes 98312 | tf_op jit(solution)/shard_map/ppermute | solution.py:27
  4.8 1.6 %collective-permute-start.2 = (bf16[4,32,128]{2,1,0:T(8,128)(2,1)S(1)}, bf16[4,32,128]{2,1,0:T(8,128)(2,1)S(1)}, u32[]{:S(2)}, u32[]{:S(2)}) collective-permute-start(bf16[4,32,128]{2,1,0:T(8,128)(2,1)S(1)} %get-tuple-element.33), channel_id=1, source_target_pairs={{0,2},{1,3},{2,0},{3,1},{4,6},{5,7},{6,4},{7,5},{8,10},{9,11},{10,... | collective-permute-start | bytes 98312 | tf_op jit(solution)/shard_map/ppermute | solution.py:27
  6.3 0.9 %collective-permute-done = bf16[2,64,128]{2,1,0:T(8,128)(2,1)S(1)} collective-permute-done((bf16[2,64,128]{2,1,0:T(8,128)(2,1)}, bf16[2,64,128]{2,1,0:T(8,128)(2,1)S(1)}, u32[]{:S(2)}, u32[]{:S(2)}) %collective-permute-start) | collective-permute-done | bytes 32800 | tf_op jit(solution)/shard_map/ppermute | solution.py:27
  7.2 1.6 %collective-permute-start.1 = (bf16[4,64,128]{2,1,0:T(8,128)(2,1)S(1)}, bf16[4,64,128]{2,1,0:T(8,128)(2,1)S(1)}, u32[]{:S(2)}, u32[]{:S(2)}) collective-permute-start(bf16[4,64,128]{2,1,0:T(8,128)(2,1)S(1)} %constant_dynamic-update-slice_fusion.refs_0_), channel_id=1, source_target_pairs={{0,8},{4,12},{8,0},{12,4},{16,24},{20,28},{24,16},{28,20},{1,9},{5... | collective-permute-start | bytes 196616 | tf_op jit(solution)/shard_map/ppermute | solution.py:27
  8.8 1.5 %collective-permute-start.4 = (bf16[4,64,128]{2,1,0:T(8,128)(2,1)S(1)}, bf16[4,64,128]{2,1,0:T(8,128)(2,1)S(1)}, u32[]{:S(2)}, u32[]{:S(2)}) collective-permute-start(bf16[4,64,128]{2,1,0:T(8,128)(2,1)S(1)} %constant_dynamic-update-slice_fusion.refs_0_), channel_id=1, source_target_pairs={{0,4},{4,0},{8,12},{12,8},{16,20},{20,16},{24,28},{28,24},{1,5},{5... | collective-permute-start | bytes 196616 | tf_op jit(solution)/shard_map/ppermute | solution.py:27
  11.9 1.4 %collective-permute-start.3 = (bf16[4,64,128]{2,1,0:T(8,128)(2,1)S(1)}, bf16[4,64,128]{2,1,0:T(8,128)(2,1)S(1)}, u32[]{:S(2)}, u32[]{:S(2)}) collective-permute-start(bf16[4,64,128]{2,1,0:T(8,128)(2,1)S(1)} %collective-permute-done.1.refs_1_), channel_id=1, source_target_pairs={{0,4},{4,0},{8,12},{12,8},{16,20},{20,16},{24,28},{28,24},{1,5},{5... | collective-permute-start | bytes 196616 | tf_op jit(solution)/shard_map/ppermute | solution.py:27
  13.7 1.0 %first_totals_over_i.1.total_ref = f32[64,32,128]{2,1,0:T(8,128)S(1)} custom-call(bf16[4,64,128]{2,1,0:T(8,128)(2,1)S(1)} %constant_dynamic-update-slice_fusion.refs_0_, bf16[4,64,128]{2,1,0:T(8,128)(2,1)S(1)} %collective-permute-done.1.refs_1_, bf16[4,64,128]{2,1,0:T(8,128)(2,1)S(1)} %collective-permute-done.4.refs_2_, ...), custom_call_target="tpu_custom_call" | custom-call | flops 6291456 | bytes 2097152 | tf_op jit(solution)/shard_map/first_totals_over_i/pallas_call | solution.py:276
  14.6 1.0 %first_sums_over_j.1.first_sums_ref = f32[12,32,128]{2,1,0:T(8,128)S(1)} custom-call(bf16[4,64,128]{2,1,0:T(8,128)(2,1)S(1)} %constant_dynamic-update-slice_fusion.refs_0_, bf16[4,64,128]{2,1,0:T(8,128)(2,1)S(1)} %collective-permute-done.1.refs_1_, bf16[4,64,128]{2,1,0:T(8,128)(2,1)S(1)} %collective-permute-done.4.refs_2_, ...), custom_call_target="tpu_custom_call" | custom-call | flops 6291456 | bytes 2097152 | tf_op jit(solution)/shard_map/first_sums_over_j/pallas_call | solution.py:242
  16.2 1.1 %last_rows.1 = (bf16[64,32,128]{2,1,0:T(8,128)(2,1)S(1)}, bf16[64,32,128]{2,1,0:T(8,128)(2,1)S(1)}, f32[2,4,32,128]{3,2,1,0:T(8,128)S(1)}, f32[2,4,32,128]{3,2,1...) custom-call(bf16[4,64,128]{2,1,0:T(8,128)(2,1)S(1)} %collective-permute-done.3.grad_ref, ...), custom_call_target="tpu_custom_call" | custom-call | flops 268435456 | bytes 4194304 | tf_op jit(solution)/shard_map/last_rows/pallas_call | solution.py:373
  17.4 1.3 %collective-permute-done.6 = f32[2,128,128]{2,1,0:T(8,128)S(1)} collective-permute-done((f32[2,128,128]{2,1,0:T(8,128)S(1)}, f32[2,128,128]{2,1,0:T(8,128)S(1)}, u32[]{:S(2)}, u32[]{:S(2)}) %collective-permute-start.6) | collective-permute-done | bytes 131104 | tf_op jit(solution)/shard_map/ppermute | solution.py:27
  18.7 1.3 %collective-permute-start.7 = (bf16[128,128]{1,0:T(8,128)(2,1)S(1)}, bf16[128,128]{1,0:T(8,128)(2,1)S(1)}, u32[]{:S(2)}, u32[]{:S(2)}) collective-permute-start(bf16[128,128]{1,0:T(8,128)(2,1)S(1)} %fusion.1), channel_id=1, source_target_pairs={{0,3},{1,2},{2,1},{3,0},{4,7},{5,6},{6,5},{7,4},{8,11},{9,10},{10,... | collective-permute-start | bytes 98312 | tf_op jit(solution)/shard_map/ppermute | solution.py:33
  20.0 2.1 %collective-permute-done.7 = bf16[128,128]{1,0:T(8,128)(2,1)S(1)} collective-permute-done((bf16[128,128]{1,0:T(8,128)(2,1)S(1)}, bf16[128,128]{1,0:T(8,128)(2,1)S(1)}, u32[]{:S(2)}, u32[]{:S(2)}) %collective-permute-start.7) | collective-permute-done | bytes 32800 | tf_op jit(solution)/shard_map/ppermute | solution.py:33
  22.2 1.2 %collective-permute-start.8 = (bf16[128,128]{1,0:T(8,128)(2,1)S(1)}, bf16[128,128]{1,0:T(8,128)(2,1)S(1)}, u32[]{:S(2)}, u32[]{:S(2)}) collective-permute-start(bf16[128,128]{1,0:T(8,128)(2,1)S(1)} %fusion), channel_id=1, source_target_pairs={{0,5},{1,4},{2,7},{3,6},{4,1},{5,0},{6,3},{7,2},{8,13},{9,12},{10,... | collective-permute-start | bytes 98312 | tf_op jit(solution)/shard_map/ppermute | solution.py:33
  23.7 1.9 %collective-permute-done.8 = bf16[128,128]{1,0:T(8,128)(2,1)S(1)} collective-permute-done((bf16[128,128]{1,0:T(8,128)(2,1)S(1)}, bf16[128,128]{1,0:T(8,128)(2,1)S(1)}, u32[]{:S(2)}, u32[]{:S(2)}) %collective-permute-start.8) | collective-permute-done | bytes 32800 | tf_op jit(solution)/shard_map/ppermute | solution.py:33
  25.6 1.0 %collective-permute-start.11 = (bf16[128,128]{1,0:T(8,128)(2,1)S(1)}, bf16[128,128]{1,0:T(8,128)(2,1)S(1)}, u32[]{:S(2)}, u32[]{:S(2)}) collective-permute-start(bf16[128,128]{1,0:T(8,128)(2,1)S(1)} %add_convert_fusion.2), channel_id=1, source_target_pairs={{0,9},{1,8},{2,11},{3,10},{4,13},{5,12},{6,15},{7,14},{8,1},{9,0},... | collective-permute-start | bytes 98312 | tf_op jit(solution)/shard_map/ppermute | solution.py:33
  26.6 1.2 %pair_input_grad.1 = bf16[2048,128]{1,0:T(8,128)(2,1)} custom-call(bf16[2048,128]{1,0:T(8,128)(2,1)S(1)} %bitcast.13, bf16[2048,128]{1,0:T(8,128)(2,1)S(1)} %bitcast.14, bf16[128,128]{1,0:T(8,128)(2,1)S(1)} %copy-done.1, bf16[128,128]{1,0:T(8,128)(2,1)S(1)} %copy-done.2), custom_call_target="tpu_custom_call" | custom-call | flops 134217728 | bytes 1572864 | tf_op jit(solution)/shard_map/pair_input_grad/pallas_call | solution.py:409
  27.8 1.2 %collective-permute-done.11 = bf16[128,128]{1,0:T(8,128)(2,1)S(1)} collective-permute-done((bf16[128,128]{1,0:T(8,128)(2,1)S(1)}, bf16[128,128]{1,0:T(8,128)(2,1)S(1)}, u32[]{:S(2)}, u32[]{:S(2)}) %collective-permute-start.11) | collective-permute-done | bytes 32800 | tf_op jit(solution)/shard_map/ppermute | solution.py:33
  29.1 2.7 %collective-permute-start.12 = (bf16[128,128]{1,0:T(8,128)(2,1)S(1)}, bf16[128,128]{1,0:T(8,128)(2,1)S(1)}, u32[]{:S(2)}, u32[]{:S(2)}) collective-permute-start(bf16[128,128]{1,0:T(8,128)(2,1)S(1)} %add_convert_fusion.1), channel_id=1, source_target_pairs={{0,17},{1,16},{2,19},{3,18},{4,21},{5,20},{6,23},{7,22},{8,25},{9,... | collective-permute-start | bytes 98312 | tf_op jit(solution)/shard_map/ppermute | solution.py:33
  31.7 1.6 %collective-permute-start.10 = (bf16[1,4,32,128]{3,2,1,0:T(8,128)(2,1)S(1)}, bf16[1,4,32,128]{3,2,1,0:T(8,128)(2,1)S(1)}, u32[]{:S(2)}, u32[]{:S(2)}) collective-permute-start(bf16[1,4,32,128]{3,2,1,0:T(8,128)(2,1)S(1)} %get-tuple-element.55), channel_id=1, source_target_pairs={{0,2},{1,3},{2,0},{3,1},{4,6},{5,7},{6,4},{7,5},{8,10},{9,11},{10,... | collective-permute-start | bytes 98312 | tf_op jit(solution)/shard_map/ppermute | solution.py:27
  33.4 2.2 %collective-permute-start.13 = (bf16[128,128]{1,0:T(8,128)(2,1)S(1)}, bf16[128,128]{1,0:T(8,128)(2,1)S(1)}, u32[]{:S(2)}, u32[]{:S(2)}) collective-permute-start(bf16[128,128]{1,0:T(8,128)(2,1)S(1)} %add_convert_fusion), channel_id=1, source_target_pairs={{0,3},{1,2},{2,1},{3,0},{4,7},{5,6},{6,5},{7,4},{8,11},{9,10},{10,... | collective-permute-start | bytes 98312 | tf_op jit(solution)/shard_map/ppermute | solution.py:33
  35.7 0.8 %slab_input_grad.1 = bf16[4,32,128]{2,1,0:T(8,128)(2,1)} custom-call(f32[4,32,128]{2,1,0:T(8,128)S(1)} %bitcast.15, bf16[4,32,128]{2,1,0:T(8,128)(2,1)S(1)} %bitcast.16, f32[16,32,128]{2,1,0:T(8,128)S(1)} %get-tuple-element.43.slab_lin_ref.lin_ref, f32[16,32,128]{2,1,0:T(8,128)S(1)} %get-tuple-element.44.slab_gate_ref.gate_ref, ...), custom_call_target="tpu_custom_call" | custom-call | flops 8388608 | bytes 262144 | tf_op jit(solution)/shard_map/slab_input_grad/pallas_call | solution.py:456
  37.2 0.7 %collective-permute-start.14 = (bf16[2,128,128]{2,1,0:T(8,128)(2,1)S(1)}, bf16[2,128,128]{2,1,0:T(8,128)(2,1)S(1)}, u32[]{:S(2)}, u32[]{:S(2)}) collective-permute-start(bf16[2,128,128]{2,1,0:T(8,128)(2,1)S(1)} %pad_maximum_fusion), channel_id=1, source_target_pairs={{0,1},{1,0},{2,3},{3,2},{4,5},{5,4},{6,7},{7,6},{8,9},{9,8},{10,11... | collective-permute-start | bytes 196616 | tf_op jit(solution)/shard_map/ppermute | solution.py:27
  37.9 0.9 %collective-permute-done.14 = bf16[2,128,128]{2,1,0:T(8,128)(2,1)S(1)} collective-permute-done((bf16[2,128,128]{2,1,0:T(8,128)(2,1)S(1)}, bf16[2,128,128]{2,1,0:T(8,128)(2,1)S(1)}, u32[]{:S(2)}, u32[]{:S(2)}) %collective-permute-start.14) | collective-permute-done | bytes 65568 | tf_op jit(solution)/shard_map/ppermute | solution.py:27
  38.8 0.7 %maximum_select_fusion = f32[4,128,128]{2,1,0:T(8,128)} fusion(f32[2,128,128]{2,1,0:T(8,128)S(1)} %convert_multiply_fusion, f32[2,128,128]{2,1,0:T(8,128)S(1)} %convert_multiply_fusion.1, pred[]{:T(512)S(6)} %eq.3), kind=kLoop, calls=%fused_computation | loop fusion | flops 196608 | bytes 524289 | tf_op jit(solution)/shard_map/jit(_where)/select_n | solution.py:536
  (52 shorter events, 3.9 us)
Async XLA Ops:
  0.6 4.1 %copy-start.6 = (bf16[2,64,128]{2,1,0:T(8,128)(2,1)S(1)}, bf16[2,64,128]{2,1,0:T(8,128)(2,1)}, u32[]{:S(2)}) copy-start(bf16[2,64,128]{2,1,0:T(8,128)(2,1)} %refs_0_.1) | copy-start | bytes 98308
  0.6 4.1 %copy-start.5 = (bf16[4,32,128]{2,1,0:T(8,128)(2,1)S(1)}, bf16[4,32,128]{2,1,0:T(8,128)(2,1)}, u32[]{:S(2)}) copy-start(bf16[4,32,128]{2,1,0:T(8,128)(2,1)} %refs_1_.1) | copy-start | bytes 98308
  0.6 6.6 %collective-permute-start = (bf16[2,64,128]{2,1,0:T(8,128)(2,1)}, bf16[2,64,128]{2,1,0:T(8,128)(2,1)S(1)}, u32[]{:S(2)}, u32[]{:S(2)}) collective-permute-start(bf16[2,64,128]{2,1,0:T(8,128)(2,1)} %refs_0_.1), channel_id=1, source_target_pairs={{0,16},{4,20},{8,24},{12,28},{16,0},{20,4},{24,8},{28,12},{1,17},{... | collective-permute-start | bytes 98312 | tf_op jit(solution)/shard_map/ppermute | solution.py:27
  4.8 5.8 %copy-start = (bf16[64,32,128]{2,1,0:T(8,128)(2,1)S(1)}, bf16[64,32,128]{2,1,0:T(8,128)(2,1)}, u32[]{:S(2)}) copy-start(bf16[64,32,128]{2,1,0:T(8,128)(2,1)} %pair_ref.3) | copy-start | bytes 1572868
  4.8 5.6 %collective-permute-start.2 = (bf16[4,32,128]{2,1,0:T(8,128)(2,1)S(1)}, bf16[4,32,128]{2,1,0:T(8,128)(2,1)S(1)}, u32[]{:S(2)}, u32[]{:S(2)}) collective-permute-start(bf16[4,32,128]{2,1,0:T(8,128)(2,1)S(1)} %get-tuple-element.33), channel_id=1, source_target_pairs={{0,2},{1,3},{2,0},{3,1},{4,6},{5,7},{6,4},{7,5},{8,10},{9,11},{10,... | collective-permute-start | bytes 98312 | tf_op jit(solution)/shard_map/ppermute | solution.py:27
  7.2 3.2 %copy-start.7 = (s32[256]{0:T(256)S(1)}, s32[256]{0:T(256)}, u32[]{:S(2)}) copy-start(s32[256]{0:T(256)} %param.17) | copy-start | bytes 3076
  7.2 4.7 %collective-permute-start.1 = (bf16[4,64,128]{2,1,0:T(8,128)(2,1)S(1)}, bf16[4,64,128]{2,1,0:T(8,128)(2,1)S(1)}, u32[]{:S(2)}, u32[]{:S(2)}) collective-permute-start(bf16[4,64,128]{2,1,0:T(8,128)(2,1)S(1)} %constant_dynamic-update-slice_fusion.refs_0_), channel_id=1, source_target_pairs={{0,8},{4,12},{8,0},{12,4},{16,24},{20,28},{24,16},{28,20},{1,9},{5... | collective-permute-start | bytes 196616 | tf_op jit(solution)/shard_map/ppermute | solution.py:27
  8.8 4.8 %collective-permute-start.4 = (bf16[4,64,128]{2,1,0:T(8,128)(2,1)S(1)}, bf16[4,64,128]{2,1,0:T(8,128)(2,1)S(1)}, u32[]{:S(2)}, u32[]{:S(2)}) collective-permute-start(bf16[4,64,128]{2,1,0:T(8,128)(2,1)S(1)} %constant_dynamic-update-slice_fusion.refs_0_), channel_id=1, source_target_pairs={{0,4},{4,0},{8,12},{12,8},{16,20},{20,16},{24,28},{28,24},{1,5},{5... | collective-permute-start | bytes 196616 | tf_op jit(solution)/shard_map/ppermute | solution.py:27
  10.4 0.8 %copy-start.1 = (bf16[128,128]{1,0:T(8,128)(2,1)S(1)}, bf16[128,128]{1,0:T(8,128)(2,1)}, u32[]{:S(2)}) copy-start(bf16[128,128]{1,0:T(8,128)(2,1)} %w_lin_ref.7) | copy-start | bytes 98308
  10.4 0.8 %copy-start.2 = (bf16[128,128]{1,0:T(8,128)(2,1)S(1)}, bf16[128,128]{1,0:T(8,128)(2,1)}, u32[]{:S(2)}) copy-start(bf16[128,128]{1,0:T(8,128)(2,1)} %w_gate_ref.7) | copy-start | bytes 98308
  10.4 2.9 %collective-permute-start.5 = (bf16[8,32,128]{2,1,0:T(8,128)(2,1)S(1)}, bf16[8,32,128]{2,1,0:T(8,128)(2,1)S(1)}, u32[]{:S(2)}, u32[]{:S(2)}) collective-permute-start(bf16[8,32,128]{2,1,0:T(8,128)(2,1)S(1)} %constant_dynamic-update-slice_fusion.2.even_ref), channel_id=1, source_target_pairs={{0,1},{1,0},{2,3},{3,2},{4,5},{5,4},{6,7},{7,6},{8,9},{9,8},{10,11... | collective-permute-start | bytes 196616 | tf_op jit(solution)/shard_map/ppermute | solution.py:27
  11.2 2.2 %copy-start.3 = (bf16[128,128]{1,0:T(8,128)(2,1)S(1)}, bf16[128,128]{1,0:T(8,128)(2,1)}, u32[]{:S(2)}) copy-start(bf16[128,128]{1,0:T(8,128)(2,1)} %w_lin_ref.6) | copy-start | bytes 98308
  11.2 2.2 %copy-start.4 = (bf16[128,128]{1,0:T(8,128)(2,1)S(1)}, bf16[128,128]{1,0:T(8,128)(2,1)}, u32[]{:S(2)}) copy-start(bf16[128,128]{1,0:T(8,128)(2,1)} %w_gate_ref.6) | copy-start | bytes 98308
  11.9 1.4 %copy-start.8 = (s32[16]{0:T(128)S(1)}, s32[16]{0:T(128)}, u32[]{:S(2)}) copy-start(s32[16]{0:T(128)} %param.16) | copy-start | bytes 196
  11.9 4.3 %collective-permute-start.3 = (bf16[4,64,128]{2,1,0:T(8,128)(2,1)S(1)}, bf16[4,64,128]{2,1,0:T(8,128)(2,1)S(1)}, u32[]{:S(2)}, u32[]{:S(2)}) collective-permute-start(bf16[4,64,128]{2,1,0:T(8,128)(2,1)S(1)} %collective-permute-done.1.refs_1_), channel_id=1, source_target_pairs={{0,4},{4,0},{8,12},{12,8},{16,20},{20,16},{24,28},{28,24},{1,5},{5... | collective-permute-start | bytes 196616 | tf_op jit(solution)/shard_map/ppermute | solution.py:27
  17.3 1.4 %collective-permute-start.6 = (f32[2,128,128]{2,1,0:T(8,128)S(1)}, f32[2,128,128]{2,1,0:T(8,128)S(1)}, u32[]{:S(2)}, u32[]{:S(2)}) collective-permute-start(f32[2,128,128]{2,1,0:T(8,128)S(1)} %get-tuple-element.47), channel_id=1, source_target_pairs={{0,1},{1,0},{2,3},{3,2},{4,5},{5,4},{6,7},{7,6},{8,9},{9,8},{10,11... | collective-permute-start | bytes 393224 | tf_op jit(solution)/shard_map/ppermute | solution.py:27
  18.7 3.4 %collective-permute-start.7 = (bf16[128,128]{1,0:T(8,128)(2,1)S(1)}, bf16[128,128]{1,0:T(8,128)(2,1)S(1)}, u32[]{:S(2)}, u32[]{:S(2)}) collective-permute-start(bf16[128,128]{1,0:T(8,128)(2,1)S(1)} %fusion.1), channel_id=1, source_target_pairs={{0,3},{1,2},{2,1},{3,0},{4,7},{5,6},{6,5},{7,4},{8,11},{9,10},{10,... | collective-permute-start | bytes 98312 | tf_op jit(solution)/shard_map/ppermute | solution.py:33
  22.2 3.4 %collective-permute-start.8 = (bf16[128,128]{1,0:T(8,128)(2,1)S(1)}, bf16[128,128]{1,0:T(8,128)(2,1)S(1)}, u32[]{:S(2)}, u32[]{:S(2)}) collective-permute-start(bf16[128,128]{1,0:T(8,128)(2,1)S(1)} %fusion), channel_id=1, source_target_pairs={{0,5},{1,4},{2,7},{3,6},{4,1},{5,0},{6,3},{7,2},{8,13},{9,12},{10,... | collective-permute-start | bytes 98312 | tf_op jit(solution)/shard_map/ppermute | solution.py:33
  23.3 2.3 %collective-permute-start.9 = (f32[2,4,32,128]{3,2,1,0:T(8,128)S(1)}, f32[2,4,32,128]{3,2,1,0:T(8,128)S(1)}, u32[]{:S(2)}, u32[]{:S(2)}) collective-permute-start(f32[2,4,32,128]{3,2,1,0:T(8,128)S(1)} %get-tuple-element.52), channel_id=1, source_target_pairs={{0,1},{1,0},{2,3},{3,2},{4,5},{5,4},{6,7},{7,6},{8,9},{9,8},{10,11... | collective-permute-start | bytes 393224 | tf_op jit(solution)/shard_map/ppermute | solution.py:27
  25.6 3.4 %collective-permute-start.11 = (bf16[128,128]{1,0:T(8,128)(2,1)S(1)}, bf16[128,128]{1,0:T(8,128)(2,1)S(1)}, u32[]{:S(2)}, u32[]{:S(2)}) collective-permute-start(bf16[128,128]{1,0:T(8,128)(2,1)S(1)} %add_convert_fusion.2), channel_id=1, source_target_pairs={{0,9},{1,8},{2,11},{3,10},{4,13},{5,12},{6,15},{7,14},{8,1},{9,0},... | collective-permute-start | bytes 98312 | tf_op jit(solution)/shard_map/ppermute | solution.py:33
  29.1 4.3 %collective-permute-start.12 = (bf16[128,128]{1,0:T(8,128)(2,1)S(1)}, bf16[128,128]{1,0:T(8,128)(2,1)S(1)}, u32[]{:S(2)}, u32[]{:S(2)}) collective-permute-start(bf16[128,128]{1,0:T(8,128)(2,1)S(1)} %add_convert_fusion.1), channel_id=1, source_target_pairs={{0,17},{1,16},{2,19},{3,18},{4,21},{5,20},{6,23},{7,22},{8,25},{9,... | collective-permute-start | bytes 98312 | tf_op jit(solution)/shard_map/ppermute | solution.py:33
  31.7 4.0 %collective-permute-start.10 = (bf16[1,4,32,128]{3,2,1,0:T(8,128)(2,1)S(1)}, bf16[1,4,32,128]{3,2,1,0:T(8,128)(2,1)S(1)}, u32[]{:S(2)}, u32[]{:S(2)}) collective-permute-start(bf16[1,4,32,128]{3,2,1,0:T(8,128)(2,1)S(1)} %get-tuple-element.55), channel_id=1, source_target_pairs={{0,2},{1,3},{2,0},{3,1},{4,6},{5,7},{6,4},{7,5},{8,10},{9,11},{10,... | collective-permute-start | bytes 98312 | tf_op jit(solution)/shard_map/ppermute | solution.py:27
  33.4 3.8 %collective-permute-start.13 = (bf16[128,128]{1,0:T(8,128)(2,1)S(1)}, bf16[128,128]{1,0:T(8,128)(2,1)S(1)}, u32[]{:S(2)}, u32[]{:S(2)}) collective-permute-start(bf16[128,128]{1,0:T(8,128)(2,1)S(1)} %add_convert_fusion), channel_id=1, source_target_pairs={{0,3},{1,2},{2,1},{3,0},{4,7},{5,6},{6,5},{7,4},{8,11},{9,10},{10,... | collective-permute-start | bytes 98312 | tf_op jit(solution)/shard_map/ppermute | solution.py:33
  37.2 1.6 %collective-permute-start.14 = (bf16[2,128,128]{2,1,0:T(8,128)(2,1)S(1)}, bf16[2,128,128]{2,1,0:T(8,128)(2,1)S(1)}, u32[]{:S(2)}, u32[]{:S(2)}) collective-permute-start(bf16[2,128,128]{2,1,0:T(8,128)(2,1)S(1)} %pad_maximum_fusion), channel_id=1, source_target_pairs={{0,1},{1,0},{2,3},{3,2},{4,5},{5,4},{6,7},{7,6},{8,9},{9,8},{10,11... | collective-permute-start | bytes 196616 | tf_op jit(solution)/shard_map/ppermute | solution.py:27

commit v5 on v4

--- a/solution.py
+++ b/solution.py
@@ -27,9 +27,9 @@
     return lax.ppermute(value, axis, [(d, d ^ bit) for d in range(size)])
 
 
-def swap_chips(value, bit):
+def swap_chips(value, bit, flip=1):
     n_row, n_col = lax.axis_size("row"), lax.axis_size("col")
-    pairs = [(d, d ^ bit ^ 1) for d in range(n_row * n_col)]
+    pairs = [(d, d ^ bit ^ flip) for d in range(n_row * n_col)]
     return lax.ppermute(value, ("row", "col"), pairs)
 
 
@@ -515,18 +515,19 @@
     part = part + swap_chips(moved, pair_bit).astype(F32)
     bits = col_bits[2:] + [bit * n_col for bit in row_bits]
     sums, got = sum_keep, swap(sum_send, "col", 1)
-    for bit in bits:
+    narrow = part.astype(BF16)
+    near, next_ = bits[0], bits[1]
+    diagonal = swap_chips(narrow, near | next_, 0)
+    part = narrow.astype(F32) + swap_chips(narrow, near).astype(F32)
+    part = part + (swap_chips(narrow, next_).astype(F32) + diagonal.astype(F32))
+    for bit in bits[2:]:
         narrow = part.astype(BF16)
-        if bit == bits[1]:
-            narrow, got = lax.optimization_barrier((narrow, got))
+        if bit == bits[2]:
+            narrow, got, d_lin, d_gate = lax.optimization_barrier((narrow, got, d_lin, d_gate))
+            grad_pair = pair_out(d_lin, d_gate, w_b_lin, w_b_gate)
             for far in col_bits[1:]:
                 sums, moved = fold(sums, got)
                 got = swap(moved, "col", far)
-        if bit == bits[0]:
-            narrow, d_lin, d_gate = lax.optimization_barrier((narrow, d_lin, d_gate))
-            grad_pair = pair_out(d_lin, d_gate, w_b_lin, w_b_gate)
-        if bit == bits[-1]:
-            narrow, grad_pair = lax.optimization_barrier((narrow, grad_pair))
         part = narrow.astype(F32) + swap_chips(narrow, bit).astype(F32)
     narrow = part.astype(BF16)
     mine = jnp.stack([narrow, swap_chips(narrow, pair_bit)])

time: 39.7 us -> 38.8 us (0.977)
  waiting for transfers between devices: 9.78 us -> 8.48 us
  starting transfers between devices: 21.2 us -> 21.6 us
    ppermute x5 -> x6, waiting for transfers between devices: 5.94 us -> 4.69 us  [swap_chips(): return lax.ppermute(value, ('row', 'col'), pairs)]
    ppermute x5 -> x6, starting transfers between devices: 8.27 us -> 9.43 us  [swap_chips(): return lax.ppermute(value, ('row', 'col'), pairs)]
    ppermute x10, starting transfers between devices: 13 us -> 12.2 us  [swap(): return lax.ppermute(value, axis, [(d, d ^ bit) for d in range(size)])]
  transfers between devices with their start and end apart: 15 -> 16, of which waited for: 10 -> 7; matrix products, arithmetic and copies ran while one was open for 1% -> 1% of each run, Pallas kernels for 13% -> 13%
where the time goes in v5:
time: 38.8 us; the launch traced here: 38.6 us
  starting transfers between devices  21.6 us (56%)
  waiting for transfers between devices  8.48 us (22%)
  Pallas kernels  5.99 us (15%)
  other arithmetic  0.85 us (2%)
  between operations  0.85 us (2%)
  local copies, waits for them, and re-layouts  0.79 us (2%)
    ppermute x10, starting transfers between devices, swap(): return lax.ppermute(value, axis, [(d, d ^ bit) for d in range(size)])  12.2 us
    ppermute x6, starting transfers between devices, swap_chips(): return lax.ppermute(value, ('row', 'col'), pairs)  9.43 us
    ppermute x6, waiting for transfers between devices, swap_chips(): return lax.ppermute(value, ('row', 'col'), pairs)  4.69 us
    ppermute x10, waiting for transfers between devices, swap(): return lax.ppermute(value, axis, [(d, d ^ bit) for d in range(size)])  3.79 us
    pallas_call x1, Pallas kernels, pair_out(): pl.pallas_call(pair_out_kernel, out_shape=jax.ShapeDtypeStruct((cols * ke...  1.22 us
    pallas_call x1, Pallas kernels, main_part(): pl.pallas_call(functools.partial(main_kernel, order, blocks), out_shape=(...  1.05 us
    pallas_call x1, Pallas kernels, first_sums(): pl.pallas_call(functools.partial(sums_kernel, len(grads)), out_shape=jax....  0.98 us
    pallas_call x1, Pallas kernels, first_totals(): pl.pallas_call(functools.partial(totals_kernel, order, len(grads)), out_s...  0.98 us
  transfers between devices with their start and end apart: 16, of which 7 were waited for; matrix products, arithmetic and copies ran while one was open for 1% of the time, Pallas kernels for 13%

profile of v5, /device:TPU:0, one launch (start us, length us, event | category | flops | bytes accessed | tf_op | source)
XLA Modules:
  0.0 38.6 jit_solution(11327106118247807567)
XLA Ops:
  0.6 4.1 %collective-permute-start = (bf16[2,64,128]{2,1,0:T(8,128)(2,1)}, bf16[2,64,128]{2,1,0:T(8,128)(2,1)S(1)}, u32[]{:S(2)}, u32[]{:S(2)}) collective-permute-start(bf16[2,64,128]{2,1,0:T(8,128)(2,1)} %refs_0_.1), channel_id=1, source_target_pairs={{0,16},{4,20},{8,24},{12,28},{16,0},{20,4},{24,8},{28,12},{1,17},{... | collective-permute-start | bytes 98312 | tf_op jit(solution)/shard_map/ppermute | solution.py:27
  4.8 1.6 %collective-permute-start.2 = (bf16[4,32,128]{2,1,0:T(8,128)(2,1)S(1)}, bf16[4,32,128]{2,1,0:T(8,128)(2,1)S(1)}, u32[]{:S(2)}, u32[]{:S(2)}) collective-permute-start(bf16[4,32,128]{2,1,0:T(8,128)(2,1)S(1)} %get-tuple-element.30), channel_id=1, source_target_pairs={{0,2},{1,3},{2,0},{3,1},{4,6},{5,7},{6,4},{7,5},{8,10},{9,11},{10,... | collective-permute-start | bytes 98312 | tf_op jit(solution)/shard_map/ppermute | solution.py:27
  6.3 0.9 %collective-permute-done = bf16[2,64,128]{2,1,0:T(8,128)(2,1)S(1)} collective-permute-done((bf16[2,64,128]{2,1,0:T(8,128)(2,1)}, bf16[2,64,128]{2,1,0:T(8,128)(2,1)S(1)}, u32[]{:S(2)}, u32[]{:S(2)}) %collective-permute-start) | collective-permute-done | bytes 32800 | tf_op jit(solution)/shard_map/ppermute | solution.py:27
  7.2 1.6 %collective-permute-start.1 = (bf16[4,64,128]{2,1,0:T(8,128)(2,1)S(1)}, bf16[4,64,128]{2,1,0:T(8,128)(2,1)S(1)}, u32[]{:S(2)}, u32[]{:S(2)}) collective-permute-start(bf16[4,64,128]{2,1,0:T(8,128)(2,1)S(1)} %constant_dynamic-update-slice_fusion.refs_0_), channel_id=1, source_target_pairs={{0,8},{4,12},{8,0},{12,4},{16,24},{20,28},{24,16},{28,20},{1,9},{5... | collective-permute-start | bytes 196616 | tf_op jit(solution)/shard_map/ppermute | solution.py:27
  8.8 1.5 %collective-permute-start.4 = (bf16[4,64,128]{2,1,0:T(8,128)(2,1)S(1)}, bf16[4,64,128]{2,1,0:T(8,128)(2,1)S(1)}, u32[]{:S(2)}, u32[]{:S(2)}) collective-permute-start(bf16[4,64,128]{2,1,0:T(8,128)(2,1)S(1)} %constant_dynamic-update-slice_fusion.refs_0_), channel_id=1, source_target_pairs={{0,4},{4,0},{8,12},{12,8},{16,20},{20,16},{24,28},{28,24},{1,5},{5... | collective-permute-start | bytes 196616 | tf_op jit(solution)/shard_map/ppermute | solution.py:27
  11.2 0.7 %pair_forward.1 = (bf16[64,32,128]{2,1,0:T(8,128)(2,1)S(1)}, f32[64,32,128]{2,1,0:T(8,128)S(1)}, f32[64,32,128]{2,1,0:T(8,128)S(1)}) custom-call(bf16[64,32,128]{2,1,0:T(8,128)(2,1)S(1)} %copy-done, bf16[128,128]{1,0:T(8,128)(2,1)S(1)} %copy-done.1, bf16[128,128]{1,0:T(8,128)(2,1)S(1)} %copy-done.2, bf16[256,128]{1,0:T(8,128)(2,1)S(1)} %broadcast_in_dim.4.flags_ref), custom_call_target="tpu_custom_call" | custom-call | flops 134217728 | bytes 3670016 | tf_op jit(solution)/shard_map/pair_forward/pallas_call | solution.py:125
  11.9 1.4 %collective-permute-start.3 = (bf16[4,64,128]{2,1,0:T(8,128)(2,1)S(1)}, bf16[4,64,128]{2,1,0:T(8,128)(2,1)S(1)}, u32[]{:S(2)}, u32[]{:S(2)}) collective-permute-start(bf16[4,64,128]{2,1,0:T(8,128)(2,1)S(1)} %collective-permute-done.1.refs_1_), channel_id=1, source_target_pairs={{0,4},{4,0},{8,12},{12,8},{16,20},{20,16},{24,28},{28,24},{1,5},{5... | collective-permute-start | bytes 196616 | tf_op jit(solution)/shard_map/ppermute | solution.py:27
  13.7 1.0 %first_totals_over_i.1.total_ref = f32[64,32,128]{2,1,0:T(8,128)S(1)} custom-call(bf16[4,64,128]{2,1,0:T(8,128)(2,1)S(1)} %constant_dynamic-update-slice_fusion.refs_0_, bf16[4,64,128]{2,1,0:T(8,128)(2,1)S(1)} %collective-permute-done.1.refs_1_, bf16[4,64,128]{2,1,0:T(8,128)(2,1)S(1)} %collective-permute-done.4.refs_2_, ...), custom_call_target="tpu_custom_call" | custom-call | flops 6291456 | bytes 2097152 | tf_op jit(solution)/shard_map/first_totals_over_i/pallas_call | solution.py:276
  14.6 1.0 %first_sums_over_j.1.first_sums_ref = f32[12,32,128]{2,1,0:T(8,128)S(1)} custom-call(bf16[4,64,128]{2,1,0:T(8,128)(2,1)S(1)} %constant_dynamic-update-slice_fusion.refs_0_, bf16[4,64,128]{2,1,0:T(8,128)(2,1)S(1)} %collective-permute-done.1.refs_1_, bf16[4,64,128]{2,1,0:T(8,128)(2,1)S(1)} %collective-permute-done.4.refs_2_, ...), custom_call_target="tpu_custom_call" | custom-call | flops 6291456 | bytes 2097152 | tf_op jit(solution)/shard_map/first_sums_over_j/pallas_call | solution.py:242
  16.2 1.1 %last_rows.1 = (bf16[64,32,128]{2,1,0:T(8,128)(2,1)S(1)}, bf16[64,32,128]{2,1,0:T(8,128)(2,1)S(1)}, f32[2,4,32,128]{3,2,1,0:T(8,128)S(1)}, f32[2,4,32,128]{3,2,1...) custom-call(bf16[4,64,128]{2,1,0:T(8,128)(2,1)S(1)} %collective-permute-done.3.grad_ref, ...), custom_call_target="tpu_custom_call" | custom-call | flops 268435456 | bytes 4194304 | tf_op jit(solution)/shard_map/last_rows/pallas_call | solution.py:373
  17.4 1.3 %collective-permute-done.6 = f32[2,128,128]{2,1,0:T(8,128)S(1)} collective-permute-done((f32[2,128,128]{2,1,0:T(8,128)S(1)}, f32[2,128,128]{2,1,0:T(8,128)S(1)}, u32[]{:S(2)}, u32[]{:S(2)}) %collective-permute-start.6) | collective-permute-done | bytes 131104 | tf_op jit(solution)/shard_map/ppermute | solution.py:27
  18.7 1.3 %collective-permute-start.7 = (bf16[128,128]{1,0:T(8,128)(2,1)S(1)}, bf16[128,128]{1,0:T(8,128)(2,1)S(1)}, u32[]{:S(2)}, u32[]{:S(2)}) collective-permute-start(bf16[128,128]{1,0:T(8,128)(2,1)S(1)} %fusion.1), channel_id=1, source_target_pairs={{0,3},{1,2},{2,1},{3,0},{4,7},{5,6},{6,5},{7,4},{8,11},{9,10},{10,... | collective-permute-start | bytes 98312 | tf_op jit(solution)/shard_map/ppermute | solution.py:33
  20.0 2.1 %collective-permute-done.7 = bf16[128,128]{1,0:T(8,128)(2,1)S(1)} collective-permute-done((bf16[128,128]{1,0:T(8,128)(2,1)S(1)}, bf16[128,128]{1,0:T(8,128)(2,1)S(1)}, u32[]{:S(2)}, u32[]{:S(2)}) %collective-permute-start.7) | collective-permute-done | bytes 32800 | tf_op jit(solution)/shard_map/ppermute | solution.py:33
  22.2 2.2 %collective-permute-start.10 = (bf16[128,128]{1,0:T(8,128)(2,1)S(1)}, bf16[128,128]{1,0:T(8,128)(2,1)S(1)}, u32[]{:S(2)}, u32[]{:S(2)}) collective-permute-start(bf16[128,128]{1,0:T(8,128)(2,1)S(1)} %fusion), channel_id=1, source_target_pairs={{0,12},{1,13},{2,14},{3,15},{4,8},{5,9},{6,10},{7,11},{8,4},{9,5},... | collective-permute-start | bytes 98312 | tf_op jit(solution)/shard_map/ppermute | solution.py:33
  24.4 1.1 %collective-permute-start.9 = (bf16[128,128]{1,0:T(8,128)(2,1)S(1)}, bf16[128,128]{1,0:T(8,128)(2,1)S(1)}, u32[]{:S(2)}, u32[]{:S(2)}) collective-permute-start(bf16[128,128]{1,0:T(8,128)(2,1)S(1)} %fusion), channel_id=1, source_target_pairs={{0,9},{1,8},{2,11},{3,10},{4,13},{5,12},{6,15},{7,14},{8,1},{9,0},... | collective-permute-start | bytes 98312 | tf_op jit(solution)/shard_map/ppermute | solution.py:33
  25.5 1.6 %collective-permute-done.10 = bf16[128,128]{1,0:T(8,128)(2,1)S(1)} collective-permute-done((bf16[128,128]{1,0:T(8,128)(2,1)S(1)}, bf16[128,128]{1,0:T(8,128)(2,1)S(1)}, u32[]{:S(2)}, u32[]{:S(2)}) %collective-permute-start.10) | collective-permute-done | bytes 32800 | tf_op jit(solution)/shard_map/ppermute | solution.py:33
  27.1 0.9 %collective-permute-done.8 = bf16[128,128]{1,0:T(8,128)(2,1)S(1)} collective-permute-done((bf16[128,128]{1,0:T(8,128)(2,1)S(1)}, bf16[128,128]{1,0:T(8,128)(2,1)S(1)}, u32[]{:S(2)}, u32[]{:S(2)}) %collective-permute-start.8) | collective-permute-done | bytes 32800 | tf_op jit(solution)/shard_map/ppermute | solution.py:33
  28.0 2.8 %collective-permute-start.13 = (bf16[128,128]{1,0:T(8,128)(2,1)S(1)}, bf16[128,128]{1,0:T(8,128)(2,1)S(1)}, u32[]{:S(2)}, u32[]{:S(2)}) collective-permute-start(bf16[128,128]{1,0:T(8,128)(2,1)S(1)} %add_convert_fusion.1), channel_id=1, source_target_pairs={{0,17},{1,16},{2,19},{3,18},{4,21},{5,20},{6,23},{7,22},{8,25},{9,... | collective-permute-start | bytes 98312 | tf_op jit(solution)/shard_map/ppermute | solution.py:33
  30.9 1.6 %collective-permute-start.12 = (bf16[1,4,32,128]{3,2,1,0:T(8,128)(2,1)S(1)}, bf16[1,4,32,128]{3,2,1,0:T(8,128)(2,1)S(1)}, u32[]{:S(2)}, u32[]{:S(2)}) collective-permute-start(bf16[1,4,32,128]{3,2,1,0:T(8,128)(2,1)S(1)} %get-tuple-element.51), channel_id=1, source_target_pairs={{0,2},{1,3},{2,0},{3,1},{4,6},{5,7},{6,4},{7,5},{8,10},{9,11},{10,... | collective-permute-start | bytes 98312 | tf_op jit(solution)/shard_map/ppermute | solution.py:27
  32.5 2.0 %collective-permute-start.14 = (bf16[128,128]{1,0:T(8,128)(2,1)S(1)}, bf16[128,128]{1,0:T(8,128)(2,1)S(1)}, u32[]{:S(2)}, u32[]{:S(2)}) collective-permute-start(bf16[128,128]{1,0:T(8,128)(2,1)S(1)} %add_convert_fusion), channel_id=1, source_target_pairs={{0,3},{1,2},{2,1},{3,0},{4,7},{5,6},{6,5},{7,4},{8,11},{9,10},{10,... | collective-permute-start | bytes 98312 | tf_op jit(solution)/shard_map/ppermute | solution.py:33
  34.5 1.2 %pair_input_grad.1 = bf16[2048,128]{1,0:T(8,128)(2,1)} custom-call(bf16[2048,128]{1,0:T(8,128)(2,1)S(1)} %bitcast.13, bf16[2048,128]{1,0:T(8,128)(2,1)S(1)} %bitcast.14, bf16[128,128]{1,0:T(8,128)(2,1)S(1)} %copy-done.1, bf16[128,128]{1,0:T(8,128)(2,1)S(1)} %copy-done.2), custom_call_target="tpu_custom_call" | custom-call | flops 134217728 | bytes 1572864 | tf_op jit(solution)/shard_map/pair_input_grad/pallas_call | solution.py:409
  35.7 0.8 %slab_input_grad.1 = bf16[4,32,128]{2,1,0:T(8,128)(2,1)} custom-call(f32[4,32,128]{2,1,0:T(8,128)S(1)} %bitcast.15, bf16[4,32,128]{2,1,0:T(8,128)(2,1)S(1)} %bitcast.16, f32[16,32,128]{2,1,0:T(8,128)S(1)} %get-tuple-element.40.slab_lin_ref.lin_ref, f32[16,32,128]{2,1,0:T(8,128)S(1)} %get-tuple-element.41.slab_gate_ref.gate_ref, ...), custom_call_target="tpu_custom_call" | custom-call | flops 8388608 | bytes 262144 | tf_op jit(solution)/shard_map/slab_input_grad/pallas_call | solution.py:456
  36.8 1.0 %collective-permute-done.15 = bf16[2,128,128]{2,1,0:T(8,128)(2,1)S(1)} collective-permute-done((bf16[2,128,128]{2,1,0:T(8,128)(2,1)S(1)}, bf16[2,128,128]{2,1,0:T(8,128)(2,1)S(1)}, u32[]{:S(2)}, u32[]{:S(2)}) %collective-permute-start.15) | collective-permute-done | bytes 65568 | tf_op jit(solution)/shard_map/ppermute | solution.py:27
  37.9 0.7 %maximum_select_fusion = f32[4,128,128]{2,1,0:T(8,128)} fusion(f32[2,128,128]{2,1,0:T(8,128)S(1)} %convert_multiply_fusion, f32[2,128,128]{2,1,0:T(8,128)S(1)} %convert_multiply_fusion.1, pred[]{:T(512)S(6)} %eq.3), kind=kLoop, calls=%fused_computation | loop fusion | flops 196608 | bytes 524289 | tf_op jit(solution)/shard_map/jit(_where)/select_n | solution.py:537
  (53 shorter events, 2.3 us)
Async XLA Ops:
  0.6 4.1 %copy-start.6 = (bf16[2,64,128]{2,1,0:T(8,128)(2,1)S(1)}, bf16[2,64,128]{2,1,0:T(8,128)(2,1)}, u32[]{:S(2)}) copy-start(bf16[2,64,128]{2,1,0:T(8,128)(2,1)} %refs_0_.1) | copy-start | bytes 98308
  0.6 4.1 %copy-start.5 = (bf16[4,32,128]{2,1,0:T(8,128)(2,1)S(1)}, bf16[4,32,128]{2,1,0:T(8,128)(2,1)}, u32[]{:S(2)}) copy-start(bf16[4,32,128]{2,1,0:T(8,128)(2,1)} %refs_1_.1) | copy-start | bytes 98308
  0.6 6.6 %collective-permute-start = (bf16[2,64,128]{2,1,0:T(8,128)(2,1)}, bf16[2,64,128]{2,1,0:T(8,128)(2,1)S(1)}, u32[]{:S(2)}, u32[]{:S(2)}) collective-permute-start(bf16[2,64,128]{2,1,0:T(8,128)(2,1)} %refs_0_.1), channel_id=1, source_target_pairs={{0,16},{4,20},{8,24},{12,28},{16,0},{20,4},{24,8},{28,12},{1,17},{... | collective-permute-start | bytes 98312 | tf_op jit(solution)/shard_map/ppermute | solution.py:27
  4.8 5.8 %copy-start = (bf16[64,32,128]{2,1,0:T(8,128)(2,1)S(1)}, bf16[64,32,128]{2,1,0:T(8,128)(2,1)}, u32[]{:S(2)}) copy-start(bf16[64,32,128]{2,1,0:T(8,128)(2,1)} %pair_ref.3) | copy-start | bytes 1572868
  4.8 5.6 %collective-permute-start.2 = (bf16[4,32,128]{2,1,0:T(8,128)(2,1)S(1)}, bf16[4,32,128]{2,1,0:T(8,128)(2,1)S(1)}, u32[]{:S(2)}, u32[]{:S(2)}) collective-permute-start(bf16[4,32,128]{2,1,0:T(8,128)(2,1)S(1)} %get-tuple-element.30), channel_id=1, source_target_pairs={{0,2},{1,3},{2,0},{3,1},{4,6},{5,7},{6,4},{7,5},{8,10},{9,11},{10,... | collective-permute-start | bytes 98312 | tf_op jit(solution)/shard_map/ppermute | solution.py:27
  7.2 3.2 %copy-start.7 = (s32[256]{0:T(256)S(1)}, s32[256]{0:T(256)}, u32[]{:S(2)}) copy-start(s32[256]{0:T(256)} %param.17) | copy-start | bytes 3076
  7.2 4.7 %collective-permute-start.1 = (bf16[4,64,128]{2,1,0:T(8,128)(2,1)S(1)}, bf16[4,64,128]{2,1,0:T(8,128)(2,1)S(1)}, u32[]{:S(2)}, u32[]{:S(2)}) collective-permute-start(bf16[4,64,128]{2,1,0:T(8,128)(2,1)S(1)} %constant_dynamic-update-slice_fusion.refs_0_), channel_id=1, source_target_pairs={{0,8},{4,12},{8,0},{12,4},{16,24},{20,28},{24,16},{28,20},{1,9},{5... | collective-permute-start | bytes 196616 | tf_op jit(solution)/shard_map/ppermute | solution.py:27
  8.8 4.8 %collective-permute-start.4 = (bf16[4,64,128]{2,1,0:T(8,128)(2,1)S(1)}, bf16[4,64,128]{2,1,0:T(8,128)(2,1)S(1)}, u32[]{:S(2)}, u32[]{:S(2)}) collective-permute-start(bf16[4,64,128]{2,1,0:T(8,128)(2,1)S(1)} %constant_dynamic-update-slice_fusion.refs_0_), channel_id=1, source_target_pairs={{0,4},{4,0},{8,12},{12,8},{16,20},{20,16},{24,28},{28,24},{1,5},{5... | collective-permute-start | bytes 196616 | tf_op jit(solution)/shard_map/ppermute | solution.py:27
  10.4 0.8 %copy-start.2 = (bf16[128,128]{1,0:T(8,128)(2,1)S(1)}, bf16[128,128]{1,0:T(8,128)(2,1)}, u32[]{:S(2)}) copy-start(bf16[128,128]{1,0:T(8,128)(2,1)} %w_gate_ref.7) | copy-start | bytes 98308
  10.4 2.9 %collective-permute-start.5 = (bf16[8,32,128]{2,1,0:T(8,128)(2,1)S(1)}, bf16[8,32,128]{2,1,0:T(8,128)(2,1)S(1)}, u32[]{:S(2)}, u32[]{:S(2)}) collective-permute-start(bf16[8,32,128]{2,1,0:T(8,128)(2,1)S(1)} %constant_dynamic-update-slice_fusion.2.even_ref), channel_id=1, source_target_pairs={{0,1},{1,0},{2,3},{3,2},{4,5},{5,4},{6,7},{7,6},{8,9},{9,8},{10,11... | collective-permute-start | bytes 196616 | tf_op jit(solution)/shard_map/ppermute | solution.py:27
  11.2 2.2 %copy-start.3 = (bf16[128,128]{1,0:T(8,128)(2,1)S(1)}, bf16[128,128]{1,0:T(8,128)(2,1)}, u32[]{:S(2)}) copy-start(bf16[128,128]{1,0:T(8,128)(2,1)} %w_lin_ref.6) | copy-start | bytes 98308
  11.2 2.2 %copy-start.4 = (bf16[128,128]{1,0:T(8,128)(2,1)S(1)}, bf16[128,128]{1,0:T(8,128)(2,1)}, u32[]{:S(2)}) copy-start(bf16[128,128]{1,0:T(8,128)(2,1)} %w_gate_ref.6) | copy-start | bytes 98308
  11.9 1.4 %copy-start.8 = (s32[16]{0:T(128)S(1)}, s32[16]{0:T(128)}, u32[]{:S(2)}) copy-start(s32[16]{0:T(128)} %param.16) | copy-start | bytes 196
  11.9 4.3 %collective-permute-start.3 = (bf16[4,64,128]{2,1,0:T(8,128)(2,1)S(1)}, bf16[4,64,128]{2,1,0:T(8,128)(2,1)S(1)}, u32[]{:S(2)}, u32[]{:S(2)}) collective-permute-start(bf16[4,64,128]{2,1,0:T(8,128)(2,1)S(1)} %collective-permute-done.1.refs_1_), channel_id=1, source_target_pairs={{0,4},{4,0},{8,12},{12,8},{16,20},{20,16},{24,28},{28,24},{1,5},{5... | collective-permute-start | bytes 196616 | tf_op jit(solution)/shard_map/ppermute | solution.py:27
  17.3 1.4 %collective-permute-start.6 = (f32[2,128,128]{2,1,0:T(8,128)S(1)}, f32[2,128,128]{2,1,0:T(8,128)S(1)}, u32[]{:S(2)}, u32[]{:S(2)}) collective-permute-start(f32[2,128,128]{2,1,0:T(8,128)S(1)} %get-tuple-element.44), channel_id=1, source_target_pairs={{0,1},{1,0},{2,3},{3,2},{4,5},{5,4},{6,7},{7,6},{8,9},{9,8},{10,11... | collective-permute-start | bytes 393224 | tf_op jit(solution)/shard_map/ppermute | solution.py:27
  18.7 3.4 %collective-permute-start.7 = (bf16[128,128]{1,0:T(8,128)(2,1)S(1)}, bf16[128,128]{1,0:T(8,128)(2,1)S(1)}, u32[]{:S(2)}, u32[]{:S(2)}) collective-permute-start(bf16[128,128]{1,0:T(8,128)(2,1)S(1)} %fusion.1), channel_id=1, source_target_pairs={{0,3},{1,2},{2,1},{3,0},{4,7},{5,6},{6,5},{7,4},{8,11},{9,10},{10,... | collective-permute-start | bytes 98312 | tf_op jit(solution)/shard_map/ppermute | solution.py:33
  22.2 4.9 %collective-permute-start.10 = (bf16[128,128]{1,0:T(8,128)(2,1)S(1)}, bf16[128,128]{1,0:T(8,128)(2,1)S(1)}, u32[]{:S(2)}, u32[]{:S(2)}) collective-permute-start(bf16[128,128]{1,0:T(8,128)(2,1)S(1)} %fusion), channel_id=1, source_target_pairs={{0,12},{1,13},{2,14},{3,15},{4,8},{5,9},{6,10},{7,11},{8,4},{9,5},... | collective-permute-start | bytes 98312 | tf_op jit(solution)/shard_map/ppermute | solution.py:33
  24.4 3.6 %collective-permute-start.8 = (bf16[128,128]{1,0:T(8,128)(2,1)S(1)}, bf16[128,128]{1,0:T(8,128)(2,1)S(1)}, u32[]{:S(2)}, u32[]{:S(2)}) collective-permute-start(bf16[128,128]{1,0:T(8,128)(2,1)S(1)} %fusion), channel_id=1, source_target_pairs={{0,5},{1,4},{2,7},{3,6},{4,1},{5,0},{6,3},{7,2},{8,13},{9,12},{10,... | collective-permute-start | bytes 98312 | tf_op jit(solution)/shard_map/ppermute | solution.py:33
  24.4 3.6 %collective-permute-start.9 = (bf16[128,128]{1,0:T(8,128)(2,1)S(1)}, bf16[128,128]{1,0:T(8,128)(2,1)S(1)}, u32[]{:S(2)}, u32[]{:S(2)}) collective-permute-start(bf16[128,128]{1,0:T(8,128)(2,1)S(1)} %fusion), channel_id=1, source_target_pairs={{0,9},{1,8},{2,11},{3,10},{4,13},{5,12},{6,15},{7,14},{8,1},{9,0},... | collective-permute-start | bytes 98312 | tf_op jit(solution)/shard_map/ppermute | solution.py:33
  25.4 2.6 %collective-permute-start.11 = (f32[2,4,32,128]{3,2,1,0:T(8,128)S(1)}, f32[2,4,32,128]{3,2,1,0:T(8,128)S(1)}, u32[]{:S(2)}, u32[]{:S(2)}) collective-permute-start(f32[2,4,32,128]{3,2,1,0:T(8,128)S(1)} %get-tuple-element.46), channel_id=1, source_target_pairs={{0,1},{1,0},{2,3},{3,2},{4,5},{5,4},{6,7},{7,6},{8,9},{9,8},{10,11... | collective-permute-start | bytes 393224 | tf_op jit(solution)/shard_map/ppermute | solution.py:27
  28.0 4.4 %collective-permute-start.13 = (bf16[128,128]{1,0:T(8,128)(2,1)S(1)}, bf16[128,128]{1,0:T(8,128)(2,1)S(1)}, u32[]{:S(2)}, u32[]{:S(2)}) collective-permute-start(bf16[128,128]{1,0:T(8,128)(2,1)S(1)} %add_convert_fusion.1), channel_id=1, source_target_pairs={{0,17},{1,16},{2,19},{3,18},{4,21},{5,20},{6,23},{7,22},{8,25},{9,... | collective-permute-start | bytes 98312 | tf_op jit(solution)/shard_map/ppermute | solution.py:33
  30.9 4.9 %collective-permute-start.12 = (bf16[1,4,32,128]{3,2,1,0:T(8,128)(2,1)S(1)}, bf16[1,4,32,128]{3,2,1,0:T(8,128)(2,1)S(1)}, u32[]{:S(2)}, u32[]{:S(2)}) collective-permute-start(bf16[1,4,32,128]{3,2,1,0:T(8,128)(2,1)S(1)} %get-tuple-element.51), channel_id=1, source_target_pairs={{0,2},{1,3},{2,0},{3,1},{4,6},{5,7},{6,4},{7,5},{8,10},{9,11},{10,... | collective-permute-start | bytes 98312 | tf_op jit(solution)/shard_map/ppermute | solution.py:27
  32.5 4.0 %collective-permute-start.14 = (bf16[128,128]{1,0:T(8,128)(2,1)S(1)}, bf16[128,128]{1,0:T(8,128)(2,1)S(1)}, u32[]{:S(2)}, u32[]{:S(2)}) collective-permute-start(bf16[128,128]{1,0:T(8,128)(2,1)S(1)} %add_convert_fusion), channel_id=1, source_target_pairs={{0,3},{1,2},{2,1},{3,0},{4,7},{5,6},{6,5},{7,4},{8,11},{9,10},{10,... | collective-permute-start | bytes 98312 | tf_op jit(solution)/shard_map/ppermute | solution.py:33
  36.5 1.3 %collective-permute-start.15 = (bf16[2,128,128]{2,1,0:T(8,128)(2,1)S(1)}, bf16[2,128,128]{2,1,0:T(8,128)(2,1)S(1)}, u32[]{:S(2)}, u32[]{:S(2)}) collective-permute-start(bf16[2,128,128]{2,1,0:T(8,128)(2,1)S(1)} %pad_maximum_fusion), channel_id=1, source_target_pairs={{0,1},{1,0},{2,3},{3,2},{4,5},{5,4},{6,7},{7,6},{8,9},{9,8},{10,11... | collective-permute-start | bytes 196616 | tf_op jit(solution)/shard_map/ppermute | solution.py:27
  (1 other events, 0.8 us)

commit v6 on v5

--- a/solution.py
+++ b/solution.py
@@ -435,6 +435,49 @@
         cost_estimate=cost(STAGE_COST * kept.size, 8 * kept.size),
         name="fold",
     )(kept, got)
+
+
+def add_pair(own, got):
+    return (own.astype(F32) + got.astype(F32)).astype(BF16)
+
+
+def four_kernel(a_ref, b_ref, c_ref, d_ref, out_ref):
+    one = d_ref[...].astype(F32) + c_ref[...].astype(F32)
+    two = b_ref[...].astype(F32) + a_ref[...].astype(F32)
+    out_ref[...] = (one + two).astype(BF16)
+
+
+def add_sums_of_four(*parts):
+    return pl.pallas_call(
+        four_kernel,
+        out_shape=jax.ShapeDtypeStruct(parts[0].shape, BF16),
+        in_specs=[VMEM] * 4,
+        out_specs=VMEM,
+        compiler_params=params(),
+        cost_estimate=cost(4 * parts[0].size, 10 * parts[0].size),
+        name="add_four",
+    )(*parts)
+
+
+def join_kernel(pair_bit, diagonal_ref, late_ref, pair_ref, own_ref, out_ref):
+    upper = jnp.minimum(lax.axis_index("col") & pair_bit, 1)
+    own = own_ref[...].astype(F32) + late_ref[...].astype(F32)
+    other = pair_ref[...].astype(F32) + diagonal_ref[...].astype(F32)
+    out_ref[upper] = own.astype(BF16)
+    out_ref[1 - upper] = other.astype(BF16)
+
+
+def join_sums(pair_bit, *parts):
+    cz, ch = parts[0].shape
+    return pl.pallas_call(
+        functools.partial(join_kernel, pair_bit),
+        out_shape=jax.ShapeDtypeStruct((2, cz, ch), BF16),
+        in_specs=[VMEM] * 4,
+        out_specs=VMEM,
+        compiler_params=params(),
+        cost_estimate=cost(4 * cz * ch, 12 * cz * ch),
+        name="join_sums",
+    )(*parts)
 
 
 def slab_out_kernel(sum_ref, got_ref, lin_ref, gate_ref, w_lin_ref, w_gate_ref, out_ref):
@@ -511,28 +554,27 @@
     side = w_keep + got_w
     upper = (col & pair_bit) != 0
     moved = jnp.where(upper, side[0], side[1]).astype(BF16)
-    part = jnp.where(upper, side[1], side[0])
-    part = part + swap_chips(moved, pair_bit).astype(F32)
-    bits = col_bits[2:] + [bit * n_col for bit in row_bits]
+    narrow = jnp.where(upper, side[1], side[0]).astype(BF16)
+    moved, d_lin, d_gate = lax.optimization_barrier((moved, d_lin, d_gate))
+    grad_pair = pair_out(d_lin, d_gate, w_b_lin, w_b_gate)
     sums, got = sum_keep, swap(sum_send, "col", 1)
-    narrow = part.astype(BF16)
-    near, next_ = bits[0], bits[1]
-    diagonal = swap_chips(narrow, near | next_, 0)
-    part = narrow.astype(F32) + swap_chips(narrow, near).astype(F32)
-    part = part + (swap_chips(narrow, next_).astype(F32) + diagonal.astype(F32))
-    for bit in bits[2:]:
-        narrow = part.astype(BF16)
-        if bit == bits[2]:
-            narrow, got, d_lin, d_gate = lax.optimization_barrier((narrow, got, d_lin, d_gate))
-            grad_pair = pair_out(d_lin, d_gate, w_b_lin, w_b_gate)
+    bits = [bit * n_col for bit in row_bits]
+    near, late = bits[0], bits[1]
+    diagonal = swap_chips(moved, pair_bit | near, 0)
+    pair_part, near_part = swap_chips(moved, pair_bit), swap_chips(narrow, near)
+    narrow = add_sums_of_four(diagonal, near_part, pair_part, narrow)
+    between = col_bits[2:] + [bit for bit in bits if bit not in (near, late)]
+    for bit in between:
+        if bit == between[-1]:
+            narrow, got, grad_pair = lax.optimization_barrier((narrow, got, grad_pair))
             for far in col_bits[1:]:
                 sums, moved = fold(sums, got)
                 got = swap(moved, "col", far)
-        part = narrow.astype(F32) + swap_chips(narrow, bit).astype(F32)
-    narrow = part.astype(BF16)
-    mine = jnp.stack([narrow, swap_chips(narrow, pair_bit)])
-    both = [mine, swap(mine, "col", 1)]
-    both = [jnp.where(upper, m[::-1], m).astype(F32) / residues for m in both]
+        narrow = add_pair(narrow, swap_chips(narrow, bit))
+    diagonal = swap_chips(narrow, pair_bit | late, 0)
+    late_part, pair_part = swap_chips(narrow, late), swap_chips(narrow, pair_bit)
+    mine = join_sums(pair_bit, diagonal, late_part, pair_part, narrow)
+    both = [m.astype(F32) / residues for m in (mine, swap(mine, "col", 1))]
     first = parity() == 0
     grad_weights = jnp.where(
         first, jnp.concatenate(both, axis=0), jnp.concatenate(both[::-1], axis=0)

time: 38.8 us -> 37.7 us (0.972)
  waiting for transfers between devices: 8.48 us -> 7.64 us
    ppermute x6 -> x7, waiting for transfers between devices: 4.69 us -> 3.81 us  [swap_chips(): return lax.ppermute(value, ('row', 'col'), pairs)]
    ppermute x6 -> x7, starting transfers between devices: 9.43 us -> 9.06 us  [swap_chips(): return lax.ppermute(value, ('row', 'col'), pairs)]
  transfers between devices with their start and end apart: 16 -> 17, of which waited for: 7 -> 10; matrix products, arithmetic and copies ran while one was open for 1% -> 1% of each run, Pallas kernels for 13% -> 13%
where the time goes in v6:
time: 37.7 us; the launch traced here: 37.5 us
  starting transfers between devices  21.4 us (57%)
  waiting for transfers between devices  7.64 us (20%)
  Pallas kernels  6.04 us (16%)
  between operations  0.85 us (2%)
  other arithmetic  0.8 us (2%)
  local copies, waits for them, and re-layouts  0.79 us (2%)
    ppermute x10, starting transfers between devices, swap(): return lax.ppermute(value, axis, [(d, d ^ bit) for d in range(size)])  12.3 us
    ppermute x7, starting transfers between devices, swap_chips(): return lax.ppermute(value, ('row', 'col'), pairs)  9.06 us
    ppermute x10, waiting for transfers between devices, swap(): return lax.ppermute(value, axis, [(d, d ^ bit) for d in range(size)])  3.83 us
    ppermute x7, waiting for transfers between devices, swap_chips(): return lax.ppermute(value, ('row', 'col'), pairs)  3.81 us
    pallas_call x1, Pallas kernels, pair_out(): pl.pallas_call(pair_out_kernel, out_shape=jax.ShapeDtypeStruct((cols * ke...  1.23 us
    pallas_call x1, Pallas kernels, main_part(): pl.pallas_call(functools.partial(main_kernel, order, blocks), out_shape=(...  1.05 us
    pallas_call x1, Pallas kernels, first_sums(): pl.pallas_call(functools.partial(sums_kernel, len(grads)), out_shape=jax....  0.98 us
    pallas_call x1, Pallas kernels, first_totals(): pl.pallas_call(functools.partial(totals_kernel, order, len(grads)), out_s...  0.98 us
  transfers between devices with their start and end apart: 17, of which 10 were waited for; matrix products, arithmetic and copies ran while one was open for 1% of the time, Pallas kernels for 13%

profile of v6, /device:TPU:0, one launch (start us, length us, event | category | flops | bytes accessed | tf_op | source)
XLA Modules:
  0.0 37.5 jit_solution(1896624104365636262)
XLA Ops:
  0.6 4.1 %collective-permute-start = (bf16[2,64,128]{2,1,0:T(8,128)(2,1)}, bf16[2,64,128]{2,1,0:T(8,128)(2,1)S(1)}, u32[]{:S(2)}, u32[]{:S(2)}) collective-permute-start(bf16[2,64,128]{2,1,0:T(8,128)(2,1)} %refs_0_.1), channel_id=1, source_target_pairs={{0,16},{4,20},{8,24},{12,28},{16,0},{20,4},{24,8},{28,12},{1,17},{... | collective-permute-start | bytes 98312 | tf_op jit(solution)/shard_map/ppermute | solution.py:27
  4.8 1.6 %collective-permute-start.2 = (bf16[4,32,128]{2,1,0:T(8,128)(2,1)S(1)}, bf16[4,32,128]{2,1,0:T(8,128)(2,1)S(1)}, u32[]{:S(2)}, u32[]{:S(2)}) collective-permute-start(bf16[4,32,128]{2,1,0:T(8,128)(2,1)S(1)} %get-tuple-element.32), channel_id=1, source_target_pairs={{0,2},{1,3},{2,0},{3,1},{4,6},{5,7},{6,4},{7,5},{8,10},{9,11},{10,... | collective-permute-start | bytes 98312 | tf_op jit(solution)/shard_map/ppermute | solution.py:27
  6.3 0.9 %collective-permute-done = bf16[2,64,128]{2,1,0:T(8,128)(2,1)S(1)} collective-permute-done((bf16[2,64,128]{2,1,0:T(8,128)(2,1)}, bf16[2,64,128]{2,1,0:T(8,128)(2,1)S(1)}, u32[]{:S(2)}, u32[]{:S(2)}) %collective-permute-start) | collective-permute-done | bytes 32800 | tf_op jit(solution)/shard_map/ppermute | solution.py:27
  7.2 1.6 %collective-permute-start.1 = (bf16[4,64,128]{2,1,0:T(8,128)(2,1)S(1)}, bf16[4,64,128]{2,1,0:T(8,128)(2,1)S(1)}, u32[]{:S(2)}, u32[]{:S(2)}) collective-permute-start(bf16[4,64,128]{2,1,0:T(8,128)(2,1)S(1)} %constant_dynamic-update-slice_fusion.refs_0_), channel_id=1, source_target_pairs={{0,8},{4,12},{8,0},{12,4},{16,24},{20,28},{24,16},{28,20},{1,9},{5... | collective-permute-start | bytes 196616 | tf_op jit(solution)/shard_map/ppermute | solution.py:27
  8.8 1.5 %collective-permute-start.4 = (bf16[4,64,128]{2,1,0:T(8,128)(2,1)S(1)}, bf16[4,64,128]{2,1,0:T(8,128)(2,1)S(1)}, u32[]{:S(2)}, u32[]{:S(2)}) collective-permute-start(bf16[4,64,128]{2,1,0:T(8,128)(2,1)S(1)} %constant_dynamic-update-slice_fusion.refs_0_), channel_id=1, source_target_pairs={{0,4},{4,0},{8,12},{12,8},{16,20},{20,16},{24,28},{28,24},{1,5},{5... | collective-permute-start | bytes 196616 | tf_op jit(solution)/shard_map/ppermute | solution.py:27
  11.2 0.7 %pair_forward.1 = (bf16[64,32,128]{2,1,0:T(8,128)(2,1)S(1)}, f32[64,32,128]{2,1,0:T(8,128)S(1)}, f32[64,32,128]{2,1,0:T(8,128)S(1)}) custom-call(bf16[64,32,128]{2,1,0:T(8,128)(2,1)S(1)} %copy-done, bf16[128,128]{1,0:T(8,128)(2,1)S(1)} %copy-done.1, bf16[128,128]{1,0:T(8,128)(2,1)S(1)} %copy-done.2, bf16[256,128]{1,0:T(8,128)(2,1)S(1)} %broadcast_in_dim.4.flags_ref), custom_call_target="tpu_custom_call" | custom-call | flops 134217728 | bytes 3670016 | tf_op jit(solution)/shard_map/pair_forward/pallas_call | solution.py:125
  11.9 1.4 %collective-permute-start.3 = (bf16[4,64,128]{2,1,0:T(8,128)(2,1)S(1)}, bf16[4,64,128]{2,1,0:T(8,128)(2,1)S(1)}, u32[]{:S(2)}, u32[]{:S(2)}) collective-permute-start(bf16[4,64,128]{2,1,0:T(8,128)(2,1)S(1)} %collective-permute-done.1.refs_1_), channel_id=1, source_target_pairs={{0,4},{4,0},{8,12},{12,8},{16,20},{20,16},{24,28},{28,24},{1,5},{5... | collective-permute-start | bytes 196616 | tf_op jit(solution)/shard_map/ppermute | solution.py:27
  13.7 1.0 %first_totals_over_i.1.total_ref = f32[64,32,128]{2,1,0:T(8,128)S(1)} custom-call(bf16[4,64,128]{2,1,0:T(8,128)(2,1)S(1)} %constant_dynamic-update-slice_fusion.refs_0_, bf16[4,64,128]{2,1,0:T(8,128)(2,1)S(1)} %collective-permute-done.1.refs_1_, bf16[4,64,128]{2,1,0:T(8,128)(2,1)S(1)} %collective-permute-done.4.refs_2_, ...), custom_call_target="tpu_custom_call" | custom-call | flops 6291456 | bytes 2097152 | tf_op jit(solution)/shard_map/first_totals_over_i/pallas_call | solution.py:276
  14.6 1.0 %first_sums_over_j.1.first_sums_ref = f32[12,32,128]{2,1,0:T(8,128)S(1)} custom-call(bf16[4,64,128]{2,1,0:T(8,128)(2,1)S(1)} %constant_dynamic-update-slice_fusion.refs_0_, bf16[4,64,128]{2,1,0:T(8,128)(2,1)S(1)} %collective-permute-done.1.refs_1_, bf16[4,64,128]{2,1,0:T(8,128)(2,1)S(1)} %collective-permute-done.4.refs_2_, ...), custom_call_target="tpu_custom_call" | custom-call | flops 6291456 | bytes 2097152 | tf_op jit(solution)/shard_map/first_sums_over_j/pallas_call | solution.py:242
  15.6 0.6 %collective-permute-done.3.grad_ref = bf16[4,64,128]{2,1,0:T(8,128)(2,1)S(1)} collective-permute-done((bf16[4,64,128]{2,1,0:T(8,128)(2,1)S(1)}, bf16[4,64,128]{2,1,0:T(8,128)(2,1)S(1)}, u32[]{:S(2)}, u32[]{:S(2)}) %collective-permute-start.3) | collective-permute-done | bytes 65568 | tf_op jit(solution)/shard_map/ppermute | solution.py:27
  16.2 1.1 %last_rows.1 = (bf16[64,32,128]{2,1,0:T(8,128)(2,1)S(1)}, bf16[64,32,128]{2,1,0:T(8,128)(2,1)S(1)}, f32[2,4,32,128]{3,2,1,0:T(8,128)S(1)}, f32[2,4,32,128]{3,2,1...) custom-call(bf16[4,64,128]{2,1,0:T(8,128)(2,1)S(1)} %collective-permute-done.3.grad_ref, ...), custom_call_target="tpu_custom_call" | custom-call | flops 268435456 | bytes 4194304 | tf_op jit(solution)/shard_map/last_rows/pallas_call | solution.py:373
  17.4 1.3 %collective-permute-done.6 = f32[2,128,128]{2,1,0:T(8,128)S(1)} collective-permute-done((f32[2,128,128]{2,1,0:T(8,128)S(1)}, f32[2,128,128]{2,1,0:T(8,128)S(1)}, u32[]{:S(2)}, u32[]{:S(2)}) %collective-permute-start.6) | collective-permute-done | bytes 131104 | tf_op jit(solution)/shard_map/ppermute | solution.py:27
  18.9 2.3 %collective-permute-start.7 = (bf16[128,128]{1,0:T(8,128)(2,1)S(1)}, bf16[128,128]{1,0:T(8,128)(2,1)S(1)}, u32[]{:S(2)}, u32[]{:S(2)}) collective-permute-start(bf16[128,128]{1,0:T(8,128)(2,1)S(1)} %get-tuple-element.49), channel_id=1, source_target_pairs={{0,6},{1,7},{2,4},{3,5},{4,2},{5,3},{6,0},{7,1},{8,14},{9,15},{10,... | collective-permute-start | bytes 98312 | tf_op jit(solution)/shard_map/ppermute | solution.py:33
  21.4 0.7 %collective-permute-start.8 = (bf16[128,128]{1,0:T(8,128)(2,1)S(1)}, bf16[128,128]{1,0:T(8,128)(2,1)S(1)}, u32[]{:S(2)}, u32[]{:S(2)}) collective-permute-start(bf16[128,128]{1,0:T(8,128)(2,1)S(1)} %get-tuple-element.59.d_ref), channel_id=1, source_target_pairs={{0,5},{1,4},{2,7},{3,6},{4,1},{5,0},{6,3},{7,2},{8,13},{9,12},{10,... | collective-permute-start | bytes 98312 | tf_op jit(solution)/shard_map/ppermute | solution.py:33
  22.2 1.2 %pair_input_grad.1 = bf16[2048,128]{1,0:T(8,128)(2,1)} custom-call(bf16[2048,128]{1,0:T(8,128)(2,1)S(1)} %bitcast.9, bf16[2048,128]{1,0:T(8,128)(2,1)S(1)} %bitcast.10, bf16[128,128]{1,0:T(8,128)(2,1)S(1)} %copy-done.1, bf16[128,128]{1,0:T(8,128)(2,1)S(1)} %copy-done.2), custom_call_target="tpu_custom_call" | custom-call | flops 134217728 | bytes 1572864 | tf_op jit(solution)/shard_map/pair_input_grad/pallas_call | solution.py:409
  23.8 0.9 %collective-permute-done.9.c_ref = bf16[128,128]{1,0:T(8,128)(2,1)S(1)} collective-permute-done((bf16[128,128]{1,0:T(8,128)(2,1)S(1)}, bf16[128,128]{1,0:T(8,128)(2,1)S(1)}, u32[]{:S(2)}, u32[]{:S(2)}) %collective-permute-start.9) | collective-permute-done | bytes 32800 | tf_op jit(solution)/shard_map/ppermute | solution.py:33
  24.8 2.5 %collective-permute-start.12 = (bf16[128,128]{1,0:T(8,128)(2,1)S(1)}, bf16[128,128]{1,0:T(8,128)(2,1)S(1)}, u32[]{:S(2)}, u32[]{:S(2)}) collective-permute-start(bf16[128,128]{1,0:T(8,128)(2,1)S(1)} %add_four.1), channel_id=1, source_target_pairs={{0,17},{1,16},{2,19},{3,18},{4,21},{5,20},{6,23},{7,22},{8,25},{9,... | collective-permute-start | bytes 98312 | tf_op jit(solution)/shard_map/ppermute | solution.py:33
  27.3 1.6 %collective-permute-start.11 = (bf16[1,4,32,128]{3,2,1,0:T(8,128)(2,1)S(1)}, bf16[1,4,32,128]{3,2,1,0:T(8,128)(2,1)S(1)}, u32[]{:S(2)}, u32[]{:S(2)}) collective-permute-start(bf16[1,4,32,128]{3,2,1,0:T(8,128)(2,1)S(1)} %get-tuple-element.56), channel_id=1, source_target_pairs={{0,2},{1,3},{2,0},{3,1},{4,6},{5,7},{6,4},{7,5},{8,10},{9,11},{10,... | collective-permute-start | bytes 98312 | tf_op jit(solution)/shard_map/ppermute | solution.py:27
  29.1 2.6 %collective-permute-start.13 = (bf16[128,128]{1,0:T(8,128)(2,1)S(1)}, bf16[128,128]{1,0:T(8,128)(2,1)S(1)}, u32[]{:S(2)}, u32[]{:S(2)}) collective-permute-start(bf16[128,128]{1,0:T(8,128)(2,1)S(1)} %add_convert_fusion.own_ref), channel_id=1, source_target_pairs={{0,10},{1,11},{2,8},{3,9},{4,14},{5,15},{6,12},{7,13},{8,2},{9,3},... | collective-permute-start | bytes 98312 | tf_op jit(solution)/shard_map/ppermute | solution.py:33
  32.4 0.8 %slab_input_grad.1 = bf16[4,32,128]{2,1,0:T(8,128)(2,1)} custom-call(f32[4,32,128]{2,1,0:T(8,128)S(1)} %bitcast.11, bf16[4,32,128]{2,1,0:T(8,128)(2,1)S(1)} %bitcast.12, f32[16,32,128]{2,1,0:T(8,128)S(1)} %get-tuple-element.42.slab_lin_ref.lin_ref, f32[16,32,128]{2,1,0:T(8,128)S(1)} %get-tuple-element.43.slab_gate_ref.gate_ref, ...), custom_call_target="tpu_custom_call" | custom-call | flops 8388608 | bytes 262144 | tf_op jit(solution)/shard_map/slab_input_grad/pallas_call | solution.py:499
  33.2 0.8 %collective-permute-done.13.diagonal_ref = bf16[128,128]{1,0:T(8,128)(2,1)S(1)} collective-permute-done((bf16[128,128]{1,0:T(8,128)(2,1)S(1)}, bf16[128,128]{1,0:T(8,128)(2,1)S(1)}, u32[]{:S(2)}, u32[]{:S(2)}) %collective-permute-start.13) | collective-permute-done | bytes 32800 | tf_op jit(solution)/shard_map/ppermute | solution.py:33
  34.0 1.4 %collective-permute-done.14.late_ref = bf16[128,128]{1,0:T(8,128)(2,1)S(1)} collective-permute-done((bf16[128,128]{1,0:T(8,128)(2,1)S(1)}, bf16[128,128]{1,0:T(8,128)(2,1)S(1)}, u32[]{:S(2)}, u32[]{:S(2)}) %collective-permute-start.14) | collective-permute-done | bytes 32800 | tf_op jit(solution)/shard_map/ppermute | solution.py:33
  35.7 1.0 %collective-permute-done.16 = bf16[2,128,128]{2,1,0:T(8,128)(2,1)S(1)} collective-permute-done((bf16[2,128,128]{2,1,0:T(8,128)(2,1)S(1)}, bf16[2,128,128]{2,1,0:T(8,128)(2,1)S(1)}, u32[]{:S(2)}, u32[]{:S(2)}) %collective-permute-start.16) | collective-permute-done | bytes 65568 | tf_op jit(solution)/shard_map/ppermute | solution.py:27
  36.8 0.7 %maximum_select_fusion = f32[4,128,128]{2,1,0:T(8,128)} fusion(f32[2,128,128]{2,1,0:T(8,128)S(1)} %convert_multiply_fusion, f32[2,128,128]{2,1,0:T(8,128)S(1)} %convert_multiply_fusion.1, pred[]{:T(512)S(6)} %eq.3), kind=kLoop, calls=%fused_computation | loop fusion | flops 196608 | bytes 524289 | tf_op jit(solution)/shard_map/jit(_where)/select_n | solution.py:579
  (54 shorter events, 3.3 us)
Async XLA Ops:
  0.6 4.1 %copy-start.6 = (bf16[2,64,128]{2,1,0:T(8,128)(2,1)S(1)}, bf16[2,64,128]{2,1,0:T(8,128)(2,1)}, u32[]{:S(2)}) copy-start(bf16[2,64,128]{2,1,0:T(8,128)(2,1)} %refs_0_.1) | copy-start | bytes 98308
  0.6 4.1 %copy-start.5 = (bf16[4,32,128]{2,1,0:T(8,128)(2,1)S(1)}, bf16[4,32,128]{2,1,0:T(8,128)(2,1)}, u32[]{:S(2)}) copy-start(bf16[4,32,128]{2,1,0:T(8,128)(2,1)} %refs_1_.1) | copy-start | bytes 98308
  0.6 6.6 %collective-permute-start = (bf16[2,64,128]{2,1,0:T(8,128)(2,1)}, bf16[2,64,128]{2,1,0:T(8,128)(2,1)S(1)}, u32[]{:S(2)}, u32[]{:S(2)}) collective-permute-start(bf16[2,64,128]{2,1,0:T(8,128)(2,1)} %refs_0_.1), channel_id=1, source_target_pairs={{0,16},{4,20},{8,24},{12,28},{16,0},{20,4},{24,8},{28,12},{1,17},{... | collective-permute-start | bytes 98312 | tf_op jit(solution)/shard_map/ppermute | solution.py:27
  4.8 5.8 %copy-start = (bf16[64,32,128]{2,1,0:T(8,128)(2,1)S(1)}, bf16[64,32,128]{2,1,0:T(8,128)(2,1)}, u32[]{:S(2)}) copy-start(bf16[64,32,128]{2,1,0:T(8,128)(2,1)} %pair_ref.3) | copy-start | bytes 1572868
  4.8 5.6 %collective-permute-start.2 = (bf16[4,32,128]{2,1,0:T(8,128)(2,1)S(1)}, bf16[4,32,128]{2,1,0:T(8,128)(2,1)S(1)}, u32[]{:S(2)}, u32[]{:S(2)}) collective-permute-start(bf16[4,32,128]{2,1,0:T(8,128)(2,1)S(1)} %get-tuple-element.32), channel_id=1, source_target_pairs={{0,2},{1,3},{2,0},{3,1},{4,6},{5,7},{6,4},{7,5},{8,10},{9,11},{10,... | collective-permute-start | bytes 98312 | tf_op jit(solution)/shard_map/ppermute | solution.py:27
  7.2 3.2 %copy-start.7 = (s32[256]{0:T(256)S(1)}, s32[256]{0:T(256)}, u32[]{:S(2)}) copy-start(s32[256]{0:T(256)} %param.17) | copy-start | bytes 3076
  7.2 4.7 %collective-permute-start.1 = (bf16[4,64,128]{2,1,0:T(8,128)(2,1)S(1)}, bf16[4,64,128]{2,1,0:T(8,128)(2,1)S(1)}, u32[]{:S(2)}, u32[]{:S(2)}) collective-permute-start(bf16[4,64,128]{2,1,0:T(8,128)(2,1)S(1)} %constant_dynamic-update-slice_fusion.refs_0_), channel_id=1, source_target_pairs={{0,8},{4,12},{8,0},{12,4},{16,24},{20,28},{24,16},{28,20},{1,9},{5... | collective-permute-start | bytes 196616 | tf_op jit(solution)/shard_map/ppermute | solution.py:27
  8.8 4.8 %collective-permute-start.4 = (bf16[4,64,128]{2,1,0:T(8,128)(2,1)S(1)}, bf16[4,64,128]{2,1,0:T(8,128)(2,1)S(1)}, u32[]{:S(2)}, u32[]{:S(2)}) collective-permute-start(bf16[4,64,128]{2,1,0:T(8,128)(2,1)S(1)} %constant_dynamic-update-slice_fusion.refs_0_), channel_id=1, source_target_pairs={{0,4},{4,0},{8,12},{12,8},{16,20},{20,16},{24,28},{28,24},{1,5},{5... | collective-permute-start | bytes 196616 | tf_op jit(solution)/shard_map/ppermute | solution.py:27
  10.4 2.9 %collective-permute-start.5 = (bf16[8,32,128]{2,1,0:T(8,128)(2,1)S(1)}, bf16[8,32,128]{2,1,0:T(8,128)(2,1)S(1)}, u32[]{:S(2)}, u32[]{:S(2)}) collective-permute-start(bf16[8,32,128]{2,1,0:T(8,128)(2,1)S(1)} %constant_dynamic-update-slice_fusion.2.even_ref), channel_id=1, source_target_pairs={{0,1},{1,0},{2,3},{3,2},{4,5},{5,4},{6,7},{7,6},{8,9},{9,8},{10,11... | collective-permute-start | bytes 196616 | tf_op jit(solution)/shard_map/ppermute | solution.py:27
  11.2 2.2 %copy-start.3 = (bf16[128,128]{1,0:T(8,128)(2,1)S(1)}, bf16[128,128]{1,0:T(8,128)(2,1)}, u32[]{:S(2)}) copy-start(bf16[128,128]{1,0:T(8,128)(2,1)} %w_lin_ref.7) | copy-start | bytes 98308
  11.2 2.2 %copy-start.4 = (bf16[128,128]{1,0:T(8,128)(2,1)S(1)}, bf16[128,128]{1,0:T(8,128)(2,1)}, u32[]{:S(2)}) copy-start(bf16[128,128]{1,0:T(8,128)(2,1)} %w_gate_ref.7) | copy-start | bytes 98308
  11.9 1.4 %copy-start.8 = (s32[16]{0:T(128)S(1)}, s32[16]{0:T(128)}, u32[]{:S(2)}) copy-start(s32[16]{0:T(128)} %param.16) | copy-start | bytes 196
  11.9 4.3 %collective-permute-start.3 = (bf16[4,64,128]{2,1,0:T(8,128)(2,1)S(1)}, bf16[4,64,128]{2,1,0:T(8,128)(2,1)S(1)}, u32[]{:S(2)}, u32[]{:S(2)}) collective-permute-start(bf16[4,64,128]{2,1,0:T(8,128)(2,1)S(1)} %collective-permute-done.1.refs_1_), channel_id=1, source_target_pairs={{0,4},{4,0},{8,12},{12,8},{16,20},{20,16},{24,28},{28,24},{1,5},{5... | collective-permute-start | bytes 196616 | tf_op jit(solution)/shard_map/ppermute | solution.py:27
  17.3 1.4 %collective-permute-start.6 = (f32[2,128,128]{2,1,0:T(8,128)S(1)}, f32[2,128,128]{2,1,0:T(8,128)S(1)}, u32[]{:S(2)}, u32[]{:S(2)}) collective-permute-start(f32[2,128,128]{2,1,0:T(8,128)S(1)} %get-tuple-element.46), channel_id=1, source_target_pairs={{0,1},{1,0},{2,3},{3,2},{4,5},{5,4},{6,7},{7,6},{8,9},{9,8},{10,11... | collective-permute-start | bytes 393224 | tf_op jit(solution)/shard_map/ppermute | solution.py:27
  18.7 6.1 %collective-permute-start.10 = (f32[2,4,32,128]{3,2,1,0:T(8,128)S(1)}, f32[2,4,32,128]{3,2,1,0:T(8,128)S(1)}, u32[]{:S(2)}, u32[]{:S(2)}) collective-permute-start(f32[2,4,32,128]{3,2,1,0:T(8,128)S(1)} %get-tuple-element.51), channel_id=1, source_target_pairs={{0,1},{1,0},{2,3},{3,2},{4,5},{5,4},{6,7},{7,6},{8,9},{9,8},{10,11... | collective-permute-start | bytes 393224 | tf_op jit(solution)/shard_map/ppermute | solution.py:27
  18.9 4.9 %collective-permute-start.7 = (bf16[128,128]{1,0:T(8,128)(2,1)S(1)}, bf16[128,128]{1,0:T(8,128)(2,1)S(1)}, u32[]{:S(2)}, u32[]{:S(2)}) collective-permute-start(bf16[128,128]{1,0:T(8,128)(2,1)S(1)} %get-tuple-element.49), channel_id=1, source_target_pairs={{0,6},{1,7},{2,4},{3,5},{4,2},{5,3},{6,0},{7,1},{8,14},{9,15},{10,... | collective-permute-start | bytes 98312 | tf_op jit(solution)/shard_map/ppermute | solution.py:33
  21.2 3.4 %collective-permute-start.9 = (bf16[128,128]{1,0:T(8,128)(2,1)S(1)}, bf16[128,128]{1,0:T(8,128)(2,1)S(1)}, u32[]{:S(2)}, u32[]{:S(2)}) collective-permute-start(bf16[128,128]{1,0:T(8,128)(2,1)S(1)} %get-tuple-element.49), channel_id=1, source_target_pairs={{0,3},{1,2},{2,1},{3,0},{4,7},{5,6},{6,5},{7,4},{8,11},{9,10},{10,... | collective-permute-start | bytes 98312 | tf_op jit(solution)/shard_map/ppermute | solution.py:33
  21.4 3.3 %collective-permute-start.8 = (bf16[128,128]{1,0:T(8,128)(2,1)S(1)}, bf16[128,128]{1,0:T(8,128)(2,1)S(1)}, u32[]{:S(2)}, u32[]{:S(2)}) collective-permute-start(bf16[128,128]{1,0:T(8,128)(2,1)S(1)} %get-tuple-element.59.d_ref), channel_id=1, source_target_pairs={{0,5},{1,4},{2,7},{3,6},{4,1},{5,0},{6,3},{7,2},{8,13},{9,12},{10,... | collective-permute-start | bytes 98312 | tf_op jit(solution)/shard_map/ppermute | solution.py:33
  24.8 4.3 %collective-permute-start.12 = (bf16[128,128]{1,0:T(8,128)(2,1)S(1)}, bf16[128,128]{1,0:T(8,128)(2,1)S(1)}, u32[]{:S(2)}, u32[]{:S(2)}) collective-permute-start(bf16[128,128]{1,0:T(8,128)(2,1)S(1)} %add_four.1), channel_id=1, source_target_pairs={{0,17},{1,16},{2,19},{3,18},{4,21},{5,20},{6,23},{7,22},{8,25},{9,... | collective-permute-start | bytes 98312 | tf_op jit(solution)/shard_map/ppermute | solution.py:33
  27.3 5.1 %collective-permute-start.11 = (bf16[1,4,32,128]{3,2,1,0:T(8,128)(2,1)S(1)}, bf16[1,4,32,128]{3,2,1,0:T(8,128)(2,1)S(1)}, u32[]{:S(2)}, u32[]{:S(2)}) collective-permute-start(bf16[1,4,32,128]{3,2,1,0:T(8,128)(2,1)S(1)} %get-tuple-element.56), channel_id=1, source_target_pairs={{0,2},{1,3},{2,0},{3,1},{4,6},{5,7},{6,4},{7,5},{8,10},{9,11},{10,... | collective-permute-start | bytes 98312 | tf_op jit(solution)/shard_map/ppermute | solution.py:27
  29.1 4.9 %collective-permute-start.13 = (bf16[128,128]{1,0:T(8,128)(2,1)S(1)}, bf16[128,128]{1,0:T(8,128)(2,1)S(1)}, u32[]{:S(2)}, u32[]{:S(2)}) collective-permute-start(bf16[128,128]{1,0:T(8,128)(2,1)S(1)} %add_convert_fusion.own_ref), channel_id=1, source_target_pairs={{0,10},{1,11},{2,8},{3,9},{4,14},{5,15},{6,12},{7,13},{8,2},{9,3},... | collective-permute-start | bytes 98312 | tf_op jit(solution)/shard_map/ppermute | solution.py:33
  31.8 3.6 %collective-permute-start.14 = (bf16[128,128]{1,0:T(8,128)(2,1)S(1)}, bf16[128,128]{1,0:T(8,128)(2,1)S(1)}, u32[]{:S(2)}, u32[]{:S(2)}) collective-permute-start(bf16[128,128]{1,0:T(8,128)(2,1)S(1)} %add_convert_fusion.own_ref), channel_id=1, source_target_pairs={{0,9},{1,8},{2,11},{3,10},{4,13},{5,12},{6,15},{7,14},{8,1},{9,0},... | collective-permute-start | bytes 98312 | tf_op jit(solution)/shard_map/ppermute | solution.py:33
  31.9 3.5 %collective-permute-start.15 = (bf16[128,128]{1,0:T(8,128)(2,1)S(1)}, bf16[128,128]{1,0:T(8,128)(2,1)S(1)}, u32[]{:S(2)}, u32[]{:S(2)}) collective-permute-start(bf16[128,128]{1,0:T(8,128)(2,1)S(1)} %add_convert_fusion.own_ref), channel_id=1, source_target_pairs={{0,3},{1,2},{2,1},{3,0},{4,7},{5,6},{6,5},{7,4},{8,11},{9,10},{10,... | collective-permute-start | bytes 98312 | tf_op jit(solution)/shard_map/ppermute | solution.py:33
  35.4 1.3 %collective-permute-start.16 = (bf16[2,128,128]{2,1,0:T(8,128)(2,1)S(1)}, bf16[2,128,128]{2,1,0:T(8,128)(2,1)S(1)}, u32[]{:S(2)}, u32[]{:S(2)}) collective-permute-start(bf16[2,128,128]{2,1,0:T(8,128)(2,1)S(1)} %join_sums.1), channel_id=1, source_target_pairs={{0,1},{1,0},{2,3},{3,2},{4,5},{5,4},{6,7},{7,6},{8,9},{9,8},{10,11... | collective-permute-start | bytes 196616 | tf_op jit(solution)/shard_map/ppermute | solution.py:27
  (2 other events, 1.5 us)

commit v7 on v6

--- a/solution.py
+++ b/solution.py
@@ -13,7 +13,7 @@
 WHOLE = pl.BlockSpec()
 SMEM = pl.BlockSpec(memory_space=pltpu.SMEM)
 J_STEP = 4
-FORWARD_STEP = 32
+FORWARD_STEP = 64
 W_STEP = 16
 STAGE_COST = 400000
 
@@ -516,7 +516,7 @@
 
     steps = [row_bits[-1]] + row_bits[1:-1] + row_bits[:1]
     ch = w_a_lin.shape[1]
-    held, own_slab = stage(lead(), grad_out, pair_slab)
+    held, own_slab, *staged = stage(lead(), grad_out, pair_slab, w_a_lin, w_a_gate, w_b_lin, w_b_gate)
     order = [0]
     blocks = {0: own_slab}
     for bit in reversed(col_bits[1:]):
@@ -531,7 +531,7 @@
     slab_flags, flags = (
         jnp.broadcast_to(m.astype(BF16)[:, None], m.shape + (ch,)) for m in masks
     )
-    value, lin, gate = pair_forward(pair_full, w_b_lin, w_b_gate, flags)
+    value, lin, gate = pair_forward(pair_full, *staged[2:], flags)
     got_last = swap(held, "row", steps[-1])
     got, value = lax.optimization_barrier((got, value))
     got_both = swap(got, "row", steps[-1])
@@ -539,7 +539,7 @@
         order = order + [r ^ bit for r in order]
     slabs = jnp.concatenate([blocks[b] for b in sorted(blocks)], axis=0)
     slabs = [slabs, swap(slabs, "col", 1)]
-    slab = slab_forward(slabs, n_col, w_a_lin, w_a_gate, slab_flags, flags)
+    slab = slab_forward(slabs, n_col, *staged[:2], slab_flags, flags)
     pieces = [held, got, got_last]
     first = (first_totals(order, pieces, slab[1]), first_sums(pieces, value))
     kept = [0]

time: 37.7 us -> 37.6 us (level)
  local copies, waits for them, and re-layouts: 0.79 us -> 0.24 us
  starting transfers between devices: 21.4 us -> 21.8 us
    unnamed x20, local copies, waits for them, and re-layouts: 0.61 us -> 0.05 us
    ppermute x10, starting transfers between devices: 12.3 us -> 12.8 us  [swap(): return lax.ppermute(value, axis, [(d, d ^ bit) for d in range(size)])]
  transfers between devices with their start and end apart: 17 -> 17, of which waited for: 10 -> 11; matrix products, arithmetic and copies ran while one was open for 1% -> 1% of each run, Pallas kernels for 13% -> 13%
where the time goes in v7:
time: 37.6 us; the launch traced here: 37.4 us
  starting transfers between devices  21.8 us (58%)
  waiting for transfers between devices  7.79 us (21%)
  Pallas kernels  5.89 us (16%)
  between operations  0.88 us (2%)
  other arithmetic  0.8 us (2%)
    ppermute x10, starting transfers between devices, swap(): return lax.ppermute(value, axis, [(d, d ^ bit) for d in range(size)])  12.8 us
    ppermute x7, starting transfers between devices, swap_chips(): return lax.ppermute(value, ('row', 'col'), pairs)  9.06 us
    ppermute x7, waiting for transfers between devices, swap_chips(): return lax.ppermute(value, ('row', 'col'), pairs)  4.1 us
    ppermute x10, waiting for transfers between devices, swap(): return lax.ppermute(value, axis, [(d, d ^ bit) for d in range(size)])  3.7 us
    pallas_call x1, Pallas kernels, pair_out(): pl.pallas_call(pair_out_kernel, out_shape=jax.ShapeDtypeStruct((cols * ke...  1.23 us
    pallas_call x1, Pallas kernels, main_part(): pl.pallas_call(functools.partial(main_kernel, order, blocks), out_shape=(...  1.05 us
    pallas_call x1, Pallas kernels, first_sums(): pl.pallas_call(functools.partial(sums_kernel, len(grads)), out_shape=jax....  0.98 us
    pallas_call x1, Pallas kernels, first_totals(): pl.pallas_call(functools.partial(totals_kernel, order, len(grads)), out_s...  0.98 us
  transfers between devices with their start and end apart: 17, of which 11 were waited for; matrix products, arithmetic and copies ran while one was open for 1% of the time, Pallas kernels for 13%

profile of v7, /device:TPU:0, one launch (start us, length us, event | category | flops | bytes accessed | tf_op | source)
XLA Modules:
  0.0 37.4 jit_solution(15183808465588594373)
XLA Ops:
  0.7 4.1 %collective-permute-start = (bf16[2,64,128]{2,1,0:T(8,128)(2,1)}, bf16[2,64,128]{2,1,0:T(8,128)(2,1)S(1)}, u32[]{:S(2)}, u32[]{:S(2)}) collective-permute-start(bf16[2,64,128]{2,1,0:T(8,128)(2,1)} %refs_0_.1), channel_id=1, source_target_pairs={{0,16},{4,20},{8,24},{12,28},{16,0},{20,4},{24,8},{28,12},{1,17},{... | collective-permute-start | bytes 98312 | tf_op jit(solution)/shard_map/ppermute | solution.py:27
  4.9 1.6 %collective-permute-start.2 = (bf16[4,32,128]{2,1,0:T(8,128)(2,1)S(1)}, bf16[4,32,128]{2,1,0:T(8,128)(2,1)S(1)}, u32[]{:S(2)}, u32[]{:S(2)}) collective-permute-start(bf16[4,32,128]{2,1,0:T(8,128)(2,1)S(1)} %get-tuple-element.38), channel_id=1, source_target_pairs={{0,2},{1,3},{2,0},{3,1},{4,6},{5,7},{6,4},{7,5},{8,10},{9,11},{10,... | collective-permute-start | bytes 98312 | tf_op jit(solution)/shard_map/ppermute | solution.py:27
  6.4 0.8 %collective-permute-done = bf16[2,64,128]{2,1,0:T(8,128)(2,1)S(1)} collective-permute-done((bf16[2,64,128]{2,1,0:T(8,128)(2,1)}, bf16[2,64,128]{2,1,0:T(8,128)(2,1)S(1)}, u32[]{:S(2)}, u32[]{:S(2)}) %collective-permute-start) | collective-permute-done | bytes 32800 | tf_op jit(solution)/shard_map/ppermute | solution.py:27
  7.3 1.6 %collective-permute-start.1 = (bf16[4,64,128]{2,1,0:T(8,128)(2,1)S(1)}, bf16[4,64,128]{2,1,0:T(8,128)(2,1)S(1)}, u32[]{:S(2)}, u32[]{:S(2)}) collective-permute-start(bf16[4,64,128]{2,1,0:T(8,128)(2,1)S(1)} %constant_dynamic-update-slice_fusion.refs_0_), channel_id=1, source_target_pairs={{0,8},{4,12},{8,0},{12,4},{16,24},{20,28},{24,16},{28,20},{1,9},{5... | collective-permute-start | bytes 196616 | tf_op jit(solution)/shard_map/ppermute | solution.py:27
  8.9 1.5 %collective-permute-start.4 = (bf16[4,64,128]{2,1,0:T(8,128)(2,1)S(1)}, bf16[4,64,128]{2,1,0:T(8,128)(2,1)S(1)}, u32[]{:S(2)}, u32[]{:S(2)}) collective-permute-start(bf16[4,64,128]{2,1,0:T(8,128)(2,1)S(1)} %constant_dynamic-update-slice_fusion.refs_0_), channel_id=1, source_target_pairs={{0,4},{4,0},{8,12},{12,8},{16,20},{20,16},{24,28},{28,24},{1,5},{5... | collective-permute-start | bytes 196616 | tf_op jit(solution)/shard_map/ppermute | solution.py:27
  10.6 0.5 %pair_forward.1 = (bf16[64,32,128]{2,1,0:T(8,128)(2,1)S(1)}, f32[64,32,128]{2,1,0:T(8,128)S(1)}, f32[64,32,128]{2,1,0:T(8,128)S(1)}) custom-call(bf16[64,32,128]{2,1,0:T(8,128)(2,1)S(1)} %copy-done, bf16[128,128]{1,0:T(8,128)(2,1)S(1)} %get-tuple-element.36.w_lin_ref, bf16[128,128]{1,0:T(8,128)(2,1)S(1)} %get-tuple-element.37.w_gate_ref, ...), custom_call_target="tpu_custom_call" | custom-call | flops 134217728 | bytes 3670016 | tf_op jit(solution)/shard_map/pair_forward/pallas_call | solution.py:125
  11.2 0.4 %collective-permute-done.1.refs_1_ = bf16[4,64,128]{2,1,0:T(8,128)(2,1)S(1)} collective-permute-done((bf16[4,64,128]{2,1,0:T(8,128)(2,1)S(1)}, bf16[4,64,128]{2,1,0:T(8,128)(2,1)S(1)}, u32[]{:S(2)}, u32[]{:S(2)}) %collective-permute-start.1) | collective-permute-done | bytes 65568 | tf_op jit(solution)/shard_map/ppermute | solution.py:27
  11.6 1.7 %collective-permute-start.3 = (bf16[4,64,128]{2,1,0:T(8,128)(2,1)S(1)}, bf16[4,64,128]{2,1,0:T(8,128)(2,1)S(1)}, u32[]{:S(2)}, u32[]{:S(2)}) collective-permute-start(bf16[4,64,128]{2,1,0:T(8,128)(2,1)S(1)} %collective-permute-done.1.refs_1_), channel_id=1, source_target_pairs={{0,4},{4,0},{8,12},{12,8},{16,20},{20,16},{24,28},{28,24},{1,5},{5... | collective-permute-start | bytes 196616 | tf_op jit(solution)/shard_map/ppermute | solution.py:27
  13.7 1.0 %first_totals_over_i.1.total_ref = f32[64,32,128]{2,1,0:T(8,128)S(1)} custom-call(bf16[4,64,128]{2,1,0:T(8,128)(2,1)S(1)} %constant_dynamic-update-slice_fusion.refs_0_, bf16[4,64,128]{2,1,0:T(8,128)(2,1)S(1)} %collective-permute-done.1.refs_1_, bf16[4,64,128]{2,1,0:T(8,128)(2,1)S(1)} %collective-permute-done.4.refs_2_, ...), custom_call_target="tpu_custom_call" | custom-call | flops 6291456 | bytes 2097152 | tf_op jit(solution)/shard_map/first_totals_over_i/pallas_call | solution.py:276
  14.7 1.0 %first_sums_over_j.1.first_sums_ref = f32[12,32,128]{2,1,0:T(8,128)S(1)} custom-call(bf16[4,64,128]{2,1,0:T(8,128)(2,1)S(1)} %constant_dynamic-update-slice_fusion.refs_0_, bf16[4,64,128]{2,1,0:T(8,128)(2,1)S(1)} %collective-permute-done.1.refs_1_, bf16[4,64,128]{2,1,0:T(8,128)(2,1)S(1)} %collective-permute-done.4.refs_2_, ...), custom_call_target="tpu_custom_call" | custom-call | flops 6291456 | bytes 2097152 | tf_op jit(solution)/shard_map/first_sums_over_j/pallas_call | solution.py:242
  15.9 1.1 %last_rows.1 = (bf16[64,32,128]{2,1,0:T(8,128)(2,1)S(1)}, bf16[64,32,128]{2,1,0:T(8,128)(2,1)S(1)}, f32[2,4,32,128]{3,2,1,0:T(8,128)S(1)}, f32[2,4,32,128]{3,2,1...) custom-call(bf16[4,64,128]{2,1,0:T(8,128)(2,1)S(1)} %collective-permute-done.3.grad_ref, ...), custom_call_target="tpu_custom_call" | custom-call | flops 268435456 | bytes 4194304 | tf_op jit(solution)/shard_map/last_rows/pallas_call | solution.py:373
  17.0 1.3 %collective-permute-done.6 = f32[2,128,128]{2,1,0:T(8,128)S(1)} collective-permute-done((f32[2,128,128]{2,1,0:T(8,128)S(1)}, f32[2,128,128]{2,1,0:T(8,128)S(1)}, u32[]{:S(2)}, u32[]{:S(2)}) %collective-permute-start.6) | collective-permute-done | bytes 131104 | tf_op jit(solution)/shard_map/ppermute | solution.py:27
  18.5 2.7 %collective-permute-start.7 = (bf16[128,128]{1,0:T(8,128)(2,1)S(1)}, bf16[128,128]{1,0:T(8,128)(2,1)S(1)}, u32[]{:S(2)}, u32[]{:S(2)}) collective-permute-start(bf16[128,128]{1,0:T(8,128)(2,1)S(1)} %get-tuple-element.57), channel_id=1, source_target_pairs={{0,6},{1,7},{2,4},{3,5},{4,2},{5,3},{6,0},{7,1},{8,14},{9,15},{10,... | collective-permute-start | bytes 98312 | tf_op jit(solution)/shard_map/ppermute | solution.py:33
  21.8 1.2 %pair_input_grad.1 = bf16[2048,128]{1,0:T(8,128)(2,1)} custom-call(bf16[2048,128]{1,0:T(8,128)(2,1)S(1)} %bitcast.9, bf16[2048,128]{1,0:T(8,128)(2,1)S(1)} %bitcast.10, bf16[128,128]{1,0:T(8,128)(2,1)S(1)} %copy-done.1, bf16[128,128]{1,0:T(8,128)(2,1)S(1)} %copy-done.2), custom_call_target="tpu_custom_call" | custom-call | flops 134217728 | bytes 1572864 | tf_op jit(solution)/shard_map/pair_input_grad/pallas_call | solution.py:409
  23.4 1.3 %collective-permute-done.9.c_ref = bf16[128,128]{1,0:T(8,128)(2,1)S(1)} collective-permute-done((bf16[128,128]{1,0:T(8,128)(2,1)S(1)}, bf16[128,128]{1,0:T(8,128)(2,1)S(1)}, u32[]{:S(2)}, u32[]{:S(2)}) %collective-permute-start.9) | collective-permute-done | bytes 32800 | tf_op jit(solution)/shard_map/ppermute | solution.py:33
  24.8 2.5 %collective-permute-start.12 = (bf16[128,128]{1,0:T(8,128)(2,1)S(1)}, bf16[128,128]{1,0:T(8,128)(2,1)S(1)}, u32[]{:S(2)}, u32[]{:S(2)}) collective-permute-start(bf16[128,128]{1,0:T(8,128)(2,1)S(1)} %add_four.1), channel_id=1, source_target_pairs={{0,17},{1,16},{2,19},{3,18},{4,21},{5,20},{6,23},{7,22},{8,25},{9,... | collective-permute-start | bytes 98312 | tf_op jit(solution)/shard_map/ppermute | solution.py:33
  27.4 1.6 %collective-permute-start.11 = (bf16[1,4,32,128]{3,2,1,0:T(8,128)(2,1)S(1)}, bf16[1,4,32,128]{3,2,1,0:T(8,128)(2,1)S(1)}, u32[]{:S(2)}, u32[]{:S(2)}) collective-permute-start(bf16[1,4,32,128]{3,2,1,0:T(8,128)(2,1)S(1)} %get-tuple-element.64), channel_id=1, source_target_pairs={{0,2},{1,3},{2,0},{3,1},{4,6},{5,7},{6,4},{7,5},{8,10},{9,11},{10,... | collective-permute-start | bytes 98312 | tf_op jit(solution)/shard_map/ppermute | solution.py:27
  29.2 2.6 %collective-permute-start.13 = (bf16[128,128]{1,0:T(8,128)(2,1)S(1)}, bf16[128,128]{1,0:T(8,128)(2,1)S(1)}, u32[]{:S(2)}, u32[]{:S(2)}) collective-permute-start(bf16[128,128]{1,0:T(8,128)(2,1)S(1)} %add_convert_fusion.own_ref), channel_id=1, source_target_pairs={{0,10},{1,11},{2,8},{3,9},{4,14},{5,15},{6,12},{7,13},{8,2},{9,3},... | collective-permute-start | bytes 98312 | tf_op jit(solution)/shard_map/ppermute | solution.py:33
  31.9 0.5 %collective-permute-start.15 = (bf16[128,128]{1,0:T(8,128)(2,1)S(1)}, bf16[128,128]{1,0:T(8,128)(2,1)S(1)}, u32[]{:S(2)}, u32[]{:S(2)}) collective-permute-start(bf16[128,128]{1,0:T(8,128)(2,1)S(1)} %add_convert_fusion.own_ref), channel_id=1, source_target_pairs={{0,3},{1,2},{2,1},{3,0},{4,7},{5,6},{6,5},{7,4},{8,11},{9,10},{10,... | collective-permute-start | bytes 98312 | tf_op jit(solution)/shard_map/ppermute | solution.py:33
  32.4 0.8 %slab_input_grad.1 = bf16[4,32,128]{2,1,0:T(8,128)(2,1)} custom-call(f32[4,32,128]{2,1,0:T(8,128)S(1)} %bitcast.11, bf16[4,32,128]{2,1,0:T(8,128)(2,1)S(1)} %bitcast.12, f32[16,32,128]{2,1,0:T(8,128)S(1)} %get-tuple-element.50.slab_lin_ref.lin_ref, f32[16,32,128]{2,1,0:T(8,128)S(1)} %get-tuple-element.51.slab_gate_ref.gate_ref, ...), custom_call_target="tpu_custom_call" | custom-call | flops 8388608 | bytes 262144 | tf_op jit(solution)/shard_map/slab_input_grad/pallas_call | solution.py:499
  33.2 0.8 %collective-permute-done.13.diagonal_ref = bf16[128,128]{1,0:T(8,128)(2,1)S(1)} collective-permute-done((bf16[128,128]{1,0:T(8,128)(2,1)S(1)}, bf16[128,128]{1,0:T(8,128)(2,1)S(1)}, u32[]{:S(2)}, u32[]{:S(2)}) %collective-permute-start.13) | collective-permute-done | bytes 32800 | tf_op jit(solution)/shard_map/ppermute | solution.py:33
  34.0 1.3 %collective-permute-done.14.late_ref = bf16[128,128]{1,0:T(8,128)(2,1)S(1)} collective-permute-done((bf16[128,128]{1,0:T(8,128)(2,1)S(1)}, bf16[128,128]{1,0:T(8,128)(2,1)S(1)}, u32[]{:S(2)}, u32[]{:S(2)}) %collective-permute-start.14) | collective-permute-done | bytes 32800 | tf_op jit(solution)/shard_map/ppermute | solution.py:33
  35.7 0.9 %collective-permute-done.16 = bf16[2,128,128]{2,1,0:T(8,128)(2,1)S(1)} collective-permute-done((bf16[2,128,128]{2,1,0:T(8,128)(2,1)S(1)}, bf16[2,128,128]{2,1,0:T(8,128)(2,1)S(1)}, u32[]{:S(2)}, u32[]{:S(2)}) %collective-permute-start.16) | collective-permute-done | bytes 65568 | tf_op jit(solution)/shard_map/ppermute | solution.py:27
  36.7 0.7 %maximum_select_fusion = f32[4,128,128]{2,1,0:T(8,128)} fusion(f32[2,128,128]{2,1,0:T(8,128)S(1)} %convert_multiply_fusion, f32[2,128,128]{2,1,0:T(8,128)S(1)} %convert_multiply_fusion.1, pred[]{:T(512)S(6)} %eq.3), kind=kLoop, calls=%fused_computation | loop fusion | flops 196608 | bytes 524289 | tf_op jit(solution)/shard_map/jit(_where)/select_n | solution.py:579
  (54 shorter events, 3.0 us)
Async XLA Ops:
  0.6 4.2 %copy-start.6 = (bf16[2,64,128]{2,1,0:T(8,128)(2,1)S(1)}, bf16[2,64,128]{2,1,0:T(8,128)(2,1)}, u32[]{:S(2)}) copy-start(bf16[2,64,128]{2,1,0:T(8,128)(2,1)} %refs_0_.1) | copy-start | bytes 98308
  0.6 4.2 %copy-start.3 = (bf16[128,128]{1,0:T(8,128)(2,1)S(1)}, bf16[128,128]{1,0:T(8,128)(2,1)}, u32[]{:S(2)}) copy-start(bf16[128,128]{1,0:T(8,128)(2,1)} %w_lin_ref.3) | copy-start | bytes 98308
  0.7 4.2 %copy-start.4 = (bf16[128,128]{1,0:T(8,128)(2,1)S(1)}, bf16[128,128]{1,0:T(8,128)(2,1)}, u32[]{:S(2)}) copy-start(bf16[128,128]{1,0:T(8,128)(2,1)} %w_gate_ref.3) | copy-start | bytes 98308
  0.7 4.1 %copy-start.1 = (bf16[128,128]{1,0:T(8,128)(2,1)S(1)}, bf16[128,128]{1,0:T(8,128)(2,1)}, u32[]{:S(2)}) copy-start(bf16[128,128]{1,0:T(8,128)(2,1)} %w_lin_ref.2) | copy-start | bytes 98308
  0.7 4.1 %copy-start.2 = (bf16[128,128]{1,0:T(8,128)(2,1)S(1)}, bf16[128,128]{1,0:T(8,128)(2,1)}, u32[]{:S(2)}) copy-start(bf16[128,128]{1,0:T(8,128)(2,1)} %w_gate_ref.2) | copy-start | bytes 98308
  0.7 4.1 %copy-start.5 = (bf16[4,32,128]{2,1,0:T(8,128)(2,1)S(1)}, bf16[4,32,128]{2,1,0:T(8,128)(2,1)}, u32[]{:S(2)}) copy-start(bf16[4,32,128]{2,1,0:T(8,128)(2,1)} %refs_1_.1) | copy-start | bytes 98308
  0.7 6.6 %collective-permute-start = (bf16[2,64,128]{2,1,0:T(8,128)(2,1)}, bf16[2,64,128]{2,1,0:T(8,128)(2,1)S(1)}, u32[]{:S(2)}, u32[]{:S(2)}) collective-permute-start(bf16[2,64,128]{2,1,0:T(8,128)(2,1)} %refs_0_.1), channel_id=1, source_target_pairs={{0,16},{4,20},{8,24},{12,28},{16,0},{20,4},{24,8},{28,12},{1,17},{... | collective-permute-start | bytes 98312 | tf_op jit(solution)/shard_map/ppermute | solution.py:27
  4.8 5.8 %copy-start = (bf16[64,32,128]{2,1,0:T(8,128)(2,1)S(1)}, bf16[64,32,128]{2,1,0:T(8,128)(2,1)}, u32[]{:S(2)}) copy-start(bf16[64,32,128]{2,1,0:T(8,128)(2,1)} %pair_ref.3) | copy-start | bytes 1572868
  4.9 5.5 %collective-permute-start.2 = (bf16[4,32,128]{2,1,0:T(8,128)(2,1)S(1)}, bf16[4,32,128]{2,1,0:T(8,128)(2,1)S(1)}, u32[]{:S(2)}, u32[]{:S(2)}) collective-permute-start(bf16[4,32,128]{2,1,0:T(8,128)(2,1)S(1)} %get-tuple-element.38), channel_id=1, source_target_pairs={{0,2},{1,3},{2,0},{3,1},{4,6},{5,7},{6,4},{7,5},{8,10},{9,11},{10,... | collective-permute-start | bytes 98312 | tf_op jit(solution)/shard_map/ppermute | solution.py:27
  7.3 4.3 %collective-permute-start.1 = (bf16[4,64,128]{2,1,0:T(8,128)(2,1)S(1)}, bf16[4,64,128]{2,1,0:T(8,128)(2,1)S(1)}, u32[]{:S(2)}, u32[]{:S(2)}) collective-permute-start(bf16[4,64,128]{2,1,0:T(8,128)(2,1)S(1)} %constant_dynamic-update-slice_fusion.refs_0_), channel_id=1, source_target_pairs={{0,8},{4,12},{8,0},{12,4},{16,24},{20,28},{24,16},{28,20},{1,9},{5... | collective-permute-start | bytes 196616 | tf_op jit(solution)/shard_map/ppermute | solution.py:27
  8.9 4.8 %collective-permute-start.4 = (bf16[4,64,128]{2,1,0:T(8,128)(2,1)S(1)}, bf16[4,64,128]{2,1,0:T(8,128)(2,1)S(1)}, u32[]{:S(2)}, u32[]{:S(2)}) collective-permute-start(bf16[4,64,128]{2,1,0:T(8,128)(2,1)S(1)} %constant_dynamic-update-slice_fusion.refs_0_), channel_id=1, source_target_pairs={{0,4},{4,0},{8,12},{12,8},{16,20},{20,16},{24,28},{28,24},{1,5},{5... | collective-permute-start | bytes 196616 | tf_op jit(solution)/shard_map/ppermute | solution.py:27
  10.4 2.9 %collective-permute-start.5 = (bf16[8,32,128]{2,1,0:T(8,128)(2,1)S(1)}, bf16[8,32,128]{2,1,0:T(8,128)(2,1)S(1)}, u32[]{:S(2)}, u32[]{:S(2)}) collective-permute-start(bf16[8,32,128]{2,1,0:T(8,128)(2,1)S(1)} %constant_dynamic-update-slice_fusion.2.even_ref), channel_id=1, source_target_pairs={{0,1},{1,0},{2,3},{3,2},{4,5},{5,4},{6,7},{7,6},{8,9},{9,8},{10,11... | collective-permute-start | bytes 196616 | tf_op jit(solution)/shard_map/ppermute | solution.py:27
  11.6 4.3 %collective-permute-start.3 = (bf16[4,64,128]{2,1,0:T(8,128)(2,1)S(1)}, bf16[4,64,128]{2,1,0:T(8,128)(2,1)S(1)}, u32[]{:S(2)}, u32[]{:S(2)}) collective-permute-start(bf16[4,64,128]{2,1,0:T(8,128)(2,1)S(1)} %collective-permute-done.1.refs_1_), channel_id=1, source_target_pairs={{0,4},{4,0},{8,12},{12,8},{16,20},{20,16},{24,28},{28,24},{1,5},{5... | collective-permute-start | bytes 196616 | tf_op jit(solution)/shard_map/ppermute | solution.py:27
  16.9 1.4 %collective-permute-start.6 = (f32[2,128,128]{2,1,0:T(8,128)S(1)}, f32[2,128,128]{2,1,0:T(8,128)S(1)}, u32[]{:S(2)}, u32[]{:S(2)}) collective-permute-start(f32[2,128,128]{2,1,0:T(8,128)S(1)} %get-tuple-element.54), channel_id=1, source_target_pairs={{0,1},{1,0},{2,3},{3,2},{4,5},{5,4},{6,7},{7,6},{8,9},{9,8},{10,11... | collective-permute-start | bytes 393224 | tf_op jit(solution)/shard_map/ppermute | solution.py:27
  18.3 6.5 %collective-permute-start.10 = (f32[2,4,32,128]{3,2,1,0:T(8,128)S(1)}, f32[2,4,32,128]{3,2,1,0:T(8,128)S(1)}, u32[]{:S(2)}, u32[]{:S(2)}) collective-permute-start(f32[2,4,32,128]{3,2,1,0:T(8,128)S(1)} %get-tuple-element.59), channel_id=1, source_target_pairs={{0,1},{1,0},{2,3},{3,2},{4,5},{5,4},{6,7},{7,6},{8,9},{9,8},{10,11... | collective-permute-start | bytes 393224 | tf_op jit(solution)/shard_map/ppermute | solution.py:27
  18.5 4.9 %collective-permute-start.7 = (bf16[128,128]{1,0:T(8,128)(2,1)S(1)}, bf16[128,128]{1,0:T(8,128)(2,1)S(1)}, u32[]{:S(2)}, u32[]{:S(2)}) collective-permute-start(bf16[128,128]{1,0:T(8,128)(2,1)S(1)} %get-tuple-element.57), channel_id=1, source_target_pairs={{0,6},{1,7},{2,4},{3,5},{4,2},{5,3},{6,0},{7,1},{8,14},{9,15},{10,... | collective-permute-start | bytes 98312 | tf_op jit(solution)/shard_map/ppermute | solution.py:33
  21.3 3.4 %collective-permute-start.9 = (bf16[128,128]{1,0:T(8,128)(2,1)S(1)}, bf16[128,128]{1,0:T(8,128)(2,1)S(1)}, u32[]{:S(2)}, u32[]{:S(2)}) collective-permute-start(bf16[128,128]{1,0:T(8,128)(2,1)S(1)} %get-tuple-element.57), channel_id=1, source_target_pairs={{0,3},{1,2},{2,1},{3,0},{4,7},{5,6},{6,5},{7,4},{8,11},{9,10},{10,... | collective-permute-start | bytes 98312 | tf_op jit(solution)/shard_map/ppermute | solution.py:33
  21.5 3.3 %collective-permute-start.8 = (bf16[128,128]{1,0:T(8,128)(2,1)S(1)}, bf16[128,128]{1,0:T(8,128)(2,1)S(1)}, u32[]{:S(2)}, u32[]{:S(2)}) collective-permute-start(bf16[128,128]{1,0:T(8,128)(2,1)S(1)} %get-tuple-element.67.d_ref), channel_id=1, source_target_pairs={{0,5},{1,4},{2,7},{3,6},{4,1},{5,0},{6,3},{7,2},{8,13},{9,12},{10,... | collective-permute-start | bytes 98312 | tf_op jit(solution)/shard_map/ppermute | solution.py:33
  24.8 4.3 %collective-permute-start.12 = (bf16[128,128]{1,0:T(8,128)(2,1)S(1)}, bf16[128,128]{1,0:T(8,128)(2,1)S(1)}, u32[]{:S(2)}, u32[]{:S(2)}) collective-permute-start(bf16[128,128]{1,0:T(8,128)(2,1)S(1)} %add_four.1), channel_id=1, source_target_pairs={{0,17},{1,16},{2,19},{3,18},{4,21},{5,20},{6,23},{7,22},{8,25},{9,... | collective-permute-start | bytes 98312 | tf_op jit(solution)/shard_map/ppermute | solution.py:33
  27.4 5.1 %collective-permute-start.11 = (bf16[1,4,32,128]{3,2,1,0:T(8,128)(2,1)S(1)}, bf16[1,4,32,128]{3,2,1,0:T(8,128)(2,1)S(1)}, u32[]{:S(2)}, u32[]{:S(2)}) collective-permute-start(bf16[1,4,32,128]{3,2,1,0:T(8,128)(2,1)S(1)} %get-tuple-element.64), channel_id=1, source_target_pairs={{0,2},{1,3},{2,0},{3,1},{4,6},{5,7},{6,4},{7,5},{8,10},{9,11},{10,... | collective-permute-start | bytes 98312 | tf_op jit(solution)/shard_map/ppermute | solution.py:27
  29.2 4.9 %collective-permute-start.13 = (bf16[128,128]{1,0:T(8,128)(2,1)S(1)}, bf16[128,128]{1,0:T(8,128)(2,1)S(1)}, u32[]{:S(2)}, u32[]{:S(2)}) collective-permute-start(bf16[128,128]{1,0:T(8,128)(2,1)S(1)} %add_convert_fusion.own_ref), channel_id=1, source_target_pairs={{0,10},{1,11},{2,8},{3,9},{4,14},{5,15},{6,12},{7,13},{8,2},{9,3},... | collective-permute-start | bytes 98312 | tf_op jit(solution)/shard_map/ppermute | solution.py:33
  31.7 3.6 %collective-permute-start.14 = (bf16[128,128]{1,0:T(8,128)(2,1)S(1)}, bf16[128,128]{1,0:T(8,128)(2,1)S(1)}, u32[]{:S(2)}, u32[]{:S(2)}) collective-permute-start(bf16[128,128]{1,0:T(8,128)(2,1)S(1)} %add_convert_fusion.own_ref), channel_id=1, source_target_pairs={{0,9},{1,8},{2,11},{3,10},{4,13},{5,12},{6,15},{7,14},{8,1},{9,0},... | collective-permute-start | bytes 98312 | tf_op jit(solution)/shard_map/ppermute | solution.py:33
  31.9 3.4 %collective-permute-start.15 = (bf16[128,128]{1,0:T(8,128)(2,1)S(1)}, bf16[128,128]{1,0:T(8,128)(2,1)S(1)}, u32[]{:S(2)}, u32[]{:S(2)}) collective-permute-start(bf16[128,128]{1,0:T(8,128)(2,1)S(1)} %add_convert_fusion.own_ref), channel_id=1, source_target_pairs={{0,3},{1,2},{2,1},{3,0},{4,7},{5,6},{6,5},{7,4},{8,11},{9,10},{10,... | collective-permute-start | bytes 98312 | tf_op jit(solution)/shard_map/ppermute | solution.py:33
  35.3 1.3 %collective-permute-start.16 = (bf16[2,128,128]{2,1,0:T(8,128)(2,1)S(1)}, bf16[2,128,128]{2,1,0:T(8,128)(2,1)S(1)}, u32[]{:S(2)}, u32[]{:S(2)}) collective-permute-start(bf16[2,128,128]{2,1,0:T(8,128)(2,1)S(1)} %join_sums.1), channel_id=1, source_target_pairs={{0,1},{1,0},{2,3},{3,2},{4,5},{5,4},{6,7},{7,6},{8,9},{9,8},{10,11... | collective-permute-start | bytes 196616 | tf_op jit(solution)/shard_map/ppermute | solution.py:27
  (2 other events, 5.3 us)

commit v8 on v7

--- a/solution.py
+++ b/solution.py
@@ -418,6 +418,22 @@
     return out.reshape(cols, keys, cz)
 
 
+def hand_on_kernel(given_ref, out_ref):
+    out_ref[...] = given_ref[...]
+
+
+def hand_on(given):
+    return pl.pallas_call(
+        hand_on_kernel,
+        out_shape=jax.ShapeDtypeStruct(given.shape, given.dtype),
+        in_specs=[VMEM],
+        out_specs=VMEM,
+        compiler_params=params(),
+        cost_estimate=cost(STAGE_COST * given.size, 8 * given.size),
+        name="hand_on",
+    )(given)
+
+
 def fold_kernel(kept_ref, got_ref, sum_ref, moved_ref):
     half = sum_ref.shape[0]
     sum_ref[...] = kept_ref[:half] + got_ref[:half].astype(F32)
@@ -550,12 +566,13 @@
     )
     pair_bit, col = col_bits[1], lax.axis_index("col")
     got_w = swap(w_send, "col", 1)
-    sum_send, _ = lax.optimization_barrier((sum_send, got_w))
     side = w_keep + got_w
     upper = (col & pair_bit) != 0
     moved = jnp.where(upper, side[0], side[1]).astype(BF16)
     narrow = jnp.where(upper, side[1], side[0]).astype(BF16)
-    moved, d_lin, d_gate = lax.optimization_barrier((moved, d_lin, d_gate))
+    moved, narrow, sum_send, d_lin, d_gate = lax.optimization_barrier(
+        (moved, narrow, sum_send, d_lin, d_gate)
+    )
     grad_pair = pair_out(d_lin, d_gate, w_b_lin, w_b_gate)
     sums, got = sum_keep, swap(sum_send, "col", 1)
     bits = [bit * n_col for bit in row_bits]

time: 37.6 us -> 37.1 us (0.987)
  starting transfers between devices: 21.8 us -> 21.2 us
    ppermute x10, starting transfers between devices: 12.8 us -> 12.1 us  [swap(): return lax.ppermute(value, axis, [(d, d ^ bit) for d in range(size)])]
where the time goes in v8:
time: 37.1 us; the launch traced here: 36.9 us
  starting transfers between devices  21.2 us (57%)
  waiting for transfers between devices  7.93 us (21%)
  Pallas kernels  5.89 us (16%)
  between operations  0.88 us (2%)
  other arithmetic  0.8 us (2%)
    ppermute x10, starting transfers between devices, swap(): return lax.ppermute(value, axis, [(d, d ^ bit) for d in range(size)])  12.1 us
    ppermute x7, starting transfers between devices, swap_chips(): return lax.ppermute(value, ('row', 'col'), pairs)  9.13 us
    ppermute x7, waiting for transfers between devices, swap_chips(): return lax.ppermute(value, ('row', 'col'), pairs)  4.27 us
    ppermute x10, waiting for transfers between devices, swap(): return lax.ppermute(value, axis, [(d, d ^ bit) for d in range(size)])  3.66 us
    pallas_call x1, Pallas kernels, pair_out(): pl.pallas_call(pair_out_kernel, out_shape=jax.ShapeDtypeStruct((cols * ke...  1.23 us
    pallas_call x1, Pallas kernels, main_part(): pl.pallas_call(functools.partial(main_kernel, order, blocks), out_shape=(...  1.05 us
    pallas_call x1, Pallas kernels, first_sums(): pl.pallas_call(functools.partial(sums_kernel, len(grads)), out_shape=jax....  0.98 us
    pallas_call x1, Pallas kernels, first_totals(): pl.pallas_call(functools.partial(totals_kernel, order, len(grads)), out_s...  0.98 us
  transfers between devices with their start and end apart: 17, of which 11 were waited for; matrix products, arithmetic and copies ran while one was open for 1% of the time, Pallas kernels for 13%

profile of v8, /device:TPU:0, one launch (start us, length us, event | category | flops | bytes accessed | tf_op | source)
XLA Modules:
  0.0 36.9 jit_solution(11080944889591961098)
XLA Ops:
  0.7 4.1 %collective-permute-start = (bf16[2,64,128]{2,1,0:T(8,128)(2,1)}, bf16[2,64,128]{2,1,0:T(8,128)(2,1)S(1)}, u32[]{:S(2)}, u32[]{:S(2)}) collective-permute-start(bf16[2,64,128]{2,1,0:T(8,128)(2,1)} %refs_0_.1), channel_id=1, source_target_pairs={{0,16},{4,20},{8,24},{12,28},{16,0},{20,4},{24,8},{28,12},{1,17},{... | collective-permute-start | bytes 98312 | tf_op jit(solution)/shard_map/ppermute | solution.py:27
  4.9 1.6 %collective-permute-start.2 = (bf16[4,32,128]{2,1,0:T(8,128)(2,1)S(1)}, bf16[4,32,128]{2,1,0:T(8,128)(2,1)S(1)}, u32[]{:S(2)}, u32[]{:S(2)}) collective-permute-start(bf16[4,32,128]{2,1,0:T(8,128)(2,1)S(1)} %get-tuple-element.39), channel_id=1, source_target_pairs={{0,2},{1,3},{2,0},{3,1},{4,6},{5,7},{6,4},{7,5},{8,10},{9,11},{10,... | collective-permute-start | bytes 98312 | tf_op jit(solution)/shard_map/ppermute | solution.py:27
  6.4 0.8 %collective-permute-done = bf16[2,64,128]{2,1,0:T(8,128)(2,1)S(1)} collective-permute-done((bf16[2,64,128]{2,1,0:T(8,128)(2,1)}, bf16[2,64,128]{2,1,0:T(8,128)(2,1)S(1)}, u32[]{:S(2)}, u32[]{:S(2)}) %collective-permute-start) | collective-permute-done | bytes 32800 | tf_op jit(solution)/shard_map/ppermute | solution.py:27
  7.3 1.6 %collective-permute-start.1 = (bf16[4,64,128]{2,1,0:T(8,128)(2,1)S(1)}, bf16[4,64,128]{2,1,0:T(8,128)(2,1)S(1)}, u32[]{:S(2)}, u32[]{:S(2)}) collective-permute-start(bf16[4,64,128]{2,1,0:T(8,128)(2,1)S(1)} %constant_dynamic-update-slice_fusion.refs_0_), channel_id=1, source_target_pairs={{0,8},{4,12},{8,0},{12,4},{16,24},{20,28},{24,16},{28,20},{1,9},{5... | collective-permute-start | bytes 196616 | tf_op jit(solution)/shard_map/ppermute | solution.py:27
  8.9 1.5 %collective-permute-start.4 = (bf16[4,64,128]{2,1,0:T(8,128)(2,1)S(1)}, bf16[4,64,128]{2,1,0:T(8,128)(2,1)S(1)}, u32[]{:S(2)}, u32[]{:S(2)}) collective-permute-start(bf16[4,64,128]{2,1,0:T(8,128)(2,1)S(1)} %constant_dynamic-update-slice_fusion.refs_0_), channel_id=1, source_target_pairs={{0,4},{4,0},{8,12},{12,8},{16,20},{20,16},{24,28},{28,24},{1,5},{5... | collective-permute-start | bytes 196616 | tf_op jit(solution)/shard_map/ppermute | solution.py:27
  11.6 1.7 %collective-permute-start.3 = (bf16[4,64,128]{2,1,0:T(8,128)(2,1)S(1)}, bf16[4,64,128]{2,1,0:T(8,128)(2,1)S(1)}, u32[]{:S(2)}, u32[]{:S(2)}) collective-permute-start(bf16[4,64,128]{2,1,0:T(8,128)(2,1)S(1)} %collective-permute-done.1.refs_1_), channel_id=1, source_target_pairs={{0,4},{4,0},{8,12},{12,8},{16,20},{20,16},{24,28},{28,24},{1,5},{5... | collective-permute-start | bytes 196616 | tf_op jit(solution)/shard_map/ppermute | solution.py:27
  13.7 1.0 %first_totals_over_i.1.total_ref = f32[64,32,128]{2,1,0:T(8,128)S(1)} custom-call(bf16[4,64,128]{2,1,0:T(8,128)(2,1)S(1)} %constant_dynamic-update-slice_fusion.refs_0_, bf16[4,64,128]{2,1,0:T(8,128)(2,1)S(1)} %collective-permute-done.1.refs_1_, bf16[4,64,128]{2,1,0:T(8,128)(2,1)S(1)} %collective-permute-done.4.refs_2_, ...), custom_call_target="tpu_custom_call" | custom-call | flops 6291456 | bytes 2097152 | tf_op jit(solution)/shard_map/first_totals_over_i/pallas_call | solution.py:276
  14.7 1.0 %first_sums_over_j.1.first_sums_ref = f32[12,32,128]{2,1,0:T(8,128)S(1)} custom-call(bf16[4,64,128]{2,1,0:T(8,128)(2,1)S(1)} %constant_dynamic-update-slice_fusion.refs_0_, bf16[4,64,128]{2,1,0:T(8,128)(2,1)S(1)} %collective-permute-done.1.refs_1_, bf16[4,64,128]{2,1,0:T(8,128)(2,1)S(1)} %collective-permute-done.4.refs_2_, ...), custom_call_target="tpu_custom_call" | custom-call | flops 6291456 | bytes 2097152 | tf_op jit(solution)/shard_map/first_sums_over_j/pallas_call | solution.py:242
  15.9 1.1 %last_rows.1 = (bf16[64,32,128]{2,1,0:T(8,128)(2,1)S(1)}, bf16[64,32,128]{2,1,0:T(8,128)(2,1)S(1)}, f32[2,4,32,128]{3,2,1,0:T(8,128)S(1)}, f32[2,4,32,128]{3,2,1...) custom-call(bf16[4,64,128]{2,1,0:T(8,128)(2,1)S(1)} %collective-permute-done.3.grad_ref, ...), custom_call_target="tpu_custom_call" | custom-call | flops 268435456 | bytes 4194304 | tf_op jit(solution)/shard_map/last_rows/pallas_call | solution.py:373
  17.0 1.3 %collective-permute-done.6 = f32[2,128,128]{2,1,0:T(8,128)S(1)} collective-permute-done((f32[2,128,128]{2,1,0:T(8,128)S(1)}, f32[2,128,128]{2,1,0:T(8,128)S(1)}, u32[]{:S(2)}, u32[]{:S(2)}) %collective-permute-start.6) | collective-permute-done | bytes 131104 | tf_op jit(solution)/shard_map/ppermute | solution.py:27
  18.6 2.7 %collective-permute-start.7 = (bf16[128,128]{1,0:T(8,128)(2,1)S(1)}, bf16[128,128]{1,0:T(8,128)(2,1)S(1)}, u32[]{:S(2)}, u32[]{:S(2)}) collective-permute-start(bf16[128,128]{1,0:T(8,128)(2,1)S(1)} %get-tuple-element.59), channel_id=1, source_target_pairs={{0,6},{1,7},{2,4},{3,5},{4,2},{5,3},{6,0},{7,1},{8,14},{9,15},{10,... | collective-permute-start | bytes 98312 | tf_op jit(solution)/shard_map/ppermute | solution.py:33
  21.8 1.2 %pair_input_grad.1 = bf16[2048,128]{1,0:T(8,128)(2,1)} custom-call(bf16[2048,128]{1,0:T(8,128)(2,1)S(1)} %bitcast.9, bf16[2048,128]{1,0:T(8,128)(2,1)S(1)} %bitcast.10, bf16[128,128]{1,0:T(8,128)(2,1)S(1)} %copy-done.1, bf16[128,128]{1,0:T(8,128)(2,1)S(1)} %copy-done.2), custom_call_target="tpu_custom_call" | custom-call | flops 134217728 | bytes 1572864 | tf_op jit(solution)/shard_map/pair_input_grad/pallas_call | solution.py:409
  23.4 1.3 %collective-permute-done.8.b_ref = bf16[128,128]{1,0:T(8,128)(2,1)S(1)} collective-permute-done((bf16[128,128]{1,0:T(8,128)(2,1)S(1)}, bf16[128,128]{1,0:T(8,128)(2,1)S(1)}, u32[]{:S(2)}, u32[]{:S(2)}) %collective-permute-start.8) | collective-permute-done | bytes 32800 | tf_op jit(solution)/shard_map/ppermute | solution.py:33
  24.8 2.6 %collective-permute-start.12 = (bf16[128,128]{1,0:T(8,128)(2,1)S(1)}, bf16[128,128]{1,0:T(8,128)(2,1)S(1)}, u32[]{:S(2)}, u32[]{:S(2)}) collective-permute-start(bf16[128,128]{1,0:T(8,128)(2,1)S(1)} %add_four.1), channel_id=1, source_target_pairs={{0,17},{1,16},{2,19},{3,18},{4,21},{5,20},{6,23},{7,22},{8,25},{9,... | collective-permute-start | bytes 98312 | tf_op jit(solution)/shard_map/ppermute | solution.py:33
  27.4 0.6 %collective-permute-start.11 = (bf16[1,4,32,128]{3,2,1,0:T(8,128)(2,1)S(1)}, bf16[1,4,32,128]{3,2,1,0:T(8,128)(2,1)S(1)}, u32[]{:S(2)}, u32[]{:S(2)}) collective-permute-start(bf16[1,4,32,128]{3,2,1,0:T(8,128)(2,1)S(1)} %get-tuple-element.66), channel_id=1, source_target_pairs={{0,2},{1,3},{2,0},{3,1},{4,6},{5,7},{6,4},{7,5},{8,10},{9,11},{10,... | collective-permute-start | bytes 98312 | tf_op jit(solution)/shard_map/ppermute | solution.py:27
  28.0 1.1 %collective-permute-done.12 = bf16[128,128]{1,0:T(8,128)(2,1)S(1)} collective-permute-done((bf16[128,128]{1,0:T(8,128)(2,1)S(1)}, bf16[128,128]{1,0:T(8,128)(2,1)S(1)}, u32[]{:S(2)}, u32[]{:S(2)}) %collective-permute-start.12) | collective-permute-done | bytes 32800 | tf_op jit(solution)/shard_map/ppermute | solution.py:33
  29.1 2.0 %collective-permute-start.13 = (bf16[128,128]{1,0:T(8,128)(2,1)S(1)}, bf16[128,128]{1,0:T(8,128)(2,1)S(1)}, u32[]{:S(2)}, u32[]{:S(2)}) collective-permute-start(bf16[128,128]{1,0:T(8,128)(2,1)S(1)} %add_convert_fusion.own_ref), channel_id=1, source_target_pairs={{0,10},{1,11},{2,8},{3,9},{4,14},{5,15},{6,12},{7,13},{8,2},{9,3},... | collective-permute-start | bytes 98312 | tf_op jit(solution)/shard_map/ppermute | solution.py:33
  31.2 1.2 %collective-permute-start.15 = (bf16[128,128]{1,0:T(8,128)(2,1)S(1)}, bf16[128,128]{1,0:T(8,128)(2,1)S(1)}, u32[]{:S(2)}, u32[]{:S(2)}) collective-permute-start(bf16[128,128]{1,0:T(8,128)(2,1)S(1)} %add_convert_fusion.own_ref), channel_id=1, source_target_pairs={{0,3},{1,2},{2,1},{3,0},{4,7},{5,6},{6,5},{7,4},{8,11},{9,10},{10,... | collective-permute-start | bytes 98312 | tf_op jit(solution)/shard_map/ppermute | solution.py:33
  32.4 0.8 %slab_input_grad.1 = bf16[4,32,128]{2,1,0:T(8,128)(2,1)} custom-call(f32[4,32,128]{2,1,0:T(8,128)S(1)} %bitcast.11, bf16[4,32,128]{2,1,0:T(8,128)(2,1)S(1)} %bitcast.12, f32[16,32,128]{2,1,0:T(8,128)S(1)} %get-tuple-element.51.slab_lin_ref.lin_ref, f32[16,32,128]{2,1,0:T(8,128)S(1)} %get-tuple-element.52.slab_gate_ref.gate_ref, ...), custom_call_target="tpu_custom_call" | custom-call | flops 8388608 | bytes 262144 | tf_op jit(solution)/shard_map/slab_input_grad/pallas_call | solution.py:515
  33.2 0.8 %collective-permute-done.13.diagonal_ref = bf16[128,128]{1,0:T(8,128)(2,1)S(1)} collective-permute-done((bf16[128,128]{1,0:T(8,128)(2,1)S(1)}, bf16[128,128]{1,0:T(8,128)(2,1)S(1)}, u32[]{:S(2)}, u32[]{:S(2)}) %collective-permute-start.13) | collective-permute-done | bytes 32800 | tf_op jit(solution)/shard_map/ppermute | solution.py:33
  34.0 0.7 %collective-permute-done.14.late_ref = bf16[128,128]{1,0:T(8,128)(2,1)S(1)} collective-permute-done((bf16[128,128]{1,0:T(8,128)(2,1)S(1)}, bf16[128,128]{1,0:T(8,128)(2,1)S(1)}, u32[]{:S(2)}, u32[]{:S(2)}) %collective-permute-start.14) | collective-permute-done | bytes 32800 | tf_op jit(solution)/shard_map/ppermute | solution.py:33
  34.7 0.6 %collective-permute-start.16 = (bf16[2,128,128]{2,1,0:T(8,128)(2,1)S(1)}, bf16[2,128,128]{2,1,0:T(8,128)(2,1)S(1)}, u32[]{:S(2)}, u32[]{:S(2)}) collective-permute-start(bf16[2,128,128]{2,1,0:T(8,128)(2,1)S(1)} %join_sums.1), channel_id=1, source_target_pairs={{0,1},{1,0},{2,3},{3,2},{4,5},{5,4},{6,7},{7,6},{8,9},{9,8},{10,11... | collective-permute-start | bytes 196616 | tf_op jit(solution)/shard_map/ppermute | solution.py:27
  35.3 0.9 %collective-permute-done.16 = bf16[2,128,128]{2,1,0:T(8,128)(2,1)S(1)} collective-permute-done((bf16[2,128,128]{2,1,0:T(8,128)(2,1)S(1)}, bf16[2,128,128]{2,1,0:T(8,128)(2,1)S(1)}, u32[]{:S(2)}, u32[]{:S(2)}) %collective-permute-start.16) | collective-permute-done | bytes 65568 | tf_op jit(solution)/shard_map/ppermute | solution.py:27
  36.2 0.7 %maximum_select_fusion = f32[4,128,128]{2,1,0:T(8,128)} fusion(f32[2,128,128]{2,1,0:T(8,128)S(1)} %convert_multiply_fusion, f32[2,128,128]{2,1,0:T(8,128)S(1)} %convert_multiply_fusion.1, pred[]{:T(512)S(6)} %eq.3), kind=kLoop, calls=%fused_computation | loop fusion | flops 196608 | bytes 524289 | tf_op jit(solution)/shard_map/jit(_where)/select_n | solution.py:596
  (54 shorter events, 3.2 us)
Async XLA Ops:
  0.6 4.2 %copy-start.6 = (bf16[2,64,128]{2,1,0:T(8,128)(2,1)S(1)}, bf16[2,64,128]{2,1,0:T(8,128)(2,1)}, u32[]{:S(2)}) copy-start(bf16[2,64,128]{2,1,0:T(8,128)(2,1)} %refs_0_.1) | copy-start | bytes 98308
  0.6 4.2 %copy-start.3 = (bf16[128,128]{1,0:T(8,128)(2,1)S(1)}, bf16[128,128]{1,0:T(8,128)(2,1)}, u32[]{:S(2)}) copy-start(bf16[128,128]{1,0:T(8,128)(2,1)} %w_lin_ref.3) | copy-start | bytes 98308
  0.7 4.2 %copy-start.4 = (bf16[128,128]{1,0:T(8,128)(2,1)S(1)}, bf16[128,128]{1,0:T(8,128)(2,1)}, u32[]{:S(2)}) copy-start(bf16[128,128]{1,0:T(8,128)(2,1)} %w_gate_ref.3) | copy-start | bytes 98308
  0.7 4.1 %copy-start.1 = (bf16[128,128]{1,0:T(8,128)(2,1)S(1)}, bf16[128,128]{1,0:T(8,128)(2,1)}, u32[]{:S(2)}) copy-start(bf16[128,128]{1,0:T(8,128)(2,1)} %w_lin_ref.2) | copy-start | bytes 98308
  0.7 4.1 %copy-start.2 = (bf16[128,128]{1,0:T(8,128)(2,1)S(1)}, bf16[128,128]{1,0:T(8,128)(2,1)}, u32[]{:S(2)}) copy-start(bf16[128,128]{1,0:T(8,128)(2,1)} %w_gate_ref.2) | copy-start | bytes 98308
  0.7 4.1 %copy-start.5 = (bf16[4,32,128]{2,1,0:T(8,128)(2,1)S(1)}, bf16[4,32,128]{2,1,0:T(8,128)(2,1)}, u32[]{:S(2)}) copy-start(bf16[4,32,128]{2,1,0:T(8,128)(2,1)} %refs_1_.1) | copy-start | bytes 98308
  0.7 6.6 %collective-permute-start = (bf16[2,64,128]{2,1,0:T(8,128)(2,1)}, bf16[2,64,128]{2,1,0:T(8,128)(2,1)S(1)}, u32[]{:S(2)}, u32[]{:S(2)}) collective-permute-start(bf16[2,64,128]{2,1,0:T(8,128)(2,1)} %refs_0_.1), channel_id=1, source_target_pairs={{0,16},{4,20},{8,24},{12,28},{16,0},{20,4},{24,8},{28,12},{1,17},{... | collective-permute-start | bytes 98312 | tf_op jit(solution)/shard_map/ppermute | solution.py:27
  4.8 5.8 %copy-start = (bf16[64,32,128]{2,1,0:T(8,128)(2,1)S(1)}, bf16[64,32,128]{2,1,0:T(8,128)(2,1)}, u32[]{:S(2)}) copy-start(bf16[64,32,128]{2,1,0:T(8,128)(2,1)} %pair_ref.3) | copy-start | bytes 1572868
  4.9 5.5 %collective-permute-start.2 = (bf16[4,32,128]{2,1,0:T(8,128)(2,1)S(1)}, bf16[4,32,128]{2,1,0:T(8,128)(2,1)S(1)}, u32[]{:S(2)}, u32[]{:S(2)}) collective-permute-start(bf16[4,32,128]{2,1,0:T(8,128)(2,1)S(1)} %get-tuple-element.39), channel_id=1, source_target_pairs={{0,2},{1,3},{2,0},{3,1},{4,6},{5,7},{6,4},{7,5},{8,10},{9,11},{10,... | collective-permute-start | bytes 98312 | tf_op jit(solution)/shard_map/ppermute | solution.py:27
  7.3 4.3 %collective-permute-start.1 = (bf16[4,64,128]{2,1,0:T(8,128)(2,1)S(1)}, bf16[4,64,128]{2,1,0:T(8,128)(2,1)S(1)}, u32[]{:S(2)}, u32[]{:S(2)}) collective-permute-start(bf16[4,64,128]{2,1,0:T(8,128)(2,1)S(1)} %constant_dynamic-update-slice_fusion.refs_0_), channel_id=1, source_target_pairs={{0,8},{4,12},{8,0},{12,4},{16,24},{20,28},{24,16},{28,20},{1,9},{5... | collective-permute-start | bytes 196616 | tf_op jit(solution)/shard_map/ppermute | solution.py:27
  8.9 4.8 %collective-permute-start.4 = (bf16[4,64,128]{2,1,0:T(8,128)(2,1)S(1)}, bf16[4,64,128]{2,1,0:T(8,128)(2,1)S(1)}, u32[]{:S(2)}, u32[]{:S(2)}) collective-permute-start(bf16[4,64,128]{2,1,0:T(8,128)(2,1)S(1)} %constant_dynamic-update-slice_fusion.refs_0_), channel_id=1, source_target_pairs={{0,4},{4,0},{8,12},{12,8},{16,20},{20,16},{24,28},{28,24},{1,5},{5... | collective-permute-start | bytes 196616 | tf_op jit(solution)/shard_map/ppermute | solution.py:27
  10.4 2.9 %collective-permute-start.5 = (bf16[8,32,128]{2,1,0:T(8,128)(2,1)S(1)}, bf16[8,32,128]{2,1,0:T(8,128)(2,1)S(1)}, u32[]{:S(2)}, u32[]{:S(2)}) collective-permute-start(bf16[8,32,128]{2,1,0:T(8,128)(2,1)S(1)} %constant_dynamic-update-slice_fusion.2.even_ref), channel_id=1, source_target_pairs={{0,1},{1,0},{2,3},{3,2},{4,5},{5,4},{6,7},{7,6},{8,9},{9,8},{10,11... | collective-permute-start | bytes 196616 | tf_op jit(solution)/shard_map/ppermute | solution.py:27
  11.6 4.3 %collective-permute-start.3 = (bf16[4,64,128]{2,1,0:T(8,128)(2,1)S(1)}, bf16[4,64,128]{2,1,0:T(8,128)(2,1)S(1)}, u32[]{:S(2)}, u32[]{:S(2)}) collective-permute-start(bf16[4,64,128]{2,1,0:T(8,128)(2,1)S(1)} %collective-permute-done.1.refs_1_), channel_id=1, source_target_pairs={{0,4},{4,0},{8,12},{12,8},{16,20},{20,16},{24,28},{28,24},{1,5},{5... | collective-permute-start | bytes 196616 | tf_op jit(solution)/shard_map/ppermute | solution.py:27
  16.9 1.4 %collective-permute-start.6 = (f32[2,128,128]{2,1,0:T(8,128)S(1)}, f32[2,128,128]{2,1,0:T(8,128)S(1)}, u32[]{:S(2)}, u32[]{:S(2)}) collective-permute-start(f32[2,128,128]{2,1,0:T(8,128)S(1)} %get-tuple-element.55), channel_id=1, source_target_pairs={{0,1},{1,0},{2,3},{3,2},{4,5},{5,4},{6,7},{7,6},{8,9},{9,8},{10,11... | collective-permute-start | bytes 393224 | tf_op jit(solution)/shard_map/ppermute | solution.py:27
  18.4 6.4 %collective-permute-start.10 = (f32[2,4,32,128]{3,2,1,0:T(8,128)S(1)}, f32[2,4,32,128]{3,2,1,0:T(8,128)S(1)}, u32[]{:S(2)}, u32[]{:S(2)}) collective-permute-start(f32[2,4,32,128]{3,2,1,0:T(8,128)S(1)} %get-tuple-element.61), channel_id=1, source_target_pairs={{0,1},{1,0},{2,3},{3,2},{4,5},{5,4},{6,7},{7,6},{8,9},{9,8},{10,11... | collective-permute-start | bytes 393224 | tf_op jit(solution)/shard_map/ppermute | solution.py:27
  18.6 4.8 %collective-permute-start.7 = (bf16[128,128]{1,0:T(8,128)(2,1)S(1)}, bf16[128,128]{1,0:T(8,128)(2,1)S(1)}, u32[]{:S(2)}, u32[]{:S(2)}) collective-permute-start(bf16[128,128]{1,0:T(8,128)(2,1)S(1)} %get-tuple-element.59), channel_id=1, source_target_pairs={{0,6},{1,7},{2,4},{3,5},{4,2},{5,3},{6,0},{7,1},{8,14},{9,15},{10,... | collective-permute-start | bytes 98312 | tf_op jit(solution)/shard_map/ppermute | solution.py:33
  21.3 3.4 %collective-permute-start.8 = (bf16[128,128]{1,0:T(8,128)(2,1)S(1)}, bf16[128,128]{1,0:T(8,128)(2,1)S(1)}, u32[]{:S(2)}, u32[]{:S(2)}) collective-permute-start(bf16[128,128]{1,0:T(8,128)(2,1)S(1)} %get-tuple-element.60.d_ref), channel_id=1, source_target_pairs={{0,5},{1,4},{2,7},{3,6},{4,1},{5,0},{6,3},{7,2},{8,13},{9,12},{10,... | collective-permute-start | bytes 98312 | tf_op jit(solution)/shard_map/ppermute | solution.py:33
  21.4 3.3 %collective-permute-start.9 = (bf16[128,128]{1,0:T(8,128)(2,1)S(1)}, bf16[128,128]{1,0:T(8,128)(2,1)S(1)}, u32[]{:S(2)}, u32[]{:S(2)}) collective-permute-start(bf16[128,128]{1,0:T(8,128)(2,1)S(1)} %get-tuple-element.59), channel_id=1, source_target_pairs={{0,3},{1,2},{2,1},{3,0},{4,7},{5,6},{6,5},{7,4},{8,11},{9,10},{10,... | collective-permute-start | bytes 98312 | tf_op jit(solution)/shard_map/ppermute | solution.py:33
  24.8 4.3 %collective-permute-start.12 = (bf16[128,128]{1,0:T(8,128)(2,1)S(1)}, bf16[128,128]{1,0:T(8,128)(2,1)S(1)}, u32[]{:S(2)}, u32[]{:S(2)}) collective-permute-start(bf16[128,128]{1,0:T(8,128)(2,1)S(1)} %add_four.1), channel_id=1, source_target_pairs={{0,17},{1,16},{2,19},{3,18},{4,21},{5,20},{6,23},{7,22},{8,25},{9,... | collective-permute-start | bytes 98312 | tf_op jit(solution)/shard_map/ppermute | solution.py:33
  27.4 5.0 %collective-permute-start.11 = (bf16[1,4,32,128]{3,2,1,0:T(8,128)(2,1)S(1)}, bf16[1,4,32,128]{3,2,1,0:T(8,128)(2,1)S(1)}, u32[]{:S(2)}, u32[]{:S(2)}) collective-permute-start(bf16[1,4,32,128]{3,2,1,0:T(8,128)(2,1)S(1)} %get-tuple-element.66), channel_id=1, source_target_pairs={{0,2},{1,3},{2,0},{3,1},{4,6},{5,7},{6,4},{7,5},{8,10},{9,11},{10,... | collective-permute-start | bytes 98312 | tf_op jit(solution)/shard_map/ppermute | solution.py:27
  29.1 4.9 %collective-permute-start.13 = (bf16[128,128]{1,0:T(8,128)(2,1)S(1)}, bf16[128,128]{1,0:T(8,128)(2,1)S(1)}, u32[]{:S(2)}, u32[]{:S(2)}) collective-permute-start(bf16[128,128]{1,0:T(8,128)(2,1)S(1)} %add_convert_fusion.own_ref), channel_id=1, source_target_pairs={{0,10},{1,11},{2,8},{3,9},{4,14},{5,15},{6,12},{7,13},{8,2},{9,3},... | collective-permute-start | bytes 98312 | tf_op jit(solution)/shard_map/ppermute | solution.py:33
  31.1 3.6 %collective-permute-start.14 = (bf16[128,128]{1,0:T(8,128)(2,1)S(1)}, bf16[128,128]{1,0:T(8,128)(2,1)S(1)}, u32[]{:S(2)}, u32[]{:S(2)}) collective-permute-start(bf16[128,128]{1,0:T(8,128)(2,1)S(1)} %add_convert_fusion.own_ref), channel_id=1, source_target_pairs={{0,9},{1,8},{2,11},{3,10},{4,13},{5,12},{6,15},{7,14},{8,1},{9,0},... | collective-permute-start | bytes 98312 | tf_op jit(solution)/shard_map/ppermute | solution.py:33
  31.2 3.5 %collective-permute-start.15 = (bf16[128,128]{1,0:T(8,128)(2,1)S(1)}, bf16[128,128]{1,0:T(8,128)(2,1)S(1)}, u32[]{:S(2)}, u32[]{:S(2)}) collective-permute-start(bf16[128,128]{1,0:T(8,128)(2,1)S(1)} %add_convert_fusion.own_ref), channel_id=1, source_target_pairs={{0,3},{1,2},{2,1},{3,0},{4,7},{5,6},{6,5},{7,4},{8,11},{9,10},{10,... | collective-permute-start | bytes 98312 | tf_op jit(solution)/shard_map/ppermute | solution.py:33
  34.7 1.5 %collective-permute-start.16 = (bf16[2,128,128]{2,1,0:T(8,128)(2,1)S(1)}, bf16[2,128,128]{2,1,0:T(8,128)(2,1)S(1)}, u32[]{:S(2)}, u32[]{:S(2)}) collective-permute-start(bf16[2,128,128]{2,1,0:T(8,128)(2,1)S(1)} %join_sums.1), channel_id=1, source_target_pairs={{0,1},{1,0},{2,3},{3,2},{4,5},{5,4},{6,7},{7,6},{8,9},{9,8},{10,11... | collective-permute-start | bytes 196616 | tf_op jit(solution)/shard_map/ppermute | solution.py:27
  (2 other events, 5.3 us)

commit v9 on v8

--- a/solution.py
+++ b/solution.py
@@ -530,7 +530,7 @@
     row_bits, col_bits = bits_of(n_row), bits_of(n_col)
     residues = mask_residue.shape[0]
 
-    steps = [row_bits[-1]] + row_bits[1:-1] + row_bits[:1]
+    steps = row_bits[1:-1] + [row_bits[-1]] + row_bits[:1]
     ch = w_a_lin.shape[1]
     held, own_slab, *staged = stage(lead(), grad_out, pair_slab, w_a_lin, w_a_gate, w_b_lin, w_b_gate)
     order = [0]

time: 37.1 us -> 36.9 us (level)
  waiting for transfers between devices: 7.93 us -> 7.07 us
  starting transfers between devices: 21.2 us -> 21.8 us
    ppermute x10, waiting for transfers between devices: 3.66 us -> 3.11 us  [swap(): return lax.ppermute(value, axis, [(d, d ^ bit) for d in range(size)])]
    ppermute x10, starting transfers between devices: 12.1 us -> 12.6 us  [swap(): return lax.ppermute(value, axis, [(d, d ^ bit) for d in range(size)])]
  transfers between devices with their start and end apart: 17 -> 17, of which waited for: 11 -> 10; matrix products, arithmetic and copies ran while one was open for 1% -> 1% of each run, Pallas kernels for 13% -> 13%
where the time goes in v9:
time: 36.9 us; the launch traced here: 36.7 us
  starting transfers between devices  21.8 us (59%)
  waiting for transfers between devices  7.07 us (19%)
  Pallas kernels  5.89 us (16%)
  between operations  0.89 us (2%)
  other arithmetic  0.8 us (2%)
    ppermute x10, starting transfers between devices, swap(): return lax.ppermute(value, axis, [(d, d ^ bit) for d in range(size)])  12.6 us
    ppermute x7, starting transfers between devices, swap_chips(): return lax.ppermute(value, ('row', 'col'), pairs)  9.25 us
    ppermute x7, waiting for transfers between devices, swap_chips(): return lax.ppermute(value, ('row', 'col'), pairs)  3.96 us
    ppermute x10, waiting for transfers between devices, swap(): return lax.ppermute(value, axis, [(d, d ^ bit) for d in range(size)])  3.11 us
    pallas_call x1, Pallas kernels, pair_out(): pl.pallas_call(pair_out_kernel, out_shape=jax.ShapeDtypeStruct((cols * ke...  1.22 us
    pallas_call x1, Pallas kernels, main_part(): pl.pallas_call(functools.partial(main_kernel, order, blocks), out_shape=(...  1.05 us
    pallas_call x1, Pallas kernels, first_sums(): pl.pallas_call(functools.partial(sums_kernel, len(grads)), out_shape=jax....  0.98 us
    pallas_call x1, Pallas kernels, first_totals(): pl.pallas_call(functools.partial(totals_kernel, order, len(grads)), out_s...  0.98 us
  transfers between devices with their start and end apart: 17, of which 10 were waited for; matrix products, arithmetic and copies ran while one was open for 1% of the time, Pallas kernels for 13%

profile of v9, /device:TPU:0, one launch (start us, length us, event | category | flops | bytes accessed | tf_op | source)
XLA Modules:
  0.0 36.7 jit_solution(7928230690600593149)
XLA Ops:
  0.7 3.1 %collective-permute-start = (bf16[2,64,128]{2,1,0:T(8,128)(2,1)}, bf16[2,64,128]{2,1,0:T(8,128)(2,1)S(1)}, u32[]{:S(2)}, u32[]{:S(2)}) collective-permute-start(bf16[2,64,128]{2,1,0:T(8,128)(2,1)} %refs_0_.1), channel_id=1, source_target_pairs={{0,8},{4,12},{8,0},{12,4},{16,24},{20,28},{24,16},{28,20},{1,9},{5... | collective-permute-start | bytes 98312 | tf_op jit(solution)/shard_map/ppermute | solution.py:27
  3.9 1.6 %collective-permute-start.2 = (bf16[4,32,128]{2,1,0:T(8,128)(2,1)S(1)}, bf16[4,32,128]{2,1,0:T(8,128)(2,1)S(1)}, u32[]{:S(2)}, u32[]{:S(2)}) collective-permute-start(bf16[4,32,128]{2,1,0:T(8,128)(2,1)S(1)} %get-tuple-element.39), channel_id=1, source_target_pairs={{0,2},{1,3},{2,0},{3,1},{4,6},{5,7},{6,4},{7,5},{8,10},{9,11},{10,... | collective-permute-start | bytes 98312 | tf_op jit(solution)/shard_map/ppermute | solution.py:27
  5.9 3.1 %collective-permute-start.1 = (bf16[4,64,128]{2,1,0:T(8,128)(2,1)S(1)}, bf16[4,64,128]{2,1,0:T(8,128)(2,1)S(1)}, u32[]{:S(2)}, u32[]{:S(2)}) collective-permute-start(bf16[4,64,128]{2,1,0:T(8,128)(2,1)S(1)} %constant_dynamic-update-slice_fusion.refs_0_), channel_id=1, source_target_pairs={{0,16},{4,20},{8,24},{12,28},{16,0},{20,4},{24,8},{28,12},{1,17},{... | collective-permute-start | bytes 196616 | tf_op jit(solution)/shard_map/ppermute | solution.py:27
  9.0 1.5 %collective-permute-start.4 = (bf16[4,64,128]{2,1,0:T(8,128)(2,1)S(1)}, bf16[4,64,128]{2,1,0:T(8,128)(2,1)S(1)}, u32[]{:S(2)}, u32[]{:S(2)}) collective-permute-start(bf16[4,64,128]{2,1,0:T(8,128)(2,1)S(1)} %constant_dynamic-update-slice_fusion.refs_0_), channel_id=1, source_target_pairs={{0,4},{4,0},{8,12},{12,8},{16,20},{20,16},{24,28},{28,24},{1,5},{5... | collective-permute-start | bytes 196616 | tf_op jit(solution)/shard_map/ppermute | solution.py:27
  10.7 0.5 %pair_forward.1 = (bf16[64,32,128]{2,1,0:T(8,128)(2,1)S(1)}, f32[64,32,128]{2,1,0:T(8,128)S(1)}, f32[64,32,128]{2,1,0:T(8,128)S(1)}) custom-call(bf16[64,32,128]{2,1,0:T(8,128)(2,1)S(1)} %copy-done, bf16[128,128]{1,0:T(8,128)(2,1)S(1)} %get-tuple-element.37.w_lin_ref, bf16[128,128]{1,0:T(8,128)(2,1)S(1)} %get-tuple-element.38.w_gate_ref, ...), custom_call_target="tpu_custom_call" | custom-call | flops 134217728 | bytes 3670016 | tf_op jit(solution)/shard_map/pair_forward/pallas_call | solution.py:125
  11.3 1.8 %collective-permute-start.3 = (bf16[4,64,128]{2,1,0:T(8,128)(2,1)S(1)}, bf16[4,64,128]{2,1,0:T(8,128)(2,1)S(1)}, u32[]{:S(2)}, u32[]{:S(2)}) collective-permute-start(bf16[4,64,128]{2,1,0:T(8,128)(2,1)S(1)} %collective-permute-done.1.refs_1_), channel_id=1, source_target_pairs={{0,4},{4,0},{8,12},{12,8},{16,20},{20,16},{24,28},{28,24},{1,5},{5... | collective-permute-start | bytes 196616 | tf_op jit(solution)/shard_map/ppermute | solution.py:27
  13.5 1.0 %first_totals_over_i.1.total_ref = f32[64,32,128]{2,1,0:T(8,128)S(1)} custom-call(bf16[4,64,128]{2,1,0:T(8,128)(2,1)S(1)} %constant_dynamic-update-slice_fusion.refs_0_, bf16[4,64,128]{2,1,0:T(8,128)(2,1)S(1)} %collective-permute-done.1.refs_1_, bf16[4,64,128]{2,1,0:T(8,128)(2,1)S(1)} %collective-permute-done.4.refs_2_, ...), custom_call_target="tpu_custom_call" | custom-call | flops 6291456 | bytes 2097152 | tf_op jit(solution)/shard_map/first_totals_over_i/pallas_call | solution.py:276
  14.4 1.0 %first_sums_over_j.1.first_sums_ref = f32[12,32,128]{2,1,0:T(8,128)S(1)} custom-call(bf16[4,64,128]{2,1,0:T(8,128)(2,1)S(1)} %constant_dynamic-update-slice_fusion.refs_0_, bf16[4,64,128]{2,1,0:T(8,128)(2,1)S(1)} %collective-permute-done.1.refs_1_, bf16[4,64,128]{2,1,0:T(8,128)(2,1)S(1)} %collective-permute-done.4.refs_2_, ...), custom_call_target="tpu_custom_call" | custom-call | flops 6291456 | bytes 2097152 | tf_op jit(solution)/shard_map/first_sums_over_j/pallas_call | solution.py:242
  15.9 1.1 %last_rows.1 = (bf16[64,32,128]{2,1,0:T(8,128)(2,1)S(1)}, bf16[64,32,128]{2,1,0:T(8,128)(2,1)S(1)}, f32[2,4,32,128]{3,2,1,0:T(8,128)S(1)}, f32[2,4,32,128]{3,2,1...) custom-call(bf16[4,64,128]{2,1,0:T(8,128)(2,1)S(1)} %collective-permute-done.3.grad_ref, ...), custom_call_target="tpu_custom_call" | custom-call | flops 268435456 | bytes 4194304 | tf_op jit(solution)/shard_map/last_rows/pallas_call | solution.py:373
  17.0 1.3 %collective-permute-done.6 = f32[2,128,128]{2,1,0:T(8,128)S(1)} collective-permute-done((f32[2,128,128]{2,1,0:T(8,128)S(1)}, f32[2,128,128]{2,1,0:T(8,128)S(1)}, u32[]{:S(2)}, u32[]{:S(2)}) %collective-permute-start.6) | collective-permute-done | bytes 131104 | tf_op jit(solution)/shard_map/ppermute | solution.py:27
  18.6 2.5 %collective-permute-start.7 = (bf16[128,128]{1,0:T(8,128)(2,1)S(1)}, bf16[128,128]{1,0:T(8,128)(2,1)S(1)}, u32[]{:S(2)}, u32[]{:S(2)}) collective-permute-start(bf16[128,128]{1,0:T(8,128)(2,1)S(1)} %get-tuple-element.59), channel_id=1, source_target_pairs={{0,6},{1,7},{2,4},{3,5},{4,2},{5,3},{6,0},{7,1},{8,14},{9,15},{10,... | collective-permute-start | bytes 98312 | tf_op jit(solution)/shard_map/ppermute | solution.py:33
  21.2 0.6 %collective-permute-start.9 = (bf16[128,128]{1,0:T(8,128)(2,1)S(1)}, bf16[128,128]{1,0:T(8,128)(2,1)S(1)}, u32[]{:S(2)}, u32[]{:S(2)}) collective-permute-start(bf16[128,128]{1,0:T(8,128)(2,1)S(1)} %get-tuple-element.59), channel_id=1, source_target_pairs={{0,3},{1,2},{2,1},{3,0},{4,7},{5,6},{6,5},{7,4},{8,11},{9,10},{10,... | collective-permute-start | bytes 98312 | tf_op jit(solution)/shard_map/ppermute | solution.py:33
  21.8 1.2 %pair_input_grad.1 = bf16[2048,128]{1,0:T(8,128)(2,1)} custom-call(bf16[2048,128]{1,0:T(8,128)(2,1)S(1)} %bitcast.9, bf16[2048,128]{1,0:T(8,128)(2,1)S(1)} %bitcast.10, bf16[128,128]{1,0:T(8,128)(2,1)S(1)} %copy-done.1, bf16[128,128]{1,0:T(8,128)(2,1)S(1)} %copy-done.2), custom_call_target="tpu_custom_call" | custom-call | flops 134217728 | bytes 1572864 | tf_op jit(solution)/shard_map/pair_input_grad/pallas_call | solution.py:409
  23.4 1.1 %collective-permute-done.8.b_ref = bf16[128,128]{1,0:T(8,128)(2,1)S(1)} collective-permute-done((bf16[128,128]{1,0:T(8,128)(2,1)S(1)}, bf16[128,128]{1,0:T(8,128)(2,1)S(1)}, u32[]{:S(2)}, u32[]{:S(2)}) %collective-permute-start.8) | collective-permute-done | bytes 32800 | tf_op jit(solution)/shard_map/ppermute | solution.py:33
  24.6 2.8 %collective-permute-start.12 = (bf16[128,128]{1,0:T(8,128)(2,1)S(1)}, bf16[128,128]{1,0:T(8,128)(2,1)S(1)}, u32[]{:S(2)}, u32[]{:S(2)}) collective-permute-start(bf16[128,128]{1,0:T(8,128)(2,1)S(1)} %add_four.1), channel_id=1, source_target_pairs={{0,17},{1,16},{2,19},{3,18},{4,21},{5,20},{6,23},{7,22},{8,25},{9,... | collective-permute-start | bytes 98312 | tf_op jit(solution)/shard_map/ppermute | solution.py:33
  27.4 0.8 %collective-permute-start.11 = (bf16[1,4,32,128]{3,2,1,0:T(8,128)(2,1)S(1)}, bf16[1,4,32,128]{3,2,1,0:T(8,128)(2,1)S(1)}, u32[]{:S(2)}, u32[]{:S(2)}) collective-permute-start(bf16[1,4,32,128]{3,2,1,0:T(8,128)(2,1)S(1)} %get-tuple-element.66), channel_id=1, source_target_pairs={{0,2},{1,3},{2,0},{3,1},{4,6},{5,7},{6,4},{7,5},{8,10},{9,11},{10,... | collective-permute-start | bytes 98312 | tf_op jit(solution)/shard_map/ppermute | solution.py:27
  28.1 0.8 %collective-permute-done.12 = bf16[128,128]{1,0:T(8,128)(2,1)S(1)} collective-permute-done((bf16[128,128]{1,0:T(8,128)(2,1)S(1)}, bf16[128,128]{1,0:T(8,128)(2,1)S(1)}, u32[]{:S(2)}, u32[]{:S(2)}) %collective-permute-start.12) | collective-permute-done | bytes 32800 | tf_op jit(solution)/shard_map/ppermute | solution.py:33
  29.0 2.3 %collective-permute-start.13 = (bf16[128,128]{1,0:T(8,128)(2,1)S(1)}, bf16[128,128]{1,0:T(8,128)(2,1)S(1)}, u32[]{:S(2)}, u32[]{:S(2)}) collective-permute-start(bf16[128,128]{1,0:T(8,128)(2,1)S(1)} %add_convert_fusion.own_ref), channel_id=1, source_target_pairs={{0,10},{1,11},{2,8},{3,9},{4,14},{5,15},{6,12},{7,13},{8,2},{9,3},... | collective-permute-start | bytes 98312 | tf_op jit(solution)/shard_map/ppermute | solution.py:33
  31.3 1.0 %collective-permute-start.15 = (bf16[128,128]{1,0:T(8,128)(2,1)S(1)}, bf16[128,128]{1,0:T(8,128)(2,1)S(1)}, u32[]{:S(2)}, u32[]{:S(2)}) collective-permute-start(bf16[128,128]{1,0:T(8,128)(2,1)S(1)} %add_convert_fusion.own_ref), channel_id=1, source_target_pairs={{0,3},{1,2},{2,1},{3,0},{4,7},{5,6},{6,5},{7,4},{8,11},{9,10},{10,... | collective-permute-start | bytes 98312 | tf_op jit(solution)/shard_map/ppermute | solution.py:33
  32.2 0.8 %slab_input_grad.1 = bf16[4,32,128]{2,1,0:T(8,128)(2,1)} custom-call(f32[4,32,128]{2,1,0:T(8,128)S(1)} %bitcast.11, bf16[4,32,128]{2,1,0:T(8,128)(2,1)S(1)} %bitcast.12, f32[16,32,128]{2,1,0:T(8,128)S(1)} %get-tuple-element.51.slab_lin_ref.lin_ref, f32[16,32,128]{2,1,0:T(8,128)S(1)} %get-tuple-element.52.slab_gate_ref.gate_ref, ...), custom_call_target="tpu_custom_call" | custom-call | flops 8388608 | bytes 262144 | tf_op jit(solution)/shard_map/slab_input_grad/pallas_call | solution.py:515
  33.0 0.8 %collective-permute-done.13.diagonal_ref = bf16[128,128]{1,0:T(8,128)(2,1)S(1)} collective-permute-done((bf16[128,128]{1,0:T(8,128)(2,1)S(1)}, bf16[128,128]{1,0:T(8,128)(2,1)S(1)}, u32[]{:S(2)}, u32[]{:S(2)}) %collective-permute-start.13) | collective-permute-done | bytes 32800 | tf_op jit(solution)/shard_map/ppermute | solution.py:33
  33.8 0.8 %collective-permute-done.14.late_ref = bf16[128,128]{1,0:T(8,128)(2,1)S(1)} collective-permute-done((bf16[128,128]{1,0:T(8,128)(2,1)S(1)}, bf16[128,128]{1,0:T(8,128)(2,1)S(1)}, u32[]{:S(2)}, u32[]{:S(2)}) %collective-permute-start.14) | collective-permute-done | bytes 32800 | tf_op jit(solution)/shard_map/ppermute | solution.py:33
  35.1 0.9 %collective-permute-done.16 = bf16[2,128,128]{2,1,0:T(8,128)(2,1)S(1)} collective-permute-done((bf16[2,128,128]{2,1,0:T(8,128)(2,1)S(1)}, bf16[2,128,128]{2,1,0:T(8,128)(2,1)S(1)}, u32[]{:S(2)}, u32[]{:S(2)}) %collective-permute-start.16) | collective-permute-done | bytes 65568 | tf_op jit(solution)/shard_map/ppermute | solution.py:27
  36.0 0.7 %maximum_select_fusion = f32[4,128,128]{2,1,0:T(8,128)} fusion(f32[2,128,128]{2,1,0:T(8,128)S(1)} %convert_multiply_fusion, f32[2,128,128]{2,1,0:T(8,128)S(1)} %convert_multiply_fusion.1, pred[]{:T(512)S(6)} %eq.3), kind=kLoop, calls=%fused_computation | loop fusion | flops 196608 | bytes 524289 | tf_op jit(solution)/shard_map/jit(_where)/select_n | solution.py:596
  (54 shorter events, 3.0 us)
Async XLA Ops:
  0.6 3.2 %copy-start.6 = (bf16[2,64,128]{2,1,0:T(8,128)(2,1)S(1)}, bf16[2,64,128]{2,1,0:T(8,128)(2,1)}, u32[]{:S(2)}) copy-start(bf16[2,64,128]{2,1,0:T(8,128)(2,1)} %refs_0_.1) | copy-start | bytes 98308
  0.6 3.1 %copy-start.3 = (bf16[128,128]{1,0:T(8,128)(2,1)S(1)}, bf16[128,128]{1,0:T(8,128)(2,1)}, u32[]{:S(2)}) copy-start(bf16[128,128]{1,0:T(8,128)(2,1)} %w_lin_ref.3) | copy-start | bytes 98308
  0.7 3.1 %copy-start.4 = (bf16[128,128]{1,0:T(8,128)(2,1)S(1)}, bf16[128,128]{1,0:T(8,128)(2,1)}, u32[]{:S(2)}) copy-start(bf16[128,128]{1,0:T(8,128)(2,1)} %w_gate_ref.3) | copy-start | bytes 98308
  0.7 3.1 %copy-start.1 = (bf16[128,128]{1,0:T(8,128)(2,1)S(1)}, bf16[128,128]{1,0:T(8,128)(2,1)}, u32[]{:S(2)}) copy-start(bf16[128,128]{1,0:T(8,128)(2,1)} %w_lin_ref.2) | copy-start | bytes 98308
  0.7 3.1 %copy-start.2 = (bf16[128,128]{1,0:T(8,128)(2,1)S(1)}, bf16[128,128]{1,0:T(8,128)(2,1)}, u32[]{:S(2)}) copy-start(bf16[128,128]{1,0:T(8,128)(2,1)} %w_gate_ref.2) | copy-start | bytes 98308
  0.7 5.2 %collective-permute-start = (bf16[2,64,128]{2,1,0:T(8,128)(2,1)}, bf16[2,64,128]{2,1,0:T(8,128)(2,1)S(1)}, u32[]{:S(2)}, u32[]{:S(2)}) collective-permute-start(bf16[2,64,128]{2,1,0:T(8,128)(2,1)} %refs_0_.1), channel_id=1, source_target_pairs={{0,8},{4,12},{8,0},{12,4},{16,24},{20,28},{24,16},{28,20},{1,9},{5... | collective-permute-start | bytes 98312 | tf_op jit(solution)/shard_map/ppermute | solution.py:27
  3.8 6.9 %copy-start = (bf16[64,32,128]{2,1,0:T(8,128)(2,1)S(1)}, bf16[64,32,128]{2,1,0:T(8,128)(2,1)}, u32[]{:S(2)}) copy-start(bf16[64,32,128]{2,1,0:T(8,128)(2,1)} %pair_ref.3) | copy-start | bytes 1572868
  3.9 6.7 %collective-permute-start.2 = (bf16[4,32,128]{2,1,0:T(8,128)(2,1)S(1)}, bf16[4,32,128]{2,1,0:T(8,128)(2,1)S(1)}, u32[]{:S(2)}, u32[]{:S(2)}) collective-permute-start(bf16[4,32,128]{2,1,0:T(8,128)(2,1)S(1)} %get-tuple-element.39), channel_id=1, source_target_pairs={{0,2},{1,3},{2,0},{3,1},{4,6},{5,7},{6,4},{7,5},{8,10},{9,11},{10,... | collective-permute-start | bytes 98312 | tf_op jit(solution)/shard_map/ppermute | solution.py:27
  5.9 4.6 %copy-start.7 = (s32[256]{0:T(256)S(1)}, s32[256]{0:T(256)}, u32[]{:S(2)}) copy-start(s32[256]{0:T(256)} %param.17) | copy-start | bytes 3076
  5.9 5.4 %collective-permute-start.1 = (bf16[4,64,128]{2,1,0:T(8,128)(2,1)S(1)}, bf16[4,64,128]{2,1,0:T(8,128)(2,1)S(1)}, u32[]{:S(2)}, u32[]{:S(2)}) collective-permute-start(bf16[4,64,128]{2,1,0:T(8,128)(2,1)S(1)} %constant_dynamic-update-slice_fusion.refs_0_), channel_id=1, source_target_pairs={{0,16},{4,20},{8,24},{12,28},{16,0},{20,4},{24,8},{28,12},{1,17},{... | collective-permute-start | bytes 196616 | tf_op jit(solution)/shard_map/ppermute | solution.py:27
  9.0 4.5 %collective-permute-start.4 = (bf16[4,64,128]{2,1,0:T(8,128)(2,1)S(1)}, bf16[4,64,128]{2,1,0:T(8,128)(2,1)S(1)}, u32[]{:S(2)}, u32[]{:S(2)}) collective-permute-start(bf16[4,64,128]{2,1,0:T(8,128)(2,1)S(1)} %constant_dynamic-update-slice_fusion.refs_0_), channel_id=1, source_target_pairs={{0,4},{4,0},{8,12},{12,8},{16,20},{20,16},{24,28},{28,24},{1,5},{5... | collective-permute-start | bytes 196616 | tf_op jit(solution)/shard_map/ppermute | solution.py:27
  10.6 2.6 %collective-permute-start.5 = (bf16[8,32,128]{2,1,0:T(8,128)(2,1)S(1)}, bf16[8,32,128]{2,1,0:T(8,128)(2,1)S(1)}, u32[]{:S(2)}, u32[]{:S(2)}) collective-permute-start(bf16[8,32,128]{2,1,0:T(8,128)(2,1)S(1)} %constant_dynamic-update-slice_fusion.2.even_ref), channel_id=1, source_target_pairs={{0,1},{1,0},{2,3},{3,2},{4,5},{5,4},{6,7},{7,6},{8,9},{9,8},{10,11... | collective-permute-start | bytes 196616 | tf_op jit(solution)/shard_map/ppermute | solution.py:27
  11.3 4.5 %collective-permute-start.3 = (bf16[4,64,128]{2,1,0:T(8,128)(2,1)S(1)}, bf16[4,64,128]{2,1,0:T(8,128)(2,1)S(1)}, u32[]{:S(2)}, u32[]{:S(2)}) collective-permute-start(bf16[4,64,128]{2,1,0:T(8,128)(2,1)S(1)} %collective-permute-done.1.refs_1_), channel_id=1, source_target_pairs={{0,4},{4,0},{8,12},{12,8},{16,20},{20,16},{24,28},{28,24},{1,5},{5... | collective-permute-start | bytes 196616 | tf_op jit(solution)/shard_map/ppermute | solution.py:27
  16.9 1.4 %collective-permute-start.6 = (f32[2,128,128]{2,1,0:T(8,128)S(1)}, f32[2,128,128]{2,1,0:T(8,128)S(1)}, u32[]{:S(2)}, u32[]{:S(2)}) collective-permute-start(f32[2,128,128]{2,1,0:T(8,128)S(1)} %get-tuple-element.55), channel_id=1, source_target_pairs={{0,1},{1,0},{2,3},{3,2},{4,5},{5,4},{6,7},{7,6},{8,9},{9,8},{10,11... | collective-permute-start | bytes 393224 | tf_op jit(solution)/shard_map/ppermute | solution.py:27
  18.4 6.2 %collective-permute-start.10 = (f32[2,4,32,128]{3,2,1,0:T(8,128)S(1)}, f32[2,4,32,128]{3,2,1,0:T(8,128)S(1)}, u32[]{:S(2)}, u32[]{:S(2)}) collective-permute-start(f32[2,4,32,128]{3,2,1,0:T(8,128)S(1)} %get-tuple-element.61), channel_id=1, source_target_pairs={{0,1},{1,0},{2,3},{3,2},{4,5},{5,4},{6,7},{7,6},{8,9},{9,8},{10,11... | collective-permute-start | bytes 393224 | tf_op jit(solution)/shard_map/ppermute | solution.py:27
  18.6 4.8 %collective-permute-start.7 = (bf16[128,128]{1,0:T(8,128)(2,1)S(1)}, bf16[128,128]{1,0:T(8,128)(2,1)S(1)}, u32[]{:S(2)}, u32[]{:S(2)}) collective-permute-start(bf16[128,128]{1,0:T(8,128)(2,1)S(1)} %get-tuple-element.59), channel_id=1, source_target_pairs={{0,6},{1,7},{2,4},{3,5},{4,2},{5,3},{6,0},{7,1},{8,14},{9,15},{10,... | collective-permute-start | bytes 98312 | tf_op jit(solution)/shard_map/ppermute | solution.py:33
  21.0 3.4 %collective-permute-start.8 = (bf16[128,128]{1,0:T(8,128)(2,1)S(1)}, bf16[128,128]{1,0:T(8,128)(2,1)S(1)}, u32[]{:S(2)}, u32[]{:S(2)}) collective-permute-start(bf16[128,128]{1,0:T(8,128)(2,1)S(1)} %get-tuple-element.60.d_ref), channel_id=1, source_target_pairs={{0,5},{1,4},{2,7},{3,6},{4,1},{5,0},{6,3},{7,2},{8,13},{9,12},{10,... | collective-permute-start | bytes 98312 | tf_op jit(solution)/shard_map/ppermute | solution.py:33
  21.2 3.3 %collective-permute-start.9 = (bf16[128,128]{1,0:T(8,128)(2,1)S(1)}, bf16[128,128]{1,0:T(8,128)(2,1)S(1)}, u32[]{:S(2)}, u32[]{:S(2)}) collective-permute-start(bf16[128,128]{1,0:T(8,128)(2,1)S(1)} %get-tuple-element.59), channel_id=1, source_target_pairs={{0,3},{1,2},{2,1},{3,0},{4,7},{5,6},{6,5},{7,4},{8,11},{9,10},{10,... | collective-permute-start | bytes 98312 | tf_op jit(solution)/shard_map/ppermute | solution.py:33
  24.6 4.4 %collective-permute-start.12 = (bf16[128,128]{1,0:T(8,128)(2,1)S(1)}, bf16[128,128]{1,0:T(8,128)(2,1)S(1)}, u32[]{:S(2)}, u32[]{:S(2)}) collective-permute-start(bf16[128,128]{1,0:T(8,128)(2,1)S(1)} %add_four.1), channel_id=1, source_target_pairs={{0,17},{1,16},{2,19},{3,18},{4,21},{5,20},{6,23},{7,22},{8,25},{9,... | collective-permute-start | bytes 98312 | tf_op jit(solution)/shard_map/ppermute | solution.py:33
  27.4 4.9 %collective-permute-start.11 = (bf16[1,4,32,128]{3,2,1,0:T(8,128)(2,1)S(1)}, bf16[1,4,32,128]{3,2,1,0:T(8,128)(2,1)S(1)}, u32[]{:S(2)}, u32[]{:S(2)}) collective-permute-start(bf16[1,4,32,128]{3,2,1,0:T(8,128)(2,1)S(1)} %get-tuple-element.66), channel_id=1, source_target_pairs={{0,2},{1,3},{2,0},{3,1},{4,6},{5,7},{6,4},{7,5},{8,10},{9,11},{10,... | collective-permute-start | bytes 98312 | tf_op jit(solution)/shard_map/ppermute | solution.py:27
  29.0 4.9 %collective-permute-start.13 = (bf16[128,128]{1,0:T(8,128)(2,1)S(1)}, bf16[128,128]{1,0:T(8,128)(2,1)S(1)}, u32[]{:S(2)}, u32[]{:S(2)}) collective-permute-start(bf16[128,128]{1,0:T(8,128)(2,1)S(1)} %add_convert_fusion.own_ref), channel_id=1, source_target_pairs={{0,10},{1,11},{2,8},{3,9},{4,14},{5,15},{6,12},{7,13},{8,2},{9,3},... | collective-permute-start | bytes 98312 | tf_op jit(solution)/shard_map/ppermute | solution.py:33
  31.3 3.4 %collective-permute-start.14 = (bf16[128,128]{1,0:T(8,128)(2,1)S(1)}, bf16[128,128]{1,0:T(8,128)(2,1)S(1)}, u32[]{:S(2)}, u32[]{:S(2)}) collective-permute-start(bf16[128,128]{1,0:T(8,128)(2,1)S(1)} %add_convert_fusion.own_ref), channel_id=1, source_target_pairs={{0,9},{1,8},{2,11},{3,10},{4,13},{5,12},{6,15},{7,14},{8,1},{9,0},... | collective-permute-start | bytes 98312 | tf_op jit(solution)/shard_map/ppermute | solution.py:33
  31.3 3.4 %collective-permute-start.15 = (bf16[128,128]{1,0:T(8,128)(2,1)S(1)}, bf16[128,128]{1,0:T(8,128)(2,1)S(1)}, u32[]{:S(2)}, u32[]{:S(2)}) collective-permute-start(bf16[128,128]{1,0:T(8,128)(2,1)S(1)} %add_convert_fusion.own_ref), channel_id=1, source_target_pairs={{0,3},{1,2},{2,1},{3,0},{4,7},{5,6},{6,5},{7,4},{8,11},{9,10},{10,... | collective-permute-start | bytes 98312 | tf_op jit(solution)/shard_map/ppermute | solution.py:33
  34.7 1.3 %collective-permute-start.16 = (bf16[2,128,128]{2,1,0:T(8,128)(2,1)S(1)}, bf16[2,128,128]{2,1,0:T(8,128)(2,1)S(1)}, u32[]{:S(2)}, u32[]{:S(2)}) collective-permute-start(bf16[2,128,128]{2,1,0:T(8,128)(2,1)S(1)} %join_sums.1), channel_id=1, source_target_pairs={{0,1},{1,0},{2,3},{3,2},{4,5},{5,4},{6,7},{7,6},{8,9},{9,8},{10,11... | collective-permute-start | bytes 196616 | tf_op jit(solution)/shard_map/ppermute | solution.py:27
  (2 other events, 5.0 us)

commit v10 on v9

--- a/solution.py
+++ b/solution.py
@@ -560,7 +560,7 @@
     first = (first_totals(order, pieces, slab[1]), first_sums(pieces, value))
     kept = [0]
     for bit in reversed(col_bits[1:]):
-        kept = kept + [b ^ bit for b in kept]
+        kept = kept + [b ^ bit ^ 1 for b in kept]
     d_lin, d_gate, sum_keep, sum_send, w_keep, w_send = main_part(
         order, kept, got_both, first, pair_full, (value, lin, gate), slab
     )
@@ -586,7 +586,7 @@
             narrow, got, grad_pair = lax.optimization_barrier((narrow, got, grad_pair))
             for far in col_bits[1:]:
                 sums, moved = fold(sums, got)
-                got = swap(moved, "col", far)
+                got = swap_chips(moved, far)
         narrow = add_pair(narrow, swap_chips(narrow, bit))
     diagonal = swap_chips(narrow, pair_bit | late, 0)
     late_part, pair_part = swap_chips(narrow, late), swap_chips(narrow, pair_bit)

time: 36.9 us -> 36.9 us (level)
    ppermute x7 -> x8, starting transfers between devices: 9.25 us -> 10 us  [swap_chips(): return lax.ppermute(value, ('row', 'col'), pairs)]
    ppermute x10 -> x9, starting transfers between devices: 12.6 us -> 11.8 us  [swap(): return lax.ppermute(value, axis, [(d, d ^ bit) for d in range(size)])]
    ppermute x7 -> x8, waiting for transfers between devices: 3.96 us -> 3.93 us  [swap_chips(): return lax.ppermute(value, ('row', 'col'), pairs)]
    ppermute x10 -> x9, waiting for transfers between devices: 3.11 us -> 3.11 us  [swap(): return lax.ppermute(value, axis, [(d, d ^ bit) for d in range(size)])]
where the time goes in v10:
time: 36.9 us; the launch traced here: 36.7 us
  starting transfers between devices  21.9 us (59%)
  waiting for transfers between devices  7.04 us (19%)
  Pallas kernels  5.89 us (16%)
  between operations  0.89 us (2%)
  other arithmetic  0.8 us (2%)
    ppermute x9, starting transfers between devices, swap(): return lax.ppermute(value, axis, [(d, d ^ bit) for d in range(size)])  11.8 us
    ppermute x8, starting transfers between devices, swap_chips(): return lax.ppermute(value, ('row', 'col'), pairs)  10 us
    ppermute x8, waiting for transfers between devices, swap_chips(): return lax.ppermute(value, ('row', 'col'), pairs)  3.93 us
    ppermute x9, waiting for transfers between devices, swap(): return lax.ppermute(value, axis, [(d, d ^ bit) for d in range(size)])  3.11 us
    pallas_call x1, Pallas kernels, pair_out(): pl.pallas_call(pair_out_kernel, out_shape=jax.ShapeDtypeStruct((cols * ke...  1.22 us
    pallas_call x1, Pallas kernels, main_part(): pl.pallas_call(functools.partial(main_kernel, order, blocks), out_shape=(...  1.05 us
    pallas_call x1, Pallas kernels, first_sums(): pl.pallas_call(functools.partial(sums_kernel, len(grads)), out_shape=jax....  0.98 us
    pallas_call x1, Pallas kernels, first_totals(): pl.pallas_call(functools.partial(totals_kernel, order, len(grads)), out_s...  0.98 us
  transfers between devices with their start and end apart: 17, of which 10 were waited for; matrix products, arithmetic and copies ran while one was open for 1% of the time, Pallas kernels for 13%

profile of v10, /device:TPU:0, one launch (start us, length us, event | category | flops | bytes accessed | tf_op | source)
XLA Modules:
  0.0 36.7 jit_solution(11145240223662242681)
XLA Ops:
  0.7 3.1 %collective-permute-start = (bf16[2,64,128]{2,1,0:T(8,128)(2,1)}, bf16[2,64,128]{2,1,0:T(8,128)(2,1)S(1)}, u32[]{:S(2)}, u32[]{:S(2)}) collective-permute-start(bf16[2,64,128]{2,1,0:T(8,128)(2,1)} %refs_0_.1), channel_id=1, source_target_pairs={{0,8},{4,12},{8,0},{12,4},{16,24},{20,28},{24,16},{28,20},{1,9},{5... | collective-permute-start | bytes 98312 | tf_op jit(solution)/shard_map/ppermute | solution.py:27
  3.9 1.6 %collective-permute-start.2 = (bf16[4,32,128]{2,1,0:T(8,128)(2,1)S(1)}, bf16[4,32,128]{2,1,0:T(8,128)(2,1)S(1)}, u32[]{:S(2)}, u32[]{:S(2)}) collective-permute-start(bf16[4,32,128]{2,1,0:T(8,128)(2,1)S(1)} %get-tuple-element.39), channel_id=1, source_target_pairs={{0,2},{1,3},{2,0},{3,1},{4,6},{5,7},{6,4},{7,5},{8,10},{9,11},{10,... | collective-permute-start | bytes 98312 | tf_op jit(solution)/shard_map/ppermute | solution.py:27
  5.9 3.1 %collective-permute-start.1 = (bf16[4,64,128]{2,1,0:T(8,128)(2,1)S(1)}, bf16[4,64,128]{2,1,0:T(8,128)(2,1)S(1)}, u32[]{:S(2)}, u32[]{:S(2)}) collective-permute-start(bf16[4,64,128]{2,1,0:T(8,128)(2,1)S(1)} %constant_dynamic-update-slice_fusion.refs_0_), channel_id=1, source_target_pairs={{0,16},{4,20},{8,24},{12,28},{16,0},{20,4},{24,8},{28,12},{1,17},{... | collective-permute-start | bytes 196616 | tf_op jit(solution)/shard_map/ppermute | solution.py:27
  9.0 1.5 %collective-permute-start.4 = (bf16[4,64,128]{2,1,0:T(8,128)(2,1)S(1)}, bf16[4,64,128]{2,1,0:T(8,128)(2,1)S(1)}, u32[]{:S(2)}, u32[]{:S(2)}) collective-permute-start(bf16[4,64,128]{2,1,0:T(8,128)(2,1)S(1)} %constant_dynamic-update-slice_fusion.refs_0_), channel_id=1, source_target_pairs={{0,4},{4,0},{8,12},{12,8},{16,20},{20,16},{24,28},{28,24},{1,5},{5... | collective-permute-start | bytes 196616 | tf_op jit(solution)/shard_map/ppermute | solution.py:27
  10.7 0.5 %pair_forward.1 = (bf16[64,32,128]{2,1,0:T(8,128)(2,1)S(1)}, f32[64,32,128]{2,1,0:T(8,128)S(1)}, f32[64,32,128]{2,1,0:T(8,128)S(1)}) custom-call(bf16[64,32,128]{2,1,0:T(8,128)(2,1)S(1)} %copy-done, bf16[128,128]{1,0:T(8,128)(2,1)S(1)} %get-tuple-element.37.w_lin_ref, bf16[128,128]{1,0:T(8,128)(2,1)S(1)} %get-tuple-element.38.w_gate_ref, ...), custom_call_target="tpu_custom_call" | custom-call | flops 134217728 | bytes 3670016 | tf_op jit(solution)/shard_map/pair_forward/pallas_call | solution.py:125
  11.3 1.8 %collective-permute-start.3 = (bf16[4,64,128]{2,1,0:T(8,128)(2,1)S(1)}, bf16[4,64,128]{2,1,0:T(8,128)(2,1)S(1)}, u32[]{:S(2)}, u32[]{:S(2)}) collective-permute-start(bf16[4,64,128]{2,1,0:T(8,128)(2,1)S(1)} %collective-permute-done.1.refs_1_), channel_id=1, source_target_pairs={{0,4},{4,0},{8,12},{12,8},{16,20},{20,16},{24,28},{28,24},{1,5},{5... | collective-permute-start | bytes 196616 | tf_op jit(solution)/shard_map/ppermute | solution.py:27
  13.5 1.0 %first_totals_over_i.1.total_ref = f32[64,32,128]{2,1,0:T(8,128)S(1)} custom-call(bf16[4,64,128]{2,1,0:T(8,128)(2,1)S(1)} %constant_dynamic-update-slice_fusion.refs_0_, bf16[4,64,128]{2,1,0:T(8,128)(2,1)S(1)} %collective-permute-done.1.refs_1_, bf16[4,64,128]{2,1,0:T(8,128)(2,1)S(1)} %collective-permute-done.4.refs_2_, ...), custom_call_target="tpu_custom_call" | custom-call | flops 6291456 | bytes 2097152 | tf_op jit(solution)/shard_map/first_totals_over_i/pallas_call | solution.py:276
  14.4 1.0 %first_sums_over_j.1.first_sums_ref = f32[12,32,128]{2,1,0:T(8,128)S(1)} custom-call(bf16[4,64,128]{2,1,0:T(8,128)(2,1)S(1)} %constant_dynamic-update-slice_fusion.refs_0_, bf16[4,64,128]{2,1,0:T(8,128)(2,1)S(1)} %collective-permute-done.1.refs_1_, bf16[4,64,128]{2,1,0:T(8,128)(2,1)S(1)} %collective-permute-done.4.refs_2_, ...), custom_call_target="tpu_custom_call" | custom-call | flops 6291456 | bytes 2097152 | tf_op jit(solution)/shard_map/first_sums_over_j/pallas_call | solution.py:242
  15.9 1.1 %last_rows.1 = (bf16[64,32,128]{2,1,0:T(8,128)(2,1)S(1)}, bf16[64,32,128]{2,1,0:T(8,128)(2,1)S(1)}, f32[2,4,32,128]{3,2,1,0:T(8,128)S(1)}, f32[2,4,32,128]{3,2,1...) custom-call(bf16[4,64,128]{2,1,0:T(8,128)(2,1)S(1)} %collective-permute-done.3.grad_ref, ...), custom_call_target="tpu_custom_call" | custom-call | flops 268435456 | bytes 4194304 | tf_op jit(solution)/shard_map/last_rows/pallas_call | solution.py:373
  17.0 1.3 %collective-permute-done.6 = f32[2,128,128]{2,1,0:T(8,128)S(1)} collective-permute-done((f32[2,128,128]{2,1,0:T(8,128)S(1)}, f32[2,128,128]{2,1,0:T(8,128)S(1)}, u32[]{:S(2)}, u32[]{:S(2)}) %collective-permute-start.6) | collective-permute-done | bytes 131104 | tf_op jit(solution)/shard_map/ppermute | solution.py:27
  18.6 2.5 %collective-permute-start.7 = (bf16[128,128]{1,0:T(8,128)(2,1)S(1)}, bf16[128,128]{1,0:T(8,128)(2,1)S(1)}, u32[]{:S(2)}, u32[]{:S(2)}) collective-permute-start(bf16[128,128]{1,0:T(8,128)(2,1)S(1)} %get-tuple-element.59), channel_id=1, source_target_pairs={{0,6},{1,7},{2,4},{3,5},{4,2},{5,3},{6,0},{7,1},{8,14},{9,15},{10,... | collective-permute-start | bytes 98312 | tf_op jit(solution)/shard_map/ppermute | solution.py:33
  21.2 0.6 %collective-permute-start.9 = (bf16[128,128]{1,0:T(8,128)(2,1)S(1)}, bf16[128,128]{1,0:T(8,128)(2,1)S(1)}, u32[]{:S(2)}, u32[]{:S(2)}) collective-permute-start(bf16[128,128]{1,0:T(8,128)(2,1)S(1)} %get-tuple-element.59), channel_id=1, source_target_pairs={{0,3},{1,2},{2,1},{3,0},{4,7},{5,6},{6,5},{7,4},{8,11},{9,10},{10,... | collective-permute-start | bytes 98312 | tf_op jit(solution)/shard_map/ppermute | solution.py:33
  21.8 1.2 %pair_input_grad.1 = bf16[2048,128]{1,0:T(8,128)(2,1)} custom-call(bf16[2048,128]{1,0:T(8,128)(2,1)S(1)} %bitcast.9, bf16[2048,128]{1,0:T(8,128)(2,1)S(1)} %bitcast.10, bf16[128,128]{1,0:T(8,128)(2,1)S(1)} %copy-done.1, bf16[128,128]{1,0:T(8,128)(2,1)S(1)} %copy-done.2), custom_call_target="tpu_custom_call" | custom-call | flops 134217728 | bytes 1572864 | tf_op jit(solution)/shard_map/pair_input_grad/pallas_call | solution.py:409
  23.4 1.1 %collective-permute-done.8.b_ref = bf16[128,128]{1,0:T(8,128)(2,1)S(1)} collective-permute-done((bf16[128,128]{1,0:T(8,128)(2,1)S(1)}, bf16[128,128]{1,0:T(8,128)(2,1)S(1)}, u32[]{:S(2)}, u32[]{:S(2)}) %collective-permute-start.8) | collective-permute-done | bytes 32800 | tf_op jit(solution)/shard_map/ppermute | solution.py:33
  24.6 2.8 %collective-permute-start.12 = (bf16[128,128]{1,0:T(8,128)(2,1)S(1)}, bf16[128,128]{1,0:T(8,128)(2,1)S(1)}, u32[]{:S(2)}, u32[]{:S(2)}) collective-permute-start(bf16[128,128]{1,0:T(8,128)(2,1)S(1)} %add_four.1), channel_id=1, source_target_pairs={{0,17},{1,16},{2,19},{3,18},{4,21},{5,20},{6,23},{7,22},{8,25},{9,... | collective-permute-start | bytes 98312 | tf_op jit(solution)/shard_map/ppermute | solution.py:33
  27.4 0.8 %collective-permute-start.11 = (bf16[1,4,32,128]{3,2,1,0:T(8,128)(2,1)S(1)}, bf16[1,4,32,128]{3,2,1,0:T(8,128)(2,1)S(1)}, u32[]{:S(2)}, u32[]{:S(2)}) collective-permute-start(bf16[1,4,32,128]{3,2,1,0:T(8,128)(2,1)S(1)} %get-tuple-element.66), channel_id=1, source_target_pairs={{0,3},{1,2},{2,1},{3,0},{4,7},{5,6},{6,5},{7,4},{8,11},{9,10},{10,... | collective-permute-start | bytes 98312 | tf_op jit(solution)/shard_map/ppermute | solution.py:33
  28.2 0.8 %collective-permute-done.12 = bf16[128,128]{1,0:T(8,128)(2,1)S(1)} collective-permute-done((bf16[128,128]{1,0:T(8,128)(2,1)S(1)}, bf16[128,128]{1,0:T(8,128)(2,1)S(1)}, u32[]{:S(2)}, u32[]{:S(2)}) %collective-permute-start.12) | collective-permute-done | bytes 32800 | tf_op jit(solution)/shard_map/ppermute | solution.py:33
  29.0 2.3 %collective-permute-start.13 = (bf16[128,128]{1,0:T(8,128)(2,1)S(1)}, bf16[128,128]{1,0:T(8,128)(2,1)S(1)}, u32[]{:S(2)}, u32[]{:S(2)}) collective-permute-start(bf16[128,128]{1,0:T(8,128)(2,1)S(1)} %add_convert_fusion.own_ref), channel_id=1, source_target_pairs={{0,10},{1,11},{2,8},{3,9},{4,14},{5,15},{6,12},{7,13},{8,2},{9,3},... | collective-permute-start | bytes 98312 | tf_op jit(solution)/shard_map/ppermute | solution.py:33
  31.3 1.0 %collective-permute-start.15 = (bf16[128,128]{1,0:T(8,128)(2,1)S(1)}, bf16[128,128]{1,0:T(8,128)(2,1)S(1)}, u32[]{:S(2)}, u32[]{:S(2)}) collective-permute-start(bf16[128,128]{1,0:T(8,128)(2,1)S(1)} %add_convert_fusion.own_ref), channel_id=1, source_target_pairs={{0,3},{1,2},{2,1},{3,0},{4,7},{5,6},{6,5},{7,4},{8,11},{9,10},{10,... | collective-permute-start | bytes 98312 | tf_op jit(solution)/shard_map/ppermute | solution.py:33
  32.2 0.8 %slab_input_grad.1 = bf16[4,32,128]{2,1,0:T(8,128)(2,1)} custom-call(f32[4,32,128]{2,1,0:T(8,128)S(1)} %bitcast.11, bf16[4,32,128]{2,1,0:T(8,128)(2,1)S(1)} %bitcast.12, f32[16,32,128]{2,1,0:T(8,128)S(1)} %get-tuple-element.51.slab_lin_ref.lin_ref, f32[16,32,128]{2,1,0:T(8,128)S(1)} %get-tuple-element.52.slab_gate_ref.gate_ref, ...), custom_call_target="tpu_custom_call" | custom-call | flops 8388608 | bytes 262144 | tf_op jit(solution)/shard_map/slab_input_grad/pallas_call | solution.py:515
  33.0 0.8 %collective-permute-done.13.diagonal_ref = bf16[128,128]{1,0:T(8,128)(2,1)S(1)} collective-permute-done((bf16[128,128]{1,0:T(8,128)(2,1)S(1)}, bf16[128,128]{1,0:T(8,128)(2,1)S(1)}, u32[]{:S(2)}, u32[]{:S(2)}) %collective-permute-start.13) | collective-permute-done | bytes 32800 | tf_op jit(solution)/shard_map/ppermute | solution.py:33
  33.8 0.8 %collective-permute-done.14.late_ref = bf16[128,128]{1,0:T(8,128)(2,1)S(1)} collective-permute-done((bf16[128,128]{1,0:T(8,128)(2,1)S(1)}, bf16[128,128]{1,0:T(8,128)(2,1)S(1)}, u32[]{:S(2)}, u32[]{:S(2)}) %collective-permute-start.14) | collective-permute-done | bytes 32800 | tf_op jit(solution)/shard_map/ppermute | solution.py:33
  35.1 0.9 %collective-permute-done.16 = bf16[2,128,128]{2,1,0:T(8,128)(2,1)S(1)} collective-permute-done((bf16[2,128,128]{2,1,0:T(8,128)(2,1)S(1)}, bf16[2,128,128]{2,1,0:T(8,128)(2,1)S(1)}, u32[]{:S(2)}, u32[]{:S(2)}) %collective-permute-start.16) | collective-permute-done | bytes 65568 | tf_op jit(solution)/shard_map/ppermute | solution.py:27
  36.0 0.7 %maximum_select_fusion = f32[4,128,128]{2,1,0:T(8,128)} fusion(f32[2,128,128]{2,1,0:T(8,128)S(1)} %convert_multiply_fusion, f32[2,128,128]{2,1,0:T(8,128)S(1)} %convert_multiply_fusion.1, pred[]{:T(512)S(6)} %eq.3), kind=kLoop, calls=%fused_computation | loop fusion | flops 196608 | bytes 524289 | tf_op jit(solution)/shard_map/jit(_where)/select_n | solution.py:596
  (54 shorter events, 3.0 us)
Async XLA Ops:
  0.6 3.2 %copy-start.6 = (bf16[2,64,128]{2,1,0:T(8,128)(2,1)S(1)}, bf16[2,64,128]{2,1,0:T(8,128)(2,1)}, u32[]{:S(2)}) copy-start(bf16[2,64,128]{2,1,0:T(8,128)(2,1)} %refs_0_.1) | copy-start | bytes 98308
  0.6 3.1 %copy-start.3 = (bf16[128,128]{1,0:T(8,128)(2,1)S(1)}, bf16[128,128]{1,0:T(8,128)(2,1)}, u32[]{:S(2)}) copy-start(bf16[128,128]{1,0:T(8,128)(2,1)} %w_lin_ref.3) | copy-start | bytes 98308
  0.7 3.1 %copy-start.4 = (bf16[128,128]{1,0:T(8,128)(2,1)S(1)}, bf16[128,128]{1,0:T(8,128)(2,1)}, u32[]{:S(2)}) copy-start(bf16[128,128]{1,0:T(8,128)(2,1)} %w_gate_ref.3) | copy-start | bytes 98308
  0.7 3.1 %copy-start.1 = (bf16[128,128]{1,0:T(8,128)(2,1)S(1)}, bf16[128,128]{1,0:T(8,128)(2,1)}, u32[]{:S(2)}) copy-start(bf16[128,128]{1,0:T(8,128)(2,1)} %w_lin_ref.2) | copy-start | bytes 98308
  0.7 3.1 %copy-start.2 = (bf16[128,128]{1,0:T(8,128)(2,1)S(1)}, bf16[128,128]{1,0:T(8,128)(2,1)}, u32[]{:S(2)}) copy-start(bf16[128,128]{1,0:T(8,128)(2,1)} %w_gate_ref.2) | copy-start | bytes 98308
  0.7 5.2 %collective-permute-start = (bf16[2,64,128]{2,1,0:T(8,128)(2,1)}, bf16[2,64,128]{2,1,0:T(8,128)(2,1)S(1)}, u32[]{:S(2)}, u32[]{:S(2)}) collective-permute-start(bf16[2,64,128]{2,1,0:T(8,128)(2,1)} %refs_0_.1), channel_id=1, source_target_pairs={{0,8},{4,12},{8,0},{12,4},{16,24},{20,28},{24,16},{28,20},{1,9},{5... | collective-permute-start | bytes 98312 | tf_op jit(solution)/shard_map/ppermute | solution.py:27
  3.8 6.9 %copy-start = (bf16[64,32,128]{2,1,0:T(8,128)(2,1)S(1)}, bf16[64,32,128]{2,1,0:T(8,128)(2,1)}, u32[]{:S(2)}) copy-start(bf16[64,32,128]{2,1,0:T(8,128)(2,1)} %pair_ref.3) | copy-start | bytes 1572868
  3.9 6.7 %collective-permute-start.2 = (bf16[4,32,128]{2,1,0:T(8,128)(2,1)S(1)}, bf16[4,32,128]{2,1,0:T(8,128)(2,1)S(1)}, u32[]{:S(2)}, u32[]{:S(2)}) collective-permute-start(bf16[4,32,128]{2,1,0:T(8,128)(2,1)S(1)} %get-tuple-element.39), channel_id=1, source_target_pairs={{0,2},{1,3},{2,0},{3,1},{4,6},{5,7},{6,4},{7,5},{8,10},{9,11},{10,... | collective-permute-start | bytes 98312 | tf_op jit(solution)/shard_map/ppermute | solution.py:27
  5.9 4.6 %copy-start.7 = (s32[256]{0:T(256)S(1)}, s32[256]{0:T(256)}, u32[]{:S(2)}) copy-start(s32[256]{0:T(256)} %param.17) | copy-start | bytes 3076
  5.9 5.4 %collective-permute-start.1 = (bf16[4,64,128]{2,1,0:T(8,128)(2,1)S(1)}, bf16[4,64,128]{2,1,0:T(8,128)(2,1)S(1)}, u32[]{:S(2)}, u32[]{:S(2)}) collective-permute-start(bf16[4,64,128]{2,1,0:T(8,128)(2,1)S(1)} %constant_dynamic-update-slice_fusion.refs_0_), channel_id=1, source_target_pairs={{0,16},{4,20},{8,24},{12,28},{16,0},{20,4},{24,8},{28,12},{1,17},{... | collective-permute-start | bytes 196616 | tf_op jit(solution)/shard_map/ppermute | solution.py:27
  9.0 4.5 %collective-permute-start.4 = (bf16[4,64,128]{2,1,0:T(8,128)(2,1)S(1)}, bf16[4,64,128]{2,1,0:T(8,128)(2,1)S(1)}, u32[]{:S(2)}, u32[]{:S(2)}) collective-permute-start(bf16[4,64,128]{2,1,0:T(8,128)(2,1)S(1)} %constant_dynamic-update-slice_fusion.refs_0_), channel_id=1, source_target_pairs={{0,4},{4,0},{8,12},{12,8},{16,20},{20,16},{24,28},{28,24},{1,5},{5... | collective-permute-start | bytes 196616 | tf_op jit(solution)/shard_map/ppermute | solution.py:27
  10.6 2.6 %collective-permute-start.5 = (bf16[8,32,128]{2,1,0:T(8,128)(2,1)S(1)}, bf16[8,32,128]{2,1,0:T(8,128)(2,1)S(1)}, u32[]{:S(2)}, u32[]{:S(2)}) collective-permute-start(bf16[8,32,128]{2,1,0:T(8,128)(2,1)S(1)} %constant_dynamic-update-slice_fusion.2.even_ref), channel_id=1, source_target_pairs={{0,1},{1,0},{2,3},{3,2},{4,5},{5,4},{6,7},{7,6},{8,9},{9,8},{10,11... | collective-permute-start | bytes 196616 | tf_op jit(solution)/shard_map/ppermute | solution.py:27
  11.3 4.5 %collective-permute-start.3 = (bf16[4,64,128]{2,1,0:T(8,128)(2,1)S(1)}, bf16[4,64,128]{2,1,0:T(8,128)(2,1)S(1)}, u32[]{:S(2)}, u32[]{:S(2)}) collective-permute-start(bf16[4,64,128]{2,1,0:T(8,128)(2,1)S(1)} %collective-permute-done.1.refs_1_), channel_id=1, source_target_pairs={{0,4},{4,0},{8,12},{12,8},{16,20},{20,16},{24,28},{28,24},{1,5},{5... | collective-permute-start | bytes 196616 | tf_op jit(solution)/shard_map/ppermute | solution.py:27
  16.9 1.4 %collective-permute-start.6 = (f32[2,128,128]{2,1,0:T(8,128)S(1)}, f32[2,128,128]{2,1,0:T(8,128)S(1)}, u32[]{:S(2)}, u32[]{:S(2)}) collective-permute-start(f32[2,128,128]{2,1,0:T(8,128)S(1)} %get-tuple-element.55), channel_id=1, source_target_pairs={{0,1},{1,0},{2,3},{3,2},{4,5},{5,4},{6,7},{7,6},{8,9},{9,8},{10,11... | collective-permute-start | bytes 393224 | tf_op jit(solution)/shard_map/ppermute | solution.py:27
  18.4 6.2 %collective-permute-start.10 = (f32[2,4,32,128]{3,2,1,0:T(8,128)S(1)}, f32[2,4,32,128]{3,2,1,0:T(8,128)S(1)}, u32[]{:S(2)}, u32[]{:S(2)}) collective-permute-start(f32[2,4,32,128]{3,2,1,0:T(8,128)S(1)} %get-tuple-element.61), channel_id=1, source_target_pairs={{0,1},{1,0},{2,3},{3,2},{4,5},{5,4},{6,7},{7,6},{8,9},{9,8},{10,11... | collective-permute-start | bytes 393224 | tf_op jit(solution)/shard_map/ppermute | solution.py:27
  18.6 4.8 %collective-permute-start.7 = (bf16[128,128]{1,0:T(8,128)(2,1)S(1)}, bf16[128,128]{1,0:T(8,128)(2,1)S(1)}, u32[]{:S(2)}, u32[]{:S(2)}) collective-permute-start(bf16[128,128]{1,0:T(8,128)(2,1)S(1)} %get-tuple-element.59), channel_id=1, source_target_pairs={{0,6},{1,7},{2,4},{3,5},{4,2},{5,3},{6,0},{7,1},{8,14},{9,15},{10,... | collective-permute-start | bytes 98312 | tf_op jit(solution)/shard_map/ppermute | solution.py:33
  21.0 3.4 %collective-permute-start.8 = (bf16[128,128]{1,0:T(8,128)(2,1)S(1)}, bf16[128,128]{1,0:T(8,128)(2,1)S(1)}, u32[]{:S(2)}, u32[]{:S(2)}) collective-permute-start(bf16[128,128]{1,0:T(8,128)(2,1)S(1)} %get-tuple-element.60.d_ref), channel_id=1, source_target_pairs={{0,5},{1,4},{2,7},{3,6},{4,1},{5,0},{6,3},{7,2},{8,13},{9,12},{10,... | collective-permute-start | bytes 98312 | tf_op jit(solution)/shard_map/ppermute | solution.py:33
  21.2 3.3 %collective-permute-start.9 = (bf16[128,128]{1,0:T(8,128)(2,1)S(1)}, bf16[128,128]{1,0:T(8,128)(2,1)S(1)}, u32[]{:S(2)}, u32[]{:S(2)}) collective-permute-start(bf16[128,128]{1,0:T(8,128)(2,1)S(1)} %get-tuple-element.59), channel_id=1, source_target_pairs={{0,3},{1,2},{2,1},{3,0},{4,7},{5,6},{6,5},{7,4},{8,11},{9,10},{10,... | collective-permute-start | bytes 98312 | tf_op jit(solution)/shard_map/ppermute | solution.py:33
  24.6 4.4 %collective-permute-start.12 = (bf16[128,128]{1,0:T(8,128)(2,1)S(1)}, bf16[128,128]{1,0:T(8,128)(2,1)S(1)}, u32[]{:S(2)}, u32[]{:S(2)}) collective-permute-start(bf16[128,128]{1,0:T(8,128)(2,1)S(1)} %add_four.1), channel_id=1, source_target_pairs={{0,17},{1,16},{2,19},{3,18},{4,21},{5,20},{6,23},{7,22},{8,25},{9,... | collective-permute-start | bytes 98312 | tf_op jit(solution)/shard_map/ppermute | solution.py:33
  27.4 4.9 %collective-permute-start.11 = (bf16[1,4,32,128]{3,2,1,0:T(8,128)(2,1)S(1)}, bf16[1,4,32,128]{3,2,1,0:T(8,128)(2,1)S(1)}, u32[]{:S(2)}, u32[]{:S(2)}) collective-permute-start(bf16[1,4,32,128]{3,2,1,0:T(8,128)(2,1)S(1)} %get-tuple-element.66), channel_id=1, source_target_pairs={{0,3},{1,2},{2,1},{3,0},{4,7},{5,6},{6,5},{7,4},{8,11},{9,10},{10,... | collective-permute-start | bytes 98312 | tf_op jit(solution)/shard_map/ppermute | solution.py:33
  29.0 4.9 %collective-permute-start.13 = (bf16[128,128]{1,0:T(8,128)(2,1)S(1)}, bf16[128,128]{1,0:T(8,128)(2,1)S(1)}, u32[]{:S(2)}, u32[]{:S(2)}) collective-permute-start(bf16[128,128]{1,0:T(8,128)(2,1)S(1)} %add_convert_fusion.own_ref), channel_id=1, source_target_pairs={{0,10},{1,11},{2,8},{3,9},{4,14},{5,15},{6,12},{7,13},{8,2},{9,3},... | collective-permute-start | bytes 98312 | tf_op jit(solution)/shard_map/ppermute | solution.py:33
  31.3 3.4 %collective-permute-start.14 = (bf16[128,128]{1,0:T(8,128)(2,1)S(1)}, bf16[128,128]{1,0:T(8,128)(2,1)S(1)}, u32[]{:S(2)}, u32[]{:S(2)}) collective-permute-start(bf16[128,128]{1,0:T(8,128)(2,1)S(1)} %add_convert_fusion.own_ref), channel_id=1, source_target_pairs={{0,9},{1,8},{2,11},{3,10},{4,13},{5,12},{6,15},{7,14},{8,1},{9,0},... | collective-permute-start | bytes 98312 | tf_op jit(solution)/shard_map/ppermute | solution.py:33
  31.3 3.4 %collective-permute-start.15 = (bf16[128,128]{1,0:T(8,128)(2,1)S(1)}, bf16[128,128]{1,0:T(8,128)(2,1)S(1)}, u32[]{:S(2)}, u32[]{:S(2)}) collective-permute-start(bf16[128,128]{1,0:T(8,128)(2,1)S(1)} %add_convert_fusion.own_ref), channel_id=1, source_target_pairs={{0,3},{1,2},{2,1},{3,0},{4,7},{5,6},{6,5},{7,4},{8,11},{9,10},{10,... | collective-permute-start | bytes 98312 | tf_op jit(solution)/shard_map/ppermute | solution.py:33
  34.7 1.3 %collective-permute-start.16 = (bf16[2,128,128]{2,1,0:T(8,128)(2,1)S(1)}, bf16[2,128,128]{2,1,0:T(8,128)(2,1)S(1)}, u32[]{:S(2)}, u32[]{:S(2)}) collective-permute-start(bf16[2,128,128]{2,1,0:T(8,128)(2,1)S(1)} %join_sums.1), channel_id=1, source_target_pairs={{0,1},{1,0},{2,3},{3,2},{4,5},{5,4},{6,7},{7,6},{8,9},{9,8},{10,11... | collective-permute-start | bytes 196616 | tf_op jit(solution)/shard_map/ppermute | solution.py:27
  (2 other events, 5.0 us)

commit v11 on v10

--- a/solution.py
+++ b/solution.py
@@ -233,7 +233,7 @@
         add_sums(wide, count, j0, keys, values, sums_ref)
         return carry
 
-    lax.fori_loop(0, cols // J_STEP, step, 0, unroll=2)
+    lax.fori_loop(0, cols // J_STEP, step, 0, unroll=4)
 
 
 def first_sums(grads, value):
@@ -266,7 +266,7 @@
             total_ref[j0 + j] = totals[j]
         return carry
 
-    lax.fori_loop(0, cols // J_STEP, step, 0, unroll=2)
+    lax.fori_loop(0, cols // J_STEP, step, 0, unroll=4)
 
 
 def first_totals(order, grads, slab_value):

time: 36.9 us -> 36.9 us (level)
  no operation moved by 1% of the time
where the time goes in v11:
time: 36.9 us; the launch traced here: 36.7 us
  starting transfers between devices  21.9 us (59%)
  waiting for transfers between devices  7.12 us (19%)
  Pallas kernels  5.81 us (16%)
  between operations  0.89 us (2%)
  other arithmetic  0.8 us (2%)
    ppermute x9, starting transfers between devices, swap(): return lax.ppermute(value, axis, [(d, d ^ bit) for d in range(size)])  11.8 us
    ppermute x8, starting transfers between devices, swap_chips(): return lax.ppermute(value, ('row', 'col'), pairs)  10 us
    ppermute x8, waiting for transfers between devices, swap_chips(): return lax.ppermute(value, ('row', 'col'), pairs)  3.93 us
    ppermute x9, waiting for transfers between devices, swap(): return lax.ppermute(value, axis, [(d, d ^ bit) for d in range(size)])  3.19 us
    pallas_call x1, Pallas kernels, pair_out(): pl.pallas_call(pair_out_kernel, out_shape=jax.ShapeDtypeStruct((cols * ke...  1.22 us
    pallas_call x1, Pallas kernels, main_part(): pl.pallas_call(functools.partial(main_kernel, order, blocks), out_shape=(...  1.05 us
    pallas_call x1, Pallas kernels, first_sums(): pl.pallas_call(functools.partial(sums_kernel, len(grads)), out_shape=jax....  0.97 us
    pallas_call x1, Pallas kernels, first_totals(): pl.pallas_call(functools.partial(totals_kernel, order, len(grads)), out_s...  0.92 us
  transfers between devices with their start and end apart: 17, of which 10 were waited for; matrix products, arithmetic and copies ran while one was open for 1% of the time, Pallas kernels for 13%

profile of v11, /device:TPU:0, one launch (start us, length us, event | category | flops | bytes accessed | tf_op | source)
XLA Modules:
  0.0 36.7 jit_solution(2798447386476584302)
XLA Ops:
  0.7 3.1 %collective-permute-start = (bf16[2,64,128]{2,1,0:T(8,128)(2,1)}, bf16[2,64,128]{2,1,0:T(8,128)(2,1)S(1)}, u32[]{:S(2)}, u32[]{:S(2)}) collective-permute-start(bf16[2,64,128]{2,1,0:T(8,128)(2,1)} %refs_0_.1), channel_id=1, source_target_pairs={{0,8},{4,12},{8,0},{12,4},{16,24},{20,28},{24,16},{28,20},{1,9},{5... | collective-permute-start | bytes 98312 | tf_op jit(solution)/shard_map/ppermute | solution.py:27
  3.9 1.6 %collective-permute-start.2 = (bf16[4,32,128]{2,1,0:T(8,128)(2,1)S(1)}, bf16[4,32,128]{2,1,0:T(8,128)(2,1)S(1)}, u32[]{:S(2)}, u32[]{:S(2)}) collective-permute-start(bf16[4,32,128]{2,1,0:T(8,128)(2,1)S(1)} %get-tuple-element.39), channel_id=1, source_target_pairs={{0,2},{1,3},{2,0},{3,1},{4,6},{5,7},{6,4},{7,5},{8,10},{9,11},{10,... | collective-permute-start | bytes 98312 | tf_op jit(solution)/shard_map/ppermute | solution.py:27
  5.9 3.1 %collective-permute-start.1 = (bf16[4,64,128]{2,1,0:T(8,128)(2,1)S(1)}, bf16[4,64,128]{2,1,0:T(8,128)(2,1)S(1)}, u32[]{:S(2)}, u32[]{:S(2)}) collective-permute-start(bf16[4,64,128]{2,1,0:T(8,128)(2,1)S(1)} %constant_dynamic-update-slice_fusion.refs_0_), channel_id=1, source_target_pairs={{0,16},{4,20},{8,24},{12,28},{16,0},{20,4},{24,8},{28,12},{1,17},{... | collective-permute-start | bytes 196616 | tf_op jit(solution)/shard_map/ppermute | solution.py:27
  9.0 1.5 %collective-permute-start.4 = (bf16[4,64,128]{2,1,0:T(8,128)(2,1)S(1)}, bf16[4,64,128]{2,1,0:T(8,128)(2,1)S(1)}, u32[]{:S(2)}, u32[]{:S(2)}) collective-permute-start(bf16[4,64,128]{2,1,0:T(8,128)(2,1)S(1)} %constant_dynamic-update-slice_fusion.refs_0_), channel_id=1, source_target_pairs={{0,4},{4,0},{8,12},{12,8},{16,20},{20,16},{24,28},{28,24},{1,5},{5... | collective-permute-start | bytes 196616 | tf_op jit(solution)/shard_map/ppermute | solution.py:27
  10.7 0.5 %pair_forward.1 = (bf16[64,32,128]{2,1,0:T(8,128)(2,1)S(1)}, f32[64,32,128]{2,1,0:T(8,128)S(1)}, f32[64,32,128]{2,1,0:T(8,128)S(1)}) custom-call(bf16[64,32,128]{2,1,0:T(8,128)(2,1)S(1)} %copy-done, bf16[128,128]{1,0:T(8,128)(2,1)S(1)} %get-tuple-element.37.w_lin_ref, bf16[128,128]{1,0:T(8,128)(2,1)S(1)} %get-tuple-element.38.w_gate_ref, ...), custom_call_target="tpu_custom_call" | custom-call | flops 134217728 | bytes 3670016 | tf_op jit(solution)/shard_map/pair_forward/pallas_call | solution.py:125
  11.3 1.8 %collective-permute-start.3 = (bf16[4,64,128]{2,1,0:T(8,128)(2,1)S(1)}, bf16[4,64,128]{2,1,0:T(8,128)(2,1)S(1)}, u32[]{:S(2)}, u32[]{:S(2)}) collective-permute-start(bf16[4,64,128]{2,1,0:T(8,128)(2,1)S(1)} %collective-permute-done.1.refs_1_), channel_id=1, source_target_pairs={{0,4},{4,0},{8,12},{12,8},{16,20},{20,16},{24,28},{28,24},{1,5},{5... | collective-permute-start | bytes 196616 | tf_op jit(solution)/shard_map/ppermute | solution.py:27
  13.5 0.9 %first_totals_over_i.1.total_ref = f32[64,32,128]{2,1,0:T(8,128)S(1)} custom-call(bf16[4,64,128]{2,1,0:T(8,128)(2,1)S(1)} %constant_dynamic-update-slice_fusion.refs_0_, bf16[4,64,128]{2,1,0:T(8,128)(2,1)S(1)} %collective-permute-done.1.refs_1_, bf16[4,64,128]{2,1,0:T(8,128)(2,1)S(1)} %collective-permute-done.4.refs_2_, ...), custom_call_target="tpu_custom_call" | custom-call | flops 6291456 | bytes 2097152 | tf_op jit(solution)/shard_map/first_totals_over_i/pallas_call | solution.py:276
  14.4 1.0 %first_sums_over_j.1.first_sums_ref = f32[12,32,128]{2,1,0:T(8,128)S(1)} custom-call(bf16[4,64,128]{2,1,0:T(8,128)(2,1)S(1)} %constant_dynamic-update-slice_fusion.refs_0_, bf16[4,64,128]{2,1,0:T(8,128)(2,1)S(1)} %collective-permute-done.1.refs_1_, bf16[4,64,128]{2,1,0:T(8,128)(2,1)S(1)} %collective-permute-done.4.refs_2_, ...), custom_call_target="tpu_custom_call" | custom-call | flops 6291456 | bytes 2097152 | tf_op jit(solution)/shard_map/first_sums_over_j/pallas_call | solution.py:242
  15.9 1.1 %last_rows.1 = (bf16[64,32,128]{2,1,0:T(8,128)(2,1)S(1)}, bf16[64,32,128]{2,1,0:T(8,128)(2,1)S(1)}, f32[2,4,32,128]{3,2,1,0:T(8,128)S(1)}, f32[2,4,32,128]{3,2,1...) custom-call(bf16[4,64,128]{2,1,0:T(8,128)(2,1)S(1)} %collective-permute-done.3.grad_ref, ...), custom_call_target="tpu_custom_call" | custom-call | flops 268435456 | bytes 4194304 | tf_op jit(solution)/shard_map/last_rows/pallas_call | solution.py:373
  17.0 1.3 %collective-permute-done.6 = f32[2,128,128]{2,1,0:T(8,128)S(1)} collective-permute-done((f32[2,128,128]{2,1,0:T(8,128)S(1)}, f32[2,128,128]{2,1,0:T(8,128)S(1)}, u32[]{:S(2)}, u32[]{:S(2)}) %collective-permute-start.6) | collective-permute-done | bytes 131104 | tf_op jit(solution)/shard_map/ppermute | solution.py:27
  18.6 2.5 %collective-permute-start.7 = (bf16[128,128]{1,0:T(8,128)(2,1)S(1)}, bf16[128,128]{1,0:T(8,128)(2,1)S(1)}, u32[]{:S(2)}, u32[]{:S(2)}) collective-permute-start(bf16[128,128]{1,0:T(8,128)(2,1)S(1)} %get-tuple-element.59), channel_id=1, source_target_pairs={{0,6},{1,7},{2,4},{3,5},{4,2},{5,3},{6,0},{7,1},{8,14},{9,15},{10,... | collective-permute-start | bytes 98312 | tf_op jit(solution)/shard_map/ppermute | solution.py:33
  21.2 0.6 %collective-permute-start.9 = (bf16[128,128]{1,0:T(8,128)(2,1)S(1)}, bf16[128,128]{1,0:T(8,128)(2,1)S(1)}, u32[]{:S(2)}, u32[]{:S(2)}) collective-permute-start(bf16[128,128]{1,0:T(8,128)(2,1)S(1)} %get-tuple-element.59), channel_id=1, source_target_pairs={{0,3},{1,2},{2,1},{3,0},{4,7},{5,6},{6,5},{7,4},{8,11},{9,10},{10,... | collective-permute-start | bytes 98312 | tf_op jit(solution)/shard_map/ppermute | solution.py:33
  21.8 1.2 %pair_input_grad.1 = bf16[2048,128]{1,0:T(8,128)(2,1)} custom-call(bf16[2048,128]{1,0:T(8,128)(2,1)S(1)} %bitcast.9, bf16[2048,128]{1,0:T(8,128)(2,1)S(1)} %bitcast.10, bf16[128,128]{1,0:T(8,128)(2,1)S(1)} %copy-done.1, bf16[128,128]{1,0:T(8,128)(2,1)S(1)} %copy-done.2), custom_call_target="tpu_custom_call" | custom-call | flops 134217728 | bytes 1572864 | tf_op jit(solution)/shard_map/pair_input_grad/pallas_call | solution.py:409
  23.4 1.1 %collective-permute-done.8.b_ref = bf16[128,128]{1,0:T(8,128)(2,1)S(1)} collective-permute-done((bf16[128,128]{1,0:T(8,128)(2,1)S(1)}, bf16[128,128]{1,0:T(8,128)(2,1)S(1)}, u32[]{:S(2)}, u32[]{:S(2)}) %collective-permute-start.8) | collective-permute-done | bytes 32800 | tf_op jit(solution)/shard_map/ppermute | solution.py:33
  24.6 2.8 %collective-permute-start.12 = (bf16[128,128]{1,0:T(8,128)(2,1)S(1)}, bf16[128,128]{1,0:T(8,128)(2,1)S(1)}, u32[]{:S(2)}, u32[]{:S(2)}) collective-permute-start(bf16[128,128]{1,0:T(8,128)(2,1)S(1)} %add_four.1), channel_id=1, source_target_pairs={{0,17},{1,16},{2,19},{3,18},{4,21},{5,20},{6,23},{7,22},{8,25},{9,... | collective-permute-start | bytes 98312 | tf_op jit(solution)/shard_map/ppermute | solution.py:33
  27.4 0.8 %collective-permute-start.11 = (bf16[1,4,32,128]{3,2,1,0:T(8,128)(2,1)S(1)}, bf16[1,4,32,128]{3,2,1,0:T(8,128)(2,1)S(1)}, u32[]{:S(2)}, u32[]{:S(2)}) collective-permute-start(bf16[1,4,32,128]{3,2,1,0:T(8,128)(2,1)S(1)} %get-tuple-element.66), channel_id=1, source_target_pairs={{0,3},{1,2},{2,1},{3,0},{4,7},{5,6},{6,5},{7,4},{8,11},{9,10},{10,... | collective-permute-start | bytes 98312 | tf_op jit(solution)/shard_map/ppermute | solution.py:33
  28.2 0.8 %collective-permute-done.12 = bf16[128,128]{1,0:T(8,128)(2,1)S(1)} collective-permute-done((bf16[128,128]{1,0:T(8,128)(2,1)S(1)}, bf16[128,128]{1,0:T(8,128)(2,1)S(1)}, u32[]{:S(2)}, u32[]{:S(2)}) %collective-permute-start.12) | collective-permute-done | bytes 32800 | tf_op jit(solution)/shard_map/ppermute | solution.py:33
  29.0 2.3 %collective-permute-start.13 = (bf16[128,128]{1,0:T(8,128)(2,1)S(1)}, bf16[128,128]{1,0:T(8,128)(2,1)S(1)}, u32[]{:S(2)}, u32[]{:S(2)}) collective-permute-start(bf16[128,128]{1,0:T(8,128)(2,1)S(1)} %add_convert_fusion.own_ref), channel_id=1, source_target_pairs={{0,10},{1,11},{2,8},{3,9},{4,14},{5,15},{6,12},{7,13},{8,2},{9,3},... | collective-permute-start | bytes 98312 | tf_op jit(solution)/shard_map/ppermute | solution.py:33
  31.3 1.0 %collective-permute-start.15 = (bf16[128,128]{1,0:T(8,128)(2,1)S(1)}, bf16[128,128]{1,0:T(8,128)(2,1)S(1)}, u32[]{:S(2)}, u32[]{:S(2)}) collective-permute-start(bf16[128,128]{1,0:T(8,128)(2,1)S(1)} %add_convert_fusion.own_ref), channel_id=1, source_target_pairs={{0,3},{1,2},{2,1},{3,0},{4,7},{5,6},{6,5},{7,4},{8,11},{9,10},{10,... | collective-permute-start | bytes 98312 | tf_op jit(solution)/shard_map/ppermute | solution.py:33
  32.2 0.8 %slab_input_grad.1 = bf16[4,32,128]{2,1,0:T(8,128)(2,1)} custom-call(f32[4,32,128]{2,1,0:T(8,128)S(1)} %bitcast.11, bf16[4,32,128]{2,1,0:T(8,128)(2,1)S(1)} %bitcast.12, f32[16,32,128]{2,1,0:T(8,128)S(1)} %get-tuple-element.51.slab_lin_ref.lin_ref, f32[16,32,128]{2,1,0:T(8,128)S(1)} %get-tuple-element.52.slab_gate_ref.gate_ref, ...), custom_call_target="tpu_custom_call" | custom-call | flops 8388608 | bytes 262144 | tf_op jit(solution)/shard_map/slab_input_grad/pallas_call | solution.py:515
  33.0 0.8 %collective-permute-done.13.diagonal_ref = bf16[128,128]{1,0:T(8,128)(2,1)S(1)} collective-permute-done((bf16[128,128]{1,0:T(8,128)(2,1)S(1)}, bf16[128,128]{1,0:T(8,128)(2,1)S(1)}, u32[]{:S(2)}, u32[]{:S(2)}) %collective-permute-start.13) | collective-permute-done | bytes 32800 | tf_op jit(solution)/shard_map/ppermute | solution.py:33
  33.8 0.8 %collective-permute-done.14.late_ref = bf16[128,128]{1,0:T(8,128)(2,1)S(1)} collective-permute-done((bf16[128,128]{1,0:T(8,128)(2,1)S(1)}, bf16[128,128]{1,0:T(8,128)(2,1)S(1)}, u32[]{:S(2)}, u32[]{:S(2)}) %collective-permute-start.14) | collective-permute-done | bytes 32800 | tf_op jit(solution)/shard_map/ppermute | solution.py:33
  35.1 0.9 %collective-permute-done.16 = bf16[2,128,128]{2,1,0:T(8,128)(2,1)S(1)} collective-permute-done((bf16[2,128,128]{2,1,0:T(8,128)(2,1)S(1)}, bf16[2,128,128]{2,1,0:T(8,128)(2,1)S(1)}, u32[]{:S(2)}, u32[]{:S(2)}) %collective-permute-start.16) | collective-permute-done | bytes 65568 | tf_op jit(solution)/shard_map/ppermute | solution.py:27
  36.0 0.7 %maximum_select_fusion = f32[4,128,128]{2,1,0:T(8,128)} fusion(f32[2,128,128]{2,1,0:T(8,128)S(1)} %convert_multiply_fusion, f32[2,128,128]{2,1,0:T(8,128)S(1)} %convert_multiply_fusion.1, pred[]{:T(512)S(6)} %eq.3), kind=kLoop, calls=%fused_computation | loop fusion | flops 196608 | bytes 524289 | tf_op jit(solution)/shard_map/jit(_where)/select_n | solution.py:596
  (54 shorter events, 3.1 us)
Async XLA Ops:
  0.6 3.2 %copy-start.6 = (bf16[2,64,128]{2,1,0:T(8,128)(2,1)S(1)}, bf16[2,64,128]{2,1,0:T(8,128)(2,1)}, u32[]{:S(2)}) copy-start(bf16[2,64,128]{2,1,0:T(8,128)(2,1)} %refs_0_.1) | copy-start | bytes 98308
  0.6 3.1 %copy-start.3 = (bf16[128,128]{1,0:T(8,128)(2,1)S(1)}, bf16[128,128]{1,0:T(8,128)(2,1)}, u32[]{:S(2)}) copy-start(bf16[128,128]{1,0:T(8,128)(2,1)} %w_lin_ref.3) | copy-start | bytes 98308
  0.7 3.1 %copy-start.4 = (bf16[128,128]{1,0:T(8,128)(2,1)S(1)}, bf16[128,128]{1,0:T(8,128)(2,1)}, u32[]{:S(2)}) copy-start(bf16[128,128]{1,0:T(8,128)(2,1)} %w_gate_ref.3) | copy-start | bytes 98308
  0.7 3.1 %copy-start.1 = (bf16[128,128]{1,0:T(8,128)(2,1)S(1)}, bf16[128,128]{1,0:T(8,128)(2,1)}, u32[]{:S(2)}) copy-start(bf16[128,128]{1,0:T(8,128)(2,1)} %w_lin_ref.2) | copy-start | bytes 98308
  0.7 3.1 %copy-start.2 = (bf16[128,128]{1,0:T(8,128)(2,1)S(1)}, bf16[128,128]{1,0:T(8,128)(2,1)}, u32[]{:S(2)}) copy-start(bf16[128,128]{1,0:T(8,128)(2,1)} %w_gate_ref.2) | copy-start | bytes 98308
  0.7 5.2 %collective-permute-start = (bf16[2,64,128]{2,1,0:T(8,128)(2,1)}, bf16[2,64,128]{2,1,0:T(8,128)(2,1)S(1)}, u32[]{:S(2)}, u32[]{:S(2)}) collective-permute-start(bf16[2,64,128]{2,1,0:T(8,128)(2,1)} %refs_0_.1), channel_id=1, source_target_pairs={{0,8},{4,12},{8,0},{12,4},{16,24},{20,28},{24,16},{28,20},{1,9},{5... | collective-permute-start | bytes 98312 | tf_op jit(solution)/shard_map/ppermute | solution.py:27
  3.8 6.9 %copy-start = (bf16[64,32,128]{2,1,0:T(8,128)(2,1)S(1)}, bf16[64,32,128]{2,1,0:T(8,128)(2,1)}, u32[]{:S(2)}) copy-start(bf16[64,32,128]{2,1,0:T(8,128)(2,1)} %pair_ref.3) | copy-start | bytes 1572868
  3.9 6.7 %collective-permute-start.2 = (bf16[4,32,128]{2,1,0:T(8,128)(2,1)S(1)}, bf16[4,32,128]{2,1,0:T(8,128)(2,1)S(1)}, u32[]{:S(2)}, u32[]{:S(2)}) collective-permute-start(bf16[4,32,128]{2,1,0:T(8,128)(2,1)S(1)} %get-tuple-element.39), channel_id=1, source_target_pairs={{0,2},{1,3},{2,0},{3,1},{4,6},{5,7},{6,4},{7,5},{8,10},{9,11},{10,... | collective-permute-start | bytes 98312 | tf_op jit(solution)/shard_map/ppermute | solution.py:27
  5.9 4.6 %copy-start.7 = (s32[256]{0:T(256)S(1)}, s32[256]{0:T(256)}, u32[]{:S(2)}) copy-start(s32[256]{0:T(256)} %param.17) | copy-start | bytes 3076
  5.9 5.4 %collective-permute-start.1 = (bf16[4,64,128]{2,1,0:T(8,128)(2,1)S(1)}, bf16[4,64,128]{2,1,0:T(8,128)(2,1)S(1)}, u32[]{:S(2)}, u32[]{:S(2)}) collective-permute-start(bf16[4,64,128]{2,1,0:T(8,128)(2,1)S(1)} %constant_dynamic-update-slice_fusion.refs_0_), channel_id=1, source_target_pairs={{0,16},{4,20},{8,24},{12,28},{16,0},{20,4},{24,8},{28,12},{1,17},{... | collective-permute-start | bytes 196616 | tf_op jit(solution)/shard_map/ppermute | solution.py:27
  9.0 4.5 %collective-permute-start.4 = (bf16[4,64,128]{2,1,0:T(8,128)(2,1)S(1)}, bf16[4,64,128]{2,1,0:T(8,128)(2,1)S(1)}, u32[]{:S(2)}, u32[]{:S(2)}) collective-permute-start(bf16[4,64,128]{2,1,0:T(8,128)(2,1)S(1)} %constant_dynamic-update-slice_fusion.refs_0_), channel_id=1, source_target_pairs={{0,4},{4,0},{8,12},{12,8},{16,20},{20,16},{24,28},{28,24},{1,5},{5... | collective-permute-start | bytes 196616 | tf_op jit(solution)/shard_map/ppermute | solution.py:27
  10.6 2.6 %collective-permute-start.5 = (bf16[8,32,128]{2,1,0:T(8,128)(2,1)S(1)}, bf16[8,32,128]{2,1,0:T(8,128)(2,1)S(1)}, u32[]{:S(2)}, u32[]{:S(2)}) collective-permute-start(bf16[8,32,128]{2,1,0:T(8,128)(2,1)S(1)} %constant_dynamic-update-slice_fusion.2.even_ref), channel_id=1, source_target_pairs={{0,1},{1,0},{2,3},{3,2},{4,5},{5,4},{6,7},{7,6},{8,9},{9,8},{10,11... | collective-permute-start | bytes 196616 | tf_op jit(solution)/shard_map/ppermute | solution.py:27
  11.3 4.5 %collective-permute-start.3 = (bf16[4,64,128]{2,1,0:T(8,128)(2,1)S(1)}, bf16[4,64,128]{2,1,0:T(8,128)(2,1)S(1)}, u32[]{:S(2)}, u32[]{:S(2)}) collective-permute-start(bf16[4,64,128]{2,1,0:T(8,128)(2,1)S(1)} %collective-permute-done.1.refs_1_), channel_id=1, source_target_pairs={{0,4},{4,0},{8,12},{12,8},{16,20},{20,16},{24,28},{28,24},{1,5},{5... | collective-permute-start | bytes 196616 | tf_op jit(solution)/shard_map/ppermute | solution.py:27
  16.9 1.4 %collective-permute-start.6 = (f32[2,128,128]{2,1,0:T(8,128)S(1)}, f32[2,128,128]{2,1,0:T(8,128)S(1)}, u32[]{:S(2)}, u32[]{:S(2)}) collective-permute-start(f32[2,128,128]{2,1,0:T(8,128)S(1)} %get-tuple-element.55), channel_id=1, source_target_pairs={{0,1},{1,0},{2,3},{3,2},{4,5},{5,4},{6,7},{7,6},{8,9},{9,8},{10,11... | collective-permute-start | bytes 393224 | tf_op jit(solution)/shard_map/ppermute | solution.py:27
  18.4 6.2 %collective-permute-start.10 = (f32[2,4,32,128]{3,2,1,0:T(8,128)S(1)}, f32[2,4,32,128]{3,2,1,0:T(8,128)S(1)}, u32[]{:S(2)}, u32[]{:S(2)}) collective-permute-start(f32[2,4,32,128]{3,2,1,0:T(8,128)S(1)} %get-tuple-element.61), channel_id=1, source_target_pairs={{0,1},{1,0},{2,3},{3,2},{4,5},{5,4},{6,7},{7,6},{8,9},{9,8},{10,11... | collective-permute-start | bytes 393224 | tf_op jit(solution)/shard_map/ppermute | solution.py:27
  18.6 4.8 %collective-permute-start.7 = (bf16[128,128]{1,0:T(8,128)(2,1)S(1)}, bf16[128,128]{1,0:T(8,128)(2,1)S(1)}, u32[]{:S(2)}, u32[]{:S(2)}) collective-permute-start(bf16[128,128]{1,0:T(8,128)(2,1)S(1)} %get-tuple-element.59), channel_id=1, source_target_pairs={{0,6},{1,7},{2,4},{3,5},{4,2},{5,3},{6,0},{7,1},{8,14},{9,15},{10,... | collective-permute-start | bytes 98312 | tf_op jit(solution)/shard_map/ppermute | solution.py:33
  21.0 3.4 %collective-permute-start.8 = (bf16[128,128]{1,0:T(8,128)(2,1)S(1)}, bf16[128,128]{1,0:T(8,128)(2,1)S(1)}, u32[]{:S(2)}, u32[]{:S(2)}) collective-permute-start(bf16[128,128]{1,0:T(8,128)(2,1)S(1)} %get-tuple-element.60.d_ref), channel_id=1, source_target_pairs={{0,5},{1,4},{2,7},{3,6},{4,1},{5,0},{6,3},{7,2},{8,13},{9,12},{10,... | collective-permute-start | bytes 98312 | tf_op jit(solution)/shard_map/ppermute | solution.py:33
  21.2 3.3 %collective-permute-start.9 = (bf16[128,128]{1,0:T(8,128)(2,1)S(1)}, bf16[128,128]{1,0:T(8,128)(2,1)S(1)}, u32[]{:S(2)}, u32[]{:S(2)}) collective-permute-start(bf16[128,128]{1,0:T(8,128)(2,1)S(1)} %get-tuple-element.59), channel_id=1, source_target_pairs={{0,3},{1,2},{2,1},{3,0},{4,7},{5,6},{6,5},{7,4},{8,11},{9,10},{10,... | collective-permute-start | bytes 98312 | tf_op jit(solution)/shard_map/ppermute | solution.py:33
  24.6 4.4 %collective-permute-start.12 = (bf16[128,128]{1,0:T(8,128)(2,1)S(1)}, bf16[128,128]{1,0:T(8,128)(2,1)S(1)}, u32[]{:S(2)}, u32[]{:S(2)}) collective-permute-start(bf16[128,128]{1,0:T(8,128)(2,1)S(1)} %add_four.1), channel_id=1, source_target_pairs={{0,17},{1,16},{2,19},{3,18},{4,21},{5,20},{6,23},{7,22},{8,25},{9,... | collective-permute-start | bytes 98312 | tf_op jit(solution)/shard_map/ppermute | solution.py:33
  27.4 4.9 %collective-permute-start.11 = (bf16[1,4,32,128]{3,2,1,0:T(8,128)(2,1)S(1)}, bf16[1,4,32,128]{3,2,1,0:T(8,128)(2,1)S(1)}, u32[]{:S(2)}, u32[]{:S(2)}) collective-permute-start(bf16[1,4,32,128]{3,2,1,0:T(8,128)(2,1)S(1)} %get-tuple-element.66), channel_id=1, source_target_pairs={{0,3},{1,2},{2,1},{3,0},{4,7},{5,6},{6,5},{7,4},{8,11},{9,10},{10,... | collective-permute-start | bytes 98312 | tf_op jit(solution)/shard_map/ppermute | solution.py:33
  29.0 4.9 %collective-permute-start.13 = (bf16[128,128]{1,0:T(8,128)(2,1)S(1)}, bf16[128,128]{1,0:T(8,128)(2,1)S(1)}, u32[]{:S(2)}, u32[]{:S(2)}) collective-permute-start(bf16[128,128]{1,0:T(8,128)(2,1)S(1)} %add_convert_fusion.own_ref), channel_id=1, source_target_pairs={{0,10},{1,11},{2,8},{3,9},{4,14},{5,15},{6,12},{7,13},{8,2},{9,3},... | collective-permute-start | bytes 98312 | tf_op jit(solution)/shard_map/ppermute | solution.py:33
  31.3 3.4 %collective-permute-start.14 = (bf16[128,128]{1,0:T(8,128)(2,1)S(1)}, bf16[128,128]{1,0:T(8,128)(2,1)S(1)}, u32[]{:S(2)}, u32[]{:S(2)}) collective-permute-start(bf16[128,128]{1,0:T(8,128)(2,1)S(1)} %add_convert_fusion.own_ref), channel_id=1, source_target_pairs={{0,9},{1,8},{2,11},{3,10},{4,13},{5,12},{6,15},{7,14},{8,1},{9,0},... | collective-permute-start | bytes 98312 | tf_op jit(solution)/shard_map/ppermute | solution.py:33
  31.3 3.4 %collective-permute-start.15 = (bf16[128,128]{1,0:T(8,128)(2,1)S(1)}, bf16[128,128]{1,0:T(8,128)(2,1)S(1)}, u32[]{:S(2)}, u32[]{:S(2)}) collective-permute-start(bf16[128,128]{1,0:T(8,128)(2,1)S(1)} %add_convert_fusion.own_ref), channel_id=1, source_target_pairs={{0,3},{1,2},{2,1},{3,0},{4,7},{5,6},{6,5},{7,4},{8,11},{9,10},{10,... | collective-permute-start | bytes 98312 | tf_op jit(solution)/shard_map/ppermute | solution.py:33
  34.7 1.3 %collective-permute-start.16 = (bf16[2,128,128]{2,1,0:T(8,128)(2,1)S(1)}, bf16[2,128,128]{2,1,0:T(8,128)(2,1)S(1)}, u32[]{:S(2)}, u32[]{:S(2)}) collective-permute-start(bf16[2,128,128]{2,1,0:T(8,128)(2,1)S(1)} %join_sums.1), channel_id=1, source_target_pairs={{0,1},{1,0},{2,3},{3,2},{4,5},{5,4},{6,7},{7,6},{8,9},{9,8},{10,11... | collective-permute-start | bytes 196616 | tf_op jit(solution)/shard_map/ppermute | solution.py:27
  (2 other events, 5.0 us)
